TPU v7x, 256 devices: a whole 4x4x8 slice. The times are simulated.
256 devices in a mesh: lon: 16 (over y, x), lat: 8 (over z), lev: 2 (over core).
Axes of the slice: x: 4, y: 4, z: 8, core: 2. Of those that a mesh axis runs over, the one named last changes fastest.
Arguments:
- prognostic: float32 [3, 32, 256, 4096], P(None, 'lev', 'lat', 'lon'), may hold values from -6 to 6
- half_width: int32 [256], P('lat'), may hold values from 1 to 16, as said below
- filter_mask: int32 [256], P('lat'), may hold values from 0 to 1, as said below
- column_inverse: float32 [256, 32, 32], P('lat'), as said below
Outputs:
- new_state: float32 [3, 32, 256, 4096], P(None, 'lev', 'lat', 'lon')
Inputs may be any that keep to these rules, and one draw needn't show every extreme that they name: half_width rises with a row's distance from the equator: it is 1 on the two rows beside the equator and 16 on the two polar rows; on every other row it lies within one of 1 + (15) times the row's distance from the equator in rows, divided by 256/2 - 1 and rounded down. `filter_mask`: 1 on every row whose distance from the equator in rows is at least a cut drawn between 64 and 3 * 256/8 (rounded down); each other row is 1 with one chance in eight. `column_inverse`: one matrix for each latitude row, applied to each column of winds: diagonal entries from 0.5 to 1.5, every other entry of magnitude at most 0.9 / sqrt(32).
All inputs are finite; a program needn't handle non-finite values.
Results may differ from a plain program's by a relative error of at most 0.000059.
Values sent between devices are 32-bit elements; how exact they have to be, the bound alone decides.
No kernel may reach another device: no remote copies, remote signals or barrier semaphores. Data moves between devices by JAX's collectives and lax.ppermute only.
A program may use at most 192 MiB of HBM per device.

v0:
```python
import jax
import jax.numpy as jnp
from jax import lax
from jax.sharding import PartitionSpec as P

TIME_STEP = 0.5
VISCOSITY = 0.05
MERIDIONAL = 0.25


def with_halo(cells, sides, width):
    for axis, dim in sides:
        count = lax.axis_size(axis)
        head = lax.slice_in_dim(cells, 0, width, axis=dim)
        tail = lax.slice_in_dim(cells, cells.shape[dim] - width, cells.shape[dim], axis=dim)
        cells = jnp.concatenate(
            [
                lax.ppermute(tail, axis, [(i, (i + 1) % count) for i in range(count)]),
                cells,
                lax.ppermute(head, axis, [((i + 1) % count, i) for i in range(count)]),
            ],
            axis=dim,
        )
    return cells


def latitudes(global_rows, row_total):
    latitude_angle = -0.5 * jnp.pi + (global_rows + 0.5) * jnp.pi / row_total
    return (jnp.cos(latitude_angle), jnp.sin(latitude_angle))


def tendency(padded, cosine, sine):
    centre = padded[:, :, 1:-1, 1:-1]
    eastward = padded[:, :, 1:-1, 2:]
    westward = padded[:, :, 1:-1, :-2]
    northward = padded[:, :, 2:, 1:-1]
    southward = padded[:, :, :-2, 1:-1]
    zonal_factor = (0.25 / (cosine + 0.05))[:, None]
    coriolis = (0.5 * sine)[:, None]
    zonal_diff = eastward - westward
    merid_diff = northward - southward
    laplace_sum = eastward + westward + northward + southward - 4.0 * centre
    wind_east = -zonal_factor * zonal_diff[2] + coriolis * centre[1] + VISCOSITY * laplace_sum[0]
    wind_north = -MERIDIONAL * merid_diff[2] - coriolis * centre[0] + VISCOSITY * laplace_sum[1]
    height_tend = -zonal_factor * zonal_diff[0] - MERIDIONAL * merid_diff[1]
    return jnp.stack([wind_east, wind_north, height_tend])


def filter_weight(distance, half_cells, block_width):
    reach_cells = (half_cells * block_width).astype(jnp.float32)
    return jnp.where(2.0 * distance <= reach_cells, 1.0, 0.0)


def per_device(prognostic, half_width, filter_mask, column_inverse):
    field_count, level_count, row_count, block_width = prognostic.shape
    lon_devices = lax.axis_size("lon")
    lat_devices = lax.axis_size("lat")
    total_width = block_width * lon_devices
    lat_index = lax.axis_index("lat")
    global_rows = (lat_index * row_count + jnp.arange(row_count)).astype(jnp.float32)
    cosine, sine = latitudes(global_rows, row_count * lat_devices)
    padded = with_halo(prognostic, (("lon", 3), ("lat", 2)), 1)
    lower_keep = jnp.where(lat_index == 0, 0.0, 1.0).astype(jnp.float32)
    upper_keep = jnp.where(lat_index == lat_devices - 1, 0.0, 1.0).astype(jnp.float32)
    padded = jnp.concatenate(
        [padded[:, :, :1] * lower_keep, padded[:, :, 1:-1], padded[:, :, -1:] * upper_keep], axis=2
    )
    tendencies = tendency(padded, cosine, sine)
    own_cols = lax.axis_index("lon") * block_width + jnp.arange(block_width)
    all_offsets = jnp.arange(total_width)
    cycle_distance = jnp.minimum(all_offsets, total_width - all_offsets).astype(jnp.float32)
    normalizer = jnp.sum(
        filter_weight(cycle_distance[None, :], half_width[:, None], block_width), axis=1
    )
    row_reach = half_width[:, None, None]

    def pair_distance(source_cols, target_cols):
        difference = (source_cols[:, None] - target_cols[None, :]) % total_width
        return jnp.minimum(difference, total_width - difference).astype(jnp.float32)

    segment = lax.all_gather(tendencies, "lon", axis=3, tiled=True)
    seg_width = segment.shape[3]
    block_total = seg_width // block_width
    pieces = jnp.moveaxis(
        segment.reshape(field_count, level_count, row_count, block_total, block_width), 3, 0
    )

    def one_block(carry, inputs):
        values, block_id = inputs
        source_cols = block_id * block_width + jnp.arange(block_width)
        weights = filter_weight(pair_distance(source_cols, own_cols)[None], row_reach, block_width)
        return (
            carry + jnp.einsum("fljp,jpb->fljb", values, weights, precision=lax.Precision.HIGHEST),
            None,
        )

    result, _ = lax.scan(
        one_block, jnp.zeros(tendencies.shape, jnp.float32), (pieces, jnp.arange(block_total))
    )
    smooth = result / normalizer[None, None, :, None]
    chosen = jnp.where((filter_mask == 1)[None, None, :, None], smooth, tendencies)
    updated = prognostic + TIME_STEP * chosen
    wind_pair = updated[:2]
    solved = jnp.einsum(
        "jlm,fmjx->fljx",
        column_inverse,
        lax.all_to_all(wind_pair, "lev", split_axis=3, concat_axis=1, tiled=True),
        precision=lax.Precision.HIGHEST,
    )
    blended = lax.all_to_all(solved, "lev", split_axis=1, concat_axis=3, tiled=True)
    return jnp.concatenate([blended, updated[2:]], axis=0)


def solution(mesh):
    placed = (P(None, "lev", "lat", "lon"), P("lat"), P("lat"), P("lat", None, None))
    return jax.shard_map(
        per_device,
        mesh=mesh,
        in_specs=placed,
        out_specs=P(None, "lev", "lat", "lon"),
        check_vma=False,
    )
```

profile of v0, /device:TPU:96, one launch (start us, length us, event | category | flops | bytes accessed | tf_op | source)
XLA Modules:
  0.0 479.8 jit_solution(9390244759573597997)
XLA Ops:
  8.6 5.3 %collective-permute-start = (f32[3,16,32,1]{2,1,3,0:T(8,128)S(1)}, f32[3,16,32,1]{2,1,3,0:T(8,128)S(1)}, u32[]{:S(2)}, u32[]{:S(2)}) collective-permute-start(f32[3,16,32,1]{2,1,3,0:T(8,128)S(1)} %copy.50), channel_id=1, source_target_pairs={{16,0},{32,16},{48,32},{64,48},{80,64},{96,80},{112,96},{128,112},... | collective-permute-start | bytes 18440 | tf_op jit(solution)/shard_map/ppermute | solution.py:20
  14.3 2.3 copy.43
  17.1 4.4 collective-permute-done.1
  23.6 3.2 collective-permute-start.3
  28.8 3.9 collective-permute-done.2
  32.7 3.6 multiply_subtract_fusion
  40.2 162.7 %all-gather.2.cloned.1.call-done = f32[3,16,32,4096]{3,1,2,0:T(8,128)} async-done(((f32[3,16,32,256]{3,1,2,0:T(8,128)}), f32[3,16,32,4096]{3,1,2,0:T(8,128)}) %all-gather.2.cloned.1.call-update) | async-done | bytes 25165840 | tf_op jit(solution)/shard_map/all_gather | solution.py:81
  202.8 15.4 %copy.52 = f32[192,8,16,256]{3,2,1,0:T(8,128)S(1)} copy(f32[192,8,16,256]{3,1,2,0:T(8,128)} %bitcast.54) | data formatting | bytes 50331648
  218.2 28.1 %copy.62 = f32[3,16,32,16,256]{4,1,0,2,3:T(8,128)} copy(f32[3,16,32,16,256]{4,3,1,2,0:T(8,128)S(1)} %bitcast.50) | data formatting | bytes 50331648 | tf_op jit(solution)/shard_map/reshape | solution.py:85
  246.3 188.7 %while.13 = (s32[]{:T(128)}, f32[3,16,32,256]{3,1,0,2:T(8,128)S(1)}, s32[16]{0:T(128)S(1)}, s32[32,1,1]{0,2,1:T(1,128)S(1)}, f32[16,3,16,32,256]{4,2,1,3,0:T(8,1...) while((s32[]{:T(128)}, f32[3,16,32,256]{3,1,0,2:T(8,128)S(1)}, s32[16]{0:T(128)S(1)}, ...), condition=%wide.region_1.2_spmd.clone, body=%wide.region_0.1_spmd.clone.sunk | while | flops 1213989504 | bytes 11538955 | solution.py:97
  249.3 6.8 %fusion.37 = f32[32,256,48]{1,2,0} fusion(f32[32,256,48]{1,2,0:T(8,128)S(1)} %bitcast.53, f32[256,256]{1,0:T(8,128)S(1)} %fusion.36, f32[32]{0:T(128)S(1)} %convert_bitcast_fusion.2), kind=kOutput, calls=%fused_computation.1.clone.1 | convolution fusion | flops 1212153856 | bytes 3408000 | tf_op jit(solution)/shard_map/while
  256.1 1.9 select_add_fusion.2
  261.1 6.8 %fusion.37 = f32[32,256,48]{1,2,0} fusion(f32[32,256,48]{1,2,0:T(8,128)S(1)} %bitcast.53, f32[256,256]{1,0:T(8,128)S(1)} %fusion.36, f32[32]{0:T(128)S(1)} %convert_bitcast_fusion.2), kind=kOutput, calls=%fused_computation.1.clone.1 | convolution fusion | flops 1212153856 | bytes 3408000 | tf_op jit(solution)/shard_map/while
  267.9 1.9 select_add_fusion.2
  272.9 6.8 %fusion.37 = f32[32,256,48]{1,2,0} fusion(f32[32,256,48]{1,2,0:T(8,128)S(1)} %bitcast.53, f32[256,256]{1,0:T(8,128)S(1)} %fusion.36, f32[32]{0:T(128)S(1)} %convert_bitcast_fusion.2), kind=kOutput, calls=%fused_computation.1.clone.1 | convolution fusion | flops 1212153856 | bytes 3408000 | tf_op jit(solution)/shard_map/while
  279.7 1.9 select_add_fusion.2
  284.7 6.8 %fusion.37 = f32[32,256,48]{1,2,0} fusion(f32[32,256,48]{1,2,0:T(8,128)S(1)} %bitcast.53, f32[256,256]{1,0:T(8,128)S(1)} %fusion.36, f32[32]{0:T(128)S(1)} %convert_bitcast_fusion.2), kind=kOutput, calls=%fused_computation.1.clone.1 | convolution fusion | flops 1212153856 | bytes 3408000 | tf_op jit(solution)/shard_map/while
  291.5 1.9 select_add_fusion.2
  296.5 6.8 %fusion.37 = f32[32,256,48]{1,2,0} fusion(f32[32,256,48]{1,2,0:T(8,128)S(1)} %bitcast.53, f32[256,256]{1,0:T(8,128)S(1)} %fusion.36, f32[32]{0:T(128)S(1)} %convert_bitcast_fusion.2), kind=kOutput, calls=%fused_computation.1.clone.1 | convolution fusion | flops 1212153856 | bytes 3408000 | tf_op jit(solution)/shard_map/while
  303.3 1.9 select_add_fusion.2
  308.3 6.8 %fusion.37 = f32[32,256,48]{1,2,0} fusion(f32[32,256,48]{1,2,0:T(8,128)S(1)} %bitcast.53, f32[256,256]{1,0:T(8,128)S(1)} %fusion.36, f32[32]{0:T(128)S(1)} %convert_bitcast_fusion.2), kind=kOutput, calls=%fused_computation.1.clone.1 | convolution fusion | flops 1212153856 | bytes 3408000 | tf_op jit(solution)/shard_map/while
  315.1 1.9 select_add_fusion.2
  320.1 6.8 %fusion.37 = f32[32,256,48]{1,2,0} fusion(f32[32,256,48]{1,2,0:T(8,128)S(1)} %bitcast.53, f32[256,256]{1,0:T(8,128)S(1)} %fusion.36, f32[32]{0:T(128)S(1)} %convert_bitcast_fusion.2), kind=kOutput, calls=%fused_computation.1.clone.1 | convolution fusion | flops 1212153856 | bytes 3408000 | tf_op jit(solution)/shard_map/while
  326.9 1.9 select_add_fusion.2
  331.9 6.8 %fusion.37 = f32[32,256,48]{1,2,0} fusion(f32[32,256,48]{1,2,0:T(8,128)S(1)} %bitcast.53, f32[256,256]{1,0:T(8,128)S(1)} %fusion.36, f32[32]{0:T(128)S(1)} %convert_bitcast_fusion.2), kind=kOutput, calls=%fused_computation.1.clone.1 | convolution fusion | flops 1212153856 | bytes 3408000 | tf_op jit(solution)/shard_map/while
  338.7 1.9 select_add_fusion.2
  343.7 6.8 %fusion.37 = f32[32,256,48]{1,2,0} fusion(f32[32,256,48]{1,2,0:T(8,128)S(1)} %bitcast.53, f32[256,256]{1,0:T(8,128)S(1)} %fusion.36, f32[32]{0:T(128)S(1)} %convert_bitcast_fusion.2), kind=kOutput, calls=%fused_computation.1.clone.1 | convolution fusion | flops 1212153856 | bytes 3408000 | tf_op jit(solution)/shard_map/while
  350.5 1.9 select_add_fusion.2
  355.5 6.8 %fusion.37 = f32[32,256,48]{1,2,0} fusion(f32[32,256,48]{1,2,0:T(8,128)S(1)} %bitcast.53, f32[256,256]{1,0:T(8,128)S(1)} %fusion.36, f32[32]{0:T(128)S(1)} %convert_bitcast_fusion.2), kind=kOutput, calls=%fused_computation.1.clone.1 | convolution fusion | flops 1212153856 | bytes 3408000 | tf_op jit(solution)/shard_map/while
  362.3 1.9 select_add_fusion.2
  367.3 6.8 %fusion.37 = f32[32,256,48]{1,2,0} fusion(f32[32,256,48]{1,2,0:T(8,128)S(1)} %bitcast.53, f32[256,256]{1,0:T(8,128)S(1)} %fusion.36, f32[32]{0:T(128)S(1)} %convert_bitcast_fusion.2), kind=kOutput, calls=%fused_computation.1.clone.1 | convolution fusion | flops 1212153856 | bytes 3408000 | tf_op jit(solution)/shard_map/while
  374.1 1.9 select_add_fusion.2
  379.0 6.8 %fusion.37 = f32[32,256,48]{1,2,0} fusion(f32[32,256,48]{1,2,0:T(8,128)S(1)} %bitcast.53, f32[256,256]{1,0:T(8,128)S(1)} %fusion.36, f32[32]{0:T(128)S(1)} %convert_bitcast_fusion.2), kind=kOutput, calls=%fused_computation.1.clone.1 | convolution fusion | flops 1212153856 | bytes 3408000 | tf_op jit(solution)/shard_map/while
  385.8 1.9 select_add_fusion.2
  390.8 6.8 %fusion.37 = f32[32,256,48]{1,2,0} fusion(f32[32,256,48]{1,2,0:T(8,128)S(1)} %bitcast.53, f32[256,256]{1,0:T(8,128)S(1)} %fusion.36, f32[32]{0:T(128)S(1)} %convert_bitcast_fusion.2), kind=kOutput, calls=%fused_computation.1.clone.1 | convolution fusion | flops 1212153856 | bytes 3408000 | tf_op jit(solution)/shard_map/while
  397.6 1.9 select_add_fusion.2
  402.6 6.8 %fusion.37 = f32[32,256,48]{1,2,0} fusion(f32[32,256,48]{1,2,0:T(8,128)S(1)} %bitcast.53, f32[256,256]{1,0:T(8,128)S(1)} %fusion.36, f32[32]{0:T(128)S(1)} %convert_bitcast_fusion.2), kind=kOutput, calls=%fused_computation.1.clone.1 | convolution fusion | flops 1212153856 | bytes 3408000 | tf_op jit(solution)/shard_map/while
  414.4 6.8 %fusion.37 = f32[32,256,48]{1,2,0} fusion(f32[32,256,48]{1,2,0:T(8,128)S(1)} %bitcast.53, f32[256,256]{1,0:T(8,128)S(1)} %fusion.36, f32[32]{0:T(128)S(1)} %convert_bitcast_fusion.2), kind=kOutput, calls=%fused_computation.1.clone.1 | convolution fusion | flops 1212153856 | bytes 3408000 | tf_op jit(solution)/shard_map/while
  421.2 1.9 select_add_fusion.2
  426.2 6.8 %fusion.37 = f32[32,256,48]{1,2,0} fusion(f32[32,256,48]{1,2,0:T(8,128)S(1)} %bitcast.53, f32[256,256]{1,0:T(8,128)S(1)} %fusion.36, f32[32]{0:T(128)S(1)} %convert_bitcast_fusion.2), kind=kOutput, calls=%fused_computation.1.clone.1 | convolution fusion | flops 1212153856 | bytes 3408000 | tf_op jit(solution)/shard_map/while
  435.0 2.8 fusion.16
  438.9 4.4 copy.44
  443.3 3.5 reshape.97
  446.8 4.6 all_to_all.36
  451.9 4.0 reduce
  455.9 3.6 reshape.98
  459.5 3.6 copy.45
  465.0 4.6 all_to_all.37
  (128 shorter events, 59.2 us)
Async XLA Ops:
  6.5 456.5 %copy-start = (f32[32,32,32]{2,1,0:T(8,128)S(1)}, f32[32,32,32]{2,1,0:T(8,128)}, u32[]{:S(2)}) copy-start(f32[32,32,32]{2,1,0:T(8,128)} %param.9) | copy-start | bytes 393220
  6.5 196.3 %all-gather.2.cloned.1.call-start = ((), (), s32[]{:S(2)}) async-start(), calls=%async_computation.2 | async-start | bytes 26738688 | tf_op jit(solution)/shard_map/all_gather | solution.py:81
  8.6 8.0 %collective-permute-start = (f32[3,16,32,1]{2,1,3,0:T(8,128)S(1)}, f32[3,16,32,1]{2,1,3,0:T(8,128)S(1)}, u32[]{:S(2)}, u32[]{:S(2)}) collective-permute-start(f32[3,16,32,1]{2,1,3,0:T(8,128)S(1)} %copy.50), channel_id=1, source_target_pairs={{16,0},{32,16},{48,32},{64,48},{80,64},{96,80},{112,96},{128,112},... | collective-permute-start | bytes 18440 | tf_op jit(solution)/shard_map/ppermute | solution.py:20
  14.2 7.2 %collective-permute-start.1 = (f32[3,16,32,1]{2,1,3,0:T(8,128)S(1)}, f32[3,16,32,1]{2,1,3,0:T(8,128)S(1)}, u32[]{:S(2)}, u32[]{:S(2)}) collective-permute-start(f32[3,16,32,1]{2,1,3,0:T(8,128)S(1)} %copy.51), channel_id=1, source_target_pairs={{0,16},{16,32},{32,48},{48,64},{64,80},{80,96},{96,112},{112,128},... | collective-permute-start | bytes 18440 | tf_op jit(solution)/shard_map/ppermute | solution.py:18
  23.6 5.2 %collective-permute-start.3 = (f32[3,16,1,258]{3,1,2,0:T(8,128)S(1)}, f32[3,16,1,258]{3,1,2,0:T(8,128)S(1)}, u32[]{:S(2)}, u32[]{:S(2)}) collective-permute-start(f32[3,16,1,258]{3,1,2,0:T(8,128)S(1)} %get-tuple-element.127), channel_id=1, source_target_pairs={{0,2},{2,4},{4,6},{6,8},{8,10},{10,12},{12,14},{14,0},{1,3},{3,5},... | collective-permute-start | bytes 148616 | tf_op jit(solution)/shard_map/ppermute | solution.py:18
  26.8 5.8 %collective-permute-start.2 = (f32[3,16,1,258]{3,1,2,0:T(8,128)S(1)}, f32[3,16,1,258]{3,1,2,0:T(8,128)S(1)}, u32[]{:S(2)}, u32[]{:S(2)}) collective-permute-start(f32[3,16,1,258]{3,1,2,0:T(8,128)S(1)} %get-tuple-element.128), channel_id=1, source_target_pairs={{2,0},{4,2},{6,4},{8,6},{10,8},{12,10},{14,12},{0,14},{3,1},{5,3},... | collective-permute-start | bytes 148616 | tf_op jit(solution)/shard_map/ppermute | solution.py:20
  32.7 3.6 copy-start.1
  37.1 0.8 copy-start.3
  39.2 0.7 copy-start.5
  39.2 0.9 copy-start.4
  437.8 1.1 copy-start.2
  470.3 1.0 slice-start
Sparse Core Ops, SparseCore 0:
  39.4 163.4 all-gather.1
where the time goes:
time: 484 us; the launch traced here: 480 us
  waiting for transfers between devices  173 us (36%)
  matrix products  110 us (23%)
  local copies, waits for them, and re-layouts  105 us (22%)
  other arithmetic  49.7 us (10%)
  between operations  13.6 us (3%)
  loops' own time  11.1 us (2%)
  blocking collectives  9.15 us (2%)
  starting transfers between devices  8.81 us (2%)
    all_gather x1, waiting for transfers between devices, per_device(): segment = lax.all_gather(tendencies, 'lon', axis=3, tiled=True)  163 us
    while x16, matrix products  109 us
    dynamic_slice x32, local copies, waits for them, and re-layouts, per_device(): lax.scan(one_block, jnp.zeros(tendencies.shape, jnp.float32), (pieces, jn...  33.9 us
    add x16, other arithmetic, one_block(): carry + jnp.einsum('fljp,jpb->fljb', values, weights, precision=lax.Preci...  31.2 us
    reshape x1, local copies, waits for them, and re-layouts, per_device(): segment.reshape(field_count, level_count, row_count, block_total, block_w...  28.1 us
    unnamed x18, local copies, waits for them, and re-layouts  27.9 us
    another operation x1, loops' own time, per_device(): lax.scan(one_block, jnp.zeros(tendencies.shape, jnp.float32), (pieces, jn...  11.1 us
  transfers between devices with their start and end apart: 5, of which 4 were waited for; matrix products, arithmetic and copies ran while one was open for 1% of the time, Pallas kernels for 0%

commit v1 on v0

v1 whole, which is shorter than its diff:
```python
import functools

import jax
import jax.numpy as jnp
from jax import lax
from jax.experimental import pallas as pl
from jax.experimental.pallas import tpu as pltpu
from jax.sharding import PartitionSpec as P

TIME_STEP = 0.5
VISCOSITY = 0.05
MERIDIONAL = 0.25
HALF = 128
VMEM_LIMIT = 32 * 1024 * 1024


def latitudes(global_rows, row_total):
    latitude_angle = -0.5 * jnp.pi + (global_rows + 0.5) * jnp.pi / row_total
    return (jnp.cos(latitude_angle), jnp.sin(latitude_angle))


def tendency_kernel(prog, zonal, coriolis, south, north, west, east, out, turn):
    _, levels, rows, width = prog.shape
    row_id = lax.broadcasted_iota(jnp.int32, (rows, width), 0)
    col_id = lax.broadcasted_iota(jnp.int32, (rows, width), 1)
    first_row, last_row = row_id == 0, row_id == rows - 1
    first_col, last_col = col_id == 0, col_id == width - 1
    zon, cor = zonal[...], coriolis[...]
    for l in range(levels):
        centre, dx, dy, sx, sy = [], [], [], [], []
        for f in range(3):
            c = f * levels + l
            here = prog[f, l]
            e = jnp.where(last_col, east[:, c : c + 1], pltpu.roll(here, width - 1, 1))
            w = jnp.where(first_col, west[:, c : c + 1], pltpu.roll(here, 1, 1))
            n = jnp.where(last_row, north[c : c + 1, :], pltpu.roll(here, rows - 1, 0))
            s = jnp.where(first_row, south[c : c + 1, :], pltpu.roll(here, 1, 0))
            centre.append(here)
            dx.append(e - w)
            dy.append(n - s)
            sx.append(e + w + n + s - 4.0 * here)
        tends = (
            -zon * dx[2] + cor * centre[1] + VISCOSITY * sx[0],
            -MERIDIONAL * dy[2] - cor * centre[0] + VISCOSITY * sx[1],
            -zon * dx[0] - MERIDIONAL * dy[1],
        )
        for f in range(3):
            for half in range(2):
                turn[f, half, l * rows : (l + 1) * rows, :] = tends[f][:, half * HALF : (half + 1) * HALF]
    for j in range(rows):
        for f in range(3):
            for half in range(2):
                out[j, f * levels : (f + 1) * levels, half * HALF : (half + 1) * HALF] = turn[
                    f, half, pl.ds(j, levels, stride=rows), :
                ]


def split3(x):
    hi = x.astype(jnp.bfloat16)
    rest = x - hi.astype(jnp.float32)
    mid = rest.astype(jnp.bfloat16)
    return hi, mid, (rest - mid.astype(jnp.float32)).astype(jnp.bfloat16)


def split2(x):
    hi = x.astype(jnp.bfloat16)
    return hi, (x - hi.astype(jnp.float32)).astype(jnp.bfloat16)


def mix_operand(matrix):
    hi, lo = split2(matrix)
    return jnp.concatenate([hi, hi, lo], axis=1)


def filter_kernel(
    own_row, half_width, filter_mask, tend, matrix, out, halves, parts
):
    blocks, lev_parts, chans, _ = tend.shape
    levels = chans // 3
    count = 2 * blocks
    both = lev_parts * chans
    row = own_row[0]
    reach = half_width[row]
    whole = reach == count // 2
    norm = jnp.where(whole, count * HALF, 2 * HALF * reach + 1).astype(jnp.float32)
    filtered = filter_mask[row] == 1
    edge_gain = jnp.where(whole, 0.0, 1.0).astype(jnp.float32)

    for g in range(count):
        b, half = divmod(g, 2)
        for part in range(lev_parts):
            halves[g, part * chans : (part + 1) * chans, :] = tend[b, part, :, half * HALF : (half + 1) * HALF]

    def add_half(i, total):
        return total + halves[lax.rem(i + count - reach, count)]

    window = lax.fori_loop(0, 2 * reach, add_half, jnp.zeros((both, HALF), jnp.float32))
    for g in range(count):
        ahead = halves[lax.rem(g + reach, count)]
        behind = halves[lax.rem(g + count - reach, count)]
        change = ahead - behind
        for k, (a, b) in enumerate(zip(split3(change), split3(window))):
            parts[k, g * both : (g + 1) * both, :HALF] = a
            parts[k, g * both : (g + 1) * both, HALF:] = b
        window = window + change

    src = lax.broadcasted_iota(jnp.int32, (2 * HALF, HALF), 0)
    dst = lax.broadcasted_iota(jnp.int32, (2 * HALF, HALF), 1)
    sums = jnp.where((src <= dst) | (src >= HALF), 1.0, 0.0).astype(jnp.bfloat16)
    mixer = mix_operand(matrix[0])
    group = 4
    scale = TIME_STEP / norm
    for g0 in range(0, count, group):
        lo, hi = g0 * both, (g0 + group) * both
        box = (
            jnp.dot(parts[2, lo:hi, :], sums, preferred_element_type=jnp.float32)
            + jnp.dot(parts[1, lo:hi, :], sums, preferred_element_type=jnp.float32)
            + jnp.dot(parts[0, lo:hi, :], sums, preferred_element_type=jnp.float32)
        )
        for pair in range(group // 2):
            b = g0 // 2 + pair
            steps = []
            for half in range(2):
                g = 2 * b + half
                at = (g - g0) * both
                behind = halves[lax.rem(g + count - reach, count)]
                smooth = (box[at : at + both] + edge_gain * behind) * scale
                steps.append(jnp.where(filtered, smooth, TIME_STEP * halves[g]))
            step = jnp.concatenate(steps, axis=1)
            for f in range(2):
                wind = jnp.concatenate(
                    [step[p * chans + f * levels : p * chans + (f + 1) * levels] for p in range(lev_parts)], axis=0
                )
                wind_hi, wind_lo = split2(wind)
                mixed = jnp.dot(
                    mixer,
                    jnp.concatenate([wind_hi, wind_lo, wind_hi], axis=0),
                    preferred_element_type=jnp.float32,
                )
                for p in range(lev_parts):
                    out[b, p, f * levels : (f + 1) * levels, :] = mixed[p * levels : (p + 1) * levels]
            for p in range(lev_parts):
                out[b, p, 2 * levels :, :] = step[p * chans + 2 * levels : (p + 1) * chans]


def mix_kernel(own_part, own, other, matrix, out):
    _, levels, rows, width = own.shape
    mine = own.reshape(2, levels * rows, width)
    theirs = other.reshape(2, levels * rows, width)
    lower = own_part[0] == 0
    for j in range(rows):
        mixer = mix_operand(matrix[j])
        winds = []
        for f in range(2):
            a = mine[f, pl.ds(j, levels, stride=rows), :]
            b = theirs[f, pl.ds(j, levels, stride=rows), :]
            winds.append(jnp.concatenate([jnp.where(lower, a, b), jnp.where(lower, b, a)], axis=0))
        wind_hi, wind_lo = split2(jnp.concatenate(winds, axis=1))
        mixed = jnp.dot(
            mixer, jnp.concatenate([wind_hi, wind_lo, wind_hi], axis=0), preferred_element_type=jnp.float32
        )
        kept = jnp.where(lower, mixed[:levels], mixed[levels:])
        for f in range(2):
            out[j, f * levels : (f + 1) * levels, :] = kept[:, f * width : (f + 1) * width]


def finish_kernel(step, mixed, height, out):
    _, levels, rows, width = out.shape
    flat = out.reshape(3, levels * rows, width)
    for j in range(rows):
        for f in range(2):
            at = slice(f * levels, (f + 1) * levels)
            flat[f, pl.ds(j, levels, stride=rows), :] = step[j, at, :] + mixed[j, at, :]
        flat[2, pl.ds(j, levels, stride=rows), :] = step[j, 2 * levels :, :]
    out[2] = out[2] + height[0]


def per_device(prognostic, half_width, filter_mask, column_inverse):
    fields, levels, rows, width = prognostic.shape
    lon_devices, lat_devices, lev_devices = (lax.axis_size(a) for a in ("lon", "lat", "lev"))
    lon_index, lat_index, lev_index = (lax.axis_index(a) for a in ("lon", "lat", "lev"))
    chans = fields * levels
    params = pltpu.CompilerParams(vmem_limit_bytes=VMEM_LIMIT)

    east_edge = prognostic[:, :, :, width - 1].reshape(chans, rows).T
    west_edge = prognostic[:, :, :, 0].reshape(chans, rows).T
    west = lax.ppermute(east_edge, "lon", [(i, (i + 1) % lon_devices) for i in range(lon_devices)])
    east = lax.ppermute(west_edge, "lon", [((i + 1) % lon_devices, i) for i in range(lon_devices)])
    south = lax.ppermute(
        prognostic[:, :, rows - 1, :].reshape(chans, width), "lat", [(i, i + 1) for i in range(lat_devices - 1)]
    )
    north = lax.ppermute(
        prognostic[:, :, 0, :].reshape(chans, width), "lat", [(i + 1, i) for i in range(lat_devices - 1)]
    )
    other = lax.ppermute(prognostic[:2], "lev", [(0, 1), (1, 0)])

    global_rows = (lat_index * rows + jnp.arange(rows)).astype(jnp.float32)
    cosine, sine = latitudes(global_rows, rows * lat_devices)
    zonal = jnp.broadcast_to((0.25 / (cosine + 0.05))[:, None], (rows, width))
    coriolis = jnp.broadcast_to((0.5 * sine)[:, None], (rows, width))

    with jax.named_scope("tendencies"):
        tend = pl.pallas_call(
            tendency_kernel,
            out_shape=jax.ShapeDtypeStruct((rows, chans, width), jnp.float32),
            scratch_shapes=[pltpu.VMEM((fields, 2, levels * rows, HALF), jnp.float32)],
            compiler_params=params,
        )(prognostic, zonal, coriolis, south, north, west, east)

    whole_rows = lax.all_to_all(tend, ("lon", "lev"), 0, 0, tiled=True)

    own_row = (lon_index * lev_devices + lev_index).astype(jnp.int32).reshape(1)
    blocked = (lon_devices, lev_devices, chans, width)
    count = 2 * lon_devices
    both = lev_devices * chans
    with jax.named_scope("row_filter"):
        stepped = pl.pallas_call(
            filter_kernel,
            out_shape=jax.ShapeDtypeStruct(blocked, jnp.float32),
            grid_spec=pltpu.PrefetchScalarGridSpec(
                num_scalar_prefetch=3,
                grid=(1,),
                in_specs=[
                    pl.BlockSpec(blocked, lambda i, *_: (0, 0, 0, 0)),
                    pl.BlockSpec(
                        (1,) + column_inverse.shape[1:], lambda i, own_row, *_: (own_row[0], 0, 0)
                    ),
                ],
                out_specs=pl.BlockSpec(blocked, lambda i, *_: (0, 0, 0, 0)),
                scratch_shapes=[
                    pltpu.VMEM((count, both, HALF), jnp.float32),
                    pltpu.VMEM((3, count * both, 2 * HALF), jnp.bfloat16),
                ],
            ),
            compiler_params=params,
        )(own_row, half_width, filter_mask, whole_rows.reshape(blocked), column_inverse)

    returned = lax.all_to_all(
        stepped.reshape(rows, chans, width), ("lon", "lev"), 0, 0, tiled=True
    )

    tile = (levels, rows, HALF)
    with jax.named_scope("wind_mix"):
        mixed = pl.pallas_call(
            mix_kernel,
            out_shape=jax.ShapeDtypeStruct((rows, 2 * levels, width), jnp.float32),
            grid_spec=pltpu.PrefetchScalarGridSpec(
                num_scalar_prefetch=1,
                grid=(width // HALF,),
                in_specs=[
                    pl.BlockSpec((2,) + tile, lambda i, *_: (0, 0, 0, i)),
                    pl.BlockSpec((2,) + tile, lambda i, *_: (0, 0, 0, i)),
                    pl.BlockSpec(column_inverse.shape, lambda i, *_: (0, 0, 0)),
                ],
                out_specs=pl.BlockSpec((rows, 2 * levels, HALF), lambda i, *_: (0, 0, i)),
            ),
            compiler_params=params,
        )(lev_index.astype(jnp.int32).reshape(1), prognostic, other, column_inverse)

    with jax.named_scope("finish"):
        return pl.pallas_call(
            finish_kernel,
            out_shape=jax.ShapeDtypeStruct(prognostic.shape, jnp.float32),
            grid=(width // HALF,),
            in_specs=[
                pl.BlockSpec((rows, chans, HALF), lambda i: (0, 0, i)),
                pl.BlockSpec((rows, 2 * levels, HALF), lambda i: (0, 0, i)),
                pl.BlockSpec((1,) + tile, lambda i: (2, 0, 0, i)),
            ],
            out_specs=pl.BlockSpec((fields,) + tile, lambda i: (0, 0, 0, i)),
            compiler_params=params,
        )(returned, mixed, prognostic)


def solution(mesh):
    placed = (P(None, "lev", "lat", "lon"), P("lat"), P("lat"), P("lat", None, None))
    return jax.shard_map(
        per_device,
        mesh=mesh,
        in_specs=placed,
        out_specs=P(None, "lev", "lat", "lon"),
        check_vma=False,
    )
```

time: 484 us -> 91.2 us (0.19)
  waiting for transfers between devices: 173 us -> 45.9 us
  matrix products: 110 us -> 0 us
  local copies, waits for them, and re-layouts: 105 us -> 8.17 us
  other arithmetic: 49.7 us -> 0.05 us
  starting transfers between devices: 8.81 us -> 23.8 us
  between operations: 13.6 us -> 0.13 us
  Pallas kernels: 0 us -> 12.6 us
  loops' own time: 11.1 us -> 0 us
  blocking collectives: 9.15 us -> 0 us
    all_gather x1 -> x0, waiting for transfers between devices: 163 us -> none  [per_device(): segment = lax.all_gather(tendencies, 'lon', axis=3, tiled=True)]
    while x16 -> x0, matrix products: 109 us -> none
    all_to_all x0 -> x2, waiting for transfers between devices: none -> 41.8 us  [the longest x1 23.9 us: per_device(): whole_rows = lax.all_to_all(tend, ('lon', 'lev'), 0, 0, tiled=True)]
    add x34 -> x0, other arithmetic: 34.4 us -> none  [the longest x16 31.2 us: one_block(): carry + jnp.einsum('fljp,jpb->fljb', values, weights, precision=lax.Preci...]
    dynamic_slice x32 -> x0, local copies, waits for them, and re-layouts: 33.9 us -> none  [per_device(): lax.scan(one_block, jnp.zeros(tendencies.shape, jnp.float32), (pieces, jn...]
    reshape x1 -> x0, local copies, waits for them, and re-layouts: 28.1 us -> none  [per_device(): segment.reshape(field_count, level_count, row_count, block_total, block_w...]
    unnamed x18, local copies, waits for them, and re-layouts: 27.9 us -> 4.41 us
    pallas_call x0 -> x4, Pallas kernels: none -> 12.6 us  [the longest x1 4.13 us: per_device(): pl.pallas_call(filter_kernel, out_shape=jax.ShapeDtypeStruct(blocked, jnp...]
  transfers between devices with their start and end apart: 5 -> 7, of which waited for: 4 -> 4; matrix products, arithmetic and copies ran while one was open for 1% -> 3% of each run, Pallas kernels for 0% -> 2%
where the time goes in v1:
time: 91.2 us; the launch traced here: 90.7 us
  waiting for transfers between devices  45.9 us (50%)
  starting transfers between devices  23.8 us (26%)
  Pallas kernels  12.6 us (14%)
  local copies, waits for them, and re-layouts  8.17 us (9%)
    all_to_all x1, waiting for transfers between devices, per_device(): whole_rows = lax.all_to_all(tend, ('lon', 'lev'), 0, 0, tiled=True)  23.9 us
    all_to_all x1, waiting for transfers between devices, per_device(): lax.all_to_all(stepped.reshape(rows, chans, width), ('lon', 'lev'), 0, 0,...  17.9 us
    all_to_all x1, starting transfers between devices, per_device(): whole_rows = lax.all_to_all(tend, ('lon', 'lev'), 0, 0, tiled=True)  7.26 us
    ppermute x1, starting transfers between devices, per_device(): lax.ppermute(prognostic[:, :, rows - 1, :].reshape(chans, width), 'lat',...  5.04 us
    unnamed x18, local copies, waits for them, and re-layouts  4.41 us
    pallas_call x1, Pallas kernels, per_device(): pl.pallas_call(filter_kernel, out_shape=jax.ShapeDtypeStruct(blocked, jnp...  4.13 us
    all_to_all x1, starting transfers between devices, per_device(): lax.all_to_all(stepped.reshape(rows, chans, width), ('lon', 'lev'), 0, 0,...  3.97 us
    ppermute x1, starting transfers between devices, per_device(): lax.ppermute(west_edge, 'lon', [((i + 1) % lon_devices, i) for i in range...  3.87 us
  transfers between devices with their start and end apart: 7, of which 4 were waited for; matrix products, arithmetic and copies ran while one was open for 3% of the time, Pallas kernels for 2%

profile of v1, /device:TPU:96, one launch (start us, length us, event | category | flops | bytes accessed | tf_op | source)
XLA Modules:
  0.0 90.7 jit_solution(10445921188406027419)
XLA Ops:
  0.0 0.0 copy-start
  0.0 1.3 %fusion = (f32[3,16,1,256]{3,2,1,0:T(1,128)S(1)}, f32[3,16,1,256]{3,2,1,0:T(1,128)S(1)}) fusion(f32[3,16,32,256]{3,2,1,0:T(8,128)} %height.1), kind=kLoop, calls=%fused_computation.5 | loop fusion | bytes 196608 | tf_op jit(solution)/shard_map/slice | solution.py:193
  1.3 5.0 %collective-permute-start = (f32[48,256]{1,0:T(8,128)S(1)}, f32[48,256]{1,0:T(8,128)S(1)}, u32[]{:S(2)}, u32[]{:S(2)}) collective-permute-start(f32[48,256]{1,0:T(8,128)S(1)} %bitcast.14), channel_id=1, source_target_pairs={{0,2},{2,4},{4,6},{6,8},{8,10},{10,12},{12,14},{1,3},{3,5},{5,7},{... | collective-permute-start | bytes 147464 | tf_op jit(solution)/shard_map/ppermute | solution.py:189
  6.4 1.9 %collective-permute-start.1 = (f32[48,256]{1,0:T(8,128)S(1)}, f32[48,256]{1,0:T(8,128)S(1)}, u32[]{:S(2)}, u32[]{:S(2)}) collective-permute-start(f32[48,256]{1,0:T(8,128)S(1)} %bitcast.15), channel_id=1, source_target_pairs={{2,0},{4,2},{6,4},{8,6},{10,8},{12,10},{14,12},{3,1},{5,3},{7,5},{... | collective-permute-start | bytes 147464 | tf_op jit(solution)/shard_map/ppermute | solution.py:192
  8.3 2.1 %slice_reduce_fusion = (f32[3,16,32]{2,1,0:T(8,128)S(1)}, f32[3,16,32]{2,1,0:T(8,128)S(1)}) fusion(f32[3,16,32,256]{3,2,1,0:T(8,128)} %height.1), kind=kLoop, calls=%fused_computation | loop fusion | bytes 24576 | tf_op jit(solution)/shard_map/slice | solution.py:186
  10.4 0.1 copy.9
  10.5 1.5 %collective-permute-start.2 = (f32[32,48]{1,0:T(8,128)S(1)}, f32[32,48]{1,0:T(8,128)S(1)}, u32[]{:S(2)}, u32[]{:S(2)}) collective-permute-start(f32[32,48]{1,0:T(8,128)S(1)} %bitcast.16), channel_id=1, source_target_pairs={{0,16},{16,32},{32,48},{48,64},{64,80},{80,96},{96,112},{112,128},... | collective-permute-start | bytes 18440 | tf_op jit(solution)/shard_map/ppermute | solution.py:187
  12.0 0.1 copy.10
  12.0 3.9 %collective-permute-start.3 = (f32[32,48]{1,0:T(8,128)S(1)}, f32[32,48]{1,0:T(8,128)S(1)}, u32[]{:S(2)}, u32[]{:S(2)}) collective-permute-start(f32[32,48]{1,0:T(8,128)S(1)} %bitcast.17), channel_id=1, source_target_pairs={{16,0},{32,16},{48,32},{64,48},{80,64},{96,80},{112,96},{128,112},... | collective-permute-start | bytes 18440 | tf_op jit(solution)/shard_map/ppermute | solution.py:188
  16.0 1.6 %collective-permute-done.2.west = f32[32,48]{1,0:T(8,128)S(1)} collective-permute-done((f32[32,48]{1,0:T(8,128)S(1)}, f32[32,48]{1,0:T(8,128)S(1)}, u32[]{:S(2)}, u32[]{:S(2)}) %collective-permute-start.2) | collective-permute-done | bytes 6176 | tf_op jit(solution)/shard_map/ppermute | solution.py:187
  17.5 0.0 collective-permute-done.3.east
  17.5 0.0 collective-permute-done.south
  17.5 0.0 collective-permute-done.1.north
  17.6 0.1 broadcast_in_dim.4.zonal
  17.6 0.1 broadcast_in_dim.5.coriolis
  17.7 0.0 copy-done
  17.7 3.5 %tendencies.1 = f32[32,48,256]{2,1,0:T(8,128)} custom-call(f32[3,16,32,256]{3,2,1,0:T(8,128)S(1)} %copy-done, f32[32,256]{1,0:T(8,128)S(1)} %broadcast_in_dim.4.zonal, f32[32,256]{1,0:T(8,128)S(1)} %broadcast_in_dim.5.coriolis, f32[48,256]{1,0:T(8,128)S(1)} %collective-permute-done.south, f32[48,256]{1,0:T(8,128)S(1)} %collective-permute-done.1.north, ...), custom_call_target="tpu_custom_call" | custom-call | tf_op jit(solution)/shard_map/tendencies/pallas_call | solution.py:203
  21.2 0.0 copy-start.6
  21.2 0.0 copy-start.7
  21.2 7.3 %all-to-all-start = ((f32[32,48,256]{2,1,0:T(8,128)}), f32[32,48,256]{2,1,0:T(8,128)S(1)}, u32[]{:S(2)}, u32[]{:S(2)}) async-start(f32[32,48,256]{2,1,0:T(8,128)} %tendencies.1), calls=%async_computation | async-start | bytes 3145728 | tf_op jit(solution)/shard_map/all_to_all | solution.py:210
  28.5 23.9 %all-to-all-done = f32[32,48,256]{2,1,0:T(8,128)S(1)} async-done(((f32[32,48,256]{2,1,0:T(8,128)}), f32[32,48,256]{2,1,0:T(8,128)S(1)}, u32[]{:S(2)}, u32[]{:S(2)}) %all-to-all-start) | async-done | bytes 1572896 | tf_op jit(solution)/shard_map/all_to_all | solution.py:210
  52.4 0.0 copy-done.6
  52.4 0.0 copy-done.7
  52.4 0.0 copy-start.4
  52.4 1.0 %copy-done.4 = f32[32,32,32]{2,1,0:T(8,128)S(1)} copy-done((f32[32,32,32]{2,1,0:T(8,128)S(1)}, f32[32,32,32]{2,1,0:T(8,128)}, u32[]{:S(2)}) %copy-start.4) | copy-done | bytes 131096
  53.5 4.1 %row_filter.1 = f32[16,2,48,256]{3,2,1,0:T(8,128)S(1)} custom-call(s32[1]{0:T(128)} %bitcast.own_row, s32[32]{0:T(128)S(1)} %copy-done.6, s32[32]{0:T(128)S(1)} %copy-done.7, f32[16,2,48,256]{3,2,1,0:T(8,128)S(1)} %bitcast.10, f32[32,32,32]{2,1,0:T(8,128)S(1)} %copy-done.4), custom_call_target="tpu_custom_call" | custom-call | tf_op jit(solution)/shard_map/row_filter/pallas_call | solution.py:217
  57.6 0.0 copy-start.1
  57.6 1.1 %copy-done.1 = f32[16,2,48,256]{3,2,1,0:T(8,128)} copy-done((f32[16,2,48,256]{3,2,1,0:T(8,128)}, f32[16,2,48,256]{3,2,1,0:T(8,128)S(1)}, u32[]{:S(2)}) %copy-start.1) | copy-done | bytes 1572888
  58.8 4.0 %all-to-all-start.1 = ((f32[32,48,256]{2,1,0:T(8,128)}), f32[32,48,256]{2,1,0:T(8,128)S(1)}, u32[]{:S(2)}, u32[]{:S(2)}) async-start(f32[32,48,256]{2,1,0:T(8,128)} %bitcast.11), calls=%async_computation.1 | async-start | bytes 3145728 | tf_op jit(solution)/shard_map/all_to_all | solution.py:238
  62.7 0.0 copy-start.5
  62.8 0.1 slice.19
  62.9 0.2 collective-permute-start.4
  63.1 2.5 %collective-permute-done.4.other = f32[2,16,32,256]{3,2,1,0:T(8,128)S(1)} collective-permute-done((f32[2,16,32,256]{3,2,1,0:T(8,128)S(1)}, f32[2,16,32,256]{3,2,1,0:T(8,128)S(1)}, u32[]{:S(2)}, u32[]{:S(2)}) %collective-permute-start.4) | collective-permute-done | bytes 1048608 | tf_op jit(solution)/shard_map/ppermute | solution.py:195
  65.6 0.0 copy-done.5
  65.6 2.2 %wind_mix.1.mixed = f32[32,32,256]{2,1,0:T(8,128)S(1)} custom-call(s32[1]{0:T(128)} %bitcast.7.own_part, f32[3,16,32,256]{3,2,1,0:T(8,128)S(1)} %copy-done, f32[2,16,32,256]{3,2,1,0:T(8,128)S(1)} %collective-permute-done.4.other, f32[32,32,32]{2,1,0:T(8,128)S(1)} %copy-done.5), custom_call_target="tpu_custom_call" | custom-call | tf_op jit(solution)/shard_map/wind_mix/pallas_call | solution.py:244
  67.8 0.0 copy-start.2
  67.8 1.0 %copy-done.2 = f32[32,32,256]{2,1,0:T(8,128)} copy-done((f32[32,32,256]{2,1,0:T(8,128)}, f32[32,32,256]{2,1,0:T(8,128)S(1)}, u32[]{:S(2)}) %copy-start.2) | copy-done | bytes 1048600
  68.8 17.9 %all-to-all-done.1.step = f32[32,48,256]{2,1,0:T(8,128)S(1)} async-done(((f32[32,48,256]{2,1,0:T(8,128)}), f32[32,48,256]{2,1,0:T(8,128)S(1)}, u32[]{:S(2)}, u32[]{:S(2)}) %all-to-all-start.1) | async-done | bytes 1572896 | tf_op jit(solution)/shard_map/all_to_all | solution.py:238
  86.7 0.0 copy-start.3
  86.7 1.2 %copy-done.3 = f32[32,32,256]{2,1,0:T(8,128)S(1)} copy-done((f32[32,32,256]{2,1,0:T(8,128)S(1)}, f32[32,32,256]{2,1,0:T(8,128)}, u32[]{:S(2)}) %copy-start.3) | copy-done | bytes 1048600
  87.9 2.8 %finish.1 = f32[3,16,32,256]{3,2,1,0:T(8,128)} custom-call(f32[32,48,256]{2,1,0:T(8,128)S(1)} %all-to-all-done.1.step, f32[32,32,256]{2,1,0:T(8,128)S(1)} %copy-done.3, f32[3,16,32,256]{3,2,1,0:T(8,128)S(1)} %copy-done), custom_call_target="tpu_custom_call" | custom-call | tf_op jit(solution)/shard_map/finish/pallas_call | solution.py:261
  (3 shorter events, 0.1 us)
Async XLA Ops:
  0.0 17.7 %copy-start = (f32[3,16,32,256]{3,2,1,0:T(8,128)S(1)}, f32[3,16,32,256]{3,2,1,0:T(8,128)}, u32[]{:S(2)}) copy-start(f32[3,16,32,256]{3,2,1,0:T(8,128)} %height.1) | copy-start | bytes 4718596
  1.3 16.2 %collective-permute-start = (f32[48,256]{1,0:T(8,128)S(1)}, f32[48,256]{1,0:T(8,128)S(1)}, u32[]{:S(2)}, u32[]{:S(2)}) collective-permute-start(f32[48,256]{1,0:T(8,128)S(1)} %bitcast.14), channel_id=1, source_target_pairs={{0,2},{2,4},{4,6},{6,8},{8,10},{10,12},{12,14},{1,3},{3,5},{5,7},{... | collective-permute-start | bytes 147464 | tf_op jit(solution)/shard_map/ppermute | solution.py:189
  6.4 11.2 %collective-permute-start.1 = (f32[48,256]{1,0:T(8,128)S(1)}, f32[48,256]{1,0:T(8,128)S(1)}, u32[]{:S(2)}, u32[]{:S(2)}) collective-permute-start(f32[48,256]{1,0:T(8,128)S(1)} %bitcast.15), channel_id=1, source_target_pairs={{2,0},{4,2},{6,4},{8,6},{10,8},{12,10},{14,12},{3,1},{5,3},{7,5},{... | collective-permute-start | bytes 147464 | tf_op jit(solution)/shard_map/ppermute | solution.py:192
  10.5 7.1 %collective-permute-start.2 = (f32[32,48]{1,0:T(8,128)S(1)}, f32[32,48]{1,0:T(8,128)S(1)}, u32[]{:S(2)}, u32[]{:S(2)}) collective-permute-start(f32[32,48]{1,0:T(8,128)S(1)} %bitcast.16), channel_id=1, source_target_pairs={{0,16},{16,32},{32,48},{48,64},{64,80},{80,96},{96,112},{112,128},... | collective-permute-start | bytes 18440 | tf_op jit(solution)/shard_map/ppermute | solution.py:187
  12.0 5.5 %collective-permute-start.3 = (f32[32,48]{1,0:T(8,128)S(1)}, f32[32,48]{1,0:T(8,128)S(1)}, u32[]{:S(2)}, u32[]{:S(2)}) collective-permute-start(f32[32,48]{1,0:T(8,128)S(1)} %bitcast.17), channel_id=1, source_target_pairs={{16,0},{32,16},{48,32},{64,48},{80,64},{96,80},{112,96},{128,112},... | collective-permute-start | bytes 18440 | tf_op jit(solution)/shard_map/ppermute | solution.py:188
  21.2 31.2 %copy-start.6 = (s32[32]{0:T(128)S(1)}, s32[32]{0:T(128)}, u32[]{:S(2)}) copy-start(s32[32]{0:T(128)} %half_width.1) | copy-start | bytes 388
  21.2 31.2 %copy-start.7 = (s32[32]{0:T(128)S(1)}, s32[32]{0:T(128)}, u32[]{:S(2)}) copy-start(s32[32]{0:T(128)} %filter_mask.1) | copy-start | bytes 388
  21.2 31.2 %all-to-all-start = ((f32[32,48,256]{2,1,0:T(8,128)}), f32[32,48,256]{2,1,0:T(8,128)S(1)}, u32[]{:S(2)}, u32[]{:S(2)}) async-start(f32[32,48,256]{2,1,0:T(8,128)} %tendencies.1), calls=%async_computation | async-start | bytes 3145728 | tf_op jit(solution)/shard_map/all_to_all | solution.py:210
  52.4 1.0 %copy-start.4 = (f32[32,32,32]{2,1,0:T(8,128)S(1)}, f32[32,32,32]{2,1,0:T(8,128)}, u32[]{:S(2)}) copy-start(f32[32,32,32]{2,1,0:T(8,128)} %matrix.3) | copy-start | bytes 393220
  57.6 1.1 %copy-start.1 = (f32[16,2,48,256]{3,2,1,0:T(8,128)}, f32[16,2,48,256]{3,2,1,0:T(8,128)S(1)}, u32[]{:S(2)}) copy-start(f32[16,2,48,256]{3,2,1,0:T(8,128)S(1)} %row_filter.1) | copy-start | bytes 4718596
  58.8 27.9 %all-to-all-start.1 = ((f32[32,48,256]{2,1,0:T(8,128)}), f32[32,48,256]{2,1,0:T(8,128)S(1)}, u32[]{:S(2)}, u32[]{:S(2)}) async-start(f32[32,48,256]{2,1,0:T(8,128)} %bitcast.11), calls=%async_computation.1 | async-start | bytes 3145728 | tf_op jit(solution)/shard_map/all_to_all | solution.py:238
  62.7 2.9 %copy-start.5 = (f32[32,32,32]{2,1,0:T(8,128)S(1)}, f32[32,32,32]{2,1,0:T(8,128)}, u32[]{:S(2)}) copy-start(f32[32,32,32]{2,1,0:T(8,128)} %matrix.3) | copy-start | bytes 393220
  62.9 2.7 %collective-permute-start.4 = (f32[2,16,32,256]{3,2,1,0:T(8,128)S(1)}, f32[2,16,32,256]{3,2,1,0:T(8,128)S(1)}, u32[]{:S(2)}, u32[]{:S(2)}) collective-permute-start(f32[2,16,32,256]{3,2,1,0:T(8,128)S(1)} %slice.19), channel_id=1, source_target_pairs={{0,1},{1,0},{2,3},{3,2},{4,5},{5,4},{6,7},{7,6},{8,9},{9,8},{10,11... | collective-permute-start | bytes 3145736 | tf_op jit(solution)/shard_map/ppermute | solution.py:195
  67.8 1.0 %copy-start.2 = (f32[32,32,256]{2,1,0:T(8,128)}, f32[32,32,256]{2,1,0:T(8,128)S(1)}, u32[]{:S(2)}) copy-start(f32[32,32,256]{2,1,0:T(8,128)S(1)} %wind_mix.1.mixed) | copy-start | bytes 3145732
  86.7 1.2 %copy-start.3 = (f32[32,32,256]{2,1,0:T(8,128)S(1)}, f32[32,32,256]{2,1,0:T(8,128)}, u32[]{:S(2)}) copy-start(f32[32,32,256]{2,1,0:T(8,128)} %copy-done.2) | copy-start | bytes 3145732

commit v2 on v1

v2 whole, which is shorter than its diff:
```python
import jax
import jax.numpy as jnp
from jax import lax
from jax.experimental import pallas as pl
from jax.experimental.pallas import tpu as pltpu
from jax.sharding import PartitionSpec as P

TIME_STEP = 0.5
VISCOSITY = 0.05
MERIDIONAL = 0.25
HALF = 128
SUBLANES = 8
VMEM_LIMIT = 32 * 1024 * 1024
CHUNKS = 4
GROUP = 4


def latitudes(global_rows, row_total):
    latitude_angle = -0.5 * jnp.pi + (global_rows + 0.5) * jnp.pi / row_total
    return (jnp.cos(latitude_angle), jnp.sin(latitude_angle))


def tendency_kernel(prog, zonal, coriolis, out, ends, tile, turn, edges, stage, in_sems, out_sems):
    _, levels, rows, width = prog.shape
    chans = 3 * levels
    payload = 2 * chans
    per_chunk = levels // CHUNKS
    loads = []
    for chunk in range(CHUNKS):
        some = pl.ds(chunk * per_chunk, per_chunk)
        loads.append(pltpu.make_async_copy(prog.at[:, some], tile.at[:, some], in_sems.at[chunk]))
        loads[-1].start()
    row_id = lax.broadcasted_iota(jnp.int32, (rows, width), 0)
    col_id = lax.broadcasted_iota(jnp.int32, (rows, width), 1)
    lane_id = lax.broadcasted_iota(jnp.int32, (rows, HALF), 1)
    first_row, last_row = row_id == 0, row_id == rows - 1
    first_col, last_col = col_id == 0, col_id == width - 1
    zon, cor = zonal[...], coriolis[...]
    edge_rows = jnp.zeros((rows, HALF), jnp.float32)
    for l in range(levels):
        if l % per_chunk == 0:
            loads[l // per_chunk].wait()
        centre, dx, dy, sx = [], [], [], []
        for f in range(3):
            c = f * levels + l
            here = tile[f, l]
            e = jnp.where(last_col, 0.0, pltpu.roll(here, width - 1, 1))
            w = jnp.where(first_col, 0.0, pltpu.roll(here, 1, 1))
            n = jnp.where(last_row, 0.0, pltpu.roll(here, rows - 1, 0))
            s = jnp.where(first_row, 0.0, pltpu.roll(here, 1, 0))
            centre.append(here)
            dx.append(e - w)
            dy.append(n - s)
            sx.append(e + w + n + s - 4.0 * here)
            first = here[:, :HALF]
            last = here[:, width - HALF :]
            if c:
                first = pltpu.roll(first, c, 1)
            last = pltpu.roll(last, (chans + c + 1) % HALF, 1)
            edge_rows = jnp.where(lane_id == c, first, jnp.where(lane_id == chans + c, last, edge_rows))
        tends = (
            -zon * dx[2] + cor * centre[1] + VISCOSITY * sx[0],
            -MERIDIONAL * dy[2] - cor * centre[0] + VISCOSITY * sx[1],
            -zon * dx[0] - MERIDIONAL * dy[1],
        )
        for f in range(3):
            for half in range(2):
                turn[f, half, l * rows : (l + 1) * rows, :] = tends[f][:, half * HALF : (half + 1) * HALF]
    edges[...] = edge_rows
    per_chunk = rows // CHUNKS
    copies = []
    for chunk in range(CHUNKS):
        for j in range(chunk * per_chunk, (chunk + 1) * per_chunk):
            for f in range(3):
                for half in range(2):
                    at = (2 * f + half) * levels
                    value = turn[f, half, pl.ds(j, levels, stride=rows), :]
                    stage[j, at : at + levels, :] = value
                    if j in (0, rows - 1):
                        ends[min(j, 1), at : at + levels, :] = value
            stage[j, payload:, :] = jnp.broadcast_to(edges[j : j + 1, :], (SUBLANES, HALF))
        some = pl.ds(chunk * per_chunk, per_chunk)
        copies.append(pltpu.make_async_copy(stage.at[some], out.at[some], out_sems.at[chunk]))
        copies[-1].start()
    for copy in copies:
        copy.wait()


def seam_kernel(ends, south, north, tend, out, stage, sems):
    del tend
    chans = south.shape[0]
    levels = chans // 3
    copies = []
    for at, beyond, sign in ((0, south, -1.0), (1, north, 1.0)):
        for half in range(2):
            lanes = slice(half * HALF, (half + 1) * HALF)
            u, v, h = (beyond[f * levels : (f + 1) * levels, lanes] for f in range(3))
            slope = sign * MERIDIONAL
            for f, term in enumerate((VISCOSITY * u, VISCOSITY * v - slope * h, -slope * v)):
                some = slice((2 * f + half) * levels, (2 * f + half + 1) * levels)
                stage[at, some, :] = ends[at, some, :] + term
        row = at * (out.shape[0] - 1)
        copies.append(pltpu.make_async_copy(stage.at[at], out.at[row, pl.ds(0, 2 * chans)], sems.at[at]))
        copies[-1].start()
    for copy in copies:
        copy.wait()


def split2(x):
    hi = x.astype(jnp.bfloat16)
    return hi, (x - hi.astype(jnp.float32)).astype(jnp.bfloat16)


def mix_operand(matrix):
    hi, lo = split2(matrix)
    return jnp.concatenate([hi, hi, lo], axis=1)


def filter_kernel(
    own_row, half_width, filter_mask, zonal, tend, matrices, out, halves, parts, seam, matrix, stage, matrix_sem, sems
):
    blocks, lev_parts, levels = out.shape[0], out.shape[1], out.shape[4]
    chans = 3 * levels
    payload = 2 * chans
    count = 2 * blocks
    both = lev_parts * chans
    row = own_row[0]
    fetch = pltpu.make_async_copy(matrices.at[row], matrix, matrix_sem)
    fetch.start()
    reach = half_width[row]
    whole = reach == count // 2
    norm = jnp.where(whole, count * HALF, 2 * HALF * reach + 1).astype(jnp.float32)
    filtered = filter_mask[row] == 1
    edge_gain = jnp.where(whole, 0.0, 1.0).astype(jnp.float32)

    for b in range(blocks):
        for part in range(lev_parts):
            at = b * lev_parts + part
            seam[at : at + 1, :] = tend[b, part, payload : payload + 1, :]
    columns = seam[...].T
    zon = zonal[row]
    u, v, h = (columns[f * levels : (f + 1) * levels] for f in range(3))
    from_east = jnp.concatenate([VISCOSITY * u - zon * h, VISCOSITY * v, -zon * u], axis=0)
    u, v, h = (columns[chans + f * levels : chans + (f + 1) * levels] for f in range(3))
    from_west = jnp.concatenate([VISCOSITY * u + zon * h, VISCOSITY * v, zon * u], axis=0)
    lane_id = lax.broadcasted_iota(jnp.int32, (levels, HALF), 1)
    window = jnp.zeros((both, HALF), jnp.float32)
    for g in range(count):
        b, half = divmod(g, 2)
        beyond = (b + 1) % blocks if half else (b + blocks - 1) % blocks
        terms, lane = (from_east, HALF - 1) if half else (from_west, 0)
        pieces = []
        for part in range(lev_parts):
            source = beyond * lev_parts + part
            for f in range(3):
                here = tend[b, part, (2 * f + half) * levels : (2 * f + half + 1) * levels, :]
                term = terms[f * levels : (f + 1) * levels, source : source + 1]
                pieces.append(here + jnp.where(lane_id == lane, term, 0.0))
        value = jnp.concatenate(pieces, axis=0)
        halves[g] = value
        inside = lax.rem(g + reach, count) < 2 * reach
        window = window + jnp.where(inside, 1.0, 0.0).astype(jnp.float32) * value

    src = lax.broadcasted_iota(jnp.int32, (2 * HALF, HALF), 0)
    dst = lax.broadcasted_iota(jnp.int32, (2 * HALF, HALF), 1)
    sums = jnp.where((src <= dst) | (src >= HALF), 1.0, 0.0).astype(jnp.bfloat16)
    fetch.wait()
    mixer = mix_operand(matrix[...])
    scale = TIME_STEP / norm

    def split_group(g0, window):
        for g in range(g0, g0 + GROUP):
            ahead = halves[lax.rem(g + reach, count)]
            behind = halves[lax.rem(g + count - reach, count)]
            change = ahead - behind
            for k, (a, b) in enumerate(zip(split2(change), split2(window))):
                parts[k, g * both : (g + 1) * both, :HALF] = a
                parts[k, g * both : (g + 1) * both, HALF:] = b
            window = window + change
        return window

    copies = []

    def finish_group(g0):
        lo, hi = g0 * both, (g0 + GROUP) * both
        box = jnp.dot(parts[1, lo:hi, :], sums, preferred_element_type=jnp.float32) + jnp.dot(
            parts[0, lo:hi, :], sums, preferred_element_type=jnp.float32
        )
        for pair in range(GROUP // 2):
            b = g0 // 2 + pair
            steps = []
            for half in range(2):
                g = 2 * b + half
                at = (g - g0) * both
                behind = halves[lax.rem(g + count - reach, count)]
                smooth = (box[at : at + both] + edge_gain * behind) * scale
                step = jnp.where(filtered, smooth, TIME_STEP * halves[g])
                for p in range(lev_parts):
                    stage[b, p, 2, half] = step[p * chans + 2 * levels : (p + 1) * chans]
                steps.append(step)
            step = jnp.concatenate(steps, axis=1)
            for f in range(2):
                wind = jnp.concatenate(
                    [step[p * chans + f * levels : p * chans + (f + 1) * levels] for p in range(lev_parts)], axis=0
                )
                wind_hi, wind_lo = split2(wind)
                mixed = jnp.dot(
                    mixer,
                    jnp.concatenate([wind_hi, wind_lo, wind_hi], axis=0),
                    preferred_element_type=jnp.float32,
                )
                for p in range(lev_parts):
                    for half in range(2):
                        stage[b, p, f, half] = mixed[
                            p * levels : (p + 1) * levels, half * HALF : (half + 1) * HALF
                        ]
            copies.append(pltpu.make_async_copy(stage.at[b], out.at[b], sems.at[b]))
            copies[-1].start()

    window = split_group(0, window)
    for g0 in range(0, count, GROUP):
        if g0 + GROUP < count:
            window = split_group(g0 + GROUP, window)
        finish_group(g0)
    for copy in copies:
        copy.wait()


def base_kernel(own_part, own, other, matrix, out):
    _, levels, rows, width = own.shape
    mine = own.reshape(3, levels * rows, width)
    theirs = other.reshape(2, levels * rows, width)
    lower = own_part[0] == 0
    for j in range(rows):
        mixer = mix_operand(matrix[j])
        winds = []
        for f in range(2):
            a = mine[f, pl.ds(j, levels, stride=rows), :]
            b = theirs[f, pl.ds(j, levels, stride=rows), :]
            winds.append(jnp.concatenate([jnp.where(lower, a, b), jnp.where(lower, b, a)], axis=0))
        wind_hi, wind_lo = split2(jnp.concatenate(winds, axis=1))
        mixed = jnp.dot(
            mixer, jnp.concatenate([wind_hi, wind_lo, wind_hi], axis=0), preferred_element_type=jnp.float32
        )
        kept = jnp.where(lower, mixed[:levels], mixed[levels:])
        for f in range(2):
            out[j, f, 0] = kept[:, f * width : (f + 1) * width]
        out[j, 2, 0] = mine[2, pl.ds(j, levels, stride=rows), :]


def finish_kernel(step, base, out, added, stage, in_sems, out_sems):
    fields, levels, rows, _ = out.shape
    loads, copies = [], []
    for f in range(fields):
        loads.append(pltpu.make_async_copy(base.at[:, f], added.at[f], in_sems.at[f]))
        loads[-1].start()
    for f in range(fields):
        loads[f].wait()
        for half in range(2):
            for j in range(rows):
                stage[f, half, pl.ds(j, levels, stride=rows), :] = step[j, f, half] + added[f, j, half]
            copies.append(
                pltpu.make_async_copy(
                    stage.at[f, half].reshape(levels, rows, HALF),
                    out.at[f, :, :, pl.ds(half * HALF, HALF)],
                    out_sems.at[2 * f + half],
                )
            )
            copies[-1].start()
    for copy in copies:
        copy.wait()


def per_device(prognostic, half_width, filter_mask, column_inverse):
    fields, levels, rows, width = prognostic.shape
    lon_devices, lat_devices, lev_devices = (lax.axis_size(a) for a in ("lon", "lat", "lev"))
    lon_index, lat_index, lev_index = (lax.axis_index(a) for a in ("lon", "lat", "lev"))
    chans = fields * levels
    halves = width // HALF
    params = pltpu.CompilerParams(vmem_limit_bytes=VMEM_LIMIT)
    hbm = pl.BlockSpec(memory_space=pltpu.HBM)
    vmem = pl.BlockSpec(memory_space=pltpu.VMEM)

    south = lax.ppermute(
        prognostic[:, :, rows - 1, :].reshape(chans, width), "lat", [(i, i + 1) for i in range(lat_devices - 1)]
    )
    north = lax.ppermute(
        prognostic[:, :, 0, :].reshape(chans, width), "lat", [(i + 1, i) for i in range(lat_devices - 1)]
    )
    other = lax.ppermute(prognostic[:2], "lev", [(0, 1), (1, 0)])

    global_rows = (lat_index * rows + jnp.arange(rows)).astype(jnp.float32)
    cosine, sine = latitudes(global_rows, rows * lat_devices)
    zonal = 0.25 / (cosine + 0.05)
    zonal_field = jnp.broadcast_to(zonal[:, None], (rows, width))
    coriolis_field = jnp.broadcast_to((0.5 * sine)[:, None], (rows, width))

    sent_rows = halves * chans + SUBLANES
    with jax.named_scope("tendencies"):
        tend, ends = pl.pallas_call(
            tendency_kernel,
            out_shape=(
                jax.ShapeDtypeStruct((rows, sent_rows, HALF), jnp.float32),
                jax.ShapeDtypeStruct((2, halves * chans, HALF), jnp.float32),
            ),
            in_specs=[hbm, vmem, vmem],
            out_specs=(hbm, vmem),
            scratch_shapes=[
                pltpu.VMEM(prognostic.shape, jnp.float32),
                pltpu.VMEM((fields, halves, levels * rows, HALF), jnp.float32),
                pltpu.VMEM((rows, HALF), jnp.float32),
                pltpu.VMEM((rows, sent_rows, HALF), jnp.float32),
                pltpu.SemaphoreType.DMA((CHUNKS,)),
                pltpu.SemaphoreType.DMA((CHUNKS,)),
            ],
            compiler_params=params,
        )(prognostic, zonal_field, coriolis_field)

    with jax.named_scope("seam_rows"):
        tend = pl.pallas_call(
            seam_kernel,
            out_shape=jax.ShapeDtypeStruct(tend.shape, jnp.float32),
            in_specs=[vmem, vmem, vmem, hbm],
            out_specs=hbm,
            input_output_aliases={3: 0},
            scratch_shapes=[pltpu.VMEM(ends.shape, jnp.float32), pltpu.SemaphoreType.DMA((2,))],
            compiler_params=params,
        )(ends, south, north, tend)

    whole_rows = lax.all_to_all(tend, ("lon", "lev"), 0, 0, tiled=True)

    own_row = (lon_index * lev_devices + lev_index).astype(jnp.int32).reshape(1)
    stepped_shape = (lon_devices, lev_devices, fields, halves, levels, HALF)
    count = halves * lon_devices
    both = lev_devices * chans
    with jax.named_scope("row_filter"):
        stepped = pl.pallas_call(
            filter_kernel,
            out_shape=jax.ShapeDtypeStruct(stepped_shape, jnp.float32),
            grid_spec=pltpu.PrefetchScalarGridSpec(
                num_scalar_prefetch=4,
                grid=(1,),
                in_specs=[vmem, hbm],
                out_specs=hbm,
                scratch_shapes=[
                    pltpu.VMEM((count, both, HALF), jnp.float32),
                    pltpu.VMEM((2, count * both, 2 * HALF), jnp.bfloat16),
                    pltpu.VMEM((HALF, HALF), jnp.float32),
                    pltpu.VMEM(column_inverse.shape[1:], jnp.float32),
                    pltpu.VMEM(stepped_shape, jnp.float32),
                    pltpu.SemaphoreType.DMA,
                    pltpu.SemaphoreType.DMA((lon_devices,)),
                ],
            ),
            compiler_params=params,
        )(
            own_row,
            half_width,
            filter_mask,
            zonal,
            whole_rows.reshape(lon_devices, lev_devices, sent_rows, HALF),
            column_inverse,
        )

    returned = lax.all_to_all(
        stepped.reshape((rows,) + stepped_shape[2:]), ("lon", "lev"), 0, 0, tiled=True
    )

    with jax.named_scope("base"):
        base = pl.pallas_call(
            base_kernel,
            out_shape=jax.ShapeDtypeStruct(returned.shape, jnp.float32),
            grid_spec=pltpu.PrefetchScalarGridSpec(
                num_scalar_prefetch=1,
                grid=(halves,),
                in_specs=[
                    pl.BlockSpec((fields, levels, rows, HALF), lambda i, *_: (0, 0, 0, i)),
                    pl.BlockSpec((2, levels, rows, HALF), lambda i, *_: (0, 0, 0, i)),
                    pl.BlockSpec(column_inverse.shape, lambda i, *_: (0, 0, 0)),
                ],
                out_specs=pl.BlockSpec((rows, fields, 1, levels, HALF), lambda i, *_: (0, 0, i, 0, 0)),
            ),
            compiler_params=params,
        )(lev_index.astype(jnp.int32).reshape(1), prognostic, other, column_inverse)

    with jax.named_scope("finish"):
        return pl.pallas_call(
            finish_kernel,
            out_shape=jax.ShapeDtypeStruct(prognostic.shape, jnp.float32),
            in_specs=[vmem, hbm],
            out_specs=hbm,
            scratch_shapes=[
                pltpu.VMEM((fields, rows, halves, levels, HALF), jnp.float32),
                pltpu.VMEM((fields, halves, levels * rows, HALF), jnp.float32),
                pltpu.SemaphoreType.DMA((fields,)),
                pltpu.SemaphoreType.DMA((fields * halves,)),
            ],
            compiler_params=params,
        )(returned, base)


def solution(mesh):
    placed = (P(None, "lev", "lat", "lon"), P("lat"), P("lat"), P("lat", None, None))
    return jax.shard_map(
        per_device,
        mesh=mesh,
        in_specs=placed,
        out_specs=P(None, "lev", "lat", "lon"),
        check_vma=False,
    )
```

time: 91.2 us -> 84.5 us (0.927)
  local copies, waits for them, and re-layouts: 8.17 us -> 2.87 us
  starting transfers between devices: 23.8 us -> 19.4 us
  Pallas kernels: 12.6 us -> 15.1 us
    ppermute x2 -> x0, starting transfers between devices: 5.39 us -> none  [the longest x1 3.87 us: per_device(): lax.ppermute(west_edge, 'lon', [((i + 1) % lon_devices, i) for i in range...]
    unnamed x18 -> x14, local copies, waits for them, and re-layouts: 4.41 us -> 1.46 us
    slice x1 -> x0, local copies, waits for them, and re-layouts: 2.07 us -> none  [per_device(): west_edge = prognostic[:, :, :, 0].reshape(chans, rows).T]
    ppermute x2 -> x0, waiting for transfers between devices: 1.58 us -> none  [the longest x1 1.58 us: per_device(): lax.ppermute(east_edge, 'lon', [(i, (i + 1) % lon_devices) for i in range...]
    pallas_call x3 -> x4, Pallas kernels: 9.86 us -> 11.4 us  [the longest x1 4.52 us: per_device(): pl.pallas_call(filter_kernel, out_shape=jax.ShapeDtypeStruct(stepped_shap...]
    all_to_all x1, waiting for transfers between devices: 23.9 us -> 25.4 us  [per_device(): whole_rows = lax.all_to_all(tend, ('lon', 'lev'), 0, 0, tiled=True)]
  transfers between devices with their start and end apart: 7 -> 5, of which waited for: 4 -> 3; matrix products, arithmetic and copies ran while one was open for 3% -> 0% of each run, Pallas kernels for 2% -> 7%
where the time goes in v2:
time: 84.5 us; the launch traced here: 84 us
  waiting for transfers between devices  46.4 us (55%)
  starting transfers between devices  19.4 us (23%)
  Pallas kernels  15.1 us (18%)
  local copies, waits for them, and re-layouts  2.87 us (3%)
    all_to_all x1, waiting for transfers between devices, per_device(): whole_rows = lax.all_to_all(tend, ('lon', 'lev'), 0, 0, tiled=True)  25.4 us
    all_to_all x1, waiting for transfers between devices, per_device(): lax.all_to_all(stepped.reshape((rows,) + stepped_shape[2:]), ('lon', 'lev...  18.4 us
    all_to_all x1, starting transfers between devices, per_device(): whole_rows = lax.all_to_all(tend, ('lon', 'lev'), 0, 0, tiled=True)  7.46 us
    ppermute x1, starting transfers between devices, per_device(): lax.ppermute(prognostic[:, :, rows - 1, :].reshape(chans, width), 'lat',...  5.04 us
    all_to_all x1, starting transfers between devices, per_device(): lax.all_to_all(stepped.reshape((rows,) + stepped_shape[2:]), ('lon', 'lev...  4.85 us
    pallas_call x1, Pallas kernels, per_device(): pl.pallas_call(filter_kernel, out_shape=jax.ShapeDtypeStruct(stepped_shap...  4.52 us
    pallas_call x1, Pallas kernels, per_device(): pl.pallas_call(finish_kernel, out_shape=jax.ShapeDtypeStruct(prognostic.s...  3.67 us
    pallas_call x1, Pallas kernels, per_device(): pl.pallas_call(tendency_kernel, out_shape=(jax.ShapeDtypeStruct((rows, se...  3.59 us
  transfers between devices with their start and end apart: 5, of which 3 were waited for; matrix products, arithmetic and copies ran while one was open for 0% of the time, Pallas kernels for 7%

profile of v2, /device:TPU:96, one launch (start us, length us, event | category | flops | bytes accessed | tf_op | source)
XLA Modules:
  0.0 84.0 jit_solution(17406160365879827782)
XLA Ops:
  0.0 1.2 %fusion = (f32[3,16,1,256]{3,2,1,0:T(1,128)S(1)}, f32[3,16,1,256]{3,2,1,0:T(1,128)S(1)}) fusion(f32[3,16,32,256]{3,2,1,0:T(8,128)} %own.1), kind=kLoop, calls=%fused_computation.3 | loop fusion | bytes 196608 | tf_op jit(solution)/shard_map/slice | solution.py:288
  1.2 5.0 %collective-permute-start = (f32[48,256]{1,0:T(8,128)S(1)}, f32[48,256]{1,0:T(8,128)S(1)}, u32[]{:S(2)}, u32[]{:S(2)}) collective-permute-start(f32[48,256]{1,0:T(8,128)S(1)} %bitcast.7), channel_id=1, source_target_pairs={{0,2},{2,4},{4,6},{6,8},{8,10},{10,12},{12,14},{1,3},{3,5},{5,7},{... | collective-permute-start | bytes 147464 | tf_op jit(solution)/shard_map/ppermute | solution.py:284
  6.3 1.9 %collective-permute-start.1 = (f32[48,256]{1,0:T(8,128)S(1)}, f32[48,256]{1,0:T(8,128)S(1)}, u32[]{:S(2)}, u32[]{:S(2)}) collective-permute-start(f32[48,256]{1,0:T(8,128)S(1)} %bitcast.8), channel_id=1, source_target_pairs={{2,0},{4,2},{6,4},{8,6},{10,8},{12,10},{14,12},{3,1},{5,3},{7,5},{... | collective-permute-start | bytes 147464 | tf_op jit(solution)/shard_map/ppermute | solution.py:287
  8.2 0.1 broadcast_in_dim.4.zonal
  8.3 0.1 broadcast_in_dim.5.coriolis
  8.4 0.0 copy-start
  8.4 1.4 %copy-done = f32[3,16,32,256]{3,2,1,0:T(8,128)S(1)} copy-done((f32[3,16,32,256]{3,2,1,0:T(8,128)S(1)}, f32[3,16,32,256]{3,2,1,0:T(8,128)}, u32[]{:S(2)}) %copy-start) | copy-done | bytes 1572888
  9.8 3.6 %tendencies.1 = (f32[32,104,128]{2,1,0:T(8,128)}, f32[2,96,128]{2,1,0:T(8,128)S(1)}) custom-call(f32[3,16,32,256]{3,2,1,0:T(8,128)S(1)} %copy-done, f32[32,256]{1,0:T(8,128)S(1)} %broadcast_in_dim.4.zonal, f32[32,256]{1,0:T(8,128)S(1)} %broadcast_in_dim.5.coriolis), custom_call_target="tpu_custom_call" | custom-call | tf_op jit(solution)/shard_map/tendencies/pallas_call | solution.py:300
  13.4 0.0 collective-permute-done.south
  13.4 0.0 collective-permute-done.1.north
  13.5 0.7 seam_rows.1
  14.1 0.0 copy-start.2
  14.2 0.0 copy-start.4
  14.2 0.0 copy-start.5
  14.2 7.5 %all-to-all-start = ((f32[32,104,128]{2,1,0:T(8,128)}), f32[32,104,128]{2,1,0:T(8,128)S(1)}, u32[]{:S(2)}, u32[]{:S(2)}) async-start(f32[32,104,128]{2,1,0:T(8,128)} %seam_rows.1), calls=%async_computation | async-start | bytes 3407872 | tf_op jit(solution)/shard_map/all_to_all | solution.py:330
  21.7 25.4 %all-to-all-done = f32[32,104,128]{2,1,0:T(8,128)S(1)} async-done(((f32[32,104,128]{2,1,0:T(8,128)}), f32[32,104,128]{2,1,0:T(8,128)S(1)}, u32[]{:S(2)}, u32[]{:S(2)}) %all-to-all-start) | async-done | bytes 1703968 | tf_op jit(solution)/shard_map/all_to_all | solution.py:330
  47.0 0.0 copy-done.2
  47.0 0.0 copy-done.4
  47.0 0.0 copy-done.5
  47.1 4.5 %row_filter.1 = f32[16,2,3,2,16,128]{5,4,3,2,1,0:T(8,128)} custom-call(s32[1]{0:T(128)} %bitcast.own_row, s32[32]{0:T(128)S(1)} %copy-done.4, s32[32]{0:T(128)S(1)} %copy-done.5, f32[32]{0:T(128)S(1)} %get-tuple-element.12.zonal, f32[16,2,104,128]{3,2,1,0:T(8,128)S(1)} %bitcast.6, f32[32,32,32]{2,1,0:T(8,128)S(1)} %copy-done.2), custom_call_target="tpu_custom_call" | custom-call | tf_op jit(solution)/shard_map/row_filter/pallas_call | solution.py:337
  51.6 0.0 copy-start.1
  51.6 4.8 %all-to-all-start.1 = ((f32[32,3,2,16,128]{4,3,2,1,0:T(8,128)}), f32[32,3,2,16,128]{4,3,2,1,0:T(8,128)}, u32[]{:S(2)}, u32[]{:S(2)}) async-start(f32[32,3,2,16,128]{4,3,2,1,0:T(8,128)} %bitcast.4), calls=%async_computation.1 | async-start | bytes 3145728 | tf_op jit(solution)/shard_map/all_to_all | solution.py:365
  56.5 0.0 copy-done.1
  56.5 0.0 copy-start.3
  56.5 0.1 slice.11
  56.6 0.2 collective-permute-start.2
  56.7 2.6 %collective-permute-done.2.other = f32[2,16,32,256]{3,2,1,0:T(8,128)S(1)} collective-permute-done((f32[2,16,32,256]{3,2,1,0:T(8,128)S(1)}, f32[2,16,32,256]{3,2,1,0:T(8,128)S(1)}, u32[]{:S(2)}, u32[]{:S(2)}) %collective-permute-start.2) | collective-permute-done | bytes 1048608 | tf_op jit(solution)/shard_map/ppermute | solution.py:290
  59.3 0.0 copy-done.3
  59.3 2.6 %base.1 = f32[32,3,2,16,128]{4,3,2,1,0:T(8,128)S(1)} custom-call(s32[1]{0:T(128)} %bitcast.5.own_part, f32[3,16,32,256]{3,2,1,0:T(8,128)S(1)} %copy-done.1, f32[2,16,32,256]{3,2,1,0:T(8,128)S(1)} %collective-permute-done.2.other, f32[32,32,32]{2,1,0:T(8,128)S(1)} %copy-done.3), custom_call_target="tpu_custom_call" | custom-call | tf_op jit(solution)/shard_map/base/pallas_call | solution.py:370
  61.9 18.4 %all-to-all-done.1.step = f32[32,3,2,16,128]{4,3,2,1,0:T(8,128)} async-done(((f32[32,3,2,16,128]{4,3,2,1,0:T(8,128)}), f32[32,3,2,16,128]{4,3,2,1,0:T(8,128)}, u32[]{:S(2)}, u32[]{:S(2)}) %all-to-all-start.1) | async-done | bytes 1572896 | tf_op jit(solution)/shard_map/all_to_all | solution.py:365
  80.4 3.7 %finish.1 = f32[3,16,32,256]{3,2,1,0:T(8,128)} custom-call(f32[32,3,2,16,128]{4,3,2,1,0:T(8,128)} %all-to-all-done.1.step, f32[32,3,2,16,128]{4,3,2,1,0:T(8,128)S(1)} %base.1), custom_call_target="tpu_custom_call" | custom-call | tf_op jit(solution)/shard_map/finish/pallas_call | solution.py:387
  (3 shorter events, 0.1 us)
Async XLA Ops:
  1.2 12.2 %collective-permute-start = (f32[48,256]{1,0:T(8,128)S(1)}, f32[48,256]{1,0:T(8,128)S(1)}, u32[]{:S(2)}, u32[]{:S(2)}) collective-permute-start(f32[48,256]{1,0:T(8,128)S(1)} %bitcast.7), channel_id=1, source_target_pairs={{0,2},{2,4},{4,6},{6,8},{8,10},{10,12},{12,14},{1,3},{3,5},{5,7},{... | collective-permute-start | bytes 147464 | tf_op jit(solution)/shard_map/ppermute | solution.py:284
  6.3 7.2 %collective-permute-start.1 = (f32[48,256]{1,0:T(8,128)S(1)}, f32[48,256]{1,0:T(8,128)S(1)}, u32[]{:S(2)}, u32[]{:S(2)}) collective-permute-start(f32[48,256]{1,0:T(8,128)S(1)} %bitcast.8), channel_id=1, source_target_pairs={{2,0},{4,2},{6,4},{8,6},{10,8},{12,10},{14,12},{3,1},{5,3},{7,5},{... | collective-permute-start | bytes 147464 | tf_op jit(solution)/shard_map/ppermute | solution.py:287
  8.4 1.4 %copy-start = (f32[3,16,32,256]{3,2,1,0:T(8,128)S(1)}, f32[3,16,32,256]{3,2,1,0:T(8,128)}, u32[]{:S(2)}) copy-start(f32[3,16,32,256]{3,2,1,0:T(8,128)} %own.1) | copy-start | bytes 4718596
  14.1 32.9 %copy-start.2 = (f32[32,32,32]{2,1,0:T(8,128)S(1)}, f32[32,32,32]{2,1,0:T(8,128)}, u32[]{:S(2)}) copy-start(f32[32,32,32]{2,1,0:T(8,128)} %matrix.1) | copy-start | bytes 393220
  14.2 32.9 %copy-start.4 = (s32[32]{0:T(128)S(1)}, s32[32]{0:T(128)}, u32[]{:S(2)}) copy-start(s32[32]{0:T(128)} %half_width.1) | copy-start | bytes 388
  14.2 32.9 %copy-start.5 = (s32[32]{0:T(128)S(1)}, s32[32]{0:T(128)}, u32[]{:S(2)}) copy-start(s32[32]{0:T(128)} %filter_mask.1) | copy-start | bytes 388
  14.2 32.9 %all-to-all-start = ((f32[32,104,128]{2,1,0:T(8,128)}), f32[32,104,128]{2,1,0:T(8,128)S(1)}, u32[]{:S(2)}, u32[]{:S(2)}) async-start(f32[32,104,128]{2,1,0:T(8,128)} %seam_rows.1), calls=%async_computation | async-start | bytes 3407872 | tf_op jit(solution)/shard_map/all_to_all | solution.py:330
  51.6 4.9 %copy-start.1 = (f32[3,16,32,256]{3,2,1,0:T(8,128)S(1)}, f32[3,16,32,256]{3,2,1,0:T(8,128)}, u32[]{:S(2)}) copy-start(f32[3,16,32,256]{3,2,1,0:T(8,128)} %own.1) | copy-start | bytes 4718596
  51.6 28.8 %all-to-all-start.1 = ((f32[32,3,2,16,128]{4,3,2,1,0:T(8,128)}), f32[32,3,2,16,128]{4,3,2,1,0:T(8,128)}, u32[]{:S(2)}, u32[]{:S(2)}) async-start(f32[32,3,2,16,128]{4,3,2,1,0:T(8,128)} %bitcast.4), calls=%async_computation.1 | async-start | bytes 3145728 | tf_op jit(solution)/shard_map/all_to_all | solution.py:365
  56.5 2.8 %copy-start.3 = (f32[32,32,32]{2,1,0:T(8,128)S(1)}, f32[32,32,32]{2,1,0:T(8,128)}, u32[]{:S(2)}) copy-start(f32[32,32,32]{2,1,0:T(8,128)} %matrix.1) | copy-start | bytes 393220
  56.6 2.7 %collective-permute-start.2 = (f32[2,16,32,256]{3,2,1,0:T(8,128)S(1)}, f32[2,16,32,256]{3,2,1,0:T(8,128)S(1)}, u32[]{:S(2)}, u32[]{:S(2)}) collective-permute-start(f32[2,16,32,256]{3,2,1,0:T(8,128)S(1)} %slice.11), channel_id=1, source_target_pairs={{0,1},{1,0},{2,3},{3,2},{4,5},{5,4},{6,7},{7,6},{8,9},{9,8},{10,11... | collective-permute-start | bytes 3145736 | tf_op jit(solution)/shard_map/ppermute | solution.py:290

commit v3 on v2

--- a/solution.py
+++ b/solution.py
@@ -11,7 +11,6 @@
 HALF = 128
 SUBLANES = 8
 VMEM_LIMIT = 32 * 1024 * 1024
-CHUNKS = 4
 GROUP = 4
 
 
@@ -20,16 +19,33 @@
     return (jnp.cos(latitude_angle), jnp.sin(latitude_angle))
 
 
-def tendency_kernel(prog, zonal, coriolis, out, ends, tile, turn, edges, stage, in_sems, out_sems):
+def flip(tiles):
+    row = lax.broadcasted_iota(jnp.int32, tiles[0].shape, 0)
+    for d in (4, 2, 1):
+        keep = (row & d) == 0
+        turned = list(tiles)
+        for i in range(SUBLANES):
+            if not i & d:
+                a, b = tiles[i], tiles[i + d]
+                turned[i] = jnp.where(keep, a, pltpu.roll(b, d, 0))
+                turned[i + d] = jnp.where(keep, pltpu.roll(a, SUBLANES - d, 0), b)
+        tiles = turned
+    return tiles
+
+
+def outer_rows_kernel(prog, last, first):
+    _, levels, rows, _ = prog.shape
+    for f in range(3):
+        for l in range(levels):
+            c = f * levels + l
+            last[c : c + 1, :] = prog[f, l, rows - 1 : rows, :]
+            first[c : c + 1, :] = prog[f, l, 0:1, :]
+
+
+def tendency_kernel(prog, zonal, coriolis, out, ends, turn, edges, stage, out_sems):
     _, levels, rows, width = prog.shape
     chans = 3 * levels
     payload = 2 * chans
-    per_chunk = levels // CHUNKS
-    loads = []
-    for chunk in range(CHUNKS):
-        some = pl.ds(chunk * per_chunk, per_chunk)
-        loads.append(pltpu.make_async_copy(prog.at[:, some], tile.at[:, some], in_sems.at[chunk]))
-        loads[-1].start()
     row_id = lax.broadcasted_iota(jnp.int32, (rows, width), 0)
     col_id = lax.broadcasted_iota(jnp.int32, (rows, width), 1)
     lane_id = lax.broadcasted_iota(jnp.int32, (rows, HALF), 1)
@@ -38,12 +54,10 @@
     zon, cor = zonal[...], coriolis[...]
     edge_rows = jnp.zeros((rows, HALF), jnp.float32)
     for l in range(levels):
-        if l % per_chunk == 0:
-            loads[l // per_chunk].wait()
         centre, dx, dy, sx = [], [], [], []
         for f in range(3):
             c = f * levels + l
-            here = tile[f, l]
+            here = prog[f, l]
             e = jnp.where(last_col, 0.0, pltpu.roll(here, width - 1, 1))
             w = jnp.where(first_col, 0.0, pltpu.roll(here, 1, 1))
             n = jnp.where(last_row, 0.0, pltpu.roll(here, rows - 1, 0))
@@ -64,22 +78,27 @@
             -zon * dx[0] - MERIDIONAL * dy[1],
         )
         for f in range(3):
+            turn[f, l] = tends[f]
+    edges[...] = edge_rows
+    copies = []
+    for chunk in range(rows // SUBLANES):
+        some = slice(chunk * SUBLANES, (chunk + 1) * SUBLANES)
+        for f in range(3):
             for half in range(2):
-                turn[f, half, l * rows : (l + 1) * rows, :] = tends[f][:, half * HALF : (half + 1) * HALF]
-    edges[...] = edge_rows
-    per_chunk = rows // CHUNKS
-    copies = []
-    for chunk in range(CHUNKS):
-        for j in range(chunk * per_chunk, (chunk + 1) * per_chunk):
-            for f in range(3):
-                for half in range(2):
-                    at = (2 * f + half) * levels
-                    value = turn[f, half, pl.ds(j, levels, stride=rows), :]
-                    stage[j, at : at + levels, :] = value
-                    if j in (0, rows - 1):
-                        ends[min(j, 1), at : at + levels, :] = value
+                for l0 in range(0, levels, SUBLANES):
+                    at = (2 * f + half) * levels + l0
+                    flipped = flip(
+                        [turn[f, l0 + i, some, half * HALF : (half + 1) * HALF] for i in range(SUBLANES)]
+                    )
+                    for k, value in enumerate(flipped):
+                        j = chunk * SUBLANES + k
+                        stage[j, at : at + SUBLANES, :] = value
+                        if j in (0, rows - 1):
+                            ends[min(j, 1), at : at + SUBLANES, :] = value
+        for k in range(SUBLANES):
+            j = chunk * SUBLANES + k
             stage[j, payload:, :] = jnp.broadcast_to(edges[j : j + 1, :], (SUBLANES, HALF))
-        some = pl.ds(chunk * per_chunk, per_chunk)
+        some = pl.ds(chunk * SUBLANES, SUBLANES)
         copies.append(pltpu.make_async_copy(stage.at[some], out.at[some], out_sems.at[chunk]))
         copies[-1].start()
     for copy in copies:
@@ -228,24 +247,34 @@
 
 def base_kernel(own_part, own, other, matrix, out):
     _, levels, rows, width = own.shape
-    mine = own.reshape(3, levels * rows, width)
-    theirs = other.reshape(2, levels * rows, width)
     lower = own_part[0] == 0
-    for j in range(rows):
-        mixer = mix_operand(matrix[j])
-        winds = []
-        for f in range(2):
-            a = mine[f, pl.ds(j, levels, stride=rows), :]
-            b = theirs[f, pl.ds(j, levels, stride=rows), :]
-            winds.append(jnp.concatenate([jnp.where(lower, a, b), jnp.where(lower, b, a)], axis=0))
-        wind_hi, wind_lo = split2(jnp.concatenate(winds, axis=1))
-        mixed = jnp.dot(
-            mixer, jnp.concatenate([wind_hi, wind_lo, wind_hi], axis=0), preferred_element_type=jnp.float32
-        )
-        kept = jnp.where(lower, mixed[:levels], mixed[levels:])
-        for f in range(2):
-            out[j, f, 0] = kept[:, f * width : (f + 1) * width]
-        out[j, 2, 0] = mine[2, pl.ds(j, levels, stride=rows), :]
+
+    def by_row(ref, f, j0):
+        flipped = [
+            flip([ref[f, l0 + i, j0 : j0 + SUBLANES, :] for i in range(SUBLANES)])
+            for l0 in range(0, levels, SUBLANES)
+        ]
+        return [jnp.concatenate([part[k] for part in flipped], axis=0) for k in range(SUBLANES)]
+
+    for j0 in range(0, rows, SUBLANES):
+        mine = [by_row(own, f, j0) for f in range(3)]
+        theirs = [by_row(other, f, j0) for f in range(2)]
+        for k in range(SUBLANES):
+            j = j0 + k
+            winds = []
+            for f in range(2):
+                a, b = mine[f][k], theirs[f][k]
+                winds.append(jnp.concatenate([jnp.where(lower, a, b), jnp.where(lower, b, a)], axis=0))
+            wind_hi, wind_lo = split2(jnp.concatenate(winds, axis=1))
+            mixed = jnp.dot(
+                mix_operand(matrix[j]),
+                jnp.concatenate([wind_hi, wind_lo, wind_hi], axis=0),
+                preferred_element_type=jnp.float32,
+            )
+            kept = jnp.where(lower, mixed[:levels], mixed[levels:])
+            for f in range(2):
+                out[j, f, 0] = kept[:, f * width : (f + 1) * width]
+            out[j, 2, 0] = mine[2][k]
 
 
 def finish_kernel(step, base, out, added, stage, in_sems, out_sems):
@@ -256,16 +285,18 @@
         loads[-1].start()
     for f in range(fields):
         loads[f].wait()
-        for half in range(2):
-            for j in range(rows):
-                stage[f, half, pl.ds(j, levels, stride=rows), :] = step[j, f, half] + added[f, j, half]
-            copies.append(
-                pltpu.make_async_copy(
-                    stage.at[f, half].reshape(levels, rows, HALF),
-                    out.at[f, :, :, pl.ds(half * HALF, HALF)],
-                    out_sems.at[2 * f + half],
-                )
-            )
+        for l0 in range(0, levels, SUBLANES):
+            some = slice(l0, l0 + SUBLANES)
+            for half in range(2):
+                for j0 in range(0, rows, SUBLANES):
+                    flipped = flip(
+                        [step[j0 + k, f, half, some, :] + added[f, j0 + k, half, some, :] for k in range(SUBLANES)]
+                    )
+                    for i, value in enumerate(flipped):
+                        stage[f, l0 + i, j0 : j0 + SUBLANES, half * HALF : (half + 1) * HALF] = value
+            at = f * (levels // SUBLANES) + l0 // SUBLANES
+            some = pl.ds(l0, SUBLANES)
+            copies.append(pltpu.make_async_copy(stage.at[f, some], out.at[f, some], out_sems.at[at]))
             copies[-1].start()
     for copy in copies:
         copy.wait()
@@ -281,12 +312,16 @@
     hbm = pl.BlockSpec(memory_space=pltpu.HBM)
     vmem = pl.BlockSpec(memory_space=pltpu.VMEM)
 
-    south = lax.ppermute(
-        prognostic[:, :, rows - 1, :].reshape(chans, width), "lat", [(i, i + 1) for i in range(lat_devices - 1)]
-    )
-    north = lax.ppermute(
-        prognostic[:, :, 0, :].reshape(chans, width), "lat", [(i + 1, i) for i in range(lat_devices - 1)]
-    )
+    with jax.named_scope("outer_rows"):
+        last, first = pl.pallas_call(
+            outer_rows_kernel,
+            out_shape=(jax.ShapeDtypeStruct((chans, width), jnp.float32),) * 2,
+            in_specs=[vmem],
+            out_specs=(vmem, vmem),
+            compiler_params=params,
+        )(prognostic)
+    south = lax.ppermute(last, "lat", [(i, i + 1) for i in range(lat_devices - 1)])
+    north = lax.ppermute(first, "lat", [(i + 1, i) for i in range(lat_devices - 1)])
     other = lax.ppermute(prognostic[:2], "lev", [(0, 1), (1, 0)])
 
     global_rows = (lat_index * rows + jnp.arange(rows)).astype(jnp.float32)
@@ -303,15 +338,13 @@
                 jax.ShapeDtypeStruct((rows, sent_rows, HALF), jnp.float32),
                 jax.ShapeDtypeStruct((2, halves * chans, HALF), jnp.float32),
             ),
-            in_specs=[hbm, vmem, vmem],
+            in_specs=[vmem, vmem, vmem],
             out_specs=(hbm, vmem),
             scratch_shapes=[
                 pltpu.VMEM(prognostic.shape, jnp.float32),
-                pltpu.VMEM((fields, halves, levels * rows, HALF), jnp.float32),
                 pltpu.VMEM((rows, HALF), jnp.float32),
                 pltpu.VMEM((rows, sent_rows, HALF), jnp.float32),
-                pltpu.SemaphoreType.DMA((CHUNKS,)),
-                pltpu.SemaphoreType.DMA((CHUNKS,)),
+                pltpu.SemaphoreType.DMA((rows // SUBLANES,)),
             ],
             compiler_params=params,
         )(prognostic, zonal_field, coriolis_field)
@@ -391,9 +424,9 @@
             out_specs=hbm,
             scratch_shapes=[
                 pltpu.VMEM((fields, rows, halves, levels, HALF), jnp.float32),
-                pltpu.VMEM((fields, halves, levels * rows, HALF), jnp.float32),
+                pltpu.VMEM(prognostic.shape, jnp.float32),
                 pltpu.SemaphoreType.DMA((fields,)),
-                pltpu.SemaphoreType.DMA((fields * halves,)),
+                pltpu.SemaphoreType.DMA((fields * levels // SUBLANES,)),
             ],
             compiler_params=params,
         )(returned, base)

time: 84.5 us -> 88.5 us (1.047)
  waiting for transfers between devices: 46.4 us -> 49.7 us
  local copies, waits for them, and re-layouts: 2.87 us -> 3.86 us
    pallas_call x1, Pallas kernels: 4.52 us -> 7.2 us  [per_device(): pl.pallas_call(filter_kernel, out_shape=jax.ShapeDtypeStruct(stepped_shap...]
    ppermute x2, waiting for transfers between devices: 0.04 us -> 2.26 us  [the longest x1 2.26 us: per_device(): lax.ppermute(first, 'lat', [(i + 1, i) for i in range(lat_devices - 1)])]
    unnamed x14, local copies, waits for them, and re-layouts: 1.46 us -> 3.61 us
    slice x1 -> x0, local copies, waits for them, and re-layouts: 1.19 us -> none  [per_device(): prognostic[:, :, 0, :].reshape(chans, width)]
    pallas_call x1, Pallas kernels: 2.61 us -> 1.6 us  [per_device(): pl.pallas_call(base_kernel, out_shape=jax.ShapeDtypeStruct(returned.shape...]
    all_to_all x1, waiting for transfers between devices: 18.4 us -> 19.4 us  [per_device(): lax.all_to_all(stepped.reshape((rows,) + stepped_shape[2:]), ('lon', 'lev...]
  transfers between devices with their start and end apart: 5 -> 5, of which waited for: 3 -> 4; matrix products, arithmetic and copies ran while one was open for 0% -> 0% of each run, Pallas kernels for 7% -> 5%
where the time goes in v3:
time: 88.5 us; the launch traced here: 88.1 us
  waiting for transfers between devices  49.7 us (56%)
  starting transfers between devices  19.3 us (22%)
  Pallas kernels  15.1 us (17%)
  local copies, waits for them, and re-layouts  3.86 us (4%)
    all_to_all x1, waiting for transfers between devices, per_device(): whole_rows = lax.all_to_all(tend, ('lon', 'lev'), 0, 0, tiled=True)  25.4 us
    all_to_all x1, waiting for transfers between devices, per_device(): lax.all_to_all(stepped.reshape((rows,) + stepped_shape[2:]), ('lon', 'lev...  19.4 us
    all_to_all x1, starting transfers between devices, per_device(): whole_rows = lax.all_to_all(tend, ('lon', 'lev'), 0, 0, tiled=True)  7.33 us
    pallas_call x1, Pallas kernels, per_device(): pl.pallas_call(filter_kernel, out_shape=jax.ShapeDtypeStruct(stepped_shap...  7.2 us
    ppermute x1, starting transfers between devices, per_device(): lax.ppermute(last, 'lat', [(i, i + 1) for i in range(lat_devices - 1)])  5.17 us
    all_to_all x1, starting transfers between devices, per_device(): lax.all_to_all(stepped.reshape((rows,) + stepped_shape[2:]), ('lon', 'lev...  4.69 us
    unnamed x14, local copies, waits for them, and re-layouts  3.61 us
    pallas_call x1, Pallas kernels, per_device(): pl.pallas_call(finish_kernel, out_shape=jax.ShapeDtypeStruct(prognostic.s...  2.8 us
  transfers between devices with their start and end apart: 5, of which 4 were waited for; matrix products, arithmetic and copies ran while one was open for 0% of the time, Pallas kernels for 5%

profile of v3, /device:TPU:96, one launch (start us, length us, event | category | flops | bytes accessed | tf_op | source)
XLA Modules:
  0.0 88.1 jit_solution(6792880046944535472)
XLA Ops:
  0.0 0.0 copy-start
  0.0 1.4 %copy-done = f32[3,16,32,256]{3,2,1,0:T(8,128)S(1)} copy-done((f32[3,16,32,256]{3,2,1,0:T(8,128)S(1)}, f32[3,16,32,256]{3,2,1,0:T(8,128)}, u32[]{:S(2)}) %copy-start) | copy-done | bytes 1572888
  1.4 0.0 copy-start.1
  1.4 0.1 outer_rows.1
  1.5 5.2 %collective-permute-start = (f32[48,256]{1,0:T(8,128)S(1)}, f32[48,256]{1,0:T(8,128)S(1)}, u32[]{:S(2)}, u32[]{:S(2)}) collective-permute-start(f32[48,256]{1,0:T(8,128)S(1)} %get-tuple-element.10), channel_id=1, source_target_pairs={{0,2},{2,4},{4,6},{6,8},{8,10},{10,12},{12,14},{1,3},{3,5},{5,7},{... | collective-permute-start | bytes 147464 | tf_op jit(solution)/shard_map/ppermute | solution.py:323
  6.6 1.9 %collective-permute-start.1 = (f32[48,256]{1,0:T(8,128)S(1)}, f32[48,256]{1,0:T(8,128)S(1)}, u32[]{:S(2)}, u32[]{:S(2)}) collective-permute-start(f32[48,256]{1,0:T(8,128)S(1)} %get-tuple-element.11), channel_id=1, source_target_pairs={{2,0},{4,2},{6,4},{8,6},{10,8},{12,10},{14,12},{3,1},{5,3},{7,5},{... | collective-permute-start | bytes 147464 | tf_op jit(solution)/shard_map/ppermute | solution.py:324
  8.6 0.1 broadcast_in_dim.4.zonal
  8.7 0.1 broadcast_in_dim.5.coriolis
  8.8 0.0 copy-done.1
  8.8 2.8 %tendencies.1 = (f32[32,104,128]{2,1,0:T(8,128)}, f32[2,96,128]{2,1,0:T(8,128)S(1)}) custom-call(f32[3,16,32,256]{3,2,1,0:T(8,128)S(1)} %copy-done.1, f32[32,256]{1,0:T(8,128)S(1)} %broadcast_in_dim.4.zonal, f32[32,256]{1,0:T(8,128)S(1)} %broadcast_in_dim.5.coriolis), custom_call_target="tpu_custom_call" | custom-call | tf_op jit(solution)/shard_map/tendencies/pallas_call | solution.py:335
  11.6 0.0 collective-permute-done.south
  11.6 2.3 %collective-permute-done.1.north = f32[48,256]{1,0:T(8,128)S(1)} collective-permute-done((f32[48,256]{1,0:T(8,128)S(1)}, f32[48,256]{1,0:T(8,128)S(1)}, u32[]{:S(2)}, u32[]{:S(2)}) %collective-permute-start.1) | collective-permute-done | bytes 49184 | tf_op jit(solution)/shard_map/ppermute | solution.py:324
  13.8 0.7 seam_rows.1
  14.5 0.0 copy-start.5
  14.5 0.0 copy-start.6
  14.5 7.3 %all-to-all-start = ((f32[32,104,128]{2,1,0:T(8,128)}), f32[32,104,128]{2,1,0:T(8,128)S(1)}, u32[]{:S(2)}, u32[]{:S(2)}) async-start(f32[32,104,128]{2,1,0:T(8,128)} %seam_rows.1), calls=%async_computation | async-start | bytes 3407872 | tf_op jit(solution)/shard_map/all_to_all | solution.py:363
  21.9 25.4 %all-to-all-done = f32[32,104,128]{2,1,0:T(8,128)S(1)} async-done(((f32[32,104,128]{2,1,0:T(8,128)}), f32[32,104,128]{2,1,0:T(8,128)S(1)}, u32[]{:S(2)}, u32[]{:S(2)}) %all-to-all-start) | async-done | bytes 1703968 | tf_op jit(solution)/shard_map/all_to_all | solution.py:363
  47.3 0.0 copy-done.5
  47.3 0.0 copy-done.6
  47.3 0.0 copy-start.3
  47.3 1.0 %copy-done.3 = f32[32,32,32]{2,1,0:T(8,128)S(1)} copy-done((f32[32,32,32]{2,1,0:T(8,128)S(1)}, f32[32,32,32]{2,1,0:T(8,128)}, u32[]{:S(2)}) %copy-start.3) | copy-done | bytes 131096
  48.3 7.2 %row_filter.1 = f32[16,2,3,2,16,128]{5,4,3,2,1,0:T(8,128)S(1)} custom-call(s32[1]{0:T(128)} %bitcast.own_row, s32[32]{0:T(128)S(1)} %copy-done.5, s32[32]{0:T(128)S(1)} %copy-done.6, f32[32]{0:T(128)S(1)} %get-tuple-element.14.zonal, f32[16,2,104,128]{3,2,1,0:T(8,128)S(1)} %bitcast.4, f32[32,32,32]{2,1,0:T(8,128)S(1)} %copy-done.3), custom_call_target="tpu_custom_call" | custom-call | tf_op jit(solution)/shard_map/row_filter/pallas_call | solution.py:370
  55.5 0.0 copy-start.2
  55.5 1.1 %copy-done.2 = f32[16,2,3,2,16,128]{5,4,3,2,1,0:T(8,128)} copy-done((f32[16,2,3,2,16,128]{5,4,3,2,1,0:T(8,128)}, f32[16,2,3,2,16,128]{5,4,3,2,1,0:T(8,128)S(1)}, u32[]{:S(2)}) %copy-start.2) | copy-done | bytes 1572888
  56.7 4.7 %all-to-all-start.1 = ((f32[32,3,2,16,128]{4,3,2,1,0:T(8,128)}), f32[32,3,2,16,128]{4,3,2,1,0:T(8,128)}, u32[]{:S(2)}, u32[]{:S(2)}) async-start(f32[32,3,2,16,128]{4,3,2,1,0:T(8,128)} %bitcast.5), calls=%async_computation.1 | async-start | bytes 3145728 | tf_op jit(solution)/shard_map/all_to_all | solution.py:398
  61.4 0.0 copy-start.4
  61.4 0.1 slice.3
  61.5 0.2 collective-permute-start.2
  61.7 2.6 %collective-permute-done.2.other = f32[2,16,32,256]{3,2,1,0:T(8,128)S(1)} collective-permute-done((f32[2,16,32,256]{3,2,1,0:T(8,128)S(1)}, f32[2,16,32,256]{3,2,1,0:T(8,128)S(1)}, u32[]{:S(2)}, u32[]{:S(2)}) %collective-permute-start.2) | collective-permute-done | bytes 1048608 | tf_op jit(solution)/shard_map/ppermute | solution.py:325
  64.2 0.0 copy-done.4
  64.2 1.6 %base.1 = f32[32,3,2,16,128]{4,3,2,1,0:T(8,128)S(1)} custom-call(s32[1]{0:T(128)} %bitcast.3.own_part, f32[3,16,32,256]{3,2,1,0:T(8,128)S(1)} %copy-done.1, f32[2,16,32,256]{3,2,1,0:T(8,128)S(1)} %collective-permute-done.2.other, f32[32,32,32]{2,1,0:T(8,128)S(1)} %copy-done.4), custom_call_target="tpu_custom_call" | custom-call | tf_op jit(solution)/shard_map/base/pallas_call | solution.py:403
  65.9 19.4 %all-to-all-done.1.step = f32[32,3,2,16,128]{4,3,2,1,0:T(8,128)} async-done(((f32[32,3,2,16,128]{4,3,2,1,0:T(8,128)}), f32[32,3,2,16,128]{4,3,2,1,0:T(8,128)}, u32[]{:S(2)}, u32[]{:S(2)}) %all-to-all-start.1) | async-done | bytes 1572896 | tf_op jit(solution)/shard_map/all_to_all | solution.py:398
  85.3 2.8 %finish.1 = f32[3,16,32,256]{3,2,1,0:T(8,128)} custom-call(f32[32,3,2,16,128]{4,3,2,1,0:T(8,128)} %all-to-all-done.1.step, f32[32,3,2,16,128]{4,3,2,1,0:T(8,128)S(1)} %base.1), custom_call_target="tpu_custom_call" | custom-call | tf_op jit(solution)/shard_map/finish/pallas_call | solution.py:420
  (1 shorter events, 0.0 us)
Async XLA Ops:
  0.0 1.4 %copy-start = (f32[3,16,32,256]{3,2,1,0:T(8,128)S(1)}, f32[3,16,32,256]{3,2,1,0:T(8,128)}, u32[]{:S(2)}) copy-start(f32[3,16,32,256]{3,2,1,0:T(8,128)} %own.1) | copy-start | bytes 4718596
  1.4 7.4 %copy-start.1 = (f32[3,16,32,256]{3,2,1,0:T(8,128)S(1)}, f32[3,16,32,256]{3,2,1,0:T(8,128)}, u32[]{:S(2)}) copy-start(f32[3,16,32,256]{3,2,1,0:T(8,128)} %own.1) | copy-start | bytes 4718596
  1.5 10.1 %collective-permute-start = (f32[48,256]{1,0:T(8,128)S(1)}, f32[48,256]{1,0:T(8,128)S(1)}, u32[]{:S(2)}, u32[]{:S(2)}) collective-permute-start(f32[48,256]{1,0:T(8,128)S(1)} %get-tuple-element.10), channel_id=1, source_target_pairs={{0,2},{2,4},{4,6},{6,8},{8,10},{10,12},{12,14},{1,3},{3,5},{5,7},{... | collective-permute-start | bytes 147464 | tf_op jit(solution)/shard_map/ppermute | solution.py:323
  6.6 7.2 %collective-permute-start.1 = (f32[48,256]{1,0:T(8,128)S(1)}, f32[48,256]{1,0:T(8,128)S(1)}, u32[]{:S(2)}, u32[]{:S(2)}) collective-permute-start(f32[48,256]{1,0:T(8,128)S(1)} %get-tuple-element.11), channel_id=1, source_target_pairs={{2,0},{4,2},{6,4},{8,6},{10,8},{12,10},{14,12},{3,1},{5,3},{7,5},{... | collective-permute-start | bytes 147464 | tf_op jit(solution)/shard_map/ppermute | solution.py:324
  14.5 32.8 %copy-start.5 = (s32[32]{0:T(128)S(1)}, s32[32]{0:T(128)}, u32[]{:S(2)}) copy-start(s32[32]{0:T(128)} %half_width.1) | copy-start | bytes 388
  14.5 32.8 %copy-start.6 = (s32[32]{0:T(128)S(1)}, s32[32]{0:T(128)}, u32[]{:S(2)}) copy-start(s32[32]{0:T(128)} %filter_mask.1) | copy-start | bytes 388
  14.5 32.7 %all-to-all-start = ((f32[32,104,128]{2,1,0:T(8,128)}), f32[32,104,128]{2,1,0:T(8,128)S(1)}, u32[]{:S(2)}, u32[]{:S(2)}) async-start(f32[32,104,128]{2,1,0:T(8,128)} %seam_rows.1), calls=%async_computation | async-start | bytes 3407872 | tf_op jit(solution)/shard_map/all_to_all | solution.py:363
  47.3 1.0 %copy-start.3 = (f32[32,32,32]{2,1,0:T(8,128)S(1)}, f32[32,32,32]{2,1,0:T(8,128)}, u32[]{:S(2)}) copy-start(f32[32,32,32]{2,1,0:T(8,128)} %matrix.1) | copy-start | bytes 393220
  55.5 1.1 %copy-start.2 = (f32[16,2,3,2,16,128]{5,4,3,2,1,0:T(8,128)}, f32[16,2,3,2,16,128]{5,4,3,2,1,0:T(8,128)S(1)}, u32[]{:S(2)}) copy-start(f32[16,2,3,2,16,128]{5,4,3,2,1,0:T(8,128)S(1)} %row_filter.1) | copy-start | bytes 4718596
  56.7 28.6 %all-to-all-start.1 = ((f32[32,3,2,16,128]{4,3,2,1,0:T(8,128)}), f32[32,3,2,16,128]{4,3,2,1,0:T(8,128)}, u32[]{:S(2)}, u32[]{:S(2)}) async-start(f32[32,3,2,16,128]{4,3,2,1,0:T(8,128)} %bitcast.5), calls=%async_computation.1 | async-start | bytes 3145728 | tf_op jit(solution)/shard_map/all_to_all | solution.py:398
  61.4 2.9 %copy-start.4 = (f32[32,32,32]{2,1,0:T(8,128)S(1)}, f32[32,32,32]{2,1,0:T(8,128)}, u32[]{:S(2)}) copy-start(f32[32,32,32]{2,1,0:T(8,128)} %matrix.1) | copy-start | bytes 393220
  61.5 2.7 %collective-permute-start.2 = (f32[2,16,32,256]{3,2,1,0:T(8,128)S(1)}, f32[2,16,32,256]{3,2,1,0:T(8,128)S(1)}, u32[]{:S(2)}, u32[]{:S(2)}) collective-permute-start(f32[2,16,32,256]{3,2,1,0:T(8,128)S(1)} %slice.3), channel_id=1, source_target_pairs={{0,1},{1,0},{2,3},{3,2},{4,5},{5,4},{6,7},{7,6},{8,9},{9,8},{10,11... | collective-permute-start | bytes 3145736 | tf_op jit(solution)/shard_map/ppermute | solution.py:325

commit v4 on v3

--- a/solution.py
+++ b/solution.py
@@ -11,6 +11,7 @@
 HALF = 128
 SUBLANES = 8
 VMEM_LIMIT = 32 * 1024 * 1024
+VMEM_MOST = 60 * 1024 * 1024
 GROUP = 4
 
 
@@ -136,7 +137,7 @@
 
 
 def filter_kernel(
-    own_row, half_width, filter_mask, zonal, tend, matrices, out, halves, parts, seam, matrix, stage, matrix_sem, sems
+    own_row, half_width, filter_mask, zonal, tend, matrix, out, halves, parts, seam, stage, sems
 ):
     blocks, lev_parts, levels = out.shape[0], out.shape[1], out.shape[4]
     chans = 3 * levels
@@ -144,8 +145,6 @@
     count = 2 * blocks
     both = lev_parts * chans
     row = own_row[0]
-    fetch = pltpu.make_async_copy(matrices.at[row], matrix, matrix_sem)
-    fetch.start()
     reach = half_width[row]
     whole = reach == count // 2
     norm = jnp.where(whole, count * HALF, 2 * HALF * reach + 1).astype(jnp.float32)
@@ -183,7 +182,6 @@
     src = lax.broadcasted_iota(jnp.int32, (2 * HALF, HALF), 0)
     dst = lax.broadcasted_iota(jnp.int32, (2 * HALF, HALF), 1)
     sums = jnp.where((src <= dst) | (src >= HALF), 1.0, 0.0).astype(jnp.bfloat16)
-    fetch.wait()
     mixer = mix_operand(matrix[...])
     scale = TIME_STEP / norm
 
@@ -309,6 +307,7 @@
     chans = fields * levels
     halves = width // HALF
     params = pltpu.CompilerParams(vmem_limit_bytes=VMEM_LIMIT)
+    most = pltpu.CompilerParams(vmem_limit_bytes=VMEM_MOST)
     hbm = pl.BlockSpec(memory_space=pltpu.HBM)
     vmem = pl.BlockSpec(memory_space=pltpu.VMEM)
 
@@ -373,26 +372,24 @@
             grid_spec=pltpu.PrefetchScalarGridSpec(
                 num_scalar_prefetch=4,
                 grid=(1,),
-                in_specs=[vmem, hbm],
+                in_specs=[vmem, vmem],
                 out_specs=hbm,
                 scratch_shapes=[
                     pltpu.VMEM((count, both, HALF), jnp.float32),
                     pltpu.VMEM((2, count * both, 2 * HALF), jnp.bfloat16),
                     pltpu.VMEM((HALF, HALF), jnp.float32),
-                    pltpu.VMEM(column_inverse.shape[1:], jnp.float32),
                     pltpu.VMEM(stepped_shape, jnp.float32),
-                    pltpu.SemaphoreType.DMA,
                     pltpu.SemaphoreType.DMA((lon_devices,)),
                 ],
             ),
-            compiler_params=params,
+            compiler_params=most,
         )(
             own_row,
             half_width,
             filter_mask,
             zonal,
             whole_rows.reshape(lon_devices, lev_devices, sent_rows, HALF),
-            column_inverse,
+            lax.dynamic_index_in_dim(column_inverse, own_row[0], 0, keepdims=False),
         )
 
     returned = lax.all_to_all(
@@ -428,7 +425,7 @@
                 pltpu.SemaphoreType.DMA((fields,)),
                 pltpu.SemaphoreType.DMA((fields * levels // SUBLANES,)),
             ],
-            compiler_params=params,
+            compiler_params=most,
         )(returned, base)
 
 

time: 88.5 us -> 86.5 us (0.977)
  waiting for transfers between devices: 49.7 us -> 47.9 us
    all_to_all x1, waiting for transfers between devices: 19.4 us -> 18.3 us  [per_device(): lax.all_to_all(stepped.reshape((rows,) + stepped_shape[2:]), ('lon', 'lev...]
    unnamed x14 -> x10, local copies, waits for them, and re-layouts: 3.61 us -> 2.55 us
    pallas_call x1, Pallas kernels: 7.2 us -> 6.17 us  [per_device(): pl.pallas_call(filter_kernel, out_shape=jax.ShapeDtypeStruct(stepped_shap...]
    pallas_call x1, Pallas kernels: 2.8 us -> 3.73 us  [per_device(): pl.pallas_call(finish_kernel, out_shape=jax.ShapeDtypeStruct(prognostic.s...]
  transfers between devices with their start and end apart: 5 -> 5, of which waited for: 4 -> 4; matrix products, arithmetic and copies ran while one was open for 0% -> 1% of each run, Pallas kernels for 5% -> 5%
where the time goes in v4:
time: 86.5 us; the launch traced here: 86.1 us
  waiting for transfers between devices  47.9 us (55%)
  starting transfers between devices  19.6 us (23%)
  Pallas kernels  15 us (17%)
  local copies, waits for them, and re-layouts  3.41 us (4%)
    all_to_all x1, waiting for transfers between devices, per_device(): whole_rows = lax.all_to_all(tend, ('lon', 'lev'), 0, 0, tiled=True)  24.8 us
    all_to_all x1, waiting for transfers between devices, per_device(): lax.all_to_all(stepped.reshape((rows,) + stepped_shape[2:]), ('lon', 'lev...  18.3 us
    all_to_all x1, starting transfers between devices, per_device(): whole_rows = lax.all_to_all(tend, ('lon', 'lev'), 0, 0, tiled=True)  7.58 us
    pallas_call x1, Pallas kernels, per_device(): pl.pallas_call(filter_kernel, out_shape=jax.ShapeDtypeStruct(stepped_shap...  6.17 us
    ppermute x1, starting transfers between devices, per_device(): lax.ppermute(last, 'lat', [(i, i + 1) for i in range(lat_devices - 1)])  5.17 us
    all_to_all x1, starting transfers between devices, per_device(): lax.all_to_all(stepped.reshape((rows,) + stepped_shape[2:]), ('lon', 'lev...  4.71 us
    pallas_call x1, Pallas kernels, per_device(): pl.pallas_call(finish_kernel, out_shape=jax.ShapeDtypeStruct(prognostic.s...  3.73 us
    pallas_call x1, Pallas kernels, per_device(): pl.pallas_call(tendency_kernel, out_shape=(jax.ShapeDtypeStruct((rows, se...  2.76 us
  transfers between devices with their start and end apart: 5, of which 4 were waited for; matrix products, arithmetic and copies ran while one was open for 1% of the time, Pallas kernels for 5%

profile of v4, /device:TPU:96, one launch (start us, length us, event | category | flops | bytes accessed | tf_op | source)
XLA Modules:
  0.0 86.1 jit_solution(16488454621505444616)
XLA Ops:
  0.0 0.0 copy-start
  0.0 1.4 %copy-done = f32[3,16,32,256]{3,2,1,0:T(8,128)S(1)} copy-done((f32[3,16,32,256]{3,2,1,0:T(8,128)S(1)}, f32[3,16,32,256]{3,2,1,0:T(8,128)}, u32[]{:S(2)}) %copy-start) | copy-done | bytes 1572888
  1.4 0.0 copy-start.1
  1.4 0.1 outer_rows.1
  1.5 5.2 %collective-permute-start = (f32[48,256]{1,0:T(8,128)S(1)}, f32[48,256]{1,0:T(8,128)S(1)}, u32[]{:S(2)}, u32[]{:S(2)}) collective-permute-start(f32[48,256]{1,0:T(8,128)S(1)} %get-tuple-element.10), channel_id=1, source_target_pairs={{0,2},{2,4},{4,6},{6,8},{8,10},{10,12},{12,14},{1,3},{3,5},{5,7},{... | collective-permute-start | bytes 147464 | tf_op jit(solution)/shard_map/ppermute | solution.py:322
  6.6 1.9 %collective-permute-start.1 = (f32[48,256]{1,0:T(8,128)S(1)}, f32[48,256]{1,0:T(8,128)S(1)}, u32[]{:S(2)}, u32[]{:S(2)}) collective-permute-start(f32[48,256]{1,0:T(8,128)S(1)} %get-tuple-element.11), channel_id=1, source_target_pairs={{2,0},{4,2},{6,4},{8,6},{10,8},{12,10},{14,12},{3,1},{5,3},{7,5},{... | collective-permute-start | bytes 147464 | tf_op jit(solution)/shard_map/ppermute | solution.py:323
  8.6 0.0 copy-start.4
  8.6 0.1 broadcast_in_dim.4.zonal
  8.7 0.1 broadcast_in_dim.5.coriolis
  8.8 0.0 copy-done.1
  8.8 2.8 %tendencies.1 = (f32[32,104,128]{2,1,0:T(8,128)}, f32[2,96,128]{2,1,0:T(8,128)S(1)}) custom-call(f32[3,16,32,256]{3,2,1,0:T(8,128)S(1)} %copy-done.1, f32[32,256]{1,0:T(8,128)S(1)} %broadcast_in_dim.4.zonal, f32[32,256]{1,0:T(8,128)S(1)} %broadcast_in_dim.5.coriolis), custom_call_target="tpu_custom_call" | custom-call | tf_op jit(solution)/shard_map/tendencies/pallas_call | solution.py:334
  11.5 0.0 collective-permute-done.south
  11.6 2.3 %collective-permute-done.1.north = f32[48,256]{1,0:T(8,128)S(1)} collective-permute-done((f32[48,256]{1,0:T(8,128)S(1)}, f32[48,256]{1,0:T(8,128)S(1)}, u32[]{:S(2)}, u32[]{:S(2)}) %collective-permute-start.1) | collective-permute-done | bytes 49184 | tf_op jit(solution)/shard_map/ppermute | solution.py:323
  13.8 0.7 seam_rows.1
  14.5 0.0 copy-done.4
  14.5 0.0 copy-start.3
  14.5 7.6 %all-to-all-start = ((f32[32,104,128]{2,1,0:T(8,128)}), f32[32,104,128]{2,1,0:T(8,128)}, u32[]{:S(2)}, u32[]{:S(2)}) async-start(f32[32,104,128]{2,1,0:T(8,128)} %seam_rows.1), calls=%async_computation | async-start | bytes 3407872 | tf_op jit(solution)/shard_map/all_to_all | solution.py:362
  22.1 0.0 copy-done.3
  22.1 0.6 dynamic-slice_bitcast_fusion.matrix
  22.7 24.8 %all-to-all-done = f32[32,104,128]{2,1,0:T(8,128)} async-done(((f32[32,104,128]{2,1,0:T(8,128)}), f32[32,104,128]{2,1,0:T(8,128)}, u32[]{:S(2)}, u32[]{:S(2)}) %all-to-all-start) | async-done | bytes 1703968 | tf_op jit(solution)/shard_map/all_to_all | solution.py:362
  47.5 6.2 %row_filter.1 = f32[16,2,3,2,16,128]{5,4,3,2,1,0:T(8,128)} custom-call(s32[1]{0:T(128)} %bitcast.own_row, s32[32]{0:T(128)} %half_width.1, s32[32]{0:T(128)} %filter_mask.1, f32[32]{0:T(128)} %copy-done.4, f32[16,2,104,128]{3,2,1,0:T(8,128)} %bitcast.1.tend, f32[32,32]{1,0:T(8,128)} %dynamic-slice_bitcast_fusion.matrix), custom_call_target="tpu_custom_call" | custom-call | tf_op jit(solution)/shard_map/row_filter/pallas_call | solution.py:369
  53.7 4.7 %all-to-all-start.1 = ((f32[32,3,2,16,128]{4,3,2,1,0:T(8,128)}), f32[32,3,2,16,128]{4,3,2,1,0:T(8,128)}, u32[]{:S(2)}, u32[]{:S(2)}) async-start(f32[32,3,2,16,128]{4,3,2,1,0:T(8,128)} %bitcast.6), calls=%async_computation.1 | async-start | bytes 3145728 | tf_op jit(solution)/shard_map/all_to_all | solution.py:395
  58.4 0.1 slice.3
  58.5 0.2 collective-permute-start.2
  58.7 2.6 %collective-permute-done.2.other = f32[2,16,32,256]{3,2,1,0:T(8,128)S(1)} collective-permute-done((f32[2,16,32,256]{3,2,1,0:T(8,128)S(1)}, f32[2,16,32,256]{3,2,1,0:T(8,128)S(1)}, u32[]{:S(2)}, u32[]{:S(2)}) %collective-permute-start.2) | collective-permute-done | bytes 1048608 | tf_op jit(solution)/shard_map/ppermute | solution.py:324
  61.3 1.6 %base.1 = f32[32,3,2,16,128]{4,3,2,1,0:T(8,128)S(1)} custom-call(s32[1]{0:T(128)} %bitcast.4.own_part, f32[3,16,32,256]{3,2,1,0:T(8,128)S(1)} %copy-done.1, f32[2,16,32,256]{3,2,1,0:T(8,128)S(1)} %collective-permute-done.2.other, f32[32,32,32]{2,1,0:T(8,128)S(1)} %copy-done.3), custom_call_target="tpu_custom_call" | custom-call | tf_op jit(solution)/shard_map/base/pallas_call | solution.py:400
  62.9 0.0 copy-start.2
  62.9 1.1 %copy-done.2 = f32[32,3,2,16,128]{4,3,2,1,0:T(8,128)} copy-done((f32[32,3,2,16,128]{4,3,2,1,0:T(8,128)}, f32[32,3,2,16,128]{4,3,2,1,0:T(8,128)S(1)}, u32[]{:S(2)}) %copy-start.2) | copy-done | bytes 1572888
  64.0 18.3 %all-to-all-done.1.step = f32[32,3,2,16,128]{4,3,2,1,0:T(8,128)} async-done(((f32[32,3,2,16,128]{4,3,2,1,0:T(8,128)}), f32[32,3,2,16,128]{4,3,2,1,0:T(8,128)}, u32[]{:S(2)}, u32[]{:S(2)}) %all-to-all-start.1) | async-done | bytes 1572896 | tf_op jit(solution)/shard_map/all_to_all | solution.py:395
  82.3 3.7 %finish.1 = f32[3,16,32,256]{3,2,1,0:T(8,128)} custom-call(f32[32,3,2,16,128]{4,3,2,1,0:T(8,128)} %all-to-all-done.1.step, f32[32,3,2,16,128]{4,3,2,1,0:T(8,128)} %copy-done.2), custom_call_target="tpu_custom_call" | custom-call | tf_op jit(solution)/shard_map/finish/pallas_call | solution.py:417
  (1 shorter events, 0.0 us)
Async XLA Ops:
  0.0 1.4 %copy-start = (f32[3,16,32,256]{3,2,1,0:T(8,128)S(1)}, f32[3,16,32,256]{3,2,1,0:T(8,128)}, u32[]{:S(2)}) copy-start(f32[3,16,32,256]{3,2,1,0:T(8,128)} %own.1) | copy-start | bytes 4718596
  1.4 7.4 %copy-start.1 = (f32[3,16,32,256]{3,2,1,0:T(8,128)S(1)}, f32[3,16,32,256]{3,2,1,0:T(8,128)}, u32[]{:S(2)}) copy-start(f32[3,16,32,256]{3,2,1,0:T(8,128)} %own.1) | copy-start | bytes 4718596
  1.5 10.1 %collective-permute-start = (f32[48,256]{1,0:T(8,128)S(1)}, f32[48,256]{1,0:T(8,128)S(1)}, u32[]{:S(2)}, u32[]{:S(2)}) collective-permute-start(f32[48,256]{1,0:T(8,128)S(1)} %get-tuple-element.10), channel_id=1, source_target_pairs={{0,2},{2,4},{4,6},{6,8},{8,10},{10,12},{12,14},{1,3},{3,5},{5,7},{... | collective-permute-start | bytes 147464 | tf_op jit(solution)/shard_map/ppermute | solution.py:322
  6.6 7.2 %collective-permute-start.1 = (f32[48,256]{1,0:T(8,128)S(1)}, f32[48,256]{1,0:T(8,128)S(1)}, u32[]{:S(2)}, u32[]{:S(2)}) collective-permute-start(f32[48,256]{1,0:T(8,128)S(1)} %get-tuple-element.11), channel_id=1, source_target_pairs={{2,0},{4,2},{6,4},{8,6},{10,8},{12,10},{14,12},{3,1},{5,3},{7,5},{... | collective-permute-start | bytes 147464 | tf_op jit(solution)/shard_map/ppermute | solution.py:323
  8.6 5.9 %copy-start.4 = (f32[32]{0:T(128)}, f32[32]{0:T(128)S(1)}, u32[]{:S(2)}) copy-start(f32[32]{0:T(128)S(1)} %get-tuple-element.14.zonal) | copy-start | bytes 388
  14.5 7.6 %copy-start.3 = (f32[32,32,32]{2,1,0:T(8,128)S(1)}, f32[32,32,32]{2,1,0:T(8,128)}, u32[]{:S(2)}) copy-start(f32[32,32,32]{2,1,0:T(8,128)} %matrix.1) | copy-start | bytes 393220
  14.5 33.0 %all-to-all-start = ((f32[32,104,128]{2,1,0:T(8,128)}), f32[32,104,128]{2,1,0:T(8,128)}, u32[]{:S(2)}, u32[]{:S(2)}) async-start(f32[32,104,128]{2,1,0:T(8,128)} %seam_rows.1), calls=%async_computation | async-start | bytes 3407872 | tf_op jit(solution)/shard_map/all_to_all | solution.py:362
  53.7 28.6 %all-to-all-start.1 = ((f32[32,3,2,16,128]{4,3,2,1,0:T(8,128)}), f32[32,3,2,16,128]{4,3,2,1,0:T(8,128)}, u32[]{:S(2)}, u32[]{:S(2)}) async-start(f32[32,3,2,16,128]{4,3,2,1,0:T(8,128)} %bitcast.6), calls=%async_computation.1 | async-start | bytes 3145728 | tf_op jit(solution)/shard_map/all_to_all | solution.py:395
  58.5 2.7 %collective-permute-start.2 = (f32[2,16,32,256]{3,2,1,0:T(8,128)S(1)}, f32[2,16,32,256]{3,2,1,0:T(8,128)S(1)}, u32[]{:S(2)}, u32[]{:S(2)}) collective-permute-start(f32[2,16,32,256]{3,2,1,0:T(8,128)S(1)} %slice.3), channel_id=1, source_target_pairs={{0,1},{1,0},{2,3},{3,2},{4,5},{5,4},{6,7},{7,6},{8,9},{9,8},{10,11... | collective-permute-start | bytes 3145736 | tf_op jit(solution)/shard_map/ppermute | solution.py:324
  62.9 1.1 %copy-start.2 = (f32[32,3,2,16,128]{4,3,2,1,0:T(8,128)}, f32[32,3,2,16,128]{4,3,2,1,0:T(8,128)S(1)}, u32[]{:S(2)}) copy-start(f32[32,3,2,16,128]{4,3,2,1,0:T(8,128)S(1)} %base.1) | copy-start | bytes 4718596

commit v5 on v3

--- a/solution.py
+++ b/solution.py
@@ -135,68 +135,64 @@
     return jnp.concatenate([hi, hi, lo], axis=1)
 
 
-def filter_kernel(
-    own_row, half_width, filter_mask, zonal, tend, matrices, out, halves, parts, seam, matrix, stage, matrix_sem, sems
-):
-    blocks, lev_parts, levels = out.shape[0], out.shape[1], out.shape[4]
+def filter_kernel(first_row, half_width, filter_mask, zonal, tend, out, halves, parts, seam, stage, sems):
+    blocks, own_rows, levels = out.shape[0], out.shape[1], out.shape[4]
     chans = 3 * levels
     payload = 2 * chans
     count = 2 * blocks
-    both = lev_parts * chans
-    row = own_row[0]
-    fetch = pltpu.make_async_copy(matrices.at[row], matrix, matrix_sem)
-    fetch.start()
-    reach = half_width[row]
-    whole = reach == count // 2
-    norm = jnp.where(whole, count * HALF, 2 * HALF * reach + 1).astype(jnp.float32)
-    filtered = filter_mask[row] == 1
-    edge_gain = jnp.where(whole, 0.0, 1.0).astype(jnp.float32)
-
+    both = own_rows * chans
+    reach, scale, filtered, edge_gain, sides = [], [], [], [], []
     for b in range(blocks):
-        for part in range(lev_parts):
-            at = b * lev_parts + part
+        for part in range(own_rows):
+            at = b * own_rows + part
             seam[at : at + 1, :] = tend[b, part, payload : payload + 1, :]
     columns = seam[...].T
-    zon = zonal[row]
-    u, v, h = (columns[f * levels : (f + 1) * levels] for f in range(3))
-    from_east = jnp.concatenate([VISCOSITY * u - zon * h, VISCOSITY * v, -zon * u], axis=0)
-    u, v, h = (columns[chans + f * levels : chans + (f + 1) * levels] for f in range(3))
-    from_west = jnp.concatenate([VISCOSITY * u + zon * h, VISCOSITY * v, zon * u], axis=0)
-    lane_id = lax.broadcasted_iota(jnp.int32, (levels, HALF), 1)
-    window = jnp.zeros((both, HALF), jnp.float32)
+    for part in range(own_rows):
+        row = first_row[0] + part
+        reach.append(half_width[row])
+        whole = reach[part] == count // 2
+        norm = jnp.where(whole, count * HALF, 2 * HALF * reach[part] + 1).astype(jnp.float32)
+        scale.append(TIME_STEP / norm)
+        filtered.append(filter_mask[row] == 1)
+        edge_gain.append(jnp.where(whole, 0.0, 1.0).astype(jnp.float32))
+        zon = zonal[row]
+        terms = []
+        for start, sign in ((chans, 1.0), (0, -1.0)):
+            u, v, h = (columns[start + f * levels : start + (f + 1) * levels] for f in range(3))
+            terms.append(jnp.concatenate([VISCOSITY * u + sign * zon * h, VISCOSITY * v, sign * zon * u], axis=0))
+        sides.append(terms)
+    lane_id = lax.broadcasted_iota(jnp.int32, (chans, HALF), 1)
+    windows = [jnp.zeros((chans, HALF), jnp.float32) for _ in range(own_rows)]
     for g in range(count):
         b, half = divmod(g, 2)
         beyond = (b + 1) % blocks if half else (b + blocks - 1) % blocks
-        terms, lane = (from_east, HALF - 1) if half else (from_west, 0)
-        pieces = []
-        for part in range(lev_parts):
-            source = beyond * lev_parts + part
-            for f in range(3):
-                here = tend[b, part, (2 * f + half) * levels : (2 * f + half + 1) * levels, :]
-                term = terms[f * levels : (f + 1) * levels, source : source + 1]
-                pieces.append(here + jnp.where(lane_id == lane, term, 0.0))
-        value = jnp.concatenate(pieces, axis=0)
-        halves[g] = value
-        inside = lax.rem(g + reach, count) < 2 * reach
-        window = window + jnp.where(inside, 1.0, 0.0).astype(jnp.float32) * value
+        lane = HALF - 1 if half else 0
+        for part in range(own_rows):
+            source = beyond * own_rows + part
+            here = jnp.concatenate(
+                [tend[b, part, (2 * f + half) * levels : (2 * f + half + 1) * levels, :] for f in range(3)], axis=0
+            )
+            value = here + jnp.where(lane_id == lane, sides[part][half][:, source : source + 1], 0.0)
+            halves[g, part * chans : (part + 1) * chans, :] = value
+            inside = lax.rem(g + reach[part], count) < 2 * reach[part]
+            windows[part] = windows[part] + jnp.where(inside, 1.0, 0.0).astype(jnp.float32) * value
 
     src = lax.broadcasted_iota(jnp.int32, (2 * HALF, HALF), 0)
     dst = lax.broadcasted_iota(jnp.int32, (2 * HALF, HALF), 1)
     sums = jnp.where((src <= dst) | (src >= HALF), 1.0, 0.0).astype(jnp.bfloat16)
-    fetch.wait()
-    mixer = mix_operand(matrix[...])
-    scale = TIME_STEP / norm
-
-    def split_group(g0, window):
+
+    def split_group(g0):
         for g in range(g0, g0 + GROUP):
-            ahead = halves[lax.rem(g + reach, count)]
-            behind = halves[lax.rem(g + count - reach, count)]
-            change = ahead - behind
-            for k, (a, b) in enumerate(zip(split2(change), split2(window))):
-                parts[k, g * both : (g + 1) * both, :HALF] = a
-                parts[k, g * both : (g + 1) * both, HALF:] = b
-            window = window + change
-        return window
+            for part in range(own_rows):
+                some = slice(part * chans, (part + 1) * chans)
+                ahead = halves[lax.rem(g + reach[part], count), some, :]
+                behind = halves[lax.rem(g + count - reach[part], count), some, :]
+                change = ahead - behind
+                at = g * both + part * chans
+                for k, (a, b) in enumerate(zip(split2(change), split2(windows[part]))):
+                    parts[k, at : at + chans, :HALF] = a
+                    parts[k, at : at + chans, HALF:] = b
+                windows[part] = windows[part] + change
 
     copies = []
 
@@ -205,41 +201,24 @@
         box = jnp.dot(parts[1, lo:hi, :], sums, preferred_element_type=jnp.float32) + jnp.dot(
             parts[0, lo:hi, :], sums, preferred_element_type=jnp.float32
         )
-        for pair in range(GROUP // 2):
-            b = g0 // 2 + pair
-            steps = []
-            for half in range(2):
-                g = 2 * b + half
-                at = (g - g0) * both
-                behind = halves[lax.rem(g + count - reach, count)]
-                smooth = (box[at : at + both] + edge_gain * behind) * scale
-                step = jnp.where(filtered, smooth, TIME_STEP * halves[g])
-                for p in range(lev_parts):
-                    stage[b, p, 2, half] = step[p * chans + 2 * levels : (p + 1) * chans]
-                steps.append(step)
-            step = jnp.concatenate(steps, axis=1)
-            for f in range(2):
-                wind = jnp.concatenate(
-                    [step[p * chans + f * levels : p * chans + (f + 1) * levels] for p in range(lev_parts)], axis=0
-                )
-                wind_hi, wind_lo = split2(wind)
-                mixed = jnp.dot(
-                    mixer,
-                    jnp.concatenate([wind_hi, wind_lo, wind_hi], axis=0),
-                    preferred_element_type=jnp.float32,
-                )
-                for p in range(lev_parts):
-                    for half in range(2):
-                        stage[b, p, f, half] = mixed[
-                            p * levels : (p + 1) * levels, half * HALF : (half + 1) * HALF
-                        ]
-            copies.append(pltpu.make_async_copy(stage.at[b], out.at[b], sems.at[b]))
-            copies[-1].start()
-
-    window = split_group(0, window)
+        for g in range(g0, g0 + GROUP):
+            b, half = divmod(g, 2)
+            for part in range(own_rows):
+                some = slice(part * chans, (part + 1) * chans)
+                at = (g - g0) * both + part * chans
+                behind = halves[lax.rem(g + count - reach[part], count), some, :]
+                smooth = (box[at : at + chans] + edge_gain[part] * behind) * scale[part]
+                step = jnp.where(filtered[part], smooth, TIME_STEP * halves[g, some, :])
+                for f in range(3):
+                    stage[b, part, f, half] = step[f * levels : (f + 1) * levels]
+            if half:
+                copies.append(pltpu.make_async_copy(stage.at[b], out.at[b], sems.at[b]))
+                copies[-1].start()
+
+    split_group(0)
     for g0 in range(0, count, GROUP):
         if g0 + GROUP < count:
-            window = split_group(g0 + GROUP, window)
+            split_group(g0 + GROUP)
         finish_group(g0)
     for copy in copies:
         copy.wait()
@@ -277,34 +256,49 @@
             out[j, 2, 0] = mine[2][k]
 
 
-def finish_kernel(step, base, out, added, stage, in_sems, out_sems):
+def finish_kernel(own_part, step, other, base, matrix, out, added, stage, in_sems, out_sems):
     fields, levels, rows, _ = out.shape
+    lower = own_part[0] == 0
     loads, copies = [], []
-    for f in range(fields):
-        loads.append(pltpu.make_async_copy(base.at[:, f], added.at[f], in_sems.at[f]))
+    for part in range(rows // SUBLANES):
+        some = pl.ds(part * SUBLANES, SUBLANES)
+        loads.append(pltpu.make_async_copy(base.at[some], added.at[some], in_sems.at[part]))
         loads[-1].start()
-    for f in range(fields):
-        loads[f].wait()
-        for l0 in range(0, levels, SUBLANES):
-            some = slice(l0, l0 + SUBLANES)
-            for half in range(2):
-                for j0 in range(0, rows, SUBLANES):
-                    flipped = flip(
-                        [step[j0 + k, f, half, some, :] + added[f, j0 + k, half, some, :] for k in range(SUBLANES)]
-                    )
-                    for i, value in enumerate(flipped):
-                        stage[f, l0 + i, j0 : j0 + SUBLANES, half * HALF : (half + 1) * HALF] = value
-            at = f * (levels // SUBLANES) + l0 // SUBLANES
-            some = pl.ds(l0, SUBLANES)
-            copies.append(pltpu.make_async_copy(stage.at[f, some], out.at[f, some], out_sems.at[at]))
-            copies[-1].start()
+    for part in range(rows // SUBLANES):
+        loads[part].wait()
+        j0 = part * SUBLANES
+        values = []
+        for j in range(j0, j0 + SUBLANES):
+            winds = []
+            for f in range(2):
+                for half in range(2):
+                    a, b = step[j, f, half], other[j, f, half]
+                    winds.append(jnp.concatenate([jnp.where(lower, a, b), jnp.where(lower, b, a)], axis=0))
+            wind_hi, wind_lo = split2(jnp.concatenate(winds, axis=1))
+            mixed = jnp.dot(
+                mix_operand(matrix[j]),
+                jnp.concatenate([wind_hi, wind_lo, wind_hi], axis=0),
+                preferred_element_type=jnp.float32,
+            )
+            kept = jnp.where(lower, mixed[:levels], mixed[levels:])
+            pieces = [kept[:, n * HALF : (n + 1) * HALF] for n in range(4)] + [step[j, 2, 0], step[j, 2, 1]]
+            values.append([piece + added[j, n // 2, n % 2] for n, piece in enumerate(pieces)])
+        for n in range(6):
+            f, half = divmod(n, 2)
+            for l0 in range(0, levels, SUBLANES):
+                flipped = flip([values[k][n][l0 : l0 + SUBLANES] for k in range(SUBLANES)])
+                for i, value in enumerate(flipped):
+                    stage[f, l0 + i, j0 : j0 + SUBLANES, half * HALF : (half + 1) * HALF] = value
+        some = pl.ds(j0, SUBLANES)
+        copies.append(pltpu.make_async_copy(stage.at[:, :, some], out.at[:, :, some], out_sems.at[part]))
+        copies[-1].start()
     for copy in copies:
         copy.wait()
 
 
 def per_device(prognostic, half_width, filter_mask, column_inverse):
     fields, levels, rows, width = prognostic.shape
-    lon_devices, lat_devices, lev_devices = (lax.axis_size(a) for a in ("lon", "lat", "lev"))
+    lon_devices, lat_devices = (lax.axis_size(a) for a in ("lon", "lat"))
     lon_index, lat_index, lev_index = (lax.axis_index(a) for a in ("lon", "lat", "lev"))
     chans = fields * levels
     halves = width // HALF
@@ -312,14 +306,21 @@
     hbm = pl.BlockSpec(memory_space=pltpu.HBM)
     vmem = pl.BlockSpec(memory_space=pltpu.VMEM)
 
+    def in_hbm(x):
+        return pltpu.with_memory_space_constraint(x, pltpu.HBM)
+
+    def in_vmem(x):
+        return pltpu.with_memory_space_constraint(x, pltpu.VMEM)
+
+
     with jax.named_scope("outer_rows"):
         last, first = pl.pallas_call(
             outer_rows_kernel,
-            out_shape=(jax.ShapeDtypeStruct((chans, width), jnp.float32),) * 2,
+            out_shape=(pltpu.VMEM((chans, width), jnp.float32),) * 2,
             in_specs=[vmem],
             out_specs=(vmem, vmem),
             compiler_params=params,
-        )(prognostic)
+        )(in_vmem(prognostic))
     south = lax.ppermute(last, "lat", [(i, i + 1) for i in range(lat_devices - 1)])
     north = lax.ppermute(first, "lat", [(i + 1, i) for i in range(lat_devices - 1)])
     other = lax.ppermute(prognostic[:2], "lev", [(0, 1), (1, 0)])
@@ -335,8 +336,8 @@
         tend, ends = pl.pallas_call(
             tendency_kernel,
             out_shape=(
-                jax.ShapeDtypeStruct((rows, sent_rows, HALF), jnp.float32),
-                jax.ShapeDtypeStruct((2, halves * chans, HALF), jnp.float32),
+                pltpu.HBM((rows, sent_rows, HALF), jnp.float32),
+                pltpu.VMEM((2, halves * chans, HALF), jnp.float32),
             ),
             in_specs=[vmem, vmem, vmem],
             out_specs=(hbm, vmem),
@@ -347,62 +348,60 @@
                 pltpu.SemaphoreType.DMA((rows // SUBLANES,)),
             ],
             compiler_params=params,
-        )(prognostic, zonal_field, coriolis_field)
+        )(in_vmem(prognostic), zonal_field, coriolis_field)
 
     with jax.named_scope("seam_rows"):
         tend = pl.pallas_call(
             seam_kernel,
-            out_shape=jax.ShapeDtypeStruct(tend.shape, jnp.float32),
+            out_shape=pltpu.HBM(tend.shape, jnp.float32),
             in_specs=[vmem, vmem, vmem, hbm],
             out_specs=hbm,
             input_output_aliases={3: 0},
             scratch_shapes=[pltpu.VMEM(ends.shape, jnp.float32), pltpu.SemaphoreType.DMA((2,))],
             compiler_params=params,
-        )(ends, south, north, tend)
-
-    whole_rows = lax.all_to_all(tend, ("lon", "lev"), 0, 0, tiled=True)
-
-    own_row = (lon_index * lev_devices + lev_index).astype(jnp.int32).reshape(1)
-    stepped_shape = (lon_devices, lev_devices, fields, halves, levels, HALF)
+        )(in_vmem(ends), in_vmem(south), in_vmem(north), in_hbm(tend))
+
+    own_rows = rows // lon_devices
+    whole_rows = lax.all_to_all(
+        tend.reshape(lon_devices, own_rows, sent_rows, HALF), "lon", 0, 0, tiled=True
+    )
+
+    stepped_shape = (lon_devices, own_rows, fields, halves, levels, HALF)
     count = halves * lon_devices
-    both = lev_devices * chans
+    both = own_rows * chans
     with jax.named_scope("row_filter"):
         stepped = pl.pallas_call(
             filter_kernel,
-            out_shape=jax.ShapeDtypeStruct(stepped_shape, jnp.float32),
+            out_shape=pltpu.HBM(stepped_shape, jnp.float32),
             grid_spec=pltpu.PrefetchScalarGridSpec(
                 num_scalar_prefetch=4,
                 grid=(1,),
-                in_specs=[vmem, hbm],
+                in_specs=[vmem],
                 out_specs=hbm,
                 scratch_shapes=[
                     pltpu.VMEM((count, both, HALF), jnp.float32),
                     pltpu.VMEM((2, count * both, 2 * HALF), jnp.bfloat16),
                     pltpu.VMEM((HALF, HALF), jnp.float32),
-                    pltpu.VMEM(column_inverse.shape[1:], jnp.float32),
                     pltpu.VMEM(stepped_shape, jnp.float32),
-                    pltpu.SemaphoreType.DMA,
                     pltpu.SemaphoreType.DMA((lon_devices,)),
                 ],
             ),
             compiler_params=params,
         )(
-            own_row,
+            (lon_index * own_rows).astype(jnp.int32).reshape(1),
             half_width,
             filter_mask,
             zonal,
-            whole_rows.reshape(lon_devices, lev_devices, sent_rows, HALF),
-            column_inverse,
+            in_vmem(whole_rows),
         )
 
-    returned = lax.all_to_all(
-        stepped.reshape((rows,) + stepped_shape[2:]), ("lon", "lev"), 0, 0, tiled=True
-    )
+    returned = lax.all_to_all(stepped, "lon", 0, 0, tiled=True).reshape((rows,) + stepped_shape[2:])
+    winds_beyond = lax.ppermute(returned[:, :2], "lev", [(0, 1), (1, 0)])
 
     with jax.named_scope("base"):
         base = pl.pallas_call(
             base_kernel,
-            out_shape=jax.ShapeDtypeStruct(returned.shape, jnp.float32),
+            out_shape=pltpu.HBM(returned.shape, jnp.float32),
             grid_spec=pltpu.PrefetchScalarGridSpec(
                 num_scalar_prefetch=1,
                 grid=(halves,),
@@ -420,16 +419,26 @@
         return pl.pallas_call(
             finish_kernel,
             out_shape=jax.ShapeDtypeStruct(prognostic.shape, jnp.float32),
-            in_specs=[vmem, hbm],
-            out_specs=hbm,
-            scratch_shapes=[
-                pltpu.VMEM((fields, rows, halves, levels, HALF), jnp.float32),
-                pltpu.VMEM(prognostic.shape, jnp.float32),
-                pltpu.SemaphoreType.DMA((fields,)),
-                pltpu.SemaphoreType.DMA((fields * levels // SUBLANES,)),
-            ],
-            compiler_params=params,
-        )(returned, base)
+            grid_spec=pltpu.PrefetchScalarGridSpec(
+                num_scalar_prefetch=1,
+                grid=(1,),
+                in_specs=[vmem, vmem, hbm, vmem],
+                out_specs=hbm,
+                scratch_shapes=[
+                    pltpu.VMEM(returned.shape, jnp.float32),
+                    pltpu.VMEM(prognostic.shape, jnp.float32),
+                    pltpu.SemaphoreType.DMA((rows // SUBLANES,)),
+                    pltpu.SemaphoreType.DMA((rows // SUBLANES,)),
+                ],
+            ),
+            compiler_params=params,
+        )(
+            lev_index.astype(jnp.int32).reshape(1),
+            in_vmem(returned),
+            in_vmem(winds_beyond),
+            in_hbm(base),
+            column_inverse,
+        )
 
 
 def solution(mesh):

time: 88.5 us -> 86.2 us (0.974)
  the two profiles are of different devices: /device:TPU:96 before, /device:TPU:129 now
where the time goes in v5:
time: 86.2 us; the launch traced here: 85.8 us
  waiting for transfers between devices  41.2 us (48%)
  starting transfers between devices  25 us (29%)
  Pallas kernels  14.7 us (17%)
  local copies, waits for them, and re-layouts  4.76 us (6%)
    all_to_all x1, waiting for transfers between devices, per_device(): lax.all_to_all(tend.reshape(lon_devices, own_rows, sent_rows, HALF), 'lon...  22.8 us
    all_to_all x1, waiting for transfers between devices, per_device(): lax.all_to_all(stepped, 'lon', 0, 0, tiled=True)  18.4 us
    all_to_all x1, starting transfers between devices, per_device(): lax.all_to_all(tend.reshape(lon_devices, own_rows, sent_rows, HALF), 'lon...  6.77 us
    all_to_all x1, starting transfers between devices, per_device(): lax.all_to_all(stepped, 'lon', 0, 0, tiled=True)  6.15 us
    pallas_call x1, Pallas kernels, per_device(): pl.pallas_call(finish_kernel, out_shape=jax.ShapeDtypeStruct(prognostic.s...  4.52 us
    ppermute x1, starting transfers between devices, per_device(): winds_beyond = lax.ppermute(returned[:, :2], 'lev', [(0, 1), (1, 0)])  3.87 us
    ppermute x1, starting transfers between devices, per_device(): lax.ppermute(first, 'lat', [(i + 1, i) for i in range(lat_devices - 1)])  3.85 us
    pallas_call x1, Pallas kernels, per_device(): pl.pallas_call(base_kernel, out_shape=pltpu.HBM(returned.shape, jnp.float...  3.45 us
  transfers between devices with their start and end apart: 6, of which 2 were waited for; matrix products, arithmetic and copies ran while one was open for 3% of the time, Pallas kernels for 7%

profile of v5, /device:TPU:129, one launch (start us, length us, event | category | flops | bytes accessed | tf_op | source)
XLA Modules:
  0.0 85.8 jit_solution(8736905205350070255)
XLA Ops:
  0.0 0.0 copy-start
  0.0 1.4 %copy-done = f32[3,16,32,256]{3,2,1,0:T(8,128)S(1)} copy-done((f32[3,16,32,256]{3,2,1,0:T(8,128)S(1)}, f32[3,16,32,256]{3,2,1,0:T(8,128)}, u32[]{:S(2)}) %copy-start) | copy-done | bytes 1572888
  1.4 0.0 copy-start.1
  1.4 0.1 outer_rows.1
  1.5 2.8 %collective-permute-start = (f32[48,256]{1,0:T(8,128)S(1)}, f32[48,256]{1,0:T(8,128)S(1)}, u32[]{:S(2)}, u32[]{:S(2)}) collective-permute-start(f32[48,256]{1,0:T(8,128)S(1)} %get-tuple-element.10), channel_id=1, source_target_pairs={{0,2},{2,4},{4,6},{6,8},{8,10},{10,12},{12,14},{1,3},{3,5},{5,7},{... | collective-permute-start | bytes 147464 | tf_op jit(solution)/shard_map/ppermute | solution.py:324
  4.3 3.8 %collective-permute-start.1 = (f32[48,256]{1,0:T(8,128)S(1)}, f32[48,256]{1,0:T(8,128)S(1)}, u32[]{:S(2)}, u32[]{:S(2)}) collective-permute-start(f32[48,256]{1,0:T(8,128)S(1)} %get-tuple-element.11), channel_id=1, source_target_pairs={{2,0},{4,2},{6,4},{8,6},{10,8},{12,10},{14,12},{3,1},{5,3},{7,5},{... | collective-permute-start | bytes 147464 | tf_op jit(solution)/shard_map/ppermute | solution.py:325
  8.2 0.1 broadcast_in_dim.5.coriolis
  8.2 0.1 broadcast_in_dim.4.zonal
  8.3 0.0 copy-done.1
  8.3 2.8 %tendencies.1 = (f32[32,104,128]{2,1,0:T(8,128)}, f32[2,96,128]{2,1,0:T(8,128)S(1)}) custom-call(f32[3,16,32,256]{3,2,1,0:T(8,128)S(1)} %copy-done.1, f32[32,256]{1,0:T(8,128)S(1)} %broadcast_in_dim.4.zonal, f32[32,256]{1,0:T(8,128)S(1)} %broadcast_in_dim.5.coriolis), custom_call_target="tpu_custom_call" | custom-call | tf_op jit(solution)/shard_map/tendencies/pallas_call | solution.py:336
  11.1 0.0 collective-permute-done.south
  11.1 0.0 collective-permute-done.1.north
  11.1 0.7 seam_rows.1
  11.8 0.0 copy-start.4
  11.8 0.0 copy-start.5
  11.8 6.8 %all-to-all-start = ((f32[16,2,104,128]{3,2,1,0:T(8,128)}), f32[16,2,104,128]{3,2,1,0:T(8,128)S(1)}, u32[]{:S(2)}, u32[]{:S(2)}) async-start(f32[16,2,104,128]{3,2,1,0:T(8,128)} %bitcast.6), calls=%async_computation | async-start | bytes 3407872 | tf_op jit(solution)/shard_map/all_to_all | solution.py:365
  18.6 22.8 %all-to-all-done.tend = f32[16,2,104,128]{3,2,1,0:T(8,128)S(1)} async-done(((f32[16,2,104,128]{3,2,1,0:T(8,128)}), f32[16,2,104,128]{3,2,1,0:T(8,128)S(1)}, u32[]{:S(2)}, u32[]{:S(2)}) %all-to-all-start) | async-done | bytes 1703968 | tf_op jit(solution)/shard_map/all_to_all | solution.py:365
  41.4 0.0 copy-done.4
  41.4 0.0 copy-done.5
  41.4 3.2 %row_filter.1 = f32[16,2,3,2,16,128]{5,4,3,2,1,0:T(8,128)} custom-call(s32[1]{0:T(128)} %bitcast.1.first_row, s32[32]{0:T(128)S(1)} %copy-done.4, s32[32]{0:T(128)S(1)} %copy-done.5, f32[32]{0:T(128)S(1)} %get-tuple-element.14.zonal, f32[16,2,104,128]{3,2,1,0:T(8,128)S(1)} %all-to-all-done.tend), custom_call_target="tpu_custom_call" | custom-call | tf_op jit(solution)/shard_map/row_filter/pallas_call | solution.py:373
  44.6 6.1 %all-to-all-start.1 = ((f32[16,2,3,2,16,128]{5,4,3,2,1,0:T(8,128)}), f32[16,2,3,2,16,128]{5,4,3,2,1,0:T(8,128)S(1)}, u32[]{:S(2)}, u32[]{:S(2)}) async-start(f32[16,2,3,2,16,128]{5,4,3,2,1,0:T(8,128)} %row_filter.1), calls=%async_computation.1 | async-start | bytes 3145728 | tf_op jit(solution)/shard_map/all_to_all | solution.py:398
  50.8 1.1 %slice.7 = f32[2,16,32,256]{3,2,1,0:T(8,128)} slice(f32[3,16,32,256]{3,2,1,0:T(8,128)S(1)} %copy-done.1), slice={[0:2], [0:16], [0:32], [0:256]} | slice | bytes 2097152 | tf_op jit(solution)/shard_map/slice | solution.py:326
  51.9 1.6 %collective-permute-start.3 = (f32[2,16,32,256]{3,2,1,0:T(8,128)}, f32[2,16,32,256]{3,2,1,0:T(8,128)}, u32[]{:S(2)}, u32[]{:S(2)}) collective-permute-start(f32[2,16,32,256]{3,2,1,0:T(8,128)} %slice.7), channel_id=1, source_target_pairs={{0,1},{1,0},{2,3},{3,2},{4,5},{5,4},{6,7},{7,6},{8,9},{9,8},{10,11... | collective-permute-start | bytes 3145736 | tf_op jit(solution)/shard_map/ppermute | solution.py:326
  53.4 18.4 %all-to-all-done.1 = f32[16,2,3,2,16,128]{5,4,3,2,1,0:T(8,128)S(1)} async-done(((f32[16,2,3,2,16,128]{5,4,3,2,1,0:T(8,128)}), f32[16,2,3,2,16,128]{5,4,3,2,1,0:T(8,128)S(1)}, u32[]{:S(2)}, u32[]{:S(2)}) %all-to-all-start.1) | async-done | bytes 1572896 | tf_op jit(solution)/shard_map/all_to_all | solution.py:398
  71.8 1.1 %slice.8 = f32[32,2,2,16,128]{4,3,2,1,0:T(8,128)} slice(f32[32,3,2,16,128]{4,3,2,1,0:T(8,128)S(1)} %bitcast.4), slice={[0:32], [0:2], [0:2], [0:16], [0:128]} | slice | bytes 2097152 | tf_op jit(solution)/shard_map/slice | solution.py:399
  72.9 3.9 %collective-permute-start.2 = (f32[32,2,2,16,128]{4,3,2,1,0:T(8,128)}, f32[32,2,2,16,128]{4,3,2,1,0:T(8,128)}, u32[]{:S(2)}, u32[]{:S(2)}) collective-permute-start(f32[32,2,2,16,128]{4,3,2,1,0:T(8,128)} %slice.8), channel_id=1, source_target_pairs={{0,1},{1,0},{2,3},{3,2},{4,5},{5,4},{6,7},{7,6},{8,9},{9,8},{10,11... | collective-permute-start | bytes 3145736 | tf_op jit(solution)/shard_map/ppermute | solution.py:399
  76.8 0.0 collective-permute-done.3.other
  76.8 0.0 copy-start.2
  76.8 1.0 %copy-done.2 = f32[32,32,32]{2,1,0:T(8,128)S(1)} copy-done((f32[32,32,32]{2,1,0:T(8,128)S(1)}, f32[32,32,32]{2,1,0:T(8,128)}, u32[]{:S(2)}) %copy-start.2) | copy-done | bytes 131096
  77.8 0.0 copy-start.3
  77.8 3.4 %base.1 = f32[32,3,2,16,128]{4,3,2,1,0:T(8,128)} custom-call(s32[1]{0:T(128)} %bitcast.own_part, f32[3,16,32,256]{3,2,1,0:T(8,128)S(1)} %copy-done.1, f32[2,16,32,256]{3,2,1,0:T(8,128)} %collective-permute-done.3.other, f32[32,32,32]{2,1,0:T(8,128)S(1)} %copy-done.2), custom_call_target="tpu_custom_call" | custom-call | tf_op jit(solution)/shard_map/base/pallas_call | solution.py:402
  81.3 0.0 collective-permute-done.2.other
  81.3 0.0 copy-done.3
  81.3 4.5 %finish.1 = f32[3,16,32,256]{3,2,1,0:T(8,128)} custom-call(s32[1]{0:T(128)} %bitcast.own_part, f32[32,3,2,16,128]{4,3,2,1,0:T(8,128)S(1)} %bitcast.5, f32[32,2,2,16,128]{4,3,2,1,0:T(8,128)} %collective-permute-done.2.other, f32[32,3,2,16,128]{4,3,2,1,0:T(8,128)} %base.1, f32[32,32,32]{2,1,0:T(8,128)S(1)} %copy-done.3), custom_call_target="tpu_custom_call" | custom-call | tf_op jit(solution)/shard_map/finish/pallas_call | solution.py:419
  (1 shorter events, 0.0 us)
Async XLA Ops:
  0.0 1.4 %copy-start = (f32[3,16,32,256]{3,2,1,0:T(8,128)S(1)}, f32[3,16,32,256]{3,2,1,0:T(8,128)}, u32[]{:S(2)}) copy-start(f32[3,16,32,256]{3,2,1,0:T(8,128)} %own.1) | copy-start | bytes 4718596
  1.4 6.9 %copy-start.1 = (f32[3,16,32,256]{3,2,1,0:T(8,128)S(1)}, f32[3,16,32,256]{3,2,1,0:T(8,128)}, u32[]{:S(2)}) copy-start(f32[3,16,32,256]{3,2,1,0:T(8,128)} %own.1) | copy-start | bytes 4718596
  1.5 9.6 %collective-permute-start = (f32[48,256]{1,0:T(8,128)S(1)}, f32[48,256]{1,0:T(8,128)S(1)}, u32[]{:S(2)}, u32[]{:S(2)}) collective-permute-start(f32[48,256]{1,0:T(8,128)S(1)} %get-tuple-element.10), channel_id=1, source_target_pairs={{0,2},{2,4},{4,6},{6,8},{8,10},{10,12},{12,14},{1,3},{3,5},{5,7},{... | collective-permute-start | bytes 147464 | tf_op jit(solution)/shard_map/ppermute | solution.py:324
  4.3 6.9 %collective-permute-start.1 = (f32[48,256]{1,0:T(8,128)S(1)}, f32[48,256]{1,0:T(8,128)S(1)}, u32[]{:S(2)}, u32[]{:S(2)}) collective-permute-start(f32[48,256]{1,0:T(8,128)S(1)} %get-tuple-element.11), channel_id=1, source_target_pairs={{2,0},{4,2},{6,4},{8,6},{10,8},{12,10},{14,12},{3,1},{5,3},{7,5},{... | collective-permute-start | bytes 147464 | tf_op jit(solution)/shard_map/ppermute | solution.py:325
  11.8 29.6 %copy-start.4 = (s32[32]{0:T(128)S(1)}, s32[32]{0:T(128)}, u32[]{:S(2)}) copy-start(s32[32]{0:T(128)} %half_width.1) | copy-start | bytes 388
  11.8 29.6 %copy-start.5 = (s32[32]{0:T(128)S(1)}, s32[32]{0:T(128)}, u32[]{:S(2)}) copy-start(s32[32]{0:T(128)} %filter_mask.1) | copy-start | bytes 388
  11.8 29.6 %all-to-all-start = ((f32[16,2,104,128]{3,2,1,0:T(8,128)}), f32[16,2,104,128]{3,2,1,0:T(8,128)S(1)}, u32[]{:S(2)}, u32[]{:S(2)}) async-start(f32[16,2,104,128]{3,2,1,0:T(8,128)} %bitcast.6), calls=%async_computation | async-start | bytes 3407872 | tf_op jit(solution)/shard_map/all_to_all | solution.py:365
  44.6 27.2 %all-to-all-start.1 = ((f32[16,2,3,2,16,128]{5,4,3,2,1,0:T(8,128)}), f32[16,2,3,2,16,128]{5,4,3,2,1,0:T(8,128)S(1)}, u32[]{:S(2)}, u32[]{:S(2)}) async-start(f32[16,2,3,2,16,128]{5,4,3,2,1,0:T(8,128)} %row_filter.1), calls=%async_computation.1 | async-start | bytes 3145728 | tf_op jit(solution)/shard_map/all_to_all | solution.py:398
  51.9 24.9 %collective-permute-start.3 = (f32[2,16,32,256]{3,2,1,0:T(8,128)}, f32[2,16,32,256]{3,2,1,0:T(8,128)}, u32[]{:S(2)}, u32[]{:S(2)}) collective-permute-start(f32[2,16,32,256]{3,2,1,0:T(8,128)} %slice.7), channel_id=1, source_target_pairs={{0,1},{1,0},{2,3},{3,2},{4,5},{5,4},{6,7},{7,6},{8,9},{9,8},{10,11... | collective-permute-start | bytes 3145736 | tf_op jit(solution)/shard_map/ppermute | solution.py:326
  72.9 8.4 %collective-permute-start.2 = (f32[32,2,2,16,128]{4,3,2,1,0:T(8,128)}, f32[32,2,2,16,128]{4,3,2,1,0:T(8,128)}, u32[]{:S(2)}, u32[]{:S(2)}) collective-permute-start(f32[32,2,2,16,128]{4,3,2,1,0:T(8,128)} %slice.8), channel_id=1, source_target_pairs={{0,1},{1,0},{2,3},{3,2},{4,5},{5,4},{6,7},{7,6},{8,9},{9,8},{10,11... | collective-permute-start | bytes 3145736 | tf_op jit(solution)/shard_map/ppermute | solution.py:399
  76.8 1.0 %copy-start.2 = (f32[32,32,32]{2,1,0:T(8,128)S(1)}, f32[32,32,32]{2,1,0:T(8,128)}, u32[]{:S(2)}) copy-start(f32[32,32,32]{2,1,0:T(8,128)} %matrix.3) | copy-start | bytes 393220
  77.8 3.5 %copy-start.3 = (f32[32,32,32]{2,1,0:T(8,128)S(1)}, f32[32,32,32]{2,1,0:T(8,128)}, u32[]{:S(2)}) copy-start(f32[32,32,32]{2,1,0:T(8,128)} %matrix.3) | copy-start | bytes 393220

commit v6 on v5

--- a/solution.py
+++ b/solution.py
@@ -42,7 +42,7 @@
             first[c : c + 1, :] = prog[f, l, 0:1, :]
 
 
-def tendency_kernel(prog, zonal, coriolis, out, ends, turn, edges, stage, out_sems):
+def tendency_kernel(prog, zonal, coriolis, out, turn, edges):
     _, levels, rows, width = prog.shape
     chans = 3 * levels
     payload = 2 * chans
@@ -80,7 +80,6 @@
         for f in range(3):
             turn[f, l] = tends[f]
     edges[...] = edge_rows
-    copies = []
     for chunk in range(rows // SUBLANES):
         some = slice(chunk * SUBLANES, (chunk + 1) * SUBLANES)
         for f in range(3):
@@ -92,39 +91,35 @@
                     )
                     for k, value in enumerate(flipped):
                         j = chunk * SUBLANES + k
-                        stage[j, at : at + SUBLANES, :] = value
-                        if j in (0, rows - 1):
-                            ends[min(j, 1), at : at + SUBLANES, :] = value
+                        out[j, at : at + SUBLANES, :] = value
         for k in range(SUBLANES):
             j = chunk * SUBLANES + k
-            stage[j, payload:, :] = jnp.broadcast_to(edges[j : j + 1, :], (SUBLANES, HALF))
-        some = pl.ds(chunk * SUBLANES, SUBLANES)
-        copies.append(pltpu.make_async_copy(stage.at[some], out.at[some], out_sems.at[chunk]))
+            out[j, payload:, :] = jnp.broadcast_to(edges[j : j + 1, :], (SUBLANES, HALF))
+
+
+def seam_kernel(own_block, south, north, tend, whole, *outs_and_sems):
+    del tend
+    outs, sems = outs_and_sems[:-1], outs_and_sems[-1]
+    chans = south.shape[0]
+    levels = chans // 3
+    rows = whole.shape[0]
+    per_owner = rows // len(outs)
+    for row, beyond, slope in ((0, south, -MERIDIONAL), (rows - 1, north, MERIDIONAL)):
+        for half in range(2):
+            lanes = slice(half * HALF, (half + 1) * HALF)
+            u, v, h = (beyond[f * levels : (f + 1) * levels, lanes] for f in range(3))
+            for f, term in enumerate((VISCOSITY * u, VISCOSITY * v - slope * h, -slope * v)):
+                some = slice((2 * f + half) * levels, (2 * f + half + 1) * levels)
+                whole[row, some, :] = whole[row, some, :] + term
+    copies = []
+    for s, out in enumerate(outs):
+        first = (own_block[0] ^ s) * per_owner
+        copies.append(pltpu.make_async_copy(whole.at[pl.ds(first, per_owner)], out, sems.at[s]))
         copies[-1].start()
     for copy in copies:
         copy.wait()
 
 
-def seam_kernel(ends, south, north, tend, out, stage, sems):
-    del tend
-    chans = south.shape[0]
-    levels = chans // 3
-    copies = []
-    for at, beyond, sign in ((0, south, -1.0), (1, north, 1.0)):
-        for half in range(2):
-            lanes = slice(half * HALF, (half + 1) * HALF)
-            u, v, h = (beyond[f * levels : (f + 1) * levels, lanes] for f in range(3))
-            slope = sign * MERIDIONAL
-            for f, term in enumerate((VISCOSITY * u, VISCOSITY * v - slope * h, -slope * v)):
-                some = slice((2 * f + half) * levels, (2 * f + half + 1) * levels)
-                stage[at, some, :] = ends[at, some, :] + term
-        row = at * (out.shape[0] - 1)
-        copies.append(pltpu.make_async_copy(stage.at[at], out.at[row, pl.ds(0, 2 * chans)], sems.at[at]))
-        copies[-1].start()
-    for copy in copies:
-        copy.wait()
-
-
 def split2(x):
     hi = x.astype(jnp.bfloat16)
     return hi, (x - hi.astype(jnp.float32)).astype(jnp.bfloat16)
@@ -135,20 +130,29 @@
     return jnp.concatenate([hi, hi, lo], axis=1)
 
 
-def filter_kernel(first_row, half_width, filter_mask, zonal, tend, out, halves, parts, seam, stage, sems):
-    blocks, own_rows, levels = out.shape[0], out.shape[1], out.shape[4]
+def filter_kernel(own_block, half_width, filter_mask, zonal, *refs):
+    halves, parts, seam, beyond_east, beyond_west = refs[-5:]
+    blocks = (len(refs) - 5) // 2
+    arrived, outs = refs[:blocks], refs[blocks : 2 * blocks]
+    own_rows, _, _, levels, _ = outs[0].shape
     chans = 3 * levels
     payload = 2 * chans
     count = 2 * blocks
     both = own_rows * chans
+    me = own_block[0]
     reach, scale, filtered, edge_gain, sides = [], [], [], [], []
-    for b in range(blocks):
+    for s, tend in enumerate(arrived):
         for part in range(own_rows):
-            at = b * own_rows + part
-            seam[at : at + 1, :] = tend[b, part, payload : payload + 1, :]
-    columns = seam[...].T
+            seam[pl.ds((me ^ s) * own_rows + part, 1), :] = tend[part, payload : payload + 1, :]
+    for s in range(blocks):
+        for side, turn in ((beyond_east, 1), (beyond_west, blocks - 1)):
+            source = lax.rem((me ^ s) + turn, blocks) * own_rows
+            for part in range(own_rows):
+                at = s * own_rows + part
+                side[at : at + 1, :] = seam[pl.ds(source + part, 1), :]
+    columns = (beyond_west[...].T, beyond_east[...].T)
     for part in range(own_rows):
-        row = first_row[0] + part
+        row = me * own_rows + part
         reach.append(half_width[row])
         whole = reach[part] == count // 2
         norm = jnp.where(whole, count * HALF, 2 * HALF * reach[part] + 1).astype(jnp.float32)
@@ -157,71 +161,67 @@
         edge_gain.append(jnp.where(whole, 0.0, 1.0).astype(jnp.float32))
         zon = zonal[row]
         terms = []
-        for start, sign in ((chans, 1.0), (0, -1.0)):
-            u, v, h = (columns[start + f * levels : start + (f + 1) * levels] for f in range(3))
+        for start, sign, side in ((chans, 1.0, columns[0]), (0, -1.0, columns[1])):
+            u, v, h = (side[start + f * levels : start + (f + 1) * levels] for f in range(3))
             terms.append(jnp.concatenate([VISCOSITY * u + sign * zon * h, VISCOSITY * v, sign * zon * u], axis=0))
         sides.append(terms)
     lane_id = lax.broadcasted_iota(jnp.int32, (chans, HALF), 1)
     windows = [jnp.zeros((chans, HALF), jnp.float32) for _ in range(own_rows)]
-    for g in range(count):
-        b, half = divmod(g, 2)
-        beyond = (b + 1) % blocks if half else (b + blocks - 1) % blocks
-        lane = HALF - 1 if half else 0
-        for part in range(own_rows):
-            source = beyond * own_rows + part
-            here = jnp.concatenate(
-                [tend[b, part, (2 * f + half) * levels : (2 * f + half + 1) * levels, :] for f in range(3)], axis=0
-            )
-            value = here + jnp.where(lane_id == lane, sides[part][half][:, source : source + 1], 0.0)
-            halves[g, part * chans : (part + 1) * chans, :] = value
-            inside = lax.rem(g + reach[part], count) < 2 * reach[part]
-            windows[part] = windows[part] + jnp.where(inside, 1.0, 0.0).astype(jnp.float32) * value
+    for s, tend in enumerate(arrived):
+        for half in range(2):
+            g = 2 * (me ^ s) + half
+            lane = HALF - 1 if half else 0
+            for part in range(own_rows):
+                source = s * own_rows + part
+                here = jnp.concatenate(
+                    [tend[part, (2 * f + half) * levels : (2 * f + half + 1) * levels, :] for f in range(3)], axis=0
+                )
+                value = here + jnp.where(lane_id == lane, sides[part][half][:, source : source + 1], 0.0)
+                halves[g, part * chans : (part + 1) * chans, :] = value
+                inside = lax.rem(g + reach[part], count) < 2 * reach[part]
+                windows[part] = windows[part] + jnp.where(inside, 1.0, 0.0).astype(jnp.float32) * value
 
     src = lax.broadcasted_iota(jnp.int32, (2 * HALF, HALF), 0)
     dst = lax.broadcasted_iota(jnp.int32, (2 * HALF, HALF), 1)
     sums = jnp.where((src <= dst) | (src >= HALF), 1.0, 0.0).astype(jnp.bfloat16)
 
-    def split_group(g0):
-        for g in range(g0, g0 + GROUP):
+    for g in range(count):
+        for part in range(own_rows):
+            some = slice(part * chans, (part + 1) * chans)
+            ahead = halves[lax.rem(g + reach[part], count), some, :]
+            behind = halves[lax.rem(g + count - reach[part], count), some, :]
+            change = ahead - behind
+            at = g * both + part * chans
+            for k, (a, b) in enumerate(zip(split2(change), split2(windows[part]))):
+                parts[k, at : at + chans, :HALF] = a
+                parts[k, at : at + chans, HALF:] = b
+            windows[part] = windows[part] + change
+
+    for s, out in enumerate(outs):
+        b = me ^ s
+        some = pl.ds(pl.multiple_of(b * 2 * both, 2 * both), 2 * both)
+        box = jnp.dot(parts[1, some, :], sums, preferred_element_type=jnp.float32) + jnp.dot(
+            parts[0, some, :], sums, preferred_element_type=jnp.float32
+        )
+        for half in range(2):
+            g = 2 * b + half
             for part in range(own_rows):
                 some = slice(part * chans, (part + 1) * chans)
-                ahead = halves[lax.rem(g + reach[part], count), some, :]
-                behind = halves[lax.rem(g + count - reach[part], count), some, :]
-                change = ahead - behind
-                at = g * both + part * chans
-                for k, (a, b) in enumerate(zip(split2(change), split2(windows[part]))):
-                    parts[k, at : at + chans, :HALF] = a
-                    parts[k, at : at + chans, HALF:] = b
-                windows[part] = windows[part] + change
-
-    copies = []
-
-    def finish_group(g0):
-        lo, hi = g0 * both, (g0 + GROUP) * both
-        box = jnp.dot(parts[1, lo:hi, :], sums, preferred_element_type=jnp.float32) + jnp.dot(
-            parts[0, lo:hi, :], sums, preferred_element_type=jnp.float32
-        )
-        for g in range(g0, g0 + GROUP):
-            b, half = divmod(g, 2)
-            for part in range(own_rows):
-                some = slice(part * chans, (part + 1) * chans)
-                at = (g - g0) * both + part * chans
+                at = half * both + part * chans
                 behind = halves[lax.rem(g + count - reach[part], count), some, :]
                 smooth = (box[at : at + chans] + edge_gain[part] * behind) * scale[part]
                 step = jnp.where(filtered[part], smooth, TIME_STEP * halves[g, some, :])
                 for f in range(3):
-                    stage[b, part, f, half] = step[f * levels : (f + 1) * levels]
-            if half:
-                copies.append(pltpu.make_async_copy(stage.at[b], out.at[b], sems.at[b]))
-                copies[-1].start()
-
-    split_group(0)
-    for g0 in range(0, count, GROUP):
-        if g0 + GROUP < count:
-            split_group(g0 + GROUP)
-        finish_group(g0)
-    for copy in copies:
-        copy.wait()
+                    out[part, f, half] = step[f * levels : (f + 1) * levels]
+
+
+def gather_kernel(own_block, *refs):
+    returned, (winds, height) = refs[:-2], refs[-2:]
+    for s, part in enumerate(returned):
+        for row in range(part.shape[0]):
+            j = (own_block[0] ^ s) * part.shape[0] + row
+            winds[j] = part[row, :2]
+            height[j] = part[row, 2]
 
 
 def base_kernel(own_part, own, other, matrix, out):
@@ -256,7 +256,7 @@
             out[j, 2, 0] = mine[2][k]
 
 
-def finish_kernel(own_part, step, other, base, matrix, out, added, stage, in_sems, out_sems):
+def finish_kernel(own_part, step, height, other, base, matrix, out, added, stage, in_sems, out_sems):
     fields, levels, rows, _ = out.shape
     lower = own_part[0] == 0
     loads, copies = [], []
@@ -281,7 +281,7 @@
                 preferred_element_type=jnp.float32,
             )
             kept = jnp.where(lower, mixed[:levels], mixed[levels:])
-            pieces = [kept[:, n * HALF : (n + 1) * HALF] for n in range(4)] + [step[j, 2, 0], step[j, 2, 1]]
+            pieces = [kept[:, n * HALF : (n + 1) * HALF] for n in range(4)] + [height[j, 0], height[j, 1]]
             values.append([piece + added[j, n // 2, n % 2] for n, piece in enumerate(pieces)])
         for n in range(6):
             f, half = divmod(n, 2)
@@ -333,75 +333,89 @@
 
     sent_rows = halves * chans + SUBLANES
     with jax.named_scope("tendencies"):
-        tend, ends = pl.pallas_call(
+        tend = pl.pallas_call(
             tendency_kernel,
-            out_shape=(
-                pltpu.HBM((rows, sent_rows, HALF), jnp.float32),
-                pltpu.VMEM((2, halves * chans, HALF), jnp.float32),
-            ),
+            out_shape=pltpu.VMEM((rows, sent_rows, HALF), jnp.float32),
             in_specs=[vmem, vmem, vmem],
-            out_specs=(hbm, vmem),
+            out_specs=vmem,
             scratch_shapes=[
                 pltpu.VMEM(prognostic.shape, jnp.float32),
                 pltpu.VMEM((rows, HALF), jnp.float32),
-                pltpu.VMEM((rows, sent_rows, HALF), jnp.float32),
-                pltpu.SemaphoreType.DMA((rows // SUBLANES,)),
             ],
             compiler_params=params,
         )(in_vmem(prognostic), zonal_field, coriolis_field)
 
+    own_rows = rows // lon_devices
+    own_block = lon_index.astype(jnp.int32).reshape(1)
+
+    def exchange(pieces):
+        return [pieces[0]] + [
+            lax.ppermute(piece, "lon", [(i, i ^ s) for i in range(lon_devices)])
+            for s, piece in enumerate(pieces)
+            if s
+        ]
+
     with jax.named_scope("seam_rows"):
-        tend = pl.pallas_call(
+        parted = pl.pallas_call(
             seam_kernel,
-            out_shape=pltpu.HBM(tend.shape, jnp.float32),
-            in_specs=[vmem, vmem, vmem, hbm],
-            out_specs=hbm,
+            out_shape=(pltpu.VMEM(tend.shape, jnp.float32),)
+            + (pltpu.VMEM((own_rows, sent_rows, HALF), jnp.float32),) * lon_devices,
+            grid_spec=pltpu.PrefetchScalarGridSpec(
+                num_scalar_prefetch=1,
+                grid=(1,),
+                in_specs=[vmem] * 3,
+                out_specs=(vmem,) * (lon_devices + 1),
+                scratch_shapes=[pltpu.SemaphoreType.DMA((lon_devices,))],
+            ),
             input_output_aliases={3: 0},
-            scratch_shapes=[pltpu.VMEM(ends.shape, jnp.float32), pltpu.SemaphoreType.DMA((2,))],
-            compiler_params=params,
-        )(in_vmem(ends), in_vmem(south), in_vmem(north), in_hbm(tend))
-
-    own_rows = rows // lon_devices
-    whole_rows = lax.all_to_all(
-        tend.reshape(lon_devices, own_rows, sent_rows, HALF), "lon", 0, 0, tiled=True
-    )
-
-    stepped_shape = (lon_devices, own_rows, fields, halves, levels, HALF)
+            compiler_params=params,
+        )(own_block, in_vmem(south), in_vmem(north), in_vmem(tend))[1:]
+
+    arrived = exchange(parted)
+
+    stepped_shape = (own_rows, fields, halves, levels, HALF)
     count = halves * lon_devices
     both = own_rows * chans
     with jax.named_scope("row_filter"):
         stepped = pl.pallas_call(
             filter_kernel,
-            out_shape=pltpu.HBM(stepped_shape, jnp.float32),
+            out_shape=(pltpu.VMEM(stepped_shape, jnp.float32),) * lon_devices,
             grid_spec=pltpu.PrefetchScalarGridSpec(
                 num_scalar_prefetch=4,
                 grid=(1,),
-                in_specs=[vmem],
-                out_specs=hbm,
+                in_specs=[vmem] * lon_devices,
+                out_specs=(vmem,) * lon_devices,
                 scratch_shapes=[
                     pltpu.VMEM((count, both, HALF), jnp.float32),
                     pltpu.VMEM((2, count * both, 2 * HALF), jnp.bfloat16),
-                    pltpu.VMEM((HALF, HALF), jnp.float32),
-                    pltpu.VMEM(stepped_shape, jnp.float32),
-                    pltpu.SemaphoreType.DMA((lon_devices,)),
-                ],
-            ),
-            compiler_params=params,
-        )(
-            (lon_index * own_rows).astype(jnp.int32).reshape(1),
-            half_width,
-            filter_mask,
-            zonal,
-            in_vmem(whole_rows),
-        )
-
-    returned = lax.all_to_all(stepped, "lon", 0, 0, tiled=True).reshape((rows,) + stepped_shape[2:])
-    winds_beyond = lax.ppermute(returned[:, :2], "lev", [(0, 1), (1, 0)])
+                ]
+                + [pltpu.VMEM((HALF, HALF), jnp.float32)] * 3,
+            ),
+            compiler_params=params,
+        )(own_block, half_width, filter_mask, zonal, *[in_vmem(piece) for piece in arrived])
+
+    returned = exchange(stepped)
+    with jax.named_scope("gather_rows"):
+        winds, height = pl.pallas_call(
+            gather_kernel,
+            out_shape=(
+                pltpu.VMEM((rows, 2) + stepped_shape[2:], jnp.float32),
+                pltpu.VMEM((rows,) + stepped_shape[2:], jnp.float32),
+            ),
+            grid_spec=pltpu.PrefetchScalarGridSpec(
+                num_scalar_prefetch=1,
+                grid=(1,),
+                in_specs=[vmem] * lon_devices,
+                out_specs=(vmem, vmem),
+            ),
+            compiler_params=params,
+        )(own_block, *[in_vmem(piece) for piece in returned])
+    winds_beyond = lax.ppermute(winds, "lev", [(0, 1), (1, 0)])
 
     with jax.named_scope("base"):
         base = pl.pallas_call(
             base_kernel,
-            out_shape=pltpu.HBM(returned.shape, jnp.float32),
+            out_shape=pltpu.HBM((rows,) + stepped_shape[1:], jnp.float32),
             grid_spec=pltpu.PrefetchScalarGridSpec(
                 num_scalar_prefetch=1,
                 grid=(halves,),
@@ -422,10 +436,10 @@
             grid_spec=pltpu.PrefetchScalarGridSpec(
                 num_scalar_prefetch=1,
                 grid=(1,),
-                in_specs=[vmem, vmem, hbm, vmem],
+                in_specs=[vmem, vmem, vmem, hbm, vmem],
                 out_specs=hbm,
                 scratch_shapes=[
-                    pltpu.VMEM(returned.shape, jnp.float32),
+                    pltpu.VMEM((rows,) + stepped_shape[1:], jnp.float32),
                     pltpu.VMEM(prognostic.shape, jnp.float32),
                     pltpu.SemaphoreType.DMA((rows // SUBLANES,)),
                     pltpu.SemaphoreType.DMA((rows // SUBLANES,)),
@@ -434,7 +448,8 @@
             compiler_params=params,
         )(
             lev_index.astype(jnp.int32).reshape(1),
-            in_vmem(returned),
+            in_vmem(winds),
+            in_vmem(height),
             in_vmem(winds_beyond),
             in_hbm(base),
             column_inverse,

time: 86.2 us -> 108 us (1.25)
  the two profiles are of different devices: /device:TPU:129 before, /device:TPU:96 now
where the time goes in v6:
time: 108 us; the launch traced here: 107 us
  starting transfers between devices  73.6 us (68%)
  Pallas kernels  15.4 us (14%)
  waiting for transfers between devices  14.2 us (13%)
  local copies, waits for them, and re-layouts  3.41 us (3%)
    ppermute x30, starting transfers between devices, exchange(): lax.ppermute(piece, 'lon', [(i, i ^ s) for i in range(lon_devices)])  66.5 us
    ppermute x30, waiting for transfers between devices, exchange(): lax.ppermute(piece, 'lon', [(i, i ^ s) for i in range(lon_devices)])  10.3 us
    ppermute x1, starting transfers between devices, per_device(): lax.ppermute(last, 'lat', [(i, i + 1) for i in range(lat_devices - 1)])  5.17 us
    pallas_call x1, Pallas kernels, per_device(): pl.pallas_call(finish_kernel, out_shape=jax.ShapeDtypeStruct(prognostic.s...  4.84 us
    ppermute x1, waiting for transfers between devices, per_device(): lax.ppermute(first, 'lat', [(i + 1, i) for i in range(lat_devices - 1)])  3.43 us
    pallas_call x1, Pallas kernels, per_device(): pl.pallas_call(filter_kernel, out_shape=(pltpu.VMEM(stepped_shape, jnp.fl...  2.91 us
    pallas_call x1, Pallas kernels, per_device(): pl.pallas_call(base_kernel, out_shape=pltpu.HBM((rows,) + stepped_shape[1...  2.52 us
    pallas_call x1, Pallas kernels, per_device(): pl.pallas_call(seam_kernel, out_shape=(pltpu.VMEM(tend.shape, jnp.float32...  2.51 us
  transfers between devices with their start and end apart: 34, of which 9 were waited for; matrix products, arithmetic and copies ran while one was open for 1% of the time, Pallas kernels for 5%

profile of v6, /device:TPU:96, one launch (start us, length us, event | category | flops | bytes accessed | tf_op | source)
XLA Modules:
  0.0 107.0 jit_solution(17551877409742502519)
XLA Ops:
  0.0 1.4 %copy-done = f32[3,16,32,256]{3,2,1,0:T(8,128)S(1)} copy-done((f32[3,16,32,256]{3,2,1,0:T(8,128)S(1)}, f32[3,16,32,256]{3,2,1,0:T(8,128)}, u32[]{:S(2)}) %copy-start) | copy-done | bytes 1572888
  1.5 5.2 %collective-permute-start = (f32[48,256]{1,0:T(8,128)S(1)}, f32[48,256]{1,0:T(8,128)S(1)}, u32[]{:S(2)}, u32[]{:S(2)}) collective-permute-start(f32[48,256]{1,0:T(8,128)S(1)} %get-tuple-element.41), channel_id=1, source_target_pairs={{0,2},{2,4},{4,6},{6,8},{8,10},{10,12},{12,14},{1,3},{3,5},{5,7},{... | collective-permute-start | bytes 147464 | tf_op jit(solution)/shard_map/ppermute | solution.py:324
  6.6 1.9 %collective-permute-start.1 = (f32[48,256]{1,0:T(8,128)S(1)}, f32[48,256]{1,0:T(8,128)S(1)}, u32[]{:S(2)}, u32[]{:S(2)}) collective-permute-start(f32[48,256]{1,0:T(8,128)S(1)} %get-tuple-element.42), channel_id=1, source_target_pairs={{2,0},{4,2},{6,4},{8,6},{10,8},{12,10},{14,12},{3,1},{5,3},{7,5},{... | collective-permute-start | bytes 147464 | tf_op jit(solution)/shard_map/ppermute | solution.py:325
  8.7 0.1 broadcast_in_dim.4.zonal
  8.8 0.1 broadcast_in_dim.5.coriolis
  8.8 1.5 %tendencies.1.tend = f32[32,104,128]{2,1,0:T(8,128)S(1)} custom-call(f32[3,16,32,256]{3,2,1,0:T(8,128)S(1)} %copy-done.1, f32[32,256]{1,0:T(8,128)S(1)} %broadcast_in_dim.4.zonal, f32[32,256]{1,0:T(8,128)S(1)} %broadcast_in_dim.5.coriolis), custom_call_target="tpu_custom_call" | custom-call | tf_op jit(solution)/shard_map/tendencies/pallas_call | solution.py:336
  10.4 3.4 %collective-permute-done.1.north = f32[48,256]{1,0:T(8,128)S(1)} collective-permute-done((f32[48,256]{1,0:T(8,128)S(1)}, f32[48,256]{1,0:T(8,128)S(1)}, u32[]{:S(2)}, u32[]{:S(2)}) %collective-permute-start.1) | collective-permute-done | bytes 49184 | tf_op jit(solution)/shard_map/ppermute | solution.py:325
  13.8 2.5 %seam_rows.1 = (f32[32,104,128]{2,1,0:T(8,128)S(1)}, f32[2,104,128]{2,1,0:T(8,128)S(1)}, f32[2,104,128]{2,1,0:T(8,128)S(1)}, f32[2,104,128]{2,1,0:T(8,128)S(1)},...) custom-call(s32[1]{0:T(128)} %bitcast.1.own_block, ...), custom_call_target="tpu_custom_call", output_to_operand_aliasing={{0}: (3, {})} | custom-call | tf_op jit(solution)/shard_map/seam_rows/pallas_call | solution.py:359
  16.4 4.2 %collective-permute-start.10 = (f32[2,104,128]{2,1,0:T(8,128)S(1)}, f32[2,104,128]{2,1,0:T(8,128)S(1)}, u32[]{:S(2)}, u32[]{:S(2)}) collective-permute-start(f32[2,104,128]{2,1,0:T(8,128)S(1)} %get-tuple-element.52), channel_id=1, source_target_pairs={{0,144},{16,128},{32,176},{48,160},{64,208},{80,192},{96,240},{112... | collective-permute-start | bytes 319496 | tf_op jit(solution)/shard_map/ppermute | solution.py:353
  20.6 2.5 %collective-permute-start.11 = (f32[2,104,128]{2,1,0:T(8,128)S(1)}, f32[2,104,128]{2,1,0:T(8,128)S(1)}, u32[]{:S(2)}, u32[]{:S(2)}) collective-permute-start(f32[2,104,128]{2,1,0:T(8,128)S(1)} %get-tuple-element.53), channel_id=1, source_target_pairs={{0,160},{16,176},{32,128},{48,144},{64,224},{80,240},{96,192},{112... | collective-permute-start | bytes 319496 | tf_op jit(solution)/shard_map/ppermute | solution.py:353
  23.1 3.1 %collective-permute-start.12 = (f32[2,104,128]{2,1,0:T(8,128)S(1)}, f32[2,104,128]{2,1,0:T(8,128)S(1)}, u32[]{:S(2)}, u32[]{:S(2)}) collective-permute-start(f32[2,104,128]{2,1,0:T(8,128)S(1)} %get-tuple-element.54), channel_id=1, source_target_pairs={{0,176},{16,160},{32,144},{48,128},{64,240},{80,224},{96,208},{112... | collective-permute-start | bytes 319496 | tf_op jit(solution)/shard_map/ppermute | solution.py:353
  26.2 1.1 collective-permute-start.13
  27.2 1.9 %collective-permute-start.14 = (f32[2,104,128]{2,1,0:T(8,128)S(1)}, f32[2,104,128]{2,1,0:T(8,128)S(1)}, u32[]{:S(2)}, u32[]{:S(2)}) collective-permute-start(f32[2,104,128]{2,1,0:T(8,128)S(1)} %get-tuple-element.56), channel_id=1, source_target_pairs={{0,208},{16,192},{32,240},{48,224},{64,144},{80,128},{96,176},{112... | collective-permute-start | bytes 319496 | tf_op jit(solution)/shard_map/ppermute | solution.py:353
  29.1 4.4 %collective-permute-start.15 = (f32[2,104,128]{2,1,0:T(8,128)S(1)}, f32[2,104,128]{2,1,0:T(8,128)S(1)}, u32[]{:S(2)}, u32[]{:S(2)}) collective-permute-start(f32[2,104,128]{2,1,0:T(8,128)S(1)} %get-tuple-element.57), channel_id=1, source_target_pairs={{0,224},{16,240},{32,192},{48,208},{64,160},{80,176},{96,128},{112... | collective-permute-start | bytes 319496 | tf_op jit(solution)/shard_map/ppermute | solution.py:353
  33.6 2.1 %collective-permute-start.16 = (f32[2,104,128]{2,1,0:T(8,128)S(1)}, f32[2,104,128]{2,1,0:T(8,128)S(1)}, u32[]{:S(2)}, u32[]{:S(2)}) collective-permute-start(f32[2,104,128]{2,1,0:T(8,128)S(1)} %get-tuple-element.58), channel_id=1, source_target_pairs={{0,240},{16,224},{32,208},{48,192},{64,176},{80,160},{96,144},{112... | collective-permute-start | bytes 319496 | tf_op jit(solution)/shard_map/ppermute | solution.py:353
  35.7 0.6 collective-permute-done.13.refs_12_
  36.3 3.6 %collective-permute-start.3 = (f32[2,104,128]{2,1,0:T(8,128)S(1)}, f32[2,104,128]{2,1,0:T(8,128)S(1)}, u32[]{:S(2)}, u32[]{:S(2)}) collective-permute-start(f32[2,104,128]{2,1,0:T(8,128)S(1)} %get-tuple-element.45), channel_id=1, source_target_pairs={{0,32},{16,48},{32,0},{48,16},{64,96},{80,112},{96,64},{112,80},{1... | collective-permute-start | bytes 319496 | tf_op jit(solution)/shard_map/ppermute | solution.py:353
  39.9 0.5 collective-permute-start.4
  40.4 2.8 %collective-permute-start.5 = (f32[2,104,128]{2,1,0:T(8,128)S(1)}, f32[2,104,128]{2,1,0:T(8,128)S(1)}, u32[]{:S(2)}, u32[]{:S(2)}) collective-permute-start(f32[2,104,128]{2,1,0:T(8,128)S(1)} %get-tuple-element.47), channel_id=1, source_target_pairs={{0,64},{16,80},{32,96},{48,112},{64,0},{80,16},{96,32},{112,48},{1... | collective-permute-start | bytes 319496 | tf_op jit(solution)/shard_map/ppermute | solution.py:353
  43.2 4.9 %collective-permute-start.7 = (f32[2,104,128]{2,1,0:T(8,128)S(1)}, f32[2,104,128]{2,1,0:T(8,128)S(1)}, u32[]{:S(2)}, u32[]{:S(2)}) collective-permute-start(f32[2,104,128]{2,1,0:T(8,128)S(1)} %get-tuple-element.49), channel_id=1, source_target_pairs={{0,96},{16,112},{32,64},{48,80},{64,32},{80,48},{96,0},{112,16},{1... | collective-permute-start | bytes 319496 | tf_op jit(solution)/shard_map/ppermute | solution.py:353
  48.1 0.3 collective-permute-start.8
  48.4 4.8 %collective-permute-start.9 = (f32[2,104,128]{2,1,0:T(8,128)S(1)}, f32[2,104,128]{2,1,0:T(8,128)S(1)}, u32[]{:S(2)}, u32[]{:S(2)}) collective-permute-start(f32[2,104,128]{2,1,0:T(8,128)S(1)} %get-tuple-element.51), channel_id=1, source_target_pairs={{0,128},{16,144},{32,160},{48,176},{64,192},{80,208},{96,224},{112... | collective-permute-start | bytes 319496 | tf_op jit(solution)/shard_map/ppermute | solution.py:353
  53.2 1.7 %collective-permute-done.8.refs_7_ = f32[2,104,128]{2,1,0:T(8,128)S(1)} collective-permute-done((f32[2,104,128]{2,1,0:T(8,128)S(1)}, f32[2,104,128]{2,1,0:T(8,128)S(1)}, u32[]{:S(2)}, u32[]{:S(2)}) %collective-permute-start.8) | collective-permute-done | bytes 106528 | tf_op jit(solution)/shard_map/ppermute | solution.py:353
  54.9 2.8 %collective-permute-done.9.refs_8_ = f32[2,104,128]{2,1,0:T(8,128)S(1)} collective-permute-done((f32[2,104,128]{2,1,0:T(8,128)S(1)}, f32[2,104,128]{2,1,0:T(8,128)S(1)}, u32[]{:S(2)}, u32[]{:S(2)}) %collective-permute-start.9) | collective-permute-done | bytes 106528 | tf_op jit(solution)/shard_map/ppermute | solution.py:353
  57.7 2.9 %row_filter.1 = (f32[2,3,2,16,128]{4,3,2,1,0:T(8,128)S(1)}, f32[2,3,2,16,128]{4,3,2,1,0:T(8,128)S(1)}, f32[2,3,2,16,128]{4,3,2,1,0:T(8,128)S(1)}, f32[2,3,2,16,1...) custom-call(s32[1]{0:T(128)} %bitcast.1.own_block, ...), custom_call_target="tpu_custom_call" | custom-call | tf_op jit(solution)/shard_map/row_filter/pallas_call | solution.py:380
  60.6 0.1 collective-permute-start.17
  60.7 3.0 %collective-permute-start.18 = (f32[2,3,2,16,128]{4,3,2,1,0:T(8,128)S(1)}, f32[2,3,2,16,128]{4,3,2,1,0:T(8,128)S(1)}, u32[]{:S(2)}, u32[]{:S(2)}) collective-permute-start(f32[2,3,2,16,128]{4,3,2,1,0:T(8,128)S(1)} %get-tuple-element.61), channel_id=1, source_target_pairs={{0,32},{16,48},{32,0},{48,16},{64,96},{80,112},{96,64},{112,80},{1... | collective-permute-start | bytes 294920 | tf_op jit(solution)/shard_map/ppermute | solution.py:353
  63.8 1.6 %collective-permute-start.19 = (f32[2,3,2,16,128]{4,3,2,1,0:T(8,128)S(1)}, f32[2,3,2,16,128]{4,3,2,1,0:T(8,128)S(1)}, u32[]{:S(2)}, u32[]{:S(2)}) collective-permute-start(f32[2,3,2,16,128]{4,3,2,1,0:T(8,128)S(1)} %get-tuple-element.62), channel_id=1, source_target_pairs={{0,48},{16,32},{32,16},{48,0},{64,112},{80,96},{96,80},{112,64},{1... | collective-permute-start | bytes 294920 | tf_op jit(solution)/shard_map/ppermute | solution.py:353
  65.4 0.3 collective-permute-start.21
  65.8 0.6 collective-permute-done.17.refs_1_
  66.4 3.0 %collective-permute-start.22 = (f32[2,3,2,16,128]{4,3,2,1,0:T(8,128)S(1)}, f32[2,3,2,16,128]{4,3,2,1,0:T(8,128)S(1)}, u32[]{:S(2)}, u32[]{:S(2)}) collective-permute-start(f32[2,3,2,16,128]{4,3,2,1,0:T(8,128)S(1)} %get-tuple-element.65), channel_id=1, source_target_pairs={{0,96},{16,112},{32,64},{48,80},{64,32},{80,48},{96,0},{112,16},{1... | collective-permute-start | bytes 294920 | tf_op jit(solution)/shard_map/ppermute | solution.py:353
  69.4 3.1 %collective-permute-start.23 = (f32[2,3,2,16,128]{4,3,2,1,0:T(8,128)S(1)}, f32[2,3,2,16,128]{4,3,2,1,0:T(8,128)S(1)}, u32[]{:S(2)}, u32[]{:S(2)}) collective-permute-start(f32[2,3,2,16,128]{4,3,2,1,0:T(8,128)S(1)} %get-tuple-element.66), channel_id=1, source_target_pairs={{0,112},{16,96},{32,80},{48,64},{64,48},{80,32},{96,16},{112,0},{1... | collective-permute-start | bytes 294920 | tf_op jit(solution)/shard_map/ppermute | solution.py:353
  72.5 1.7 %collective-permute-start.24 = (f32[2,3,2,16,128]{4,3,2,1,0:T(8,128)S(1)}, f32[2,3,2,16,128]{4,3,2,1,0:T(8,128)S(1)}, u32[]{:S(2)}, u32[]{:S(2)}) collective-permute-start(f32[2,3,2,16,128]{4,3,2,1,0:T(8,128)S(1)} %get-tuple-element.67), channel_id=1, source_target_pairs={{0,128},{16,144},{32,160},{48,176},{64,192},{80,208},{96,224},{112... | collective-permute-start | bytes 294920 | tf_op jit(solution)/shard_map/ppermute | solution.py:353
  74.2 0.5 collective-permute-done.20.refs_4_
  74.7 4.7 %collective-permute-start.26 = (f32[2,3,2,16,128]{4,3,2,1,0:T(8,128)S(1)}, f32[2,3,2,16,128]{4,3,2,1,0:T(8,128)S(1)}, u32[]{:S(2)}, u32[]{:S(2)}) collective-permute-start(f32[2,3,2,16,128]{4,3,2,1,0:T(8,128)S(1)} %get-tuple-element.69), channel_id=1, source_target_pairs={{0,160},{16,176},{32,128},{48,144},{64,224},{80,240},{96,192},{112... | collective-permute-start | bytes 294920 | tf_op jit(solution)/shard_map/ppermute | solution.py:353
  79.4 3.2 %collective-permute-start.27 = (f32[2,3,2,16,128]{4,3,2,1,0:T(8,128)S(1)}, f32[2,3,2,16,128]{4,3,2,1,0:T(8,128)S(1)}, u32[]{:S(2)}, u32[]{:S(2)}) collective-permute-start(f32[2,3,2,16,128]{4,3,2,1,0:T(8,128)S(1)} %get-tuple-element.70), channel_id=1, source_target_pairs={{0,176},{16,160},{32,144},{48,128},{64,240},{80,224},{96,208},{112... | collective-permute-start | bytes 294920 | tf_op jit(solution)/shard_map/ppermute | solution.py:353
  82.6 1.2 %collective-permute-start.28 = (f32[2,3,2,16,128]{4,3,2,1,0:T(8,128)S(1)}, f32[2,3,2,16,128]{4,3,2,1,0:T(8,128)S(1)}, u32[]{:S(2)}, u32[]{:S(2)}) collective-permute-start(f32[2,3,2,16,128]{4,3,2,1,0:T(8,128)S(1)} %get-tuple-element.71), channel_id=1, source_target_pairs={{0,192},{16,208},{32,224},{48,240},{64,128},{80,144},{96,160},{112... | collective-permute-start | bytes 294920 | tf_op jit(solution)/shard_map/ppermute | solution.py:353
  83.8 0.4 collective-permute-start.29
  84.3 5.0 %collective-permute-start.30 = (f32[2,3,2,16,128]{4,3,2,1,0:T(8,128)S(1)}, f32[2,3,2,16,128]{4,3,2,1,0:T(8,128)S(1)}, u32[]{:S(2)}, u32[]{:S(2)}) collective-permute-start(f32[2,3,2,16,128]{4,3,2,1,0:T(8,128)S(1)} %get-tuple-element.73), channel_id=1, source_target_pairs={{0,224},{16,240},{32,192},{48,208},{64,160},{80,176},{96,128},{112... | collective-permute-start | bytes 294920 | tf_op jit(solution)/shard_map/ppermute | solution.py:353
  89.2 2.9 %collective-permute-start.31 = (f32[2,3,2,16,128]{4,3,2,1,0:T(8,128)S(1)}, f32[2,3,2,16,128]{4,3,2,1,0:T(8,128)S(1)}, u32[]{:S(2)}, u32[]{:S(2)}) collective-permute-start(f32[2,3,2,16,128]{4,3,2,1,0:T(8,128)S(1)} %get-tuple-element.74), channel_id=1, source_target_pairs={{0,240},{16,224},{32,208},{48,192},{64,176},{80,160},{96,144},{112... | collective-permute-start | bytes 294920 | tf_op jit(solution)/shard_map/ppermute | solution.py:353
  92.1 1.0 slice.3
  93.1 0.8 collective-permute-done.28.refs_12_
  93.9 3.2 %collective-permute-done.31.refs_15_ = f32[2,3,2,16,128]{4,3,2,1,0:T(8,128)S(1)} collective-permute-done((f32[2,3,2,16,128]{4,3,2,1,0:T(8,128)S(1)}, f32[2,3,2,16,128]{4,3,2,1,0:T(8,128)S(1)}, u32[]{:S(2)}, u32[]{:S(2)}) %collective-permute-start.31) | collective-permute-done | bytes 98336 | tf_op jit(solution)/shard_map/ppermute | solution.py:353
  97.2 1.1 %gather_rows.1 = (f32[32,2,2,16,128]{4,3,2,1,0:T(8,128)}, f32[32,2,16,128]{3,2,1,0:T(8,128)S(1)}) custom-call(s32[1]{0:T(128)} %bitcast.1.own_block, f32[2,3,2,16,128]{4,3,2,1,0:T(8,128)S(1)} %get-tuple-element.59.refs_0_, f32[2,3,2,16,128]{4,3,2,1,0:T(8,128)S(1)} %collective-permute-done.17.refs_1_, ...), custom_call_target="tpu_custom_call" | custom-call | tf_op jit(solution)/shard_map/gather_rows/pallas_call | solution.py:399
  98.2 0.8 copy-done.3
  99.1 2.5 %base.1 = f32[32,3,2,16,128]{4,3,2,1,0:T(8,128)} custom-call(s32[1]{0:T(128)} %bitcast.own_part, f32[3,16,32,256]{3,2,1,0:T(8,128)S(1)} %copy-done.1, f32[2,16,32,256]{3,2,1,0:T(8,128)S(1)} %collective-permute-done.33.other, f32[32,32,32]{2,1,0:T(8,128)S(1)} %copy-done.2), custom_call_target="tpu_custom_call" | custom-call | tf_op jit(solution)/shard_map/base/pallas_call | solution.py:416
  101.6 0.5 collective-permute-done.32.other
  102.0 4.8 %finish.1 = f32[3,16,32,256]{3,2,1,0:T(8,128)} custom-call(s32[1]{0:T(128)} %bitcast.own_part, f32[32,2,2,16,128]{4,3,2,1,0:T(8,128)} %get-tuple-element.75.step, f32[32,2,16,128]{3,2,1,0:T(8,128)S(1)} %copy-done.4, f32[32,2,2,16,128]{4,3,2,1,0:T(8,128)} %collective-permute-done.32.other, f32[32,3,2,16,128]{4,3,2,1,0:T(8,128)} %base.1, ...), custom_call_target="tpu_custom_call" | custom-call | tf_op jit(solution)/shard_map/finish/pallas_call | solution.py:433
  (46 shorter events, 0.3 us)
Async XLA Ops:
  0.0 1.4 %copy-start = (f32[3,16,32,256]{3,2,1,0:T(8,128)S(1)}, f32[3,16,32,256]{3,2,1,0:T(8,128)}, u32[]{:S(2)}) copy-start(f32[3,16,32,256]{3,2,1,0:T(8,128)} %own.1) | copy-start | bytes 4718596
  1.4 7.4 %copy-start.1 = (f32[3,16,32,256]{3,2,1,0:T(8,128)S(1)}, f32[3,16,32,256]{3,2,1,0:T(8,128)}, u32[]{:S(2)}) copy-start(f32[3,16,32,256]{3,2,1,0:T(8,128)} %own.1) | copy-start | bytes 4718596
  1.5 8.9 %collective-permute-start = (f32[48,256]{1,0:T(8,128)S(1)}, f32[48,256]{1,0:T(8,128)S(1)}, u32[]{:S(2)}, u32[]{:S(2)}) collective-permute-start(f32[48,256]{1,0:T(8,128)S(1)} %get-tuple-element.41), channel_id=1, source_target_pairs={{0,2},{2,4},{4,6},{6,8},{8,10},{10,12},{12,14},{1,3},{3,5},{5,7},{... | collective-permute-start | bytes 147464 | tf_op jit(solution)/shard_map/ppermute | solution.py:324
  6.6 7.2 %collective-permute-start.1 = (f32[48,256]{1,0:T(8,128)S(1)}, f32[48,256]{1,0:T(8,128)S(1)}, u32[]{:S(2)}, u32[]{:S(2)}) collective-permute-start(f32[48,256]{1,0:T(8,128)S(1)} %get-tuple-element.42), channel_id=1, source_target_pairs={{2,0},{4,2},{6,4},{8,6},{10,8},{12,10},{14,12},{3,1},{5,3},{7,5},{... | collective-permute-start | bytes 147464 | tf_op jit(solution)/shard_map/ppermute | solution.py:325
  10.4 47.3 %copy-start.5 = (s32[32]{0:T(128)S(1)}, s32[32]{0:T(128)}, u32[]{:S(2)}) copy-start(s32[32]{0:T(128)} %half_width.1) | copy-start | bytes 388
  10.4 47.3 %copy-start.6 = (s32[32]{0:T(128)S(1)}, s32[32]{0:T(128)}, u32[]{:S(2)}) copy-start(s32[32]{0:T(128)} %filter_mask.1) | copy-start | bytes 388
  16.4 12.8 %collective-permute-start.10 = (f32[2,104,128]{2,1,0:T(8,128)S(1)}, f32[2,104,128]{2,1,0:T(8,128)S(1)}, u32[]{:S(2)}, u32[]{:S(2)}) collective-permute-start(f32[2,104,128]{2,1,0:T(8,128)S(1)} %get-tuple-element.52), channel_id=1, source_target_pairs={{0,144},{16,128},{32,176},{48,160},{64,208},{80,192},{96,240},{112... | collective-permute-start | bytes 319496 | tf_op jit(solution)/shard_map/ppermute | solution.py:353
  20.6 13.0 %collective-permute-start.11 = (f32[2,104,128]{2,1,0:T(8,128)S(1)}, f32[2,104,128]{2,1,0:T(8,128)S(1)}, u32[]{:S(2)}, u32[]{:S(2)}) collective-permute-start(f32[2,104,128]{2,1,0:T(8,128)S(1)} %get-tuple-element.53), channel_id=1, source_target_pairs={{0,160},{16,176},{32,128},{48,144},{64,224},{80,240},{96,192},{112... | collective-permute-start | bytes 319496 | tf_op jit(solution)/shard_map/ppermute | solution.py:353
  23.1 12.6 %collective-permute-start.12 = (f32[2,104,128]{2,1,0:T(8,128)S(1)}, f32[2,104,128]{2,1,0:T(8,128)S(1)}, u32[]{:S(2)}, u32[]{:S(2)}) collective-permute-start(f32[2,104,128]{2,1,0:T(8,128)S(1)} %get-tuple-element.54), channel_id=1, source_target_pairs={{0,176},{16,160},{32,144},{48,128},{64,240},{80,224},{96,208},{112... | collective-permute-start | bytes 319496 | tf_op jit(solution)/shard_map/ppermute | solution.py:353
  26.2 10.1 %collective-permute-start.13 = (f32[2,104,128]{2,1,0:T(8,128)S(1)}, f32[2,104,128]{2,1,0:T(8,128)S(1)}, u32[]{:S(2)}, u32[]{:S(2)}) collective-permute-start(f32[2,104,128]{2,1,0:T(8,128)S(1)} %get-tuple-element.55), channel_id=1, source_target_pairs={{0,192},{16,208},{32,224},{48,240},{64,128},{80,144},{96,160},{112... | collective-permute-start | bytes 319496 | tf_op jit(solution)/shard_map/ppermute | solution.py:353
  27.2 12.7 %collective-permute-start.14 = (f32[2,104,128]{2,1,0:T(8,128)S(1)}, f32[2,104,128]{2,1,0:T(8,128)S(1)}, u32[]{:S(2)}, u32[]{:S(2)}) collective-permute-start(f32[2,104,128]{2,1,0:T(8,128)S(1)} %get-tuple-element.56), channel_id=1, source_target_pairs={{0,208},{16,192},{32,240},{48,224},{64,144},{80,128},{96,176},{112... | collective-permute-start | bytes 319496 | tf_op jit(solution)/shard_map/ppermute | solution.py:353
  29.1 11.3 %collective-permute-start.15 = (f32[2,104,128]{2,1,0:T(8,128)S(1)}, f32[2,104,128]{2,1,0:T(8,128)S(1)}, u32[]{:S(2)}, u32[]{:S(2)}) collective-permute-start(f32[2,104,128]{2,1,0:T(8,128)S(1)} %get-tuple-element.57), channel_id=1, source_target_pairs={{0,224},{16,240},{32,192},{48,208},{64,160},{80,176},{96,128},{112... | collective-permute-start | bytes 319496 | tf_op jit(solution)/shard_map/ppermute | solution.py:353
  33.6 9.7 %collective-permute-start.16 = (f32[2,104,128]{2,1,0:T(8,128)S(1)}, f32[2,104,128]{2,1,0:T(8,128)S(1)}, u32[]{:S(2)}, u32[]{:S(2)}) collective-permute-start(f32[2,104,128]{2,1,0:T(8,128)S(1)} %get-tuple-element.58), channel_id=1, source_target_pairs={{0,240},{16,224},{32,208},{48,192},{64,176},{80,160},{96,144},{112... | collective-permute-start | bytes 319496 | tf_op jit(solution)/shard_map/ppermute | solution.py:353
  35.7 7.6 %collective-permute-start.2 = (f32[2,104,128]{2,1,0:T(8,128)S(1)}, f32[2,104,128]{2,1,0:T(8,128)S(1)}, u32[]{:S(2)}, u32[]{:S(2)}) collective-permute-start(f32[2,104,128]{2,1,0:T(8,128)S(1)} %get-tuple-element.44), channel_id=1, source_target_pairs={{0,16},{16,0},{32,48},{48,32},{64,80},{80,64},{96,112},{112,96},{1... | collective-permute-start | bytes 319496 | tf_op jit(solution)/shard_map/ppermute | solution.py:353
  36.3 11.8 %collective-permute-start.3 = (f32[2,104,128]{2,1,0:T(8,128)S(1)}, f32[2,104,128]{2,1,0:T(8,128)S(1)}, u32[]{:S(2)}, u32[]{:S(2)}) collective-permute-start(f32[2,104,128]{2,1,0:T(8,128)S(1)} %get-tuple-element.45), channel_id=1, source_target_pairs={{0,32},{16,48},{32,0},{48,16},{64,96},{80,112},{96,64},{112,80},{1... | collective-permute-start | bytes 319496 | tf_op jit(solution)/shard_map/ppermute | solution.py:353
  39.9 8.5 %collective-permute-start.4 = (f32[2,104,128]{2,1,0:T(8,128)S(1)}, f32[2,104,128]{2,1,0:T(8,128)S(1)}, u32[]{:S(2)}, u32[]{:S(2)}) collective-permute-start(f32[2,104,128]{2,1,0:T(8,128)S(1)} %get-tuple-element.46), channel_id=1, source_target_pairs={{0,48},{16,32},{32,16},{48,0},{64,112},{80,96},{96,80},{112,64},{1... | collective-permute-start | bytes 319496 | tf_op jit(solution)/shard_map/ppermute | solution.py:353
  40.4 12.8 %collective-permute-start.5 = (f32[2,104,128]{2,1,0:T(8,128)S(1)}, f32[2,104,128]{2,1,0:T(8,128)S(1)}, u32[]{:S(2)}, u32[]{:S(2)}) collective-permute-start(f32[2,104,128]{2,1,0:T(8,128)S(1)} %get-tuple-element.47), channel_id=1, source_target_pairs={{0,64},{16,80},{32,96},{48,112},{64,0},{80,16},{96,32},{112,48},{1... | collective-permute-start | bytes 319496 | tf_op jit(solution)/shard_map/ppermute | solution.py:353
  43.2 10.0 %collective-permute-start.6 = (f32[2,104,128]{2,1,0:T(8,128)S(1)}, f32[2,104,128]{2,1,0:T(8,128)S(1)}, u32[]{:S(2)}, u32[]{:S(2)}) collective-permute-start(f32[2,104,128]{2,1,0:T(8,128)S(1)} %get-tuple-element.48), channel_id=1, source_target_pairs={{0,80},{16,64},{32,112},{48,96},{64,16},{80,0},{96,48},{112,32},{1... | collective-permute-start | bytes 319496 | tf_op jit(solution)/shard_map/ppermute | solution.py:353
  43.2 9.9 %collective-permute-start.7 = (f32[2,104,128]{2,1,0:T(8,128)S(1)}, f32[2,104,128]{2,1,0:T(8,128)S(1)}, u32[]{:S(2)}, u32[]{:S(2)}) collective-permute-start(f32[2,104,128]{2,1,0:T(8,128)S(1)} %get-tuple-element.49), channel_id=1, source_target_pairs={{0,96},{16,112},{32,64},{48,80},{64,32},{80,48},{96,0},{112,16},{1... | collective-permute-start | bytes 319496 | tf_op jit(solution)/shard_map/ppermute | solution.py:353
  48.1 6.8 %collective-permute-start.8 = (f32[2,104,128]{2,1,0:T(8,128)S(1)}, f32[2,104,128]{2,1,0:T(8,128)S(1)}, u32[]{:S(2)}, u32[]{:S(2)}) collective-permute-start(f32[2,104,128]{2,1,0:T(8,128)S(1)} %get-tuple-element.50), channel_id=1, source_target_pairs={{0,112},{16,96},{32,80},{48,64},{64,48},{80,32},{96,16},{112,0},{1... | collective-permute-start | bytes 319496 | tf_op jit(solution)/shard_map/ppermute | solution.py:353
  48.4 9.3 %collective-permute-start.9 = (f32[2,104,128]{2,1,0:T(8,128)S(1)}, f32[2,104,128]{2,1,0:T(8,128)S(1)}, u32[]{:S(2)}, u32[]{:S(2)}) collective-permute-start(f32[2,104,128]{2,1,0:T(8,128)S(1)} %get-tuple-element.51), channel_id=1, source_target_pairs={{0,128},{16,144},{32,160},{48,176},{64,192},{80,208},{96,224},{112... | collective-permute-start | bytes 319496 | tf_op jit(solution)/shard_map/ppermute | solution.py:353
  60.6 5.7 %collective-permute-start.17 = (f32[2,3,2,16,128]{4,3,2,1,0:T(8,128)S(1)}, f32[2,3,2,16,128]{4,3,2,1,0:T(8,128)S(1)}, u32[]{:S(2)}, u32[]{:S(2)}) collective-permute-start(f32[2,3,2,16,128]{4,3,2,1,0:T(8,128)S(1)} %get-tuple-element.60), channel_id=1, source_target_pairs={{0,16},{16,0},{32,48},{48,32},{64,80},{80,64},{96,112},{112,96},{1... | collective-permute-start | bytes 294920 | tf_op jit(solution)/shard_map/ppermute | solution.py:353
  60.7 8.6 %collective-permute-start.18 = (f32[2,3,2,16,128]{4,3,2,1,0:T(8,128)S(1)}, f32[2,3,2,16,128]{4,3,2,1,0:T(8,128)S(1)}, u32[]{:S(2)}, u32[]{:S(2)}) collective-permute-start(f32[2,3,2,16,128]{4,3,2,1,0:T(8,128)S(1)} %get-tuple-element.61), channel_id=1, source_target_pairs={{0,32},{16,48},{32,0},{48,16},{64,96},{80,112},{96,64},{112,80},{1... | collective-permute-start | bytes 294920 | tf_op jit(solution)/shard_map/ppermute | solution.py:353
  63.8 8.7 %collective-permute-start.19 = (f32[2,3,2,16,128]{4,3,2,1,0:T(8,128)S(1)}, f32[2,3,2,16,128]{4,3,2,1,0:T(8,128)S(1)}, u32[]{:S(2)}, u32[]{:S(2)}) collective-permute-start(f32[2,3,2,16,128]{4,3,2,1,0:T(8,128)S(1)} %get-tuple-element.62), channel_id=1, source_target_pairs={{0,48},{16,32},{32,16},{48,0},{64,112},{80,96},{96,80},{112,64},{1... | collective-permute-start | bytes 294920 | tf_op jit(solution)/shard_map/ppermute | solution.py:353
  65.4 9.3 %collective-permute-start.20 = (f32[2,3,2,16,128]{4,3,2,1,0:T(8,128)S(1)}, f32[2,3,2,16,128]{4,3,2,1,0:T(8,128)S(1)}, u32[]{:S(2)}, u32[]{:S(2)}) collective-permute-start(f32[2,3,2,16,128]{4,3,2,1,0:T(8,128)S(1)} %get-tuple-element.63), channel_id=1, source_target_pairs={{0,64},{16,80},{32,96},{48,112},{64,0},{80,16},{96,32},{112,48},{1... | collective-permute-start | bytes 294920 | tf_op jit(solution)/shard_map/ppermute | solution.py:353
  65.4 9.3 %collective-permute-start.21 = (f32[2,3,2,16,128]{4,3,2,1,0:T(8,128)S(1)}, f32[2,3,2,16,128]{4,3,2,1,0:T(8,128)S(1)}, u32[]{:S(2)}, u32[]{:S(2)}) collective-permute-start(f32[2,3,2,16,128]{4,3,2,1,0:T(8,128)S(1)} %get-tuple-element.64), channel_id=1, source_target_pairs={{0,80},{16,64},{32,112},{48,96},{64,16},{80,0},{96,48},{112,32},{1... | collective-permute-start | bytes 294920 | tf_op jit(solution)/shard_map/ppermute | solution.py:353
  66.4 13.0 %collective-permute-start.22 = (f32[2,3,2,16,128]{4,3,2,1,0:T(8,128)S(1)}, f32[2,3,2,16,128]{4,3,2,1,0:T(8,128)S(1)}, u32[]{:S(2)}, u32[]{:S(2)}) collective-permute-start(f32[2,3,2,16,128]{4,3,2,1,0:T(8,128)S(1)} %get-tuple-element.65), channel_id=1, source_target_pairs={{0,96},{16,112},{32,64},{48,80},{64,32},{80,48},{96,0},{112,16},{1... | collective-permute-start | bytes 294920 | tf_op jit(solution)/shard_map/ppermute | solution.py:353
  69.4 13.2 %collective-permute-start.23 = (f32[2,3,2,16,128]{4,3,2,1,0:T(8,128)S(1)}, f32[2,3,2,16,128]{4,3,2,1,0:T(8,128)S(1)}, u32[]{:S(2)}, u32[]{:S(2)}) collective-permute-start(f32[2,3,2,16,128]{4,3,2,1,0:T(8,128)S(1)} %get-tuple-element.66), channel_id=1, source_target_pairs={{0,112},{16,96},{32,80},{48,64},{64,48},{80,32},{96,16},{112,0},{1... | collective-permute-start | bytes 294920 | tf_op jit(solution)/shard_map/ppermute | solution.py:353
  72.5 11.3 %collective-permute-start.24 = (f32[2,3,2,16,128]{4,3,2,1,0:T(8,128)S(1)}, f32[2,3,2,16,128]{4,3,2,1,0:T(8,128)S(1)}, u32[]{:S(2)}, u32[]{:S(2)}) collective-permute-start(f32[2,3,2,16,128]{4,3,2,1,0:T(8,128)S(1)} %get-tuple-element.67), channel_id=1, source_target_pairs={{0,128},{16,144},{32,160},{48,176},{64,192},{80,208},{96,224},{112... | collective-permute-start | bytes 294920 | tf_op jit(solution)/shard_map/ppermute | solution.py:353
  74.7 9.6 %collective-permute-start.25 = (f32[2,3,2,16,128]{4,3,2,1,0:T(8,128)S(1)}, f32[2,3,2,16,128]{4,3,2,1,0:T(8,128)S(1)}, u32[]{:S(2)}, u32[]{:S(2)}) collective-permute-start(f32[2,3,2,16,128]{4,3,2,1,0:T(8,128)S(1)} %get-tuple-element.68), channel_id=1, source_target_pairs={{0,144},{16,128},{32,176},{48,160},{64,208},{80,192},{96,240},{112... | collective-permute-start | bytes 294920 | tf_op jit(solution)/shard_map/ppermute | solution.py:353
  74.7 14.5 %collective-permute-start.26 = (f32[2,3,2,16,128]{4,3,2,1,0:T(8,128)S(1)}, f32[2,3,2,16,128]{4,3,2,1,0:T(8,128)S(1)}, u32[]{:S(2)}, u32[]{:S(2)}) collective-permute-start(f32[2,3,2,16,128]{4,3,2,1,0:T(8,128)S(1)} %get-tuple-element.69), channel_id=1, source_target_pairs={{0,160},{16,176},{32,128},{48,144},{64,224},{80,240},{96,192},{112... | collective-permute-start | bytes 294920 | tf_op jit(solution)/shard_map/ppermute | solution.py:353
  79.4 13.8 %collective-permute-start.27 = (f32[2,3,2,16,128]{4,3,2,1,0:T(8,128)S(1)}, f32[2,3,2,16,128]{4,3,2,1,0:T(8,128)S(1)}, u32[]{:S(2)}, u32[]{:S(2)}) collective-permute-start(f32[2,3,2,16,128]{4,3,2,1,0:T(8,128)S(1)} %get-tuple-element.70), channel_id=1, source_target_pairs={{0,176},{16,160},{32,144},{48,128},{64,240},{80,224},{96,208},{112... | collective-permute-start | bytes 294920 | tf_op jit(solution)/shard_map/ppermute | solution.py:353
  82.6 11.3 %collective-permute-start.28 = (f32[2,3,2,16,128]{4,3,2,1,0:T(8,128)S(1)}, f32[2,3,2,16,128]{4,3,2,1,0:T(8,128)S(1)}, u32[]{:S(2)}, u32[]{:S(2)}) collective-permute-start(f32[2,3,2,16,128]{4,3,2,1,0:T(8,128)S(1)} %get-tuple-element.71), channel_id=1, source_target_pairs={{0,192},{16,208},{32,224},{48,240},{64,128},{80,144},{96,160},{112... | collective-permute-start | bytes 294920 | tf_op jit(solution)/shard_map/ppermute | solution.py:353
  83.8 10.1 %collective-permute-start.29 = (f32[2,3,2,16,128]{4,3,2,1,0:T(8,128)S(1)}, f32[2,3,2,16,128]{4,3,2,1,0:T(8,128)S(1)}, u32[]{:S(2)}, u32[]{:S(2)}) collective-permute-start(f32[2,3,2,16,128]{4,3,2,1,0:T(8,128)S(1)} %get-tuple-element.72), channel_id=1, source_target_pairs={{0,208},{16,192},{32,240},{48,224},{64,144},{80,128},{96,176},{112... | collective-permute-start | bytes 294920 | tf_op jit(solution)/shard_map/ppermute | solution.py:353
  84.3 9.7 %collective-permute-start.30 = (f32[2,3,2,16,128]{4,3,2,1,0:T(8,128)S(1)}, f32[2,3,2,16,128]{4,3,2,1,0:T(8,128)S(1)}, u32[]{:S(2)}, u32[]{:S(2)}) collective-permute-start(f32[2,3,2,16,128]{4,3,2,1,0:T(8,128)S(1)} %get-tuple-element.73), channel_id=1, source_target_pairs={{0,224},{16,240},{32,192},{48,208},{64,160},{80,176},{96,128},{112... | collective-permute-start | bytes 294920 | tf_op jit(solution)/shard_map/ppermute | solution.py:353
  89.2 9.8 %copy-start.2 = (f32[32,32,32]{2,1,0:T(8,128)S(1)}, f32[32,32,32]{2,1,0:T(8,128)}, u32[]{:S(2)}) copy-start(f32[32,32,32]{2,1,0:T(8,128)} %matrix.3) | copy-start | bytes 393220
  89.2 7.9 %collective-permute-start.31 = (f32[2,3,2,16,128]{4,3,2,1,0:T(8,128)S(1)}, f32[2,3,2,16,128]{4,3,2,1,0:T(8,128)S(1)}, u32[]{:S(2)}, u32[]{:S(2)}) collective-permute-start(f32[2,3,2,16,128]{4,3,2,1,0:T(8,128)S(1)} %get-tuple-element.74), channel_id=1, source_target_pairs={{0,240},{16,224},{32,208},{48,192},{64,176},{80,160},{96,144},{112... | collective-permute-start | bytes 294920 | tf_op jit(solution)/shard_map/ppermute | solution.py:353
  93.1 5.9 %collective-permute-start.33 = (f32[2,16,32,256]{3,2,1,0:T(8,128)}, f32[2,16,32,256]{3,2,1,0:T(8,128)S(1)}, u32[]{:S(2)}, u32[]{:S(2)}) collective-permute-start(f32[2,16,32,256]{3,2,1,0:T(8,128)} %slice.3), channel_id=1, source_target_pairs={{0,1},{1,0},{2,3},{3,2},{4,5},{5,4},{6,7},{7,6},{8,9},{9,8},{10,11... | collective-permute-start | bytes 3145736 | tf_op jit(solution)/shard_map/ppermute | solution.py:326
  98.2 0.8 copy-start.3
  99.0 3.0 %collective-permute-start.32 = (f32[32,2,2,16,128]{4,3,2,1,0:T(8,128)}, f32[32,2,2,16,128]{4,3,2,1,0:T(8,128)}, u32[]{:S(2)}, u32[]{:S(2)}) collective-permute-start(f32[32,2,2,16,128]{4,3,2,1,0:T(8,128)} %get-tuple-element.75.step), channel_id=1, source_target_pairs={{0,1},{1,0},{2,3},{3,2},{4,5},{5,4},{6,7},{7,6},{8,9},{9,8},{10,11... | collective-permute-start | bytes 3145736 | tf_op jit(solution)/shard_map/ppermute | solution.py:413
  99.0 3.0 %copy-start.4 = (f32[32,2,16,128]{3,2,1,0:T(8,128)S(1)}, f32[32,2,16,128]{3,2,1,0:T(8,128)}, u32[]{:S(2)}) copy-start(f32[32,2,16,128]{3,2,1,0:T(8,128)} %copy-done.3) | copy-start | bytes 1572868

commit v7 on v3

--- a/solution.py
+++ b/solution.py
@@ -12,6 +12,7 @@
 SUBLANES = 8
 VMEM_LIMIT = 32 * 1024 * 1024
 GROUP = 4
+LOADS = 4
 
 
 def latitudes(global_rows, row_total):
@@ -33,13 +34,22 @@
     return tiles
 
 
-def outer_rows_kernel(prog, last, first):
-    _, levels, rows, _ = prog.shape
-    for f in range(3):
+def fetch_kernel(prog, tile, last, first, sems):
+    fields, levels, rows, _ = prog.shape
+    per_load = levels // LOADS
+    loads = []
+    for f in range(fields):
+        for load in range(LOADS):
+            some = pl.ds(load * per_load, per_load)
+            loads.append(pltpu.make_async_copy(prog.at[f, some], tile.at[f, some], sems.at[f, load]))
+            loads[-1].start()
+    for f in range(fields):
         for l in range(levels):
+            if l % per_load == 0:
+                loads[f * LOADS + l // per_load].wait()
             c = f * levels + l
-            last[c : c + 1, :] = prog[f, l, rows - 1 : rows, :]
-            first[c : c + 1, :] = prog[f, l, 0:1, :]
+            last[c : c + 1, :] = tile[f, l, rows - 1 : rows, :]
+            first[c : c + 1, :] = tile[f, l, 0:1, :]
 
 
 def tendency_kernel(prog, zonal, coriolis, out, ends, turn, edges, stage, out_sems):
@@ -135,6 +145,20 @@
     return jnp.concatenate([hi, hi, lo], axis=1)
 
 
+def pair_mix_operand(matrix):
+    hi, lo = split2(matrix)
+    none = jnp.zeros_like(hi)
+    return jnp.concatenate(
+        [
+            jnp.concatenate([hi, hi, none, none], axis=1),
+            jnp.concatenate([none, none, hi, hi], axis=1),
+            jnp.concatenate([lo, none, none, none], axis=1),
+            jnp.concatenate([none, none, lo, none], axis=1),
+        ],
+        axis=0,
+    )
+
+
 def filter_kernel(
     own_row, half_width, filter_mask, zonal, tend, matrices, out, halves, parts, seam, matrix, stage, matrix_sem, sems
 ):
@@ -180,31 +204,28 @@
         inside = lax.rem(g + reach, count) < 2 * reach
         window = window + jnp.where(inside, 1.0, 0.0).astype(jnp.float32) * value
 
-    src = lax.broadcasted_iota(jnp.int32, (2 * HALF, HALF), 0)
-    dst = lax.broadcasted_iota(jnp.int32, (2 * HALF, HALF), 1)
-    sums = jnp.where((src <= dst) | (src >= HALF), 1.0, 0.0).astype(jnp.bfloat16)
+    src = lax.broadcasted_iota(jnp.int32, (2 * HALF, 2 * HALF), 0)
+    dst = lax.broadcasted_iota(jnp.int32, (2 * HALF, 2 * HALF), 1)
+    sums = jnp.where((src & (HALF - 1)) <= dst, 1.0, 0.0).astype(jnp.bfloat16)
     fetch.wait()
-    mixer = mix_operand(matrix[...])
+    mixer = pair_mix_operand(matrix[...])
     scale = TIME_STEP / norm
-
-    def split_group(g0, window):
+    total = jnp.dot(
+        jnp.concatenate(split2(window), axis=1), sums, preferred_element_type=jnp.float32
+    )[:, HALF:]
+
+    def split_group(g0):
         for g in range(g0, g0 + GROUP):
             ahead = halves[lax.rem(g + reach, count)]
             behind = halves[lax.rem(g + count - reach, count)]
-            change = ahead - behind
-            for k, (a, b) in enumerate(zip(split2(change), split2(window))):
-                parts[k, g * both : (g + 1) * both, :HALF] = a
-                parts[k, g * both : (g + 1) * both, HALF:] = b
-            window = window + change
-        return window
+            hi, lo = split2(ahead - behind)
+            parts[g * both : (g + 1) * both, :HALF] = hi
+            parts[g * both : (g + 1) * both, HALF:] = lo
 
     copies = []
 
-    def finish_group(g0):
-        lo, hi = g0 * both, (g0 + GROUP) * both
-        box = jnp.dot(parts[1, lo:hi, :], sums, preferred_element_type=jnp.float32) + jnp.dot(
-            parts[0, lo:hi, :], sums, preferred_element_type=jnp.float32
-        )
+    def finish_group(g0, total):
+        box = jnp.dot(parts[g0 * both : (g0 + GROUP) * both, :], sums, preferred_element_type=jnp.float32)
         for pair in range(GROUP // 2):
             b = g0 // 2 + pair
             steps = []
@@ -212,35 +233,37 @@
                 g = 2 * b + half
                 at = (g - g0) * both
                 behind = halves[lax.rem(g + count - reach, count)]
-                smooth = (box[at : at + both] + edge_gain * behind) * scale
+                smooth = (box[at : at + both, :HALF] + total + edge_gain * behind) * scale
+                total = total + box[at : at + both, HALF:]
                 step = jnp.where(filtered, smooth, TIME_STEP * halves[g])
                 for p in range(lev_parts):
                     stage[b, p, 2, half] = step[p * chans + 2 * levels : (p + 1) * chans]
                 steps.append(step)
             step = jnp.concatenate(steps, axis=1)
+            winds = []
             for f in range(2):
-                wind = jnp.concatenate(
-                    [step[p * chans + f * levels : p * chans + (f + 1) * levels] for p in range(lev_parts)], axis=0
+                winds += split2(
+                    jnp.concatenate(
+                        [step[p * chans + f * levels : p * chans + (f + 1) * levels] for p in range(lev_parts)],
+                        axis=0,
+                    )
                 )
-                wind_hi, wind_lo = split2(wind)
-                mixed = jnp.dot(
-                    mixer,
-                    jnp.concatenate([wind_hi, wind_lo, wind_hi], axis=0),
-                    preferred_element_type=jnp.float32,
-                )
+            mixed = jnp.dot(mixer, jnp.concatenate(winds, axis=0), preferred_element_type=jnp.float32)
+            mixed = mixed[: 2 * lev_parts * levels] + mixed[2 * lev_parts * levels :]
+            for f in range(2):
                 for p in range(lev_parts):
+                    at = (f * lev_parts + p) * levels
                     for half in range(2):
-                        stage[b, p, f, half] = mixed[
-                            p * levels : (p + 1) * levels, half * HALF : (half + 1) * HALF
-                        ]
+                        stage[b, p, f, half] = mixed[at : at + levels, half * HALF : (half + 1) * HALF]
             copies.append(pltpu.make_async_copy(stage.at[b], out.at[b], sems.at[b]))
             copies[-1].start()
-
-    window = split_group(0, window)
+        return total
+
+    split_group(0)
     for g0 in range(0, count, GROUP):
         if g0 + GROUP < count:
-            window = split_group(g0 + GROUP, window)
-        finish_group(g0)
+            split_group(g0 + GROUP)
+        total = finish_group(g0, total)
     for copy in copies:
         copy.wait()
 
@@ -279,24 +302,31 @@
 
 def finish_kernel(step, base, out, added, stage, in_sems, out_sems):
     fields, levels, rows, _ = out.shape
+    blocks = levels // SUBLANES
     loads, copies = [], []
     for f in range(fields):
-        loads.append(pltpu.make_async_copy(base.at[:, f], added.at[f], in_sems.at[f]))
-        loads[-1].start()
+        for n in range(blocks):
+            some = pl.ds(n * SUBLANES, SUBLANES)
+            loads.append(
+                pltpu.make_async_copy(base.at[:, f, :, some], added.at[:, f, :, some], in_sems.at[f * blocks + n])
+            )
+            loads[-1].start()
     for f in range(fields):
-        loads[f].wait()
-        for l0 in range(0, levels, SUBLANES):
+        for n in range(blocks):
+            loads[f * blocks + n].wait()
+            l0 = n * SUBLANES
             some = slice(l0, l0 + SUBLANES)
             for half in range(2):
                 for j0 in range(0, rows, SUBLANES):
                     flipped = flip(
-                        [step[j0 + k, f, half, some, :] + added[f, j0 + k, half, some, :] for k in range(SUBLANES)]
+                        [step[j0 + k, f, half, some, :] + added[j0 + k, f, half, some, :] for k in range(SUBLANES)]
                     )
                     for i, value in enumerate(flipped):
                         stage[f, l0 + i, j0 : j0 + SUBLANES, half * HALF : (half + 1) * HALF] = value
-            at = f * (levels // SUBLANES) + l0 // SUBLANES
             some = pl.ds(l0, SUBLANES)
-            copies.append(pltpu.make_async_copy(stage.at[f, some], out.at[f, some], out_sems.at[at]))
+            copies.append(
+                pltpu.make_async_copy(stage.at[f, some], out.at[f, some], out_sems.at[f * blocks + n])
+            )
             copies[-1].start()
     for copy in copies:
         copy.wait()
@@ -312,14 +342,26 @@
     hbm = pl.BlockSpec(memory_space=pltpu.HBM)
     vmem = pl.BlockSpec(memory_space=pltpu.VMEM)
 
-    with jax.named_scope("outer_rows"):
-        last, first = pl.pallas_call(
-            outer_rows_kernel,
-            out_shape=(jax.ShapeDtypeStruct((chans, width), jnp.float32),) * 2,
-            in_specs=[vmem],
-            out_specs=(vmem, vmem),
-            compiler_params=params,
-        )(prognostic)
+    def in_hbm(x):
+        return pltpu.with_memory_space_constraint(x, pltpu.HBM)
+
+    def in_vmem(x):
+        return pltpu.with_memory_space_constraint(x, pltpu.VMEM)
+
+
+    with jax.named_scope("fetch"):
+        tile, last, first = pl.pallas_call(
+            fetch_kernel,
+            out_shape=(
+                pltpu.VMEM(prognostic.shape, jnp.float32),
+                pltpu.VMEM((chans, width), jnp.float32),
+                pltpu.VMEM((chans, width), jnp.float32),
+            ),
+            in_specs=[hbm],
+            out_specs=(vmem, vmem, vmem),
+            scratch_shapes=[pltpu.SemaphoreType.DMA((fields, LOADS))],
+            compiler_params=params,
+        )(in_hbm(prognostic))
     south = lax.ppermute(last, "lat", [(i, i + 1) for i in range(lat_devices - 1)])
     north = lax.ppermute(first, "lat", [(i + 1, i) for i in range(lat_devices - 1)])
     other = lax.ppermute(prognostic[:2], "lev", [(0, 1), (1, 0)])
@@ -335,8 +377,8 @@
         tend, ends = pl.pallas_call(
             tendency_kernel,
             out_shape=(
-                jax.ShapeDtypeStruct((rows, sent_rows, HALF), jnp.float32),
-                jax.ShapeDtypeStruct((2, halves * chans, HALF), jnp.float32),
+                pltpu.HBM((rows, sent_rows, HALF), jnp.float32),
+                pltpu.VMEM((2, halves * chans, HALF), jnp.float32),
             ),
             in_specs=[vmem, vmem, vmem],
             out_specs=(hbm, vmem),
@@ -347,18 +389,18 @@
                 pltpu.SemaphoreType.DMA((rows // SUBLANES,)),
             ],
             compiler_params=params,
-        )(prognostic, zonal_field, coriolis_field)
+        )(in_vmem(tile), zonal_field, coriolis_field)
 
     with jax.named_scope("seam_rows"):
         tend = pl.pallas_call(
             seam_kernel,
-            out_shape=jax.ShapeDtypeStruct(tend.shape, jnp.float32),
+            out_shape=pltpu.HBM(tend.shape, jnp.float32),
             in_specs=[vmem, vmem, vmem, hbm],
             out_specs=hbm,
             input_output_aliases={3: 0},
             scratch_shapes=[pltpu.VMEM(ends.shape, jnp.float32), pltpu.SemaphoreType.DMA((2,))],
             compiler_params=params,
-        )(ends, south, north, tend)
+        )(in_vmem(ends), in_vmem(south), in_vmem(north), in_hbm(tend))
 
     whole_rows = lax.all_to_all(tend, ("lon", "lev"), 0, 0, tiled=True)
 
@@ -369,7 +411,7 @@
     with jax.named_scope("row_filter"):
         stepped = pl.pallas_call(
             filter_kernel,
-            out_shape=jax.ShapeDtypeStruct(stepped_shape, jnp.float32),
+            out_shape=pltpu.HBM(stepped_shape, jnp.float32),
             grid_spec=pltpu.PrefetchScalarGridSpec(
                 num_scalar_prefetch=4,
                 grid=(1,),
@@ -377,7 +419,7 @@
                 out_specs=hbm,
                 scratch_shapes=[
                     pltpu.VMEM((count, both, HALF), jnp.float32),
-                    pltpu.VMEM((2, count * both, 2 * HALF), jnp.bfloat16),
+                    pltpu.VMEM((count * both, 2 * HALF), jnp.bfloat16),
                     pltpu.VMEM((HALF, HALF), jnp.float32),
                     pltpu.VMEM(column_inverse.shape[1:], jnp.float32),
                     pltpu.VMEM(stepped_shape, jnp.float32),
@@ -391,8 +433,8 @@
             half_width,
             filter_mask,
             zonal,
-            whole_rows.reshape(lon_devices, lev_devices, sent_rows, HALF),
-            column_inverse,
+            in_vmem(whole_rows.reshape(lon_devices, lev_devices, sent_rows, HALF)),
+            in_hbm(column_inverse),
         )
 
     returned = lax.all_to_all(
@@ -402,7 +444,7 @@
     with jax.named_scope("base"):
         base = pl.pallas_call(
             base_kernel,
-            out_shape=jax.ShapeDtypeStruct(returned.shape, jnp.float32),
+            out_shape=pltpu.HBM(returned.shape, jnp.float32),
             grid_spec=pltpu.PrefetchScalarGridSpec(
                 num_scalar_prefetch=1,
                 grid=(halves,),
@@ -423,13 +465,13 @@
             in_specs=[vmem, hbm],
             out_specs=hbm,
             scratch_shapes=[
-                pltpu.VMEM((fields, rows, halves, levels, HALF), jnp.float32),
+                pltpu.VMEM(returned.shape, jnp.float32),
                 pltpu.VMEM(prognostic.shape, jnp.float32),
-                pltpu.SemaphoreType.DMA((fields,)),
+                pltpu.SemaphoreType.DMA((fields * levels // SUBLANES,)),
                 pltpu.SemaphoreType.DMA((fields * levels // SUBLANES,)),
             ],
             compiler_params=params,
-        )(returned, base)
+        )(in_vmem(returned), in_hbm(base))
 
 
 def solution(mesh):

time: 88.5 us -> 82.8 us (0.936)
  local copies, waits for them, and re-layouts: 3.86 us -> 0.24 us
  waiting for transfers between devices: 49.7 us -> 48.6 us
    unnamed x14 -> x8, local copies, waits for them, and re-layouts: 3.61 us -> 0.03 us
  transfers between devices with their start and end apart: 5 -> 5, of which waited for: 4 -> 4; matrix products, arithmetic and copies ran while one was open for 0% -> 0% of each run, Pallas kernels for 5% -> 7%
where the time goes in v7:
time: 82.8 us; the launch traced here: 82.4 us
  waiting for transfers between devices  48.6 us (59%)
  starting transfers between devices  18.7 us (23%)
  Pallas kernels  14.6 us (18%)
    all_to_all x1, waiting for transfers between devices, per_device(): whole_rows = lax.all_to_all(tend, ('lon', 'lev'), 0, 0, tiled=True)  25.4 us
    all_to_all x1, waiting for transfers between devices, per_device(): lax.all_to_all(stepped.reshape((rows,) + stepped_shape[2:]), ('lon', 'lev...  18.6 us
    all_to_all x1, starting transfers between devices, per_device(): whole_rows = lax.all_to_all(tend, ('lon', 'lev'), 0, 0, tiled=True)  7.33 us
    ppermute x1, starting transfers between devices, per_device(): lax.ppermute(last, 'lat', [(i, i + 1) for i in range(lat_devices - 1)])  5.04 us
    pallas_call x1, Pallas kernels, per_device(): pl.pallas_call(filter_kernel, out_shape=pltpu.HBM(stepped_shape, jnp.floa...  4.79 us
    all_to_all x1, starting transfers between devices, per_device(): lax.all_to_all(stepped.reshape((rows,) + stepped_shape[2:]), ('lon', 'lev...  4.12 us
    pallas_call x1, Pallas kernels, per_device(): pl.pallas_call(tendency_kernel, out_shape=(pltpu.HBM((rows, sent_rows, HA...  2.87 us
    ppermute x1, waiting for transfers between devices, per_device(): other = lax.ppermute(prognostic[:2], 'lev', [(0, 1), (1, 0)])  2.5 us
  transfers between devices with their start and end apart: 5, of which 4 were waited for; matrix products, arithmetic and copies ran while one was open for 0% of the time, Pallas kernels for 7%

profile of v7, /device:TPU:96, one launch (start us, length us, event | category | flops | bytes accessed | tf_op | source)
XLA Modules:
  0.0 82.4 jit_solution(5947617185765338933)
XLA Ops:
  0.0 1.5 %fetch.1 = (f32[3,16,32,256]{3,2,1,0:T(8,128)S(1)}, f32[48,256]{1,0:T(8,128)S(1)}, f32[48,256]{1,0:T(8,128)S(1)}) custom-call(f32[3,16,32,256]{3,2,1,0:T(8,128)} %own.1), custom_call_target="tpu_custom_call" | custom-call | tf_op jit(solution)/shard_map/fetch/pallas_call | solution.py:353
  1.6 5.0 %collective-permute-start = (f32[48,256]{1,0:T(8,128)S(1)}, f32[48,256]{1,0:T(8,128)S(1)}, u32[]{:S(2)}, u32[]{:S(2)}) collective-permute-start(f32[48,256]{1,0:T(8,128)S(1)} %get-tuple-element.12), channel_id=1, source_target_pairs={{0,2},{2,4},{4,6},{6,8},{8,10},{10,12},{12,14},{1,3},{3,5},{5,7},{... | collective-permute-start | bytes 147464 | tf_op jit(solution)/shard_map/ppermute | solution.py:365
  6.6 1.9 %collective-permute-start.1 = (f32[48,256]{1,0:T(8,128)S(1)}, f32[48,256]{1,0:T(8,128)S(1)}, u32[]{:S(2)}, u32[]{:S(2)}) collective-permute-start(f32[48,256]{1,0:T(8,128)S(1)} %get-tuple-element.13), channel_id=1, source_target_pairs={{2,0},{4,2},{6,4},{8,6},{10,8},{12,10},{14,12},{3,1},{5,3},{7,5},{... | collective-permute-start | bytes 147464 | tf_op jit(solution)/shard_map/ppermute | solution.py:366
  8.6 0.1 broadcast_in_dim.4.zonal
  8.7 0.1 broadcast_in_dim.5.coriolis
  8.7 2.9 %tendencies.1 = (f32[32,104,128]{2,1,0:T(8,128)}, f32[2,96,128]{2,1,0:T(8,128)S(1)}) custom-call(f32[3,16,32,256]{3,2,1,0:T(8,128)S(1)} %get-tuple-element.10.prog, f32[32,256]{1,0:T(8,128)S(1)} %broadcast_in_dim.4.zonal, f32[32,256]{1,0:T(8,128)S(1)} %broadcast_in_dim.5.coriolis), custom_call_target="tpu_custom_call" | custom-call | tf_op jit(solution)/shard_map/tendencies/pallas_call | solution.py:377
  11.6 0.0 collective-permute-done.south
  11.6 2.2 %collective-permute-done.1.north = f32[48,256]{1,0:T(8,128)S(1)} collective-permute-done((f32[48,256]{1,0:T(8,128)S(1)}, f32[48,256]{1,0:T(8,128)S(1)}, u32[]{:S(2)}, u32[]{:S(2)}) %collective-permute-start.1) | collective-permute-done | bytes 49184 | tf_op jit(solution)/shard_map/ppermute | solution.py:366
  13.8 0.7 seam_rows.1
  14.5 0.0 copy-start.2
  14.5 0.0 copy-start.3
  14.5 7.3 %all-to-all-start = ((f32[32,104,128]{2,1,0:T(8,128)}), f32[32,104,128]{2,1,0:T(8,128)S(1)}, u32[]{:S(2)}, u32[]{:S(2)}) async-start(f32[32,104,128]{2,1,0:T(8,128)} %seam_rows.1), calls=%async_computation | async-start | bytes 3407872 | tf_op jit(solution)/shard_map/all_to_all | solution.py:405
  21.8 25.4 %all-to-all-done = f32[32,104,128]{2,1,0:T(8,128)S(1)} async-done(((f32[32,104,128]{2,1,0:T(8,128)}), f32[32,104,128]{2,1,0:T(8,128)S(1)}, u32[]{:S(2)}, u32[]{:S(2)}) %all-to-all-start) | async-done | bytes 1703968 | tf_op jit(solution)/shard_map/all_to_all | solution.py:405
  47.2 0.0 copy-done.2
  47.2 0.0 copy-done.3
  47.2 4.8 %row_filter.1 = f32[16,2,3,2,16,128]{5,4,3,2,1,0:T(8,128)} custom-call(s32[1]{0:T(128)} %bitcast.own_row, s32[32]{0:T(128)S(1)} %copy-done.2, s32[32]{0:T(128)S(1)} %copy-done.3, f32[32]{0:T(128)S(1)} %get-tuple-element.16.zonal, f32[16,2,104,128]{3,2,1,0:T(8,128)S(1)} %bitcast.4, f32[32,32,32]{2,1,0:T(8,128)} %matrix.1), custom_call_target="tpu_custom_call" | custom-call | tf_op jit(solution)/shard_map/row_filter/pallas_call | solution.py:412
  52.0 0.0 copy-start
  52.0 4.1 %all-to-all-start.1 = ((f32[32,3,2,16,128]{4,3,2,1,0:T(8,128)}), f32[32,3,2,16,128]{4,3,2,1,0:T(8,128)S(1)}, u32[]{:S(2)}, u32[]{:S(2)}) async-start(f32[32,3,2,16,128]{4,3,2,1,0:T(8,128)} %bitcast.5), calls=%async_computation.1 | async-start | bytes 3145728 | tf_op jit(solution)/shard_map/all_to_all | solution.py:440
  56.2 0.0 copy-done
  56.2 0.0 copy-start.1
  56.2 0.1 slice.3
  56.3 0.2 collective-permute-start.2
  56.5 2.5 %collective-permute-done.2.other = f32[2,16,32,256]{3,2,1,0:T(8,128)S(1)} collective-permute-done((f32[2,16,32,256]{3,2,1,0:T(8,128)S(1)}, f32[2,16,32,256]{3,2,1,0:T(8,128)S(1)}, u32[]{:S(2)}, u32[]{:S(2)}) %collective-permute-start.2) | collective-permute-done | bytes 1048608 | tf_op jit(solution)/shard_map/ppermute | solution.py:367
  59.0 0.0 copy-done.1
  59.0 2.5 %base.1 = f32[32,3,2,16,128]{4,3,2,1,0:T(8,128)} custom-call(s32[1]{0:T(128)} %bitcast.3.own_part, f32[3,16,32,256]{3,2,1,0:T(8,128)S(1)} %copy-done, f32[2,16,32,256]{3,2,1,0:T(8,128)S(1)} %collective-permute-done.2.other, f32[32,32,32]{2,1,0:T(8,128)S(1)} %copy-done.1), custom_call_target="tpu_custom_call" | custom-call | tf_op jit(solution)/shard_map/base/pallas_call | solution.py:445
  61.5 18.6 %all-to-all-done.1.step = f32[32,3,2,16,128]{4,3,2,1,0:T(8,128)S(1)} async-done(((f32[32,3,2,16,128]{4,3,2,1,0:T(8,128)}), f32[32,3,2,16,128]{4,3,2,1,0:T(8,128)S(1)}, u32[]{:S(2)}, u32[]{:S(2)}) %all-to-all-start.1) | async-done | bytes 1572896 | tf_op jit(solution)/shard_map/all_to_all | solution.py:440
  80.1 2.3 %finish.1 = f32[3,16,32,256]{3,2,1,0:T(8,128)} custom-call(f32[32,3,2,16,128]{4,3,2,1,0:T(8,128)S(1)} %all-to-all-done.1.step, f32[32,3,2,16,128]{4,3,2,1,0:T(8,128)} %base.1), custom_call_target="tpu_custom_call" | custom-call | tf_op jit(solution)/shard_map/finish/pallas_call | solution.py:462
  (1 shorter events, 0.0 us)
Async XLA Ops:
  1.6 10.1 %collective-permute-start = (f32[48,256]{1,0:T(8,128)S(1)}, f32[48,256]{1,0:T(8,128)S(1)}, u32[]{:S(2)}, u32[]{:S(2)}) collective-permute-start(f32[48,256]{1,0:T(8,128)S(1)} %get-tuple-element.12), channel_id=1, source_target_pairs={{0,2},{2,4},{4,6},{6,8},{8,10},{10,12},{12,14},{1,3},{3,5},{5,7},{... | collective-permute-start | bytes 147464 | tf_op jit(solution)/shard_map/ppermute | solution.py:365
  6.6 7.2 %collective-permute-start.1 = (f32[48,256]{1,0:T(8,128)S(1)}, f32[48,256]{1,0:T(8,128)S(1)}, u32[]{:S(2)}, u32[]{:S(2)}) collective-permute-start(f32[48,256]{1,0:T(8,128)S(1)} %get-tuple-element.13), channel_id=1, source_target_pairs={{2,0},{4,2},{6,4},{8,6},{10,8},{12,10},{14,12},{3,1},{5,3},{7,5},{... | collective-permute-start | bytes 147464 | tf_op jit(solution)/shard_map/ppermute | solution.py:366
  14.5 32.8 %copy-start.2 = (s32[32]{0:T(128)S(1)}, s32[32]{0:T(128)}, u32[]{:S(2)}) copy-start(s32[32]{0:T(128)} %half_width.1) | copy-start | bytes 388
  14.5 32.8 %copy-start.3 = (s32[32]{0:T(128)S(1)}, s32[32]{0:T(128)}, u32[]{:S(2)}) copy-start(s32[32]{0:T(128)} %filter_mask.1) | copy-start | bytes 388
  14.5 32.7 %all-to-all-start = ((f32[32,104,128]{2,1,0:T(8,128)}), f32[32,104,128]{2,1,0:T(8,128)S(1)}, u32[]{:S(2)}, u32[]{:S(2)}) async-start(f32[32,104,128]{2,1,0:T(8,128)} %seam_rows.1), calls=%async_computation | async-start | bytes 3407872 | tf_op jit(solution)/shard_map/all_to_all | solution.py:405
  52.0 4.1 %copy-start = (f32[3,16,32,256]{3,2,1,0:T(8,128)S(1)}, f32[3,16,32,256]{3,2,1,0:T(8,128)}, u32[]{:S(2)}) copy-start(f32[3,16,32,256]{3,2,1,0:T(8,128)} %own.1) | copy-start | bytes 4718596
  52.0 28.1 %all-to-all-start.1 = ((f32[32,3,2,16,128]{4,3,2,1,0:T(8,128)}), f32[32,3,2,16,128]{4,3,2,1,0:T(8,128)S(1)}, u32[]{:S(2)}, u32[]{:S(2)}) async-start(f32[32,3,2,16,128]{4,3,2,1,0:T(8,128)} %bitcast.5), calls=%async_computation.1 | async-start | bytes 3145728 | tf_op jit(solution)/shard_map/all_to_all | solution.py:440
  56.2 2.8 %copy-start.1 = (f32[32,32,32]{2,1,0:T(8,128)S(1)}, f32[32,32,32]{2,1,0:T(8,128)}, u32[]{:S(2)}) copy-start(f32[32,32,32]{2,1,0:T(8,128)} %matrix.1) | copy-start | bytes 393220
  56.3 2.7 %collective-permute-start.2 = (f32[2,16,32,256]{3,2,1,0:T(8,128)S(1)}, f32[2,16,32,256]{3,2,1,0:T(8,128)S(1)}, u32[]{:S(2)}, u32[]{:S(2)}) collective-permute-start(f32[2,16,32,256]{3,2,1,0:T(8,128)S(1)} %slice.3), channel_id=1, source_target_pairs={{0,1},{1,0},{2,3},{3,2},{4,5},{5,4},{6,7},{7,6},{8,9},{9,8},{10,11... | collective-permute-start | bytes 3145736 | tf_op jit(solution)/shard_map/ppermute | solution.py:367

commit v8 on v7

--- a/solution.py
+++ b/solution.py
@@ -162,7 +162,7 @@
 def filter_kernel(
     own_row, half_width, filter_mask, zonal, tend, matrices, out, halves, parts, seam, matrix, stage, matrix_sem, sems
 ):
-    blocks, lev_parts, levels = out.shape[0], out.shape[1], out.shape[4]
+    lev_parts, blocks, levels = out.shape[0], out.shape[1], out.shape[4]
     chans = 3 * levels
     payload = 2 * chans
     count = 2 * blocks
@@ -179,7 +179,7 @@
     for b in range(blocks):
         for part in range(lev_parts):
             at = b * lev_parts + part
-            seam[at : at + 1, :] = tend[b, part, payload : payload + 1, :]
+            seam[at : at + 1, :] = tend[part, b, payload : payload + 1, :]
     columns = seam[...].T
     zon = zonal[row]
     u, v, h = (columns[f * levels : (f + 1) * levels] for f in range(3))
@@ -196,7 +196,7 @@
         for part in range(lev_parts):
             source = beyond * lev_parts + part
             for f in range(3):
-                here = tend[b, part, (2 * f + half) * levels : (2 * f + half + 1) * levels, :]
+                here = tend[part, b, (2 * f + half) * levels : (2 * f + half + 1) * levels, :]
                 term = terms[f * levels : (f + 1) * levels, source : source + 1]
                 pieces.append(here + jnp.where(lane_id == lane, term, 0.0))
         value = jnp.concatenate(pieces, axis=0)
@@ -237,7 +237,7 @@
                 total = total + box[at : at + both, HALF:]
                 step = jnp.where(filtered, smooth, TIME_STEP * halves[g])
                 for p in range(lev_parts):
-                    stage[b, p, 2, half] = step[p * chans + 2 * levels : (p + 1) * chans]
+                    stage[p, b, 2, half] = step[p * chans + 2 * levels : (p + 1) * chans]
                 steps.append(step)
             step = jnp.concatenate(steps, axis=1)
             winds = []
@@ -254,8 +254,8 @@
                 for p in range(lev_parts):
                     at = (f * lev_parts + p) * levels
                     for half in range(2):
-                        stage[b, p, f, half] = mixed[at : at + levels, half * HALF : (half + 1) * HALF]
-            copies.append(pltpu.make_async_copy(stage.at[b], out.at[b], sems.at[b]))
+                        stage[p, b, f, half] = mixed[at : at + levels, half * HALF : (half + 1) * HALF]
+            copies.append(pltpu.make_async_copy(stage.at[:, b], out.at[:, b], sems.at[b]))
             copies[-1].start()
         return total
 
@@ -402,10 +402,10 @@
             compiler_params=params,
         )(in_vmem(ends), in_vmem(south), in_vmem(north), in_hbm(tend))
 
-    whole_rows = lax.all_to_all(tend, ("lon", "lev"), 0, 0, tiled=True)
-
-    own_row = (lon_index * lev_devices + lev_index).astype(jnp.int32).reshape(1)
-    stepped_shape = (lon_devices, lev_devices, fields, halves, levels, HALF)
+    whole_rows = lax.all_to_all(tend, ("lev", "lon"), 0, 0, tiled=True)
+
+    own_row = (lev_index * lon_devices + lon_index).astype(jnp.int32).reshape(1)
+    stepped_shape = (lev_devices, lon_devices, fields, halves, levels, HALF)
     count = halves * lon_devices
     both = lev_devices * chans
     with jax.named_scope("row_filter"):
@@ -433,12 +433,12 @@
             half_width,
             filter_mask,
             zonal,
-            in_vmem(whole_rows.reshape(lon_devices, lev_devices, sent_rows, HALF)),
+            in_vmem(whole_rows.reshape(lev_devices, lon_devices, sent_rows, HALF)),
             in_hbm(column_inverse),
         )
 
     returned = lax.all_to_all(
-        stepped.reshape((rows,) + stepped_shape[2:]), ("lon", "lev"), 0, 0, tiled=True
+        stepped.reshape((rows,) + stepped_shape[2:]), ("lev", "lon"), 0, 0, tiled=True
     )
 
     with jax.named_scope("base"):

time: 82.8 us -> 81.6 us (0.986)
  waiting for transfers between devices: 48.6 us -> 47.4 us
    all_to_all x2, waiting for transfers between devices: 44 us -> 42.8 us  [the longest x1 24.8 us: per_device(): whole_rows = lax.all_to_all(tend, ('lev', 'lon'), 0, 0, tiled=True)]
where the time goes in v8:
time: 81.6 us; the launch traced here: 81.2 us
  waiting for transfers between devices  47.4 us (58%)
  starting transfers between devices  18.8 us (23%)
  Pallas kernels  14.6 us (18%)
    all_to_all x1, waiting for transfers between devices, per_device(): whole_rows = lax.all_to_all(tend, ('lev', 'lon'), 0, 0, tiled=True)  24.8 us
    all_to_all x1, waiting for transfers between devices, per_device(): lax.all_to_all(stepped.reshape((rows,) + stepped_shape[2:]), ('lev', 'lon...  18 us
    all_to_all x1, starting transfers between devices, per_device(): whole_rows = lax.all_to_all(tend, ('lev', 'lon'), 0, 0, tiled=True)  7.33 us
    ppermute x1, starting transfers between devices, per_device(): lax.ppermute(last, 'lat', [(i, i + 1) for i in range(lat_devices - 1)])  5.04 us
    pallas_call x1, Pallas kernels, per_device(): pl.pallas_call(filter_kernel, out_shape=pltpu.HBM(stepped_shape, jnp.floa...  4.8 us
    all_to_all x1, starting transfers between devices, per_device(): lax.all_to_all(stepped.reshape((rows,) + stepped_shape[2:]), ('lev', 'lon...  4.12 us
    pallas_call x1, Pallas kernels, per_device(): pl.pallas_call(tendency_kernel, out_shape=(pltpu.HBM((rows, sent_rows, HA...  2.87 us
    pallas_call x1, Pallas kernels, per_device(): pl.pallas_call(base_kernel, out_shape=pltpu.HBM(returned.shape, jnp.float...  2.5 us
  transfers between devices with their start and end apart: 5, of which 4 were waited for; matrix products, arithmetic and copies ran while one was open for 0% of the time, Pallas kernels for 7%

profile of v8, /device:TPU:96, one launch (start us, length us, event | category | flops | bytes accessed | tf_op | source)
XLA Modules:
  0.0 81.2 jit_solution(16991460382267723483)
XLA Ops:
  0.0 1.5 %fetch.1 = (f32[3,16,32,256]{3,2,1,0:T(8,128)S(1)}, f32[48,256]{1,0:T(8,128)S(1)}, f32[48,256]{1,0:T(8,128)S(1)}) custom-call(f32[3,16,32,256]{3,2,1,0:T(8,128)} %own.1), custom_call_target="tpu_custom_call" | custom-call | tf_op jit(solution)/shard_map/fetch/pallas_call | solution.py:353
  1.6 5.0 %collective-permute-start = (f32[48,256]{1,0:T(8,128)S(1)}, f32[48,256]{1,0:T(8,128)S(1)}, u32[]{:S(2)}, u32[]{:S(2)}) collective-permute-start(f32[48,256]{1,0:T(8,128)S(1)} %get-tuple-element.12), channel_id=1, source_target_pairs={{0,2},{2,4},{4,6},{6,8},{8,10},{10,12},{12,14},{1,3},{3,5},{5,7},{... | collective-permute-start | bytes 147464 | tf_op jit(solution)/shard_map/ppermute | solution.py:365
  6.6 1.9 %collective-permute-start.1 = (f32[48,256]{1,0:T(8,128)S(1)}, f32[48,256]{1,0:T(8,128)S(1)}, u32[]{:S(2)}, u32[]{:S(2)}) collective-permute-start(f32[48,256]{1,0:T(8,128)S(1)} %get-tuple-element.13), channel_id=1, source_target_pairs={{2,0},{4,2},{6,4},{8,6},{10,8},{12,10},{14,12},{3,1},{5,3},{7,5},{... | collective-permute-start | bytes 147464 | tf_op jit(solution)/shard_map/ppermute | solution.py:366
  8.6 0.1 broadcast_in_dim.4.zonal
  8.7 0.1 broadcast_in_dim.5.coriolis
  8.7 2.9 %tendencies.1 = (f32[32,104,128]{2,1,0:T(8,128)}, f32[2,96,128]{2,1,0:T(8,128)S(1)}) custom-call(f32[3,16,32,256]{3,2,1,0:T(8,128)S(1)} %get-tuple-element.10.prog, f32[32,256]{1,0:T(8,128)S(1)} %broadcast_in_dim.4.zonal, f32[32,256]{1,0:T(8,128)S(1)} %broadcast_in_dim.5.coriolis), custom_call_target="tpu_custom_call" | custom-call | tf_op jit(solution)/shard_map/tendencies/pallas_call | solution.py:377
  11.6 0.0 collective-permute-done.south
  11.6 2.2 %collective-permute-done.1.north = f32[48,256]{1,0:T(8,128)S(1)} collective-permute-done((f32[48,256]{1,0:T(8,128)S(1)}, f32[48,256]{1,0:T(8,128)S(1)}, u32[]{:S(2)}, u32[]{:S(2)}) %collective-permute-start.1) | collective-permute-done | bytes 49184 | tf_op jit(solution)/shard_map/ppermute | solution.py:366
  13.8 0.7 seam_rows.1
  14.5 0.0 copy-start.2
  14.5 0.0 copy-start.3
  14.5 7.3 %all-to-all-start = ((f32[32,104,128]{2,1,0:T(8,128)}), f32[32,104,128]{2,1,0:T(8,128)S(1)}, u32[]{:S(2)}, u32[]{:S(2)}) async-start(f32[32,104,128]{2,1,0:T(8,128)} %seam_rows.1), calls=%async_computation | async-start | bytes 3407872 | tf_op jit(solution)/shard_map/all_to_all | solution.py:405
  21.8 24.8 %all-to-all-done = f32[32,104,128]{2,1,0:T(8,128)S(1)} async-done(((f32[32,104,128]{2,1,0:T(8,128)}), f32[32,104,128]{2,1,0:T(8,128)S(1)}, u32[]{:S(2)}, u32[]{:S(2)}) %all-to-all-start) | async-done | bytes 1703968 | tf_op jit(solution)/shard_map/all_to_all | solution.py:405
  46.6 0.0 copy-done.2
  46.6 0.0 copy-done.3
  46.6 4.8 %row_filter.1 = f32[2,16,3,2,16,128]{5,4,3,2,1,0:T(8,128)} custom-call(s32[1]{0:T(128)} %bitcast.own_row, s32[32]{0:T(128)S(1)} %copy-done.2, s32[32]{0:T(128)S(1)} %copy-done.3, f32[32]{0:T(128)S(1)} %get-tuple-element.16.zonal, f32[2,16,104,128]{3,2,1,0:T(8,128)S(1)} %bitcast.4, f32[32,32,32]{2,1,0:T(8,128)} %matrix.1), custom_call_target="tpu_custom_call" | custom-call | tf_op jit(solution)/shard_map/row_filter/pallas_call | solution.py:412
  51.4 0.0 copy-start
  51.4 4.1 %all-to-all-start.1 = ((f32[32,3,2,16,128]{4,3,2,1,0:T(8,128)}), f32[32,3,2,16,128]{4,3,2,1,0:T(8,128)S(1)}, u32[]{:S(2)}, u32[]{:S(2)}) async-start(f32[32,3,2,16,128]{4,3,2,1,0:T(8,128)} %bitcast.5), calls=%async_computation.1 | async-start | bytes 3145728 | tf_op jit(solution)/shard_map/all_to_all | solution.py:440
  55.6 0.0 copy-done
  55.6 0.0 copy-start.1
  55.6 0.1 slice.3
  55.7 0.4 collective-permute-start.2
  56.0 2.4 %collective-permute-done.2.other = f32[2,16,32,256]{3,2,1,0:T(8,128)S(1)} collective-permute-done((f32[2,16,32,256]{3,2,1,0:T(8,128)S(1)}, f32[2,16,32,256]{3,2,1,0:T(8,128)S(1)}, u32[]{:S(2)}, u32[]{:S(2)}) %collective-permute-start.2) | collective-permute-done | bytes 1048608 | tf_op jit(solution)/shard_map/ppermute | solution.py:367
  58.4 0.0 copy-done.1
  58.4 2.5 %base.1 = f32[32,3,2,16,128]{4,3,2,1,0:T(8,128)} custom-call(s32[1]{0:T(128)} %bitcast.3.own_part, f32[3,16,32,256]{3,2,1,0:T(8,128)S(1)} %copy-done, f32[2,16,32,256]{3,2,1,0:T(8,128)S(1)} %collective-permute-done.2.other, f32[32,32,32]{2,1,0:T(8,128)S(1)} %copy-done.1), custom_call_target="tpu_custom_call" | custom-call | tf_op jit(solution)/shard_map/base/pallas_call | solution.py:445
  60.9 18.0 %all-to-all-done.1.step = f32[32,3,2,16,128]{4,3,2,1,0:T(8,128)S(1)} async-done(((f32[32,3,2,16,128]{4,3,2,1,0:T(8,128)}), f32[32,3,2,16,128]{4,3,2,1,0:T(8,128)S(1)}, u32[]{:S(2)}, u32[]{:S(2)}) %all-to-all-start.1) | async-done | bytes 1572896 | tf_op jit(solution)/shard_map/all_to_all | solution.py:440
  78.9 2.3 %finish.1 = f32[3,16,32,256]{3,2,1,0:T(8,128)} custom-call(f32[32,3,2,16,128]{4,3,2,1,0:T(8,128)S(1)} %all-to-all-done.1.step, f32[32,3,2,16,128]{4,3,2,1,0:T(8,128)} %base.1), custom_call_target="tpu_custom_call" | custom-call | tf_op jit(solution)/shard_map/finish/pallas_call | solution.py:462
  (1 shorter events, 0.0 us)
Async XLA Ops:
  1.6 10.1 %collective-permute-start = (f32[48,256]{1,0:T(8,128)S(1)}, f32[48,256]{1,0:T(8,128)S(1)}, u32[]{:S(2)}, u32[]{:S(2)}) collective-permute-start(f32[48,256]{1,0:T(8,128)S(1)} %get-tuple-element.12), channel_id=1, source_target_pairs={{0,2},{2,4},{4,6},{6,8},{8,10},{10,12},{12,14},{1,3},{3,5},{5,7},{... | collective-permute-start | bytes 147464 | tf_op jit(solution)/shard_map/ppermute | solution.py:365
  6.6 7.2 %collective-permute-start.1 = (f32[48,256]{1,0:T(8,128)S(1)}, f32[48,256]{1,0:T(8,128)S(1)}, u32[]{:S(2)}, u32[]{:S(2)}) collective-permute-start(f32[48,256]{1,0:T(8,128)S(1)} %get-tuple-element.13), channel_id=1, source_target_pairs={{2,0},{4,2},{6,4},{8,6},{10,8},{12,10},{14,12},{3,1},{5,3},{7,5},{... | collective-permute-start | bytes 147464 | tf_op jit(solution)/shard_map/ppermute | solution.py:366
  14.5 32.2 %copy-start.2 = (s32[32]{0:T(128)S(1)}, s32[32]{0:T(128)}, u32[]{:S(2)}) copy-start(s32[32]{0:T(128)} %half_width.1) | copy-start | bytes 388
  14.5 32.1 %copy-start.3 = (s32[32]{0:T(128)S(1)}, s32[32]{0:T(128)}, u32[]{:S(2)}) copy-start(s32[32]{0:T(128)} %filter_mask.1) | copy-start | bytes 388
  14.5 32.1 %all-to-all-start = ((f32[32,104,128]{2,1,0:T(8,128)}), f32[32,104,128]{2,1,0:T(8,128)S(1)}, u32[]{:S(2)}, u32[]{:S(2)}) async-start(f32[32,104,128]{2,1,0:T(8,128)} %seam_rows.1), calls=%async_computation | async-start | bytes 3407872 | tf_op jit(solution)/shard_map/all_to_all | solution.py:405
  51.4 4.1 %copy-start = (f32[3,16,32,256]{3,2,1,0:T(8,128)S(1)}, f32[3,16,32,256]{3,2,1,0:T(8,128)}, u32[]{:S(2)}) copy-start(f32[3,16,32,256]{3,2,1,0:T(8,128)} %own.1) | copy-start | bytes 4718596
  51.4 27.5 %all-to-all-start.1 = ((f32[32,3,2,16,128]{4,3,2,1,0:T(8,128)}), f32[32,3,2,16,128]{4,3,2,1,0:T(8,128)S(1)}, u32[]{:S(2)}, u32[]{:S(2)}) async-start(f32[32,3,2,16,128]{4,3,2,1,0:T(8,128)} %bitcast.5), calls=%async_computation.1 | async-start | bytes 3145728 | tf_op jit(solution)/shard_map/all_to_all | solution.py:440
  55.6 2.8 %copy-start.1 = (f32[32,32,32]{2,1,0:T(8,128)S(1)}, f32[32,32,32]{2,1,0:T(8,128)}, u32[]{:S(2)}) copy-start(f32[32,32,32]{2,1,0:T(8,128)} %matrix.1) | copy-start | bytes 393220
  55.7 2.7 %collective-permute-start.2 = (f32[2,16,32,256]{3,2,1,0:T(8,128)S(1)}, f32[2,16,32,256]{3,2,1,0:T(8,128)S(1)}, u32[]{:S(2)}, u32[]{:S(2)}) collective-permute-start(f32[2,16,32,256]{3,2,1,0:T(8,128)S(1)} %slice.3), channel_id=1, source_target_pairs={{0,1},{1,0},{2,3},{3,2},{4,5},{5,4},{6,7},{7,6},{8,9},{9,8},{10,11... | collective-permute-start | bytes 3145736 | tf_op jit(solution)/shard_map/ppermute | solution.py:367

commit v9 on v8

--- a/solution.py
+++ b/solution.py
@@ -34,28 +34,37 @@
     return tiles
 
 
-def fetch_kernel(prog, tile, last, first, sems):
+def outer_rows_kernel(prog, first, last, tiles, sems):
     fields, levels, rows, _ = prog.shape
-    per_load = levels // LOADS
     loads = []
     for f in range(fields):
-        for load in range(LOADS):
-            some = pl.ds(load * per_load, per_load)
-            loads.append(pltpu.make_async_copy(prog.at[f, some], tile.at[f, some], sems.at[f, load]))
+        for n, start in enumerate((rows - SUBLANES, 0)):
+            some = pl.ds(start, SUBLANES)
+            loads.append(pltpu.make_async_copy(prog.at[f, :, some], tiles.at[n, f], sems.at[f, n]))
             loads[-1].start()
     for f in range(fields):
-        for l in range(levels):
-            if l % per_load == 0:
-                loads[f * LOADS + l // per_load].wait()
-            c = f * levels + l
-            last[c : c + 1, :] = tile[f, l, rows - 1 : rows, :]
-            first[c : c + 1, :] = tile[f, l, 0:1, :]
-
-
-def tendency_kernel(prog, zonal, coriolis, out, ends, turn, edges, stage, out_sems):
+        for n, (row, out) in enumerate(((SUBLANES - 1, last), (0, first))):
+            loads[2 * f + n].wait()
+            for l in range(levels):
+                out[f * levels + l : f * levels + l + 1, :] = tiles[n, f, l, row : row + 1, :]
+
+
+def tendency_kernel(prog, zonal, coriolis, out, ends, tile, turn, stage, in_sems, out_sems):
     _, levels, rows, width = prog.shape
     chans = 3 * levels
     payload = 2 * chans
+    per_load = levels // LOADS
+    loads, copies = [], []
+    for load in range(LOADS):
+        some = pl.ds(load * per_load, per_load)
+        loads.append(pltpu.make_async_copy(prog.at[:, some], tile.at[:, some], in_sems.at[load]))
+        loads[-1].start()
+
+    def send(first, sem):
+        some = pl.ds(first, SUBLANES)
+        copies.append(pltpu.make_async_copy(stage.at[:, some], out.at[:, some], out_sems.at[sem]))
+        copies[-1].start()
+
     row_id = lax.broadcasted_iota(jnp.int32, (rows, width), 0)
     col_id = lax.broadcasted_iota(jnp.int32, (rows, width), 1)
     lane_id = lax.broadcasted_iota(jnp.int32, (rows, HALF), 1)
@@ -64,10 +73,12 @@
     zon, cor = zonal[...], coriolis[...]
     edge_rows = jnp.zeros((rows, HALF), jnp.float32)
     for l in range(levels):
+        if l % per_load == 0:
+            loads[l // per_load].wait()
         centre, dx, dy, sx = [], [], [], []
         for f in range(3):
             c = f * levels + l
-            here = prog[f, l]
+            here = tile[f, l]
             e = jnp.where(last_col, 0.0, pltpu.roll(here, width - 1, 1))
             w = jnp.where(first_col, 0.0, pltpu.roll(here, 1, 1))
             n = jnp.where(last_row, 0.0, pltpu.roll(here, rows - 1, 0))
@@ -89,33 +100,33 @@
         )
         for f in range(3):
             turn[f, l] = tends[f]
-    edges[...] = edge_rows
-    copies = []
-    for chunk in range(rows // SUBLANES):
-        some = slice(chunk * SUBLANES, (chunk + 1) * SUBLANES)
+        if (l + 1) % SUBLANES:
+            continue
+        l0 = l + 1 - SUBLANES
         for f in range(3):
             for half in range(2):
-                for l0 in range(0, levels, SUBLANES):
-                    at = (2 * f + half) * levels + l0
+                at = (2 * f + half) * levels + l0
+                for j0 in range(0, rows, SUBLANES):
                     flipped = flip(
-                        [turn[f, l0 + i, some, half * HALF : (half + 1) * HALF] for i in range(SUBLANES)]
+                        [
+                            turn[f, l0 + i, j0 : j0 + SUBLANES, half * HALF : (half + 1) * HALF]
+                            for i in range(SUBLANES)
+                        ]
                     )
                     for k, value in enumerate(flipped):
-                        j = chunk * SUBLANES + k
+                        j = j0 + k
                         stage[j, at : at + SUBLANES, :] = value
                         if j in (0, rows - 1):
                             ends[min(j, 1), at : at + SUBLANES, :] = value
-        for k in range(SUBLANES):
-            j = chunk * SUBLANES + k
-            stage[j, payload:, :] = jnp.broadcast_to(edges[j : j + 1, :], (SUBLANES, HALF))
-        some = pl.ds(chunk * SUBLANES, SUBLANES)
-        copies.append(pltpu.make_async_copy(stage.at[some], out.at[some], out_sems.at[chunk]))
-        copies[-1].start()
+                send(at, at // SUBLANES)
+    for j in range(rows):
+        stage[j, payload:, :] = jnp.broadcast_to(edge_rows[j : j + 1, :], (SUBLANES, HALF))
+    send(payload, payload // SUBLANES)
     for copy in copies:
         copy.wait()
 
 
-def seam_kernel(ends, south, north, tend, out, stage, sems):
+def seam_kernel(ends, north, south, tend, out, stage, sems):
     del tend
     chans = south.shape[0]
     levels = chans // 3
@@ -349,21 +360,20 @@
         return pltpu.with_memory_space_constraint(x, pltpu.VMEM)
 
 
-    with jax.named_scope("fetch"):
-        tile, last, first = pl.pallas_call(
-            fetch_kernel,
-            out_shape=(
-                pltpu.VMEM(prognostic.shape, jnp.float32),
-                pltpu.VMEM((chans, width), jnp.float32),
-                pltpu.VMEM((chans, width), jnp.float32),
-            ),
+    with jax.named_scope("outer_rows"):
+        first, last = pl.pallas_call(
+            outer_rows_kernel,
+            out_shape=(pltpu.VMEM((chans, width), jnp.float32),) * 2,
             in_specs=[hbm],
-            out_specs=(vmem, vmem, vmem),
-            scratch_shapes=[pltpu.SemaphoreType.DMA((fields, LOADS))],
+            out_specs=(vmem, vmem),
+            scratch_shapes=[
+                pltpu.VMEM((2, fields, levels, SUBLANES, width), jnp.float32),
+                pltpu.SemaphoreType.DMA((fields, 2)),
+            ],
             compiler_params=params,
         )(in_hbm(prognostic))
+    north = lax.ppermute(first, "lat", [(i + 1, i) for i in range(lat_devices - 1)])
     south = lax.ppermute(last, "lat", [(i, i + 1) for i in range(lat_devices - 1)])
-    north = lax.ppermute(first, "lat", [(i + 1, i) for i in range(lat_devices - 1)])
     other = lax.ppermute(prognostic[:2], "lev", [(0, 1), (1, 0)])
 
     global_rows = (lat_index * rows + jnp.arange(rows)).astype(jnp.float32)
@@ -380,16 +390,17 @@
                 pltpu.HBM((rows, sent_rows, HALF), jnp.float32),
                 pltpu.VMEM((2, halves * chans, HALF), jnp.float32),
             ),
-            in_specs=[vmem, vmem, vmem],
+            in_specs=[hbm, vmem, vmem],
             out_specs=(hbm, vmem),
             scratch_shapes=[
                 pltpu.VMEM(prognostic.shape, jnp.float32),
-                pltpu.VMEM((rows, HALF), jnp.float32),
+                pltpu.VMEM(prognostic.shape, jnp.float32),
                 pltpu.VMEM((rows, sent_rows, HALF), jnp.float32),
-                pltpu.SemaphoreType.DMA((rows // SUBLANES,)),
+                pltpu.SemaphoreType.DMA((LOADS,)),
+                pltpu.SemaphoreType.DMA((sent_rows // SUBLANES,)),
             ],
             compiler_params=params,
-        )(in_vmem(tile), zonal_field, coriolis_field)
+        )(in_hbm(prognostic), in_vmem(zonal_field), in_vmem(coriolis_field))
 
     with jax.named_scope("seam_rows"):
         tend = pl.pallas_call(
@@ -400,7 +411,7 @@
             input_output_aliases={3: 0},
             scratch_shapes=[pltpu.VMEM(ends.shape, jnp.float32), pltpu.SemaphoreType.DMA((2,))],
             compiler_params=params,
-        )(in_vmem(ends), in_vmem(south), in_vmem(north), in_hbm(tend))
+        )(in_vmem(ends), in_vmem(north), in_vmem(south), in_hbm(tend))
 
     whole_rows = lax.all_to_all(tend, ("lev", "lon"), 0, 0, tiled=True)
 

time: 81.6 us -> 80.2 us (0.983)
  waiting for transfers between devices: 47.4 us -> 45.2 us
    ppermute x1, waiting for transfers between devices: 2.17 us -> 0.01 us  [per_device(): lax.ppermute(first, 'lat', [(i + 1, i) for i in range(lat_devices - 1)])]
    pallas_call x1, Pallas kernels: 2.87 us -> 3.83 us  [per_device(): pl.pallas_call(tendency_kernel, out_shape=(pltpu.HBM((rows, sent_rows, HA...]
  transfers between devices with their start and end apart: 5 -> 5, of which waited for: 4 -> 3; matrix products, arithmetic and copies ran while one was open for 0% -> 0% of each run, Pallas kernels for 7% -> 8%
where the time goes in v9:
time: 80.2 us; the launch traced here: 79.8 us
  waiting for transfers between devices  45.2 us (56%)
  starting transfers between devices  18.9 us (24%)
  Pallas kernels  15.3 us (19%)
    all_to_all x1, waiting for transfers between devices, per_device(): whole_rows = lax.all_to_all(tend, ('lev', 'lon'), 0, 0, tiled=True)  24.8 us
    all_to_all x1, waiting for transfers between devices, per_device(): lax.all_to_all(stepped.reshape((rows,) + stepped_shape[2:]), ('lev', 'lon...  18 us
    all_to_all x1, starting transfers between devices, per_device(): whole_rows = lax.all_to_all(tend, ('lev', 'lon'), 0, 0, tiled=True)  7.33 us
    ppermute x1, starting transfers between devices, per_device(): lax.ppermute(last, 'lat', [(i, i + 1) for i in range(lat_devices - 1)])  5.04 us
    pallas_call x1, Pallas kernels, per_device(): pl.pallas_call(filter_kernel, out_shape=pltpu.HBM(stepped_shape, jnp.floa...  4.79 us
    all_to_all x1, starting transfers between devices, per_device(): lax.all_to_all(stepped.reshape((rows,) + stepped_shape[2:]), ('lev', 'lon...  4.12 us
    pallas_call x1, Pallas kernels, per_device(): pl.pallas_call(tendency_kernel, out_shape=(pltpu.HBM((rows, sent_rows, HA...  3.83 us
    pallas_call x1, Pallas kernels, per_device(): pl.pallas_call(base_kernel, out_shape=pltpu.HBM(returned.shape, jnp.float...  2.5 us
  transfers between devices with their start and end apart: 5, of which 3 were waited for; matrix products, arithmetic and copies ran while one was open for 0% of the time, Pallas kernels for 8%

profile of v9, /device:TPU:96, one launch (start us, length us, event | category | flops | bytes accessed | tf_op | source)
XLA Modules:
  0.0 79.8 jit_solution(14515213750276607299)
XLA Ops:
  0.0 1.3 %outer_rows.1 = (f32[48,256]{1,0:T(8,128)S(1)}, f32[48,256]{1,0:T(8,128)S(1)}) custom-call(f32[3,16,32,256]{3,2,1,0:T(8,128)} %own.1), custom_call_target="tpu_custom_call" | custom-call | tf_op jit(solution)/shard_map/outer_rows/pallas_call | solution.py:364
  1.3 2.0 %collective-permute-start = (f32[48,256]{1,0:T(8,128)S(1)}, f32[48,256]{1,0:T(8,128)S(1)}, u32[]{:S(2)}, u32[]{:S(2)}) collective-permute-start(f32[48,256]{1,0:T(8,128)S(1)} %get-tuple-element.10), channel_id=1, source_target_pairs={{2,0},{4,2},{6,4},{8,6},{10,8},{12,10},{14,12},{3,1},{5,3},{7,5},{... | collective-permute-start | bytes 147464 | tf_op jit(solution)/shard_map/ppermute | solution.py:375
  3.3 5.0 %collective-permute-start.1 = (f32[48,256]{1,0:T(8,128)S(1)}, f32[48,256]{1,0:T(8,128)S(1)}, u32[]{:S(2)}, u32[]{:S(2)}) collective-permute-start(f32[48,256]{1,0:T(8,128)S(1)} %get-tuple-element.11), channel_id=1, source_target_pairs={{0,2},{2,4},{4,6},{6,8},{8,10},{10,12},{12,14},{1,3},{3,5},{5,7},{... | collective-permute-start | bytes 147464 | tf_op jit(solution)/shard_map/ppermute | solution.py:376
  8.4 0.1 broadcast_in_dim.4.zonal
  8.5 0.1 broadcast_in_dim.5.coriolis
  8.5 3.8 %tendencies.1 = (f32[32,104,128]{2,1,0:T(8,128)}, f32[2,96,128]{2,1,0:T(8,128)S(1)}) custom-call(f32[3,16,32,256]{3,2,1,0:T(8,128)} %own.1, f32[32,256]{1,0:T(8,128)S(1)} %broadcast_in_dim.4.zonal, f32[32,256]{1,0:T(8,128)S(1)} %broadcast_in_dim.5.coriolis), custom_call_target="tpu_custom_call" | custom-call | tf_op jit(solution)/shard_map/tendencies/pallas_call | solution.py:387
  12.4 0.0 collective-permute-done.north
  12.4 0.0 collective-permute-done.1.south
  12.4 0.7 seam_rows.1
  13.1 0.0 copy-start.2
  13.1 0.0 copy-start.3
  13.1 7.3 %all-to-all-start = ((f32[32,104,128]{2,1,0:T(8,128)}), f32[32,104,128]{2,1,0:T(8,128)S(1)}, u32[]{:S(2)}, u32[]{:S(2)}) async-start(f32[32,104,128]{2,1,0:T(8,128)} %seam_rows.1), calls=%async_computation | async-start | bytes 3407872 | tf_op jit(solution)/shard_map/all_to_all | solution.py:416
  20.4 24.8 %all-to-all-done = f32[32,104,128]{2,1,0:T(8,128)S(1)} async-done(((f32[32,104,128]{2,1,0:T(8,128)}), f32[32,104,128]{2,1,0:T(8,128)S(1)}, u32[]{:S(2)}, u32[]{:S(2)}) %all-to-all-start) | async-done | bytes 1703968 | tf_op jit(solution)/shard_map/all_to_all | solution.py:416
  45.2 0.0 copy-done.2
  45.2 0.0 copy-done.3
  45.2 4.8 %row_filter.1 = f32[2,16,3,2,16,128]{5,4,3,2,1,0:T(8,128)} custom-call(s32[1]{0:T(128)} %bitcast.own_row, s32[32]{0:T(128)S(1)} %copy-done.2, s32[32]{0:T(128)S(1)} %copy-done.3, f32[32]{0:T(128)S(1)} %get-tuple-element.14.zonal, f32[2,16,104,128]{3,2,1,0:T(8,128)S(1)} %bitcast.4, f32[32,32,32]{2,1,0:T(8,128)} %matrix.1), custom_call_target="tpu_custom_call" | custom-call | tf_op jit(solution)/shard_map/row_filter/pallas_call | solution.py:423
  50.0 0.0 copy-start
  50.0 4.1 %all-to-all-start.1 = ((f32[32,3,2,16,128]{4,3,2,1,0:T(8,128)}), f32[32,3,2,16,128]{4,3,2,1,0:T(8,128)S(1)}, u32[]{:S(2)}, u32[]{:S(2)}) async-start(f32[32,3,2,16,128]{4,3,2,1,0:T(8,128)} %bitcast.5), calls=%async_computation.1 | async-start | bytes 3145728 | tf_op jit(solution)/shard_map/all_to_all | solution.py:451
  54.2 0.0 copy-done
  54.2 0.0 copy-start.1
  54.2 0.1 slice.3
  54.3 0.4 collective-permute-start.2
  54.6 2.4 %collective-permute-done.2.other = f32[2,16,32,256]{3,2,1,0:T(8,128)S(1)} collective-permute-done((f32[2,16,32,256]{3,2,1,0:T(8,128)S(1)}, f32[2,16,32,256]{3,2,1,0:T(8,128)S(1)}, u32[]{:S(2)}, u32[]{:S(2)}) %collective-permute-start.2) | collective-permute-done | bytes 1048608 | tf_op jit(solution)/shard_map/ppermute | solution.py:377
  57.0 0.0 copy-done.1
  57.0 2.5 %base.1 = f32[32,3,2,16,128]{4,3,2,1,0:T(8,128)} custom-call(s32[1]{0:T(128)} %bitcast.3.own_part, f32[3,16,32,256]{3,2,1,0:T(8,128)S(1)} %copy-done, f32[2,16,32,256]{3,2,1,0:T(8,128)S(1)} %collective-permute-done.2.other, f32[32,32,32]{2,1,0:T(8,128)S(1)} %copy-done.1), custom_call_target="tpu_custom_call" | custom-call | tf_op jit(solution)/shard_map/base/pallas_call | solution.py:456
  59.5 18.0 %all-to-all-done.1.step = f32[32,3,2,16,128]{4,3,2,1,0:T(8,128)S(1)} async-done(((f32[32,3,2,16,128]{4,3,2,1,0:T(8,128)}), f32[32,3,2,16,128]{4,3,2,1,0:T(8,128)S(1)}, u32[]{:S(2)}, u32[]{:S(2)}) %all-to-all-start.1) | async-done | bytes 1572896 | tf_op jit(solution)/shard_map/all_to_all | solution.py:451
  77.5 2.3 %finish.1 = f32[3,16,32,256]{3,2,1,0:T(8,128)} custom-call(f32[32,3,2,16,128]{4,3,2,1,0:T(8,128)S(1)} %all-to-all-done.1.step, f32[32,3,2,16,128]{4,3,2,1,0:T(8,128)} %base.1), custom_call_target="tpu_custom_call" | custom-call | tf_op jit(solution)/shard_map/finish/pallas_call | solution.py:473
  (1 shorter events, 0.0 us)
Async XLA Ops:
  1.3 11.1 %collective-permute-start = (f32[48,256]{1,0:T(8,128)S(1)}, f32[48,256]{1,0:T(8,128)S(1)}, u32[]{:S(2)}, u32[]{:S(2)}) collective-permute-start(f32[48,256]{1,0:T(8,128)S(1)} %get-tuple-element.10), channel_id=1, source_target_pairs={{2,0},{4,2},{6,4},{8,6},{10,8},{12,10},{14,12},{3,1},{5,3},{7,5},{... | collective-permute-start | bytes 147464 | tf_op jit(solution)/shard_map/ppermute | solution.py:375
  3.3 9.1 %collective-permute-start.1 = (f32[48,256]{1,0:T(8,128)S(1)}, f32[48,256]{1,0:T(8,128)S(1)}, u32[]{:S(2)}, u32[]{:S(2)}) collective-permute-start(f32[48,256]{1,0:T(8,128)S(1)} %get-tuple-element.11), channel_id=1, source_target_pairs={{0,2},{2,4},{4,6},{6,8},{8,10},{10,12},{12,14},{1,3},{3,5},{5,7},{... | collective-permute-start | bytes 147464 | tf_op jit(solution)/shard_map/ppermute | solution.py:376
  13.1 32.2 %copy-start.2 = (s32[32]{0:T(128)S(1)}, s32[32]{0:T(128)}, u32[]{:S(2)}) copy-start(s32[32]{0:T(128)} %half_width.1) | copy-start | bytes 388
  13.1 32.1 %copy-start.3 = (s32[32]{0:T(128)S(1)}, s32[32]{0:T(128)}, u32[]{:S(2)}) copy-start(s32[32]{0:T(128)} %filter_mask.1) | copy-start | bytes 388
  13.1 32.1 %all-to-all-start = ((f32[32,104,128]{2,1,0:T(8,128)}), f32[32,104,128]{2,1,0:T(8,128)S(1)}, u32[]{:S(2)}, u32[]{:S(2)}) async-start(f32[32,104,128]{2,1,0:T(8,128)} %seam_rows.1), calls=%async_computation | async-start | bytes 3407872 | tf_op jit(solution)/shard_map/all_to_all | solution.py:416
  50.0 4.1 %copy-start = (f32[3,16,32,256]{3,2,1,0:T(8,128)S(1)}, f32[3,16,32,256]{3,2,1,0:T(8,128)}, u32[]{:S(2)}) copy-start(f32[3,16,32,256]{3,2,1,0:T(8,128)} %own.1) | copy-start | bytes 4718596
  50.0 27.5 %all-to-all-start.1 = ((f32[32,3,2,16,128]{4,3,2,1,0:T(8,128)}), f32[32,3,2,16,128]{4,3,2,1,0:T(8,128)S(1)}, u32[]{:S(2)}, u32[]{:S(2)}) async-start(f32[32,3,2,16,128]{4,3,2,1,0:T(8,128)} %bitcast.5), calls=%async_computation.1 | async-start | bytes 3145728 | tf_op jit(solution)/shard_map/all_to_all | solution.py:451
  54.2 2.8 %copy-start.1 = (f32[32,32,32]{2,1,0:T(8,128)S(1)}, f32[32,32,32]{2,1,0:T(8,128)}, u32[]{:S(2)}) copy-start(f32[32,32,32]{2,1,0:T(8,128)} %matrix.1) | copy-start | bytes 393220
  54.3 2.7 %collective-permute-start.2 = (f32[2,16,32,256]{3,2,1,0:T(8,128)S(1)}, f32[2,16,32,256]{3,2,1,0:T(8,128)S(1)}, u32[]{:S(2)}, u32[]{:S(2)}) collective-permute-start(f32[2,16,32,256]{3,2,1,0:T(8,128)S(1)} %slice.3), channel_id=1, source_target_pairs={{0,1},{1,0},{2,3},{3,2},{4,5},{5,4},{6,7},{7,6},{8,9},{9,8},{10,11... | collective-permute-start | bytes 3145736 | tf_op jit(solution)/shard_map/ppermute | solution.py:377

commit v10 on v9

--- a/solution.py
+++ b/solution.py
@@ -12,7 +12,7 @@
 SUBLANES = 8
 VMEM_LIMIT = 32 * 1024 * 1024
 GROUP = 4
-LOADS = 4
+LOADS = 8
 
 
 def latitudes(global_rows, row_total):
@@ -34,19 +34,17 @@
     return tiles
 
 
-def outer_rows_kernel(prog, first, last, tiles, sems):
+def outer_rows_kernel(prog, first, last, sems):
     fields, levels, rows, _ = prog.shape
-    loads = []
+    copies = []
     for f in range(fields):
-        for n, start in enumerate((rows - SUBLANES, 0)):
-            some = pl.ds(start, SUBLANES)
-            loads.append(pltpu.make_async_copy(prog.at[f, :, some], tiles.at[n, f], sems.at[f, n]))
-            loads[-1].start()
-    for f in range(fields):
-        for n, (row, out) in enumerate(((SUBLANES - 1, last), (0, first))):
-            loads[2 * f + n].wait()
-            for l in range(levels):
-                out[f * levels + l : f * levels + l + 1, :] = tiles[n, f, l, row : row + 1, :]
+        for n, (row, out) in enumerate(((0, first), (rows - 1, last))):
+            copies.append(
+                pltpu.make_async_copy(prog.at[f, :, row], out.at[pl.ds(f * levels, levels)], sems.at[f, n])
+            )
+            copies[-1].start()
+    for copy in copies:
+        copy.wait()
 
 
 def tendency_kernel(prog, zonal, coriolis, out, ends, tile, turn, stage, in_sems, out_sems):
@@ -367,7 +365,6 @@
             in_specs=[hbm],
             out_specs=(vmem, vmem),
             scratch_shapes=[
-                pltpu.VMEM((2, fields, levels, SUBLANES, width), jnp.float32),
                 pltpu.SemaphoreType.DMA((fields, 2)),
             ],
             compiler_params=params,

time: 80.2 us -> 80.1 us (level)
  no operation moved by 1% of the time
where the time goes in v10:
time: 80.1 us; the launch traced here: 79.7 us
  waiting for transfers between devices  45.2 us (56%)
  starting transfers between devices  18.9 us (24%)
  Pallas kernels  15.2 us (19%)
    all_to_all x1, waiting for transfers between devices, per_device(): whole_rows = lax.all_to_all(tend, ('lev', 'lon'), 0, 0, tiled=True)  24.8 us
    all_to_all x1, waiting for transfers between devices, per_device(): lax.all_to_all(stepped.reshape((rows,) + stepped_shape[2:]), ('lev', 'lon...  18 us
    all_to_all x1, starting transfers between devices, per_device(): whole_rows = lax.all_to_all(tend, ('lev', 'lon'), 0, 0, tiled=True)  7.33 us
    ppermute x1, starting transfers between devices, per_device(): lax.ppermute(last, 'lat', [(i, i + 1) for i in range(lat_devices - 1)])  5.04 us
    pallas_call x1, Pallas kernels, per_device(): pl.pallas_call(filter_kernel, out_shape=pltpu.HBM(stepped_shape, jnp.floa...  4.79 us
    all_to_all x1, starting transfers between devices, per_device(): lax.all_to_all(stepped.reshape((rows,) + stepped_shape[2:]), ('lev', 'lon...  4.12 us
    pallas_call x1, Pallas kernels, per_device(): pl.pallas_call(tendency_kernel, out_shape=(pltpu.HBM((rows, sent_rows, HA...  4.08 us
    pallas_call x1, Pallas kernels, per_device(): pl.pallas_call(base_kernel, out_shape=pltpu.HBM(returned.shape, jnp.float...  2.5 us
  transfers between devices with their start and end apart: 5, of which 3 were waited for; matrix products, arithmetic and copies ran while one was open for 0% of the time, Pallas kernels for 8%

profile of v10, /device:TPU:96, one launch (start us, length us, event | category | flops | bytes accessed | tf_op | source)
XLA Modules:
  0.0 79.7 jit_solution(13315777941109403777)
XLA Ops:
  0.0 0.9 %outer_rows.1 = (f32[48,256]{1,0:T(8,128)S(1)}, f32[48,256]{1,0:T(8,128)S(1)}) custom-call(f32[3,16,32,256]{3,2,1,0:T(8,128)} %own.1), custom_call_target="tpu_custom_call" | custom-call | tf_op jit(solution)/shard_map/outer_rows/pallas_call | solution.py:362
  0.9 2.0 %collective-permute-start = (f32[48,256]{1,0:T(8,128)S(1)}, f32[48,256]{1,0:T(8,128)S(1)}, u32[]{:S(2)}, u32[]{:S(2)}) collective-permute-start(f32[48,256]{1,0:T(8,128)S(1)} %get-tuple-element.10), channel_id=1, source_target_pairs={{2,0},{4,2},{6,4},{8,6},{10,8},{12,10},{14,12},{3,1},{5,3},{7,5},{... | collective-permute-start | bytes 147464 | tf_op jit(solution)/shard_map/ppermute | solution.py:372
  2.9 5.0 %collective-permute-start.1 = (f32[48,256]{1,0:T(8,128)S(1)}, f32[48,256]{1,0:T(8,128)S(1)}, u32[]{:S(2)}, u32[]{:S(2)}) collective-permute-start(f32[48,256]{1,0:T(8,128)S(1)} %get-tuple-element.11), channel_id=1, source_target_pairs={{0,2},{2,4},{4,6},{6,8},{8,10},{10,12},{12,14},{1,3},{3,5},{5,7},{... | collective-permute-start | bytes 147464 | tf_op jit(solution)/shard_map/ppermute | solution.py:373
  8.0 0.1 broadcast_in_dim.4.zonal
  8.1 0.1 broadcast_in_dim.5.coriolis
  8.1 4.1 %tendencies.1 = (f32[32,104,128]{2,1,0:T(8,128)}, f32[2,96,128]{2,1,0:T(8,128)S(1)}) custom-call(f32[3,16,32,256]{3,2,1,0:T(8,128)} %own.1, f32[32,256]{1,0:T(8,128)S(1)} %broadcast_in_dim.4.zonal, f32[32,256]{1,0:T(8,128)S(1)} %broadcast_in_dim.5.coriolis), custom_call_target="tpu_custom_call" | custom-call | tf_op jit(solution)/shard_map/tendencies/pallas_call | solution.py:384
  12.2 0.0 collective-permute-done.north
  12.2 0.0 collective-permute-done.1.south
  12.2 0.7 seam_rows.1
  12.9 0.0 copy-start.2
  12.9 0.0 copy-start.3
  12.9 7.3 %all-to-all-start = ((f32[32,104,128]{2,1,0:T(8,128)}), f32[32,104,128]{2,1,0:T(8,128)S(1)}, u32[]{:S(2)}, u32[]{:S(2)}) async-start(f32[32,104,128]{2,1,0:T(8,128)} %seam_rows.1), calls=%async_computation | async-start | bytes 3407872 | tf_op jit(solution)/shard_map/all_to_all | solution.py:413
  20.3 24.8 %all-to-all-done = f32[32,104,128]{2,1,0:T(8,128)S(1)} async-done(((f32[32,104,128]{2,1,0:T(8,128)}), f32[32,104,128]{2,1,0:T(8,128)S(1)}, u32[]{:S(2)}, u32[]{:S(2)}) %all-to-all-start) | async-done | bytes 1703968 | tf_op jit(solution)/shard_map/all_to_all | solution.py:413
  45.1 0.0 copy-done.2
  45.1 0.0 copy-done.3
  45.1 4.8 %row_filter.1 = f32[2,16,3,2,16,128]{5,4,3,2,1,0:T(8,128)} custom-call(s32[1]{0:T(128)} %bitcast.own_row, s32[32]{0:T(128)S(1)} %copy-done.2, s32[32]{0:T(128)S(1)} %copy-done.3, f32[32]{0:T(128)S(1)} %get-tuple-element.14.zonal, f32[2,16,104,128]{3,2,1,0:T(8,128)S(1)} %bitcast.4, f32[32,32,32]{2,1,0:T(8,128)} %matrix.1), custom_call_target="tpu_custom_call" | custom-call | tf_op jit(solution)/shard_map/row_filter/pallas_call | solution.py:420
  49.9 0.0 copy-start
  49.9 4.1 %all-to-all-start.1 = ((f32[32,3,2,16,128]{4,3,2,1,0:T(8,128)}), f32[32,3,2,16,128]{4,3,2,1,0:T(8,128)S(1)}, u32[]{:S(2)}, u32[]{:S(2)}) async-start(f32[32,3,2,16,128]{4,3,2,1,0:T(8,128)} %bitcast.5), calls=%async_computation.1 | async-start | bytes 3145728 | tf_op jit(solution)/shard_map/all_to_all | solution.py:448
  54.0 0.0 copy-done
  54.0 0.0 copy-start.1
  54.0 0.1 slice.3
  54.1 0.4 collective-permute-start.2
  54.5 2.4 %collective-permute-done.2.other = f32[2,16,32,256]{3,2,1,0:T(8,128)S(1)} collective-permute-done((f32[2,16,32,256]{3,2,1,0:T(8,128)S(1)}, f32[2,16,32,256]{3,2,1,0:T(8,128)S(1)}, u32[]{:S(2)}, u32[]{:S(2)}) %collective-permute-start.2) | collective-permute-done | bytes 1048608 | tf_op jit(solution)/shard_map/ppermute | solution.py:374
  56.9 0.0 copy-done.1
  56.9 2.5 %base.1 = f32[32,3,2,16,128]{4,3,2,1,0:T(8,128)} custom-call(s32[1]{0:T(128)} %bitcast.3.own_part, f32[3,16,32,256]{3,2,1,0:T(8,128)S(1)} %copy-done, f32[2,16,32,256]{3,2,1,0:T(8,128)S(1)} %collective-permute-done.2.other, f32[32,32,32]{2,1,0:T(8,128)S(1)} %copy-done.1), custom_call_target="tpu_custom_call" | custom-call | tf_op jit(solution)/shard_map/base/pallas_call | solution.py:453
  59.4 18.0 %all-to-all-done.1.step = f32[32,3,2,16,128]{4,3,2,1,0:T(8,128)S(1)} async-done(((f32[32,3,2,16,128]{4,3,2,1,0:T(8,128)}), f32[32,3,2,16,128]{4,3,2,1,0:T(8,128)S(1)}, u32[]{:S(2)}, u32[]{:S(2)}) %all-to-all-start.1) | async-done | bytes 1572896 | tf_op jit(solution)/shard_map/all_to_all | solution.py:448
  77.4 2.3 %finish.1 = f32[3,16,32,256]{3,2,1,0:T(8,128)} custom-call(f32[32,3,2,16,128]{4,3,2,1,0:T(8,128)S(1)} %all-to-all-done.1.step, f32[32,3,2,16,128]{4,3,2,1,0:T(8,128)} %base.1), custom_call_target="tpu_custom_call" | custom-call | tf_op jit(solution)/shard_map/finish/pallas_call | solution.py:470
  (1 shorter events, 0.0 us)
Async XLA Ops:
  0.9 11.4 %collective-permute-start = (f32[48,256]{1,0:T(8,128)S(1)}, f32[48,256]{1,0:T(8,128)S(1)}, u32[]{:S(2)}, u32[]{:S(2)}) collective-permute-start(f32[48,256]{1,0:T(8,128)S(1)} %get-tuple-element.10), channel_id=1, source_target_pairs={{2,0},{4,2},{6,4},{8,6},{10,8},{12,10},{14,12},{3,1},{5,3},{7,5},{... | collective-permute-start | bytes 147464 | tf_op jit(solution)/shard_map/ppermute | solution.py:372
  2.9 9.3 %collective-permute-start.1 = (f32[48,256]{1,0:T(8,128)S(1)}, f32[48,256]{1,0:T(8,128)S(1)}, u32[]{:S(2)}, u32[]{:S(2)}) collective-permute-start(f32[48,256]{1,0:T(8,128)S(1)} %get-tuple-element.11), channel_id=1, source_target_pairs={{0,2},{2,4},{4,6},{6,8},{8,10},{10,12},{12,14},{1,3},{3,5},{5,7},{... | collective-permute-start | bytes 147464 | tf_op jit(solution)/shard_map/ppermute | solution.py:373
  12.9 32.2 %copy-start.2 = (s32[32]{0:T(128)S(1)}, s32[32]{0:T(128)}, u32[]{:S(2)}) copy-start(s32[32]{0:T(128)} %half_width.1) | copy-start | bytes 388
  12.9 32.1 %copy-start.3 = (s32[32]{0:T(128)S(1)}, s32[32]{0:T(128)}, u32[]{:S(2)}) copy-start(s32[32]{0:T(128)} %filter_mask.1) | copy-start | bytes 388
  12.9 32.1 %all-to-all-start = ((f32[32,104,128]{2,1,0:T(8,128)}), f32[32,104,128]{2,1,0:T(8,128)S(1)}, u32[]{:S(2)}, u32[]{:S(2)}) async-start(f32[32,104,128]{2,1,0:T(8,128)} %seam_rows.1), calls=%async_computation | async-start | bytes 3407872 | tf_op jit(solution)/shard_map/all_to_all | solution.py:413
  49.9 4.1 %copy-start = (f32[3,16,32,256]{3,2,1,0:T(8,128)S(1)}, f32[3,16,32,256]{3,2,1,0:T(8,128)}, u32[]{:S(2)}) copy-start(f32[3,16,32,256]{3,2,1,0:T(8,128)} %own.1) | copy-start | bytes 4718596
  49.9 27.5 %all-to-all-start.1 = ((f32[32,3,2,16,128]{4,3,2,1,0:T(8,128)}), f32[32,3,2,16,128]{4,3,2,1,0:T(8,128)S(1)}, u32[]{:S(2)}, u32[]{:S(2)}) async-start(f32[32,3,2,16,128]{4,3,2,1,0:T(8,128)} %bitcast.5), calls=%async_computation.1 | async-start | bytes 3145728 | tf_op jit(solution)/shard_map/all_to_all | solution.py:448
  54.0 2.8 %copy-start.1 = (f32[32,32,32]{2,1,0:T(8,128)S(1)}, f32[32,32,32]{2,1,0:T(8,128)}, u32[]{:S(2)}) copy-start(f32[32,32,32]{2,1,0:T(8,128)} %matrix.1) | copy-start | bytes 393220
  54.1 2.7 %collective-permute-start.2 = (f32[2,16,32,256]{3,2,1,0:T(8,128)S(1)}, f32[2,16,32,256]{3,2,1,0:T(8,128)S(1)}, u32[]{:S(2)}, u32[]{:S(2)}) collective-permute-start(f32[2,16,32,256]{3,2,1,0:T(8,128)S(1)} %slice.3), channel_id=1, source_target_pairs={{0,1},{1,0},{2,3},{3,2},{4,5},{5,4},{6,7},{7,6},{8,9},{9,8},{10,11... | collective-permute-start | bytes 3145736 | tf_op jit(solution)/shard_map/ppermute | solution.py:374

commit v11 on v8

--- a/solution.py
+++ b/solution.py
@@ -34,7 +34,7 @@
     return tiles
 
 
-def fetch_kernel(prog, tile, last, first, sems):
+def fetch_kernel(prog, tile, first, last, sems):
     fields, levels, rows, _ = prog.shape
     per_load = levels // LOADS
     loads = []
@@ -52,10 +52,17 @@
             first[c : c + 1, :] = tile[f, l, 0:1, :]
 
 
-def tendency_kernel(prog, zonal, coriolis, out, ends, turn, edges, stage, out_sems):
-    _, levels, rows, width = prog.shape
+def tendency_kernel(tile, zonal, coriolis, out, ends, turn, stage, out_sems):
+    _, levels, rows, width = tile.shape
     chans = 3 * levels
     payload = 2 * chans
+    copies = []
+
+    def send(first, sem):
+        some = pl.ds(first, SUBLANES)
+        copies.append(pltpu.make_async_copy(stage.at[:, some], out.at[:, some], out_sems.at[sem]))
+        copies[-1].start()
+
     row_id = lax.broadcasted_iota(jnp.int32, (rows, width), 0)
     col_id = lax.broadcasted_iota(jnp.int32, (rows, width), 1)
     lane_id = lax.broadcasted_iota(jnp.int32, (rows, HALF), 1)
@@ -67,7 +74,7 @@
         centre, dx, dy, sx = [], [], [], []
         for f in range(3):
             c = f * levels + l
-            here = prog[f, l]
+            here = tile[f, l]
             e = jnp.where(last_col, 0.0, pltpu.roll(here, width - 1, 1))
             w = jnp.where(first_col, 0.0, pltpu.roll(here, 1, 1))
             n = jnp.where(last_row, 0.0, pltpu.roll(here, rows - 1, 0))
@@ -89,33 +96,33 @@
         )
         for f in range(3):
             turn[f, l] = tends[f]
-    edges[...] = edge_rows
-    copies = []
-    for chunk in range(rows // SUBLANES):
-        some = slice(chunk * SUBLANES, (chunk + 1) * SUBLANES)
+        if (l + 1) % SUBLANES:
+            continue
+        l0 = l + 1 - SUBLANES
         for f in range(3):
             for half in range(2):
-                for l0 in range(0, levels, SUBLANES):
-                    at = (2 * f + half) * levels + l0
+                at = (2 * f + half) * levels + l0
+                for j0 in range(0, rows, SUBLANES):
                     flipped = flip(
-                        [turn[f, l0 + i, some, half * HALF : (half + 1) * HALF] for i in range(SUBLANES)]
+                        [
+                            turn[f, l0 + i, j0 : j0 + SUBLANES, half * HALF : (half + 1) * HALF]
+                            for i in range(SUBLANES)
+                        ]
                     )
                     for k, value in enumerate(flipped):
-                        j = chunk * SUBLANES + k
+                        j = j0 + k
                         stage[j, at : at + SUBLANES, :] = value
                         if j in (0, rows - 1):
                             ends[min(j, 1), at : at + SUBLANES, :] = value
-        for k in range(SUBLANES):
-            j = chunk * SUBLANES + k
-            stage[j, payload:, :] = jnp.broadcast_to(edges[j : j + 1, :], (SUBLANES, HALF))
-        some = pl.ds(chunk * SUBLANES, SUBLANES)
-        copies.append(pltpu.make_async_copy(stage.at[some], out.at[some], out_sems.at[chunk]))
-        copies[-1].start()
+                send(at, at // SUBLANES)
+    for j in range(rows):
+        stage[j, payload:, :] = jnp.broadcast_to(edge_rows[j : j + 1, :], (SUBLANES, HALF))
+    send(payload, payload // SUBLANES)
     for copy in copies:
         copy.wait()
 
 
-def seam_kernel(ends, south, north, tend, out, stage, sems):
+def seam_kernel(ends, north, south, tend, out, stage, sems):
     del tend
     chans = south.shape[0]
     levels = chans // 3
@@ -350,7 +357,7 @@
 
 
     with jax.named_scope("fetch"):
-        tile, last, first = pl.pallas_call(
+        tile, first, last = pl.pallas_call(
             fetch_kernel,
             out_shape=(
                 pltpu.VMEM(prognostic.shape, jnp.float32),
@@ -362,8 +369,8 @@
             scratch_shapes=[pltpu.SemaphoreType.DMA((fields, LOADS))],
             compiler_params=params,
         )(in_hbm(prognostic))
+    north = lax.ppermute(first, "lat", [(i + 1, i) for i in range(lat_devices - 1)])
     south = lax.ppermute(last, "lat", [(i, i + 1) for i in range(lat_devices - 1)])
-    north = lax.ppermute(first, "lat", [(i + 1, i) for i in range(lat_devices - 1)])
     other = lax.ppermute(prognostic[:2], "lev", [(0, 1), (1, 0)])
 
     global_rows = (lat_index * rows + jnp.arange(rows)).astype(jnp.float32)
@@ -384,12 +391,11 @@
             out_specs=(hbm, vmem),
             scratch_shapes=[
                 pltpu.VMEM(prognostic.shape, jnp.float32),
-                pltpu.VMEM((rows, HALF), jnp.float32),
                 pltpu.VMEM((rows, sent_rows, HALF), jnp.float32),
-                pltpu.SemaphoreType.DMA((rows // SUBLANES,)),
+                pltpu.SemaphoreType.DMA((sent_rows // SUBLANES,)),
             ],
             compiler_params=params,
-        )(in_vmem(tile), zonal_field, coriolis_field)
+        )(in_vmem(tile), in_vmem(zonal_field), in_vmem(coriolis_field))
 
     with jax.named_scope("seam_rows"):
         tend = pl.pallas_call(
@@ -400,7 +406,7 @@
             input_output_aliases={3: 0},
             scratch_shapes=[pltpu.VMEM(ends.shape, jnp.float32), pltpu.SemaphoreType.DMA((2,))],
             compiler_params=params,
-        )(in_vmem(ends), in_vmem(south), in_vmem(north), in_hbm(tend))
+        )(in_vmem(ends), in_vmem(north), in_vmem(south), in_hbm(tend))
 
     whole_rows = lax.all_to_all(tend, ("lev", "lon"), 0, 0, tiled=True)
 

time: 81.6 us -> 79.4 us (0.973)
  waiting for transfers between devices: 47.4 us -> 45.2 us
    ppermute x1, waiting for transfers between devices: 2.17 us -> 0.01 us  [per_device(): lax.ppermute(first, 'lat', [(i + 1, i) for i in range(lat_devices - 1)])]
  transfers between devices with their start and end apart: 5 -> 5, of which waited for: 4 -> 3; matrix products, arithmetic and copies ran while one was open for 0% -> 0% of each run, Pallas kernels for 7% -> 7%
where the time goes in v11:
time: 79.4 us; the launch traced here: 79 us
  waiting for transfers between devices  45.2 us (57%)
  starting transfers between devices  18.9 us (24%)
  Pallas kernels  14.5 us (18%)
    all_to_all x1, waiting for transfers between devices, per_device(): whole_rows = lax.all_to_all(tend, ('lev', 'lon'), 0, 0, tiled=True)  24.8 us
    all_to_all x1, waiting for transfers between devices, per_device(): lax.all_to_all(stepped.reshape((rows,) + stepped_shape[2:]), ('lev', 'lon...  18 us
    all_to_all x1, starting transfers between devices, per_device(): whole_rows = lax.all_to_all(tend, ('lev', 'lon'), 0, 0, tiled=True)  7.33 us
    ppermute x1, starting transfers between devices, per_device(): lax.ppermute(last, 'lat', [(i, i + 1) for i in range(lat_devices - 1)])  5.04 us
    pallas_call x1, Pallas kernels, per_device(): pl.pallas_call(filter_kernel, out_shape=pltpu.HBM(stepped_shape, jnp.floa...  4.8 us
    all_to_all x1, starting transfers between devices, per_device(): lax.all_to_all(stepped.reshape((rows,) + stepped_shape[2:]), ('lev', 'lon...  4.12 us
    pallas_call x1, Pallas kernels, per_device(): pl.pallas_call(tendency_kernel, out_shape=(pltpu.HBM((rows, sent_rows, HA...  2.71 us
    pallas_call x1, Pallas kernels, per_device(): pl.pallas_call(base_kernel, out_shape=pltpu.HBM(returned.shape, jnp.float...  2.5 us
  transfers between devices with their start and end apart: 5, of which 3 were waited for; matrix products, arithmetic and copies ran while one was open for 0% of the time, Pallas kernels for 7%

profile of v11, /device:TPU:96, one launch (start us, length us, event | category | flops | bytes accessed | tf_op | source)
XLA Modules:
  0.0 79.0 jit_solution(1624538631297668566)
XLA Ops:
  0.0 1.5 %fetch.1 = (f32[3,16,32,256]{3,2,1,0:T(8,128)S(1)}, f32[48,256]{1,0:T(8,128)S(1)}, f32[48,256]{1,0:T(8,128)S(1)}) custom-call(f32[3,16,32,256]{3,2,1,0:T(8,128)} %own.1), custom_call_target="tpu_custom_call" | custom-call | tf_op jit(solution)/shard_map/fetch/pallas_call | solution.py:360
  1.6 2.0 %collective-permute-start = (f32[48,256]{1,0:T(8,128)S(1)}, f32[48,256]{1,0:T(8,128)S(1)}, u32[]{:S(2)}, u32[]{:S(2)}) collective-permute-start(f32[48,256]{1,0:T(8,128)S(1)} %get-tuple-element.12), channel_id=1, source_target_pairs={{2,0},{4,2},{6,4},{8,6},{10,8},{12,10},{14,12},{3,1},{5,3},{7,5},{... | collective-permute-start | bytes 147464 | tf_op jit(solution)/shard_map/ppermute | solution.py:372
  3.6 5.0 %collective-permute-start.1 = (f32[48,256]{1,0:T(8,128)S(1)}, f32[48,256]{1,0:T(8,128)S(1)}, u32[]{:S(2)}, u32[]{:S(2)}) collective-permute-start(f32[48,256]{1,0:T(8,128)S(1)} %get-tuple-element.13), channel_id=1, source_target_pairs={{0,2},{2,4},{4,6},{6,8},{8,10},{10,12},{12,14},{1,3},{3,5},{5,7},{... | collective-permute-start | bytes 147464 | tf_op jit(solution)/shard_map/ppermute | solution.py:373
  8.7 0.1 broadcast_in_dim.4.zonal
  8.8 0.1 broadcast_in_dim.5.coriolis
  8.8 2.7 %tendencies.1 = (f32[32,104,128]{2,1,0:T(8,128)}, f32[2,96,128]{2,1,0:T(8,128)S(1)}) custom-call(f32[3,16,32,256]{3,2,1,0:T(8,128)S(1)} %get-tuple-element.10.tile, f32[32,256]{1,0:T(8,128)S(1)} %broadcast_in_dim.4.zonal, f32[32,256]{1,0:T(8,128)S(1)} %broadcast_in_dim.5.coriolis), custom_call_target="tpu_custom_call" | custom-call | tf_op jit(solution)/shard_map/tendencies/pallas_call | solution.py:384
  11.5 0.0 collective-permute-done.north
  11.6 0.0 collective-permute-done.1.south
  11.6 0.7 seam_rows.1
  12.2 0.0 copy-start.2
  12.2 0.0 copy-start.3
  12.3 7.3 %all-to-all-start = ((f32[32,104,128]{2,1,0:T(8,128)}), f32[32,104,128]{2,1,0:T(8,128)S(1)}, u32[]{:S(2)}, u32[]{:S(2)}) async-start(f32[32,104,128]{2,1,0:T(8,128)} %seam_rows.1), calls=%async_computation | async-start | bytes 3407872 | tf_op jit(solution)/shard_map/all_to_all | solution.py:411
  19.6 24.8 %all-to-all-done = f32[32,104,128]{2,1,0:T(8,128)S(1)} async-done(((f32[32,104,128]{2,1,0:T(8,128)}), f32[32,104,128]{2,1,0:T(8,128)S(1)}, u32[]{:S(2)}, u32[]{:S(2)}) %all-to-all-start) | async-done | bytes 1703968 | tf_op jit(solution)/shard_map/all_to_all | solution.py:411
  44.4 0.0 copy-done.2
  44.4 0.0 copy-done.3
  44.4 4.8 %row_filter.1 = f32[2,16,3,2,16,128]{5,4,3,2,1,0:T(8,128)} custom-call(s32[1]{0:T(128)} %bitcast.own_row, s32[32]{0:T(128)S(1)} %copy-done.2, s32[32]{0:T(128)S(1)} %copy-done.3, f32[32]{0:T(128)S(1)} %get-tuple-element.16.zonal, f32[2,16,104,128]{3,2,1,0:T(8,128)S(1)} %bitcast.4, f32[32,32,32]{2,1,0:T(8,128)} %matrix.1), custom_call_target="tpu_custom_call" | custom-call | tf_op jit(solution)/shard_map/row_filter/pallas_call | solution.py:418
  49.2 0.0 copy-start
  49.2 4.1 %all-to-all-start.1 = ((f32[32,3,2,16,128]{4,3,2,1,0:T(8,128)}), f32[32,3,2,16,128]{4,3,2,1,0:T(8,128)S(1)}, u32[]{:S(2)}, u32[]{:S(2)}) async-start(f32[32,3,2,16,128]{4,3,2,1,0:T(8,128)} %bitcast.5), calls=%async_computation.1 | async-start | bytes 3145728 | tf_op jit(solution)/shard_map/all_to_all | solution.py:446
  53.3 0.0 copy-done
  53.3 0.0 copy-start.1
  53.4 0.1 slice.3
  53.4 0.4 collective-permute-start.2
  53.8 2.4 %collective-permute-done.2.other = f32[2,16,32,256]{3,2,1,0:T(8,128)S(1)} collective-permute-done((f32[2,16,32,256]{3,2,1,0:T(8,128)S(1)}, f32[2,16,32,256]{3,2,1,0:T(8,128)S(1)}, u32[]{:S(2)}, u32[]{:S(2)}) %collective-permute-start.2) | collective-permute-done | bytes 1048608 | tf_op jit(solution)/shard_map/ppermute | solution.py:374
  56.2 0.0 copy-done.1
  56.2 2.5 %base.1 = f32[32,3,2,16,128]{4,3,2,1,0:T(8,128)} custom-call(s32[1]{0:T(128)} %bitcast.3.own_part, f32[3,16,32,256]{3,2,1,0:T(8,128)S(1)} %copy-done, f32[2,16,32,256]{3,2,1,0:T(8,128)S(1)} %collective-permute-done.2.other, f32[32,32,32]{2,1,0:T(8,128)S(1)} %copy-done.1), custom_call_target="tpu_custom_call" | custom-call | tf_op jit(solution)/shard_map/base/pallas_call | solution.py:451
  58.7 18.0 %all-to-all-done.1.step = f32[32,3,2,16,128]{4,3,2,1,0:T(8,128)S(1)} async-done(((f32[32,3,2,16,128]{4,3,2,1,0:T(8,128)}), f32[32,3,2,16,128]{4,3,2,1,0:T(8,128)S(1)}, u32[]{:S(2)}, u32[]{:S(2)}) %all-to-all-start.1) | async-done | bytes 1572896 | tf_op jit(solution)/shard_map/all_to_all | solution.py:446
  76.7 2.3 %finish.1 = f32[3,16,32,256]{3,2,1,0:T(8,128)} custom-call(f32[32,3,2,16,128]{4,3,2,1,0:T(8,128)S(1)} %all-to-all-done.1.step, f32[32,3,2,16,128]{4,3,2,1,0:T(8,128)} %base.1), custom_call_target="tpu_custom_call" | custom-call | tf_op jit(solution)/shard_map/finish/pallas_call | solution.py:468
  (1 shorter events, 0.0 us)
Async XLA Ops:
  1.6 10.0 %collective-permute-start = (f32[48,256]{1,0:T(8,128)S(1)}, f32[48,256]{1,0:T(8,128)S(1)}, u32[]{:S(2)}, u32[]{:S(2)}) collective-permute-start(f32[48,256]{1,0:T(8,128)S(1)} %get-tuple-element.12), channel_id=1, source_target_pairs={{2,0},{4,2},{6,4},{8,6},{10,8},{12,10},{14,12},{3,1},{5,3},{7,5},{... | collective-permute-start | bytes 147464 | tf_op jit(solution)/shard_map/ppermute | solution.py:372
  3.6 8.0 %collective-permute-start.1 = (f32[48,256]{1,0:T(8,128)S(1)}, f32[48,256]{1,0:T(8,128)S(1)}, u32[]{:S(2)}, u32[]{:S(2)}) collective-permute-start(f32[48,256]{1,0:T(8,128)S(1)} %get-tuple-element.13), channel_id=1, source_target_pairs={{0,2},{2,4},{4,6},{6,8},{8,10},{10,12},{12,14},{1,3},{3,5},{5,7},{... | collective-permute-start | bytes 147464 | tf_op jit(solution)/shard_map/ppermute | solution.py:373
  12.2 32.2 %copy-start.2 = (s32[32]{0:T(128)S(1)}, s32[32]{0:T(128)}, u32[]{:S(2)}) copy-start(s32[32]{0:T(128)} %half_width.1) | copy-start | bytes 388
  12.2 32.1 %copy-start.3 = (s32[32]{0:T(128)S(1)}, s32[32]{0:T(128)}, u32[]{:S(2)}) copy-start(s32[32]{0:T(128)} %filter_mask.1) | copy-start | bytes 388
  12.3 32.1 %all-to-all-start = ((f32[32,104,128]{2,1,0:T(8,128)}), f32[32,104,128]{2,1,0:T(8,128)S(1)}, u32[]{:S(2)}, u32[]{:S(2)}) async-start(f32[32,104,128]{2,1,0:T(8,128)} %seam_rows.1), calls=%async_computation | async-start | bytes 3407872 | tf_op jit(solution)/shard_map/all_to_all | solution.py:411
  49.2 4.1 %copy-start = (f32[3,16,32,256]{3,2,1,0:T(8,128)S(1)}, f32[3,16,32,256]{3,2,1,0:T(8,128)}, u32[]{:S(2)}) copy-start(f32[3,16,32,256]{3,2,1,0:T(8,128)} %own.1) | copy-start | bytes 4718596
  49.2 27.5 %all-to-all-start.1 = ((f32[32,3,2,16,128]{4,3,2,1,0:T(8,128)}), f32[32,3,2,16,128]{4,3,2,1,0:T(8,128)S(1)}, u32[]{:S(2)}, u32[]{:S(2)}) async-start(f32[32,3,2,16,128]{4,3,2,1,0:T(8,128)} %bitcast.5), calls=%async_computation.1 | async-start | bytes 3145728 | tf_op jit(solution)/shard_map/all_to_all | solution.py:446
  53.3 2.8 %copy-start.1 = (f32[32,32,32]{2,1,0:T(8,128)S(1)}, f32[32,32,32]{2,1,0:T(8,128)}, u32[]{:S(2)}) copy-start(f32[32,32,32]{2,1,0:T(8,128)} %matrix.1) | copy-start | bytes 393220
  53.4 2.7 %collective-permute-start.2 = (f32[2,16,32,256]{3,2,1,0:T(8,128)S(1)}, f32[2,16,32,256]{3,2,1,0:T(8,128)S(1)}, u32[]{:S(2)}, u32[]{:S(2)}) collective-permute-start(f32[2,16,32,256]{3,2,1,0:T(8,128)S(1)} %slice.3), channel_id=1, source_target_pairs={{0,1},{1,0},{2,3},{3,2},{4,5},{5,4},{6,7},{7,6},{8,9},{9,8},{10,11... | collective-permute-start | bytes 3145736 | tf_op jit(solution)/shard_map/ppermute | solution.py:374

commit v12 on v11

--- a/solution.py
+++ b/solution.py
@@ -52,72 +52,60 @@
             first[c : c + 1, :] = tile[f, l, 0:1, :]
 
 
-def tendency_kernel(tile, zonal, coriolis, out, ends, turn, stage, out_sems):
+def tendency_kernel(tile, zonal, coriolis, out, ends, stage, sems):
     _, levels, rows, width = tile.shape
     chans = 3 * levels
     payload = 2 * chans
+    row_id = lax.broadcasted_iota(jnp.int32, (SUBLANES, width), 0)
+    col_id = lax.broadcasted_iota(jnp.int32, (SUBLANES, width), 1)
+    lane_id = lax.broadcasted_iota(jnp.int32, (SUBLANES, HALF), 1)
+    first_row, last_row = row_id == 0, row_id == SUBLANES - 1
+    first_col, last_col = col_id == 0, col_id == width - 1
     copies = []
-
-    def send(first, sem):
-        some = pl.ds(first, SUBLANES)
-        copies.append(pltpu.make_async_copy(stage.at[:, some], out.at[:, some], out_sems.at[sem]))
-        copies[-1].start()
-
-    row_id = lax.broadcasted_iota(jnp.int32, (rows, width), 0)
-    col_id = lax.broadcasted_iota(jnp.int32, (rows, width), 1)
-    lane_id = lax.broadcasted_iota(jnp.int32, (rows, HALF), 1)
-    first_row, last_row = row_id == 0, row_id == rows - 1
-    first_col, last_col = col_id == 0, col_id == width - 1
-    zon, cor = zonal[...], coriolis[...]
-    edge_rows = jnp.zeros((rows, HALF), jnp.float32)
-    for l in range(levels):
-        centre, dx, dy, sx = [], [], [], []
-        for f in range(3):
-            c = f * levels + l
-            here = tile[f, l]
-            e = jnp.where(last_col, 0.0, pltpu.roll(here, width - 1, 1))
-            w = jnp.where(first_col, 0.0, pltpu.roll(here, 1, 1))
-            n = jnp.where(last_row, 0.0, pltpu.roll(here, rows - 1, 0))
-            s = jnp.where(first_row, 0.0, pltpu.roll(here, 1, 0))
-            centre.append(here)
-            dx.append(e - w)
-            dy.append(n - s)
-            sx.append(e + w + n + s - 4.0 * here)
-            first = here[:, :HALF]
-            last = here[:, width - HALF :]
-            if c:
-                first = pltpu.roll(first, c, 1)
-            last = pltpu.roll(last, (chans + c + 1) % HALF, 1)
-            edge_rows = jnp.where(lane_id == c, first, jnp.where(lane_id == chans + c, last, edge_rows))
-        tends = (
-            -zon * dx[2] + cor * centre[1] + VISCOSITY * sx[0],
-            -MERIDIONAL * dy[2] - cor * centre[0] + VISCOSITY * sx[1],
-            -zon * dx[0] - MERIDIONAL * dy[1],
-        )
-        for f in range(3):
-            turn[f, l] = tends[f]
-        if (l + 1) % SUBLANES:
-            continue
-        l0 = l + 1 - SUBLANES
-        for f in range(3):
-            for half in range(2):
-                at = (2 * f + half) * levels + l0
-                for j0 in range(0, rows, SUBLANES):
-                    flipped = flip(
-                        [
-                            turn[f, l0 + i, j0 : j0 + SUBLANES, half * HALF : (half + 1) * HALF]
-                            for i in range(SUBLANES)
-                        ]
-                    )
+    for j0 in range(0, rows, SUBLANES):
+        j1 = j0 + SUBLANES
+        zon, cor = zonal[j0:j1, :], coriolis[j0:j1, :]
+        edge_rows = jnp.zeros((SUBLANES, HALF), jnp.float32)
+        for l0 in range(0, levels, SUBLANES):
+            tends = [[], [], []]
+            for l in range(l0, l0 + SUBLANES):
+                centre, dx, dy, sx = [], [], [], []
+                for f in range(3):
+                    c = f * levels + l
+                    here = tile[f, l, j0:j1, :]
+                    after = tile[f, l, j1 : j1 + 1, :] if j1 < rows else 0.0
+                    before = tile[f, l, j0 - 1 : j0, :] if j0 else 0.0
+                    e = jnp.where(last_col, 0.0, pltpu.roll(here, width - 1, 1))
+                    w = jnp.where(first_col, 0.0, pltpu.roll(here, 1, 1))
+                    n = jnp.where(last_row, after, pltpu.roll(here, SUBLANES - 1, 0))
+                    s = jnp.where(first_row, before, pltpu.roll(here, 1, 0))
+                    centre.append(here)
+                    dx.append(e - w)
+                    dy.append(n - s)
+                    sx.append(e + w + n + s - 4.0 * here)
+                    first = here[:, :HALF]
+                    last = here[:, width - HALF :]
+                    if c:
+                        first = pltpu.roll(first, c, 1)
+                    last = pltpu.roll(last, (chans + c + 1) % HALF, 1)
+                    edge_rows = jnp.where(lane_id == c, first, jnp.where(lane_id == chans + c, last, edge_rows))
+                tends[0].append(-zon * dx[2] + cor * centre[1] + VISCOSITY * sx[0])
+                tends[1].append(-MERIDIONAL * dy[2] - cor * centre[0] + VISCOSITY * sx[1])
+                tends[2].append(-zon * dx[0] - MERIDIONAL * dy[1])
+            for f in range(3):
+                for half in range(2):
+                    at = (2 * f + half) * levels + l0
+                    flipped = flip([value[:, half * HALF : (half + 1) * HALF] for value in tends[f]])
                     for k, value in enumerate(flipped):
                         j = j0 + k
                         stage[j, at : at + SUBLANES, :] = value
                         if j in (0, rows - 1):
                             ends[min(j, 1), at : at + SUBLANES, :] = value
-                send(at, at // SUBLANES)
-    for j in range(rows):
-        stage[j, payload:, :] = jnp.broadcast_to(edge_rows[j : j + 1, :], (SUBLANES, HALF))
-    send(payload, payload // SUBLANES)
+        for k in range(SUBLANES):
+            stage[j0 + k, payload:, :] = jnp.broadcast_to(edge_rows[k : k + 1, :], (SUBLANES, HALF))
+        some = pl.ds(j0, SUBLANES)
+        copies.append(pltpu.make_async_copy(stage.at[some], out.at[some], sems.at[j0 // SUBLANES]))
+        copies[-1].start()
     for copy in copies:
         copy.wait()
 
@@ -229,50 +217,55 @@
             parts[g * both : (g + 1) * both, :HALF] = hi
             parts[g * both : (g + 1) * both, HALF:] = lo
 
-    copies = []
-
-    def finish_group(g0, total):
-        box = jnp.dot(parts[g0 * both : (g0 + GROUP) * both, :], sums, preferred_element_type=jnp.float32)
-        for pair in range(GROUP // 2):
-            b = g0 // 2 + pair
-            steps = []
-            for half in range(2):
-                g = 2 * b + half
-                at = (g - g0) * both
-                behind = halves[lax.rem(g + count - reach, count)]
-                smooth = (box[at : at + both, :HALF] + total + edge_gain * behind) * scale
-                total = total + box[at : at + both, HALF:]
-                step = jnp.where(filtered, smooth, TIME_STEP * halves[g])
-                for p in range(lev_parts):
-                    stage[p, b, 2, half] = step[p * chans + 2 * levels : (p + 1) * chans]
-                steps.append(step)
-            step = jnp.concatenate(steps, axis=1)
-            winds = []
-            for f in range(2):
-                winds += split2(
-                    jnp.concatenate(
-                        [step[p * chans + f * levels : p * chans + (f + 1) * levels] for p in range(lev_parts)],
-                        axis=0,
-                    )
+    def emit(b, steps):
+        for half, step in enumerate(steps):
+            for p in range(lev_parts):
+                stage[p, b, 2, half] = step[p * chans + 2 * levels : (p + 1) * chans]
+        step = jnp.concatenate(steps, axis=1)
+        winds = []
+        for f in range(2):
+            winds += split2(
+                jnp.concatenate(
+                    [step[p * chans + f * levels : p * chans + (f + 1) * levels] for p in range(lev_parts)],
+                    axis=0,
                 )
-            mixed = jnp.dot(mixer, jnp.concatenate(winds, axis=0), preferred_element_type=jnp.float32)
-            mixed = mixed[: 2 * lev_parts * levels] + mixed[2 * lev_parts * levels :]
-            for f in range(2):
-                for p in range(lev_parts):
-                    at = (f * lev_parts + p) * levels
-                    for half in range(2):
-                        stage[p, b, f, half] = mixed[at : at + levels, half * HALF : (half + 1) * HALF]
-            copies.append(pltpu.make_async_copy(stage.at[:, b], out.at[:, b], sems.at[b]))
-            copies[-1].start()
-        return total
-
-    split_group(0)
-    for g0 in range(0, count, GROUP):
-        if g0 + GROUP < count:
-            split_group(g0 + GROUP)
-        total = finish_group(g0, total)
-    for copy in copies:
-        copy.wait()
+            )
+        mixed = jnp.dot(mixer, jnp.concatenate(winds, axis=0), preferred_element_type=jnp.float32)
+        mixed = mixed[: 2 * lev_parts * levels] + mixed[2 * lev_parts * levels :]
+        for f in range(2):
+            for p in range(lev_parts):
+                at = (f * lev_parts + p) * levels
+                for half in range(2):
+                    stage[p, b, f, half] = mixed[at : at + levels, half * HALF : (half + 1) * HALF]
+        copy = pltpu.make_async_copy(stage.at[:, b], out.at[:, b], sems.at[b])
+        copy.start()
+        return copy
+
+    @pl.when(filtered)
+    def _():
+        copies = []
+        running = total
+        split_group(0)
+        for g0 in range(0, count, GROUP):
+            if g0 + GROUP < count:
+                split_group(g0 + GROUP)
+            box = jnp.dot(parts[g0 * both : (g0 + GROUP) * both, :], sums, preferred_element_type=jnp.float32)
+            for b in range(g0 // 2, (g0 + GROUP) // 2):
+                steps = []
+                for g in (2 * b, 2 * b + 1):
+                    at = (g - g0) * both
+                    behind = halves[lax.rem(g + count - reach, count)]
+                    steps.append((box[at : at + both, :HALF] + running + edge_gain * behind) * scale)
+                    running = running + box[at : at + both, HALF:]
+                copies.append(emit(b, steps))
+        for copy in copies:
+            copy.wait()
+
+    @pl.when(jnp.logical_not(filtered))
+    def _():
+        copies = [emit(b, [TIME_STEP * halves[2 * b], TIME_STEP * halves[2 * b + 1]]) for b in range(blocks)]
+        for copy in copies:
+            copy.wait()
 
 
 def base_kernel(own_part, own, other, matrix, out):
@@ -390,9 +383,8 @@
             in_specs=[vmem, vmem, vmem],
             out_specs=(hbm, vmem),
             scratch_shapes=[
-                pltpu.VMEM(prognostic.shape, jnp.float32),
                 pltpu.VMEM((rows, sent_rows, HALF), jnp.float32),
-                pltpu.SemaphoreType.DMA((sent_rows // SUBLANES,)),
+                pltpu.SemaphoreType.DMA((rows // SUBLANES,)),
             ],
             compiler_params=params,
         )(in_vmem(tile), in_vmem(zonal_field), in_vmem(coriolis_field))

time: 79.4 us -> 78.4 us (0.987); the launches traced: 79 us -> 77 us
  Pallas kernels: 14.5 us -> 12.5 us
    pallas_call x1, Pallas kernels: 4.8 us -> 3.34 us  [per_device(): pl.pallas_call(filter_kernel, out_shape=pltpu.HBM(stepped_shape, jnp.floa...]
  transfers between devices with their start and end apart: 5 -> 5, of which waited for: 3 -> 3; matrix products, arithmetic and copies ran while one was open for 0% -> 0% of each run, Pallas kernels for 7% -> 6%
where the time goes in v12:
time: 78.4 us; the launch traced here: 77 us
  waiting for transfers between devices  45.2 us (58%)
  starting transfers between devices  18.9 us (24%)
  Pallas kernels  12.5 us (16%)
    all_to_all x1, waiting for transfers between devices, per_device(): whole_rows = lax.all_to_all(tend, ('lev', 'lon'), 0, 0, tiled=True)  24.8 us
    all_to_all x1, waiting for transfers between devices, per_device(): lax.all_to_all(stepped.reshape((rows,) + stepped_shape[2:]), ('lev', 'lon...  18 us
    all_to_all x1, starting transfers between devices, per_device(): whole_rows = lax.all_to_all(tend, ('lev', 'lon'), 0, 0, tiled=True)  7.33 us
    ppermute x1, starting transfers between devices, per_device(): lax.ppermute(last, 'lat', [(i, i + 1) for i in range(lat_devices - 1)])  5.04 us
    all_to_all x1, starting transfers between devices, per_device(): lax.all_to_all(stepped.reshape((rows,) + stepped_shape[2:]), ('lev', 'lon...  4.12 us
    pallas_call x1, Pallas kernels, per_device(): pl.pallas_call(filter_kernel, out_shape=pltpu.HBM(stepped_shape, jnp.floa...  3.34 us
    pallas_call x1, Pallas kernels, per_device(): pl.pallas_call(base_kernel, out_shape=pltpu.HBM(returned.shape, jnp.float...  2.5 us
    ppermute x1, waiting for transfers between devices, per_device(): other = lax.ppermute(prognostic[:2], 'lev', [(0, 1), (1, 0)])  2.4 us
  transfers between devices with their start and end apart: 5, of which 3 were waited for; matrix products, arithmetic and copies ran while one was open for 0% of the time, Pallas kernels for 6%

profile of v12, /device:TPU:96, one launch (start us, length us, event | category | flops | bytes accessed | tf_op | source)
XLA Modules:
  0.0 77.0 jit_solution(12654523080185007267)
XLA Ops:
  0.0 1.5 %fetch.1 = (f32[3,16,32,256]{3,2,1,0:T(8,128)S(1)}, f32[48,256]{1,0:T(8,128)S(1)}, f32[48,256]{1,0:T(8,128)S(1)}) custom-call(f32[3,16,32,256]{3,2,1,0:T(8,128)} %own.1), custom_call_target="tpu_custom_call" | custom-call | tf_op jit(solution)/shard_map/fetch/pallas_call | solution.py:353
  1.6 2.0 %collective-permute-start = (f32[48,256]{1,0:T(8,128)S(1)}, f32[48,256]{1,0:T(8,128)S(1)}, u32[]{:S(2)}, u32[]{:S(2)}) collective-permute-start(f32[48,256]{1,0:T(8,128)S(1)} %get-tuple-element.12), channel_id=1, source_target_pairs={{2,0},{4,2},{6,4},{8,6},{10,8},{12,10},{14,12},{3,1},{5,3},{7,5},{... | collective-permute-start | bytes 147464 | tf_op jit(solution)/shard_map/ppermute | solution.py:365
  3.6 5.0 %collective-permute-start.1 = (f32[48,256]{1,0:T(8,128)S(1)}, f32[48,256]{1,0:T(8,128)S(1)}, u32[]{:S(2)}, u32[]{:S(2)}) collective-permute-start(f32[48,256]{1,0:T(8,128)S(1)} %get-tuple-element.13), channel_id=1, source_target_pairs={{0,2},{2,4},{4,6},{6,8},{8,10},{10,12},{12,14},{1,3},{3,5},{5,7},{... | collective-permute-start | bytes 147464 | tf_op jit(solution)/shard_map/ppermute | solution.py:366
  8.7 0.1 broadcast_in_dim.4.zonal
  8.8 0.1 broadcast_in_dim.5.coriolis
  8.8 2.2 %tendencies.1 = (f32[32,104,128]{2,1,0:T(8,128)}, f32[2,96,128]{2,1,0:T(8,128)S(1)}) custom-call(f32[3,16,32,256]{3,2,1,0:T(8,128)S(1)} %get-tuple-element.10.tile, f32[32,256]{1,0:T(8,128)S(1)} %broadcast_in_dim.4.zonal, f32[32,256]{1,0:T(8,128)S(1)} %broadcast_in_dim.5.coriolis), custom_call_target="tpu_custom_call" | custom-call | tf_op jit(solution)/shard_map/tendencies/pallas_call | solution.py:377
  11.1 0.0 collective-permute-done.north
  11.1 0.0 collective-permute-done.1.south
  11.1 0.7 seam_rows.1
  11.7 0.0 copy-start.2
  11.8 0.0 copy-start.3
  11.8 7.3 %all-to-all-start = ((f32[32,104,128]{2,1,0:T(8,128)}), f32[32,104,128]{2,1,0:T(8,128)S(1)}, u32[]{:S(2)}, u32[]{:S(2)}) async-start(f32[32,104,128]{2,1,0:T(8,128)} %seam_rows.1), calls=%async_computation | async-start | bytes 3407872 | tf_op jit(solution)/shard_map/all_to_all | solution.py:403
  19.1 24.8 %all-to-all-done = f32[32,104,128]{2,1,0:T(8,128)S(1)} async-done(((f32[32,104,128]{2,1,0:T(8,128)}), f32[32,104,128]{2,1,0:T(8,128)S(1)}, u32[]{:S(2)}, u32[]{:S(2)}) %all-to-all-start) | async-done | bytes 1703968 | tf_op jit(solution)/shard_map/all_to_all | solution.py:403
  43.9 0.0 copy-done.2
  43.9 0.0 copy-done.3
  43.9 3.3 %row_filter.1 = f32[2,16,3,2,16,128]{5,4,3,2,1,0:T(8,128)} custom-call(s32[1]{0:T(128)} %bitcast.own_row, s32[32]{0:T(128)S(1)} %copy-done.2, s32[32]{0:T(128)S(1)} %copy-done.3, f32[32]{0:T(128)S(1)} %get-tuple-element.16.zonal, f32[2,16,104,128]{3,2,1,0:T(8,128)S(1)} %bitcast.4, f32[32,32,32]{2,1,0:T(8,128)} %matrix.1), custom_call_target="tpu_custom_call" | custom-call | tf_op jit(solution)/shard_map/row_filter/pallas_call | solution.py:410
  47.2 0.0 copy-start
  47.3 4.1 %all-to-all-start.1 = ((f32[32,3,2,16,128]{4,3,2,1,0:T(8,128)}), f32[32,3,2,16,128]{4,3,2,1,0:T(8,128)S(1)}, u32[]{:S(2)}, u32[]{:S(2)}) async-start(f32[32,3,2,16,128]{4,3,2,1,0:T(8,128)} %bitcast.5), calls=%async_computation.1 | async-start | bytes 3145728 | tf_op jit(solution)/shard_map/all_to_all | solution.py:438
  51.4 0.0 copy-done
  51.4 0.0 copy-start.1
  51.4 0.1 slice.3
  51.5 0.4 collective-permute-start.2
  51.8 2.4 %collective-permute-done.2.other = f32[2,16,32,256]{3,2,1,0:T(8,128)S(1)} collective-permute-done((f32[2,16,32,256]{3,2,1,0:T(8,128)S(1)}, f32[2,16,32,256]{3,2,1,0:T(8,128)S(1)}, u32[]{:S(2)}, u32[]{:S(2)}) %collective-permute-start.2) | collective-permute-done | bytes 1048608 | tf_op jit(solution)/shard_map/ppermute | solution.py:367
  54.2 0.0 copy-done.1
  54.2 2.5 %base.1 = f32[32,3,2,16,128]{4,3,2,1,0:T(8,128)} custom-call(s32[1]{0:T(128)} %bitcast.3.own_part, f32[3,16,32,256]{3,2,1,0:T(8,128)S(1)} %copy-done, f32[2,16,32,256]{3,2,1,0:T(8,128)S(1)} %collective-permute-done.2.other, f32[32,32,32]{2,1,0:T(8,128)S(1)} %copy-done.1), custom_call_target="tpu_custom_call" | custom-call | tf_op jit(solution)/shard_map/base/pallas_call | solution.py:443
  56.7 18.0 %all-to-all-done.1.step = f32[32,3,2,16,128]{4,3,2,1,0:T(8,128)S(1)} async-done(((f32[32,3,2,16,128]{4,3,2,1,0:T(8,128)}), f32[32,3,2,16,128]{4,3,2,1,0:T(8,128)S(1)}, u32[]{:S(2)}, u32[]{:S(2)}) %all-to-all-start.1) | async-done | bytes 1572896 | tf_op jit(solution)/shard_map/all_to_all | solution.py:438
  74.8 2.3 %finish.1 = f32[3,16,32,256]{3,2,1,0:T(8,128)} custom-call(f32[32,3,2,16,128]{4,3,2,1,0:T(8,128)S(1)} %all-to-all-done.1.step, f32[32,3,2,16,128]{4,3,2,1,0:T(8,128)} %base.1), custom_call_target="tpu_custom_call" | custom-call | tf_op jit(solution)/shard_map/finish/pallas_call | solution.py:460
  (1 shorter events, 0.0 us)
Async XLA Ops:
  1.6 9.5 %collective-permute-start = (f32[48,256]{1,0:T(8,128)S(1)}, f32[48,256]{1,0:T(8,128)S(1)}, u32[]{:S(2)}, u32[]{:S(2)}) collective-permute-start(f32[48,256]{1,0:T(8,128)S(1)} %get-tuple-element.12), channel_id=1, source_target_pairs={{2,0},{4,2},{6,4},{8,6},{10,8},{12,10},{14,12},{3,1},{5,3},{7,5},{... | collective-permute-start | bytes 147464 | tf_op jit(solution)/shard_map/ppermute | solution.py:365
  3.6 7.5 %collective-permute-start.1 = (f32[48,256]{1,0:T(8,128)S(1)}, f32[48,256]{1,0:T(8,128)S(1)}, u32[]{:S(2)}, u32[]{:S(2)}) collective-permute-start(f32[48,256]{1,0:T(8,128)S(1)} %get-tuple-element.13), channel_id=1, source_target_pairs={{0,2},{2,4},{4,6},{6,8},{8,10},{10,12},{12,14},{1,3},{3,5},{5,7},{... | collective-permute-start | bytes 147464 | tf_op jit(solution)/shard_map/ppermute | solution.py:366
  11.7 32.2 %copy-start.2 = (s32[32]{0:T(128)S(1)}, s32[32]{0:T(128)}, u32[]{:S(2)}) copy-start(s32[32]{0:T(128)} %half_width.1) | copy-start | bytes 388
  11.8 32.1 %copy-start.3 = (s32[32]{0:T(128)S(1)}, s32[32]{0:T(128)}, u32[]{:S(2)}) copy-start(s32[32]{0:T(128)} %filter_mask.1) | copy-start | bytes 388
  11.8 32.1 %all-to-all-start = ((f32[32,104,128]{2,1,0:T(8,128)}), f32[32,104,128]{2,1,0:T(8,128)S(1)}, u32[]{:S(2)}, u32[]{:S(2)}) async-start(f32[32,104,128]{2,1,0:T(8,128)} %seam_rows.1), calls=%async_computation | async-start | bytes 3407872 | tf_op jit(solution)/shard_map/all_to_all | solution.py:403
  47.2 4.1 %copy-start = (f32[3,16,32,256]{3,2,1,0:T(8,128)S(1)}, f32[3,16,32,256]{3,2,1,0:T(8,128)}, u32[]{:S(2)}) copy-start(f32[3,16,32,256]{3,2,1,0:T(8,128)} %own.1) | copy-start | bytes 4718596
  47.3 27.5 %all-to-all-start.1 = ((f32[32,3,2,16,128]{4,3,2,1,0:T(8,128)}), f32[32,3,2,16,128]{4,3,2,1,0:T(8,128)S(1)}, u32[]{:S(2)}, u32[]{:S(2)}) async-start(f32[32,3,2,16,128]{4,3,2,1,0:T(8,128)} %bitcast.5), calls=%async_computation.1 | async-start | bytes 3145728 | tf_op jit(solution)/shard_map/all_to_all | solution.py:438
  51.4 2.8 %copy-start.1 = (f32[32,32,32]{2,1,0:T(8,128)S(1)}, f32[32,32,32]{2,1,0:T(8,128)}, u32[]{:S(2)}) copy-start(f32[32,32,32]{2,1,0:T(8,128)} %matrix.1) | copy-start | bytes 393220
  51.5 2.7 %collective-permute-start.2 = (f32[2,16,32,256]{3,2,1,0:T(8,128)S(1)}, f32[2,16,32,256]{3,2,1,0:T(8,128)S(1)}, u32[]{:S(2)}, u32[]{:S(2)}) collective-permute-start(f32[2,16,32,256]{3,2,1,0:T(8,128)S(1)} %slice.3), channel_id=1, source_target_pairs={{0,1},{1,0},{2,3},{3,2},{4,5},{5,4},{6,7},{7,6},{8,9},{9,8},{10,11... | collective-permute-start | bytes 3145736 | tf_op jit(solution)/shard_map/ppermute | solution.py:367

commit v13 on v12

--- a/solution.py
+++ b/solution.py
@@ -11,7 +11,7 @@
 HALF = 128
 SUBLANES = 8
 VMEM_LIMIT = 32 * 1024 * 1024
-GROUP = 4
+GROUP = 8
 LOADS = 4
 
 
@@ -302,32 +302,28 @@
 
 def finish_kernel(step, base, out, added, stage, in_sems, out_sems):
     fields, levels, rows, _ = out.shape
-    blocks = levels // SUBLANES
-    loads, copies = [], []
-    for f in range(fields):
-        for n in range(blocks):
-            some = pl.ds(n * SUBLANES, SUBLANES)
-            loads.append(
-                pltpu.make_async_copy(base.at[:, f, :, some], added.at[:, f, :, some], in_sems.at[f * blocks + n])
+    pieces = [(f, l0) for f in range(fields) for l0 in range(0, levels, SUBLANES)]
+    loads, copies = {}, []
+    for n, (f, l0) in enumerate(pieces):
+        some = pl.ds(l0, SUBLANES)
+        for half in range(2):
+            loads[f, l0, half] = pltpu.make_async_copy(
+                base.at[:, f, half, some], added.at[:, f, half, some], in_sems.at[2 * n + half]
             )
-            loads[-1].start()
-    for f in range(fields):
-        for n in range(blocks):
-            loads[f * blocks + n].wait()
-            l0 = n * SUBLANES
-            some = slice(l0, l0 + SUBLANES)
-            for half in range(2):
-                for j0 in range(0, rows, SUBLANES):
-                    flipped = flip(
-                        [step[j0 + k, f, half, some, :] + added[j0 + k, f, half, some, :] for k in range(SUBLANES)]
-                    )
-                    for i, value in enumerate(flipped):
-                        stage[f, l0 + i, j0 : j0 + SUBLANES, half * HALF : (half + 1) * HALF] = value
-            some = pl.ds(l0, SUBLANES)
-            copies.append(
-                pltpu.make_async_copy(stage.at[f, some], out.at[f, some], out_sems.at[f * blocks + n])
-            )
-            copies[-1].start()
+            loads[f, l0, half].start()
+    for n, (f, l0) in enumerate(pieces):
+        some = slice(l0, l0 + SUBLANES)
+        for half in range(2):
+            loads[f, l0, half].wait()
+            for j0 in range(0, rows, SUBLANES):
+                flipped = flip(
+                    [step[j0 + k, f, half, some, :] + added[j0 + k, f, half, some, :] for k in range(SUBLANES)]
+                )
+                for i, value in enumerate(flipped):
+                    stage[f, l0 + i, j0 : j0 + SUBLANES, half * HALF : (half + 1) * HALF] = value
+        some = pl.ds(l0, SUBLANES)
+        copies.append(pltpu.make_async_copy(stage.at[f, some], out.at[f, some], out_sems.at[n]))
+        copies[-1].start()
     for copy in copies:
         copy.wait()
 
@@ -465,7 +461,7 @@
             scratch_shapes=[
                 pltpu.VMEM(returned.shape, jnp.float32),
                 pltpu.VMEM(prognostic.shape, jnp.float32),
-                pltpu.SemaphoreType.DMA((fields * levels // SUBLANES,)),
+                pltpu.SemaphoreType.DMA((fields * halves * levels // SUBLANES,)),
                 pltpu.SemaphoreType.DMA((fields * levels // SUBLANES,)),
             ],
             compiler_params=params,

time: 78.4 us -> 78 us (level)
  no operation moved by 1% of the time
where the time goes in v13:
time: 78 us; the launch traced here: 77.1 us
  waiting for transfers between devices  45.2 us (58%)
  starting transfers between devices  18.9 us (24%)
  Pallas kernels  12.6 us (16%)
    all_to_all x1, waiting for transfers between devices, per_device(): whole_rows = lax.all_to_all(tend, ('lev', 'lon'), 0, 0, tiled=True)  24.8 us
    all_to_all x1, waiting for transfers between devices, per_device(): lax.all_to_all(stepped.reshape((rows,) + stepped_shape[2:]), ('lev', 'lon...  18 us
    all_to_all x1, starting transfers between devices, per_device(): whole_rows = lax.all_to_all(tend, ('lev', 'lon'), 0, 0, tiled=True)  7.33 us
    ppermute x1, starting transfers between devices, per_device(): lax.ppermute(last, 'lat', [(i, i + 1) for i in range(lat_devices - 1)])  5.04 us
    all_to_all x1, starting transfers between devices, per_device(): lax.all_to_all(stepped.reshape((rows,) + stepped_shape[2:]), ('lev', 'lon...  4.12 us
    pallas_call x1, Pallas kernels, per_device(): pl.pallas_call(filter_kernel, out_shape=pltpu.HBM(stepped_shape, jnp.floa...  3.34 us
    pallas_call x1, Pallas kernels, per_device(): pl.pallas_call(base_kernel, out_shape=pltpu.HBM(returned.shape, jnp.float...  2.5 us
    ppermute x1, waiting for transfers between devices, per_device(): other = lax.ppermute(prognostic[:2], 'lev', [(0, 1), (1, 0)])  2.4 us
  transfers between devices with their start and end apart: 5, of which 3 were waited for; matrix products, arithmetic and copies ran while one was open for 0% of the time, Pallas kernels for 6%

profile of v13, /device:TPU:96, one launch (start us, length us, event | category | flops | bytes accessed | tf_op | source)
XLA Modules:
  0.0 77.1 jit_solution(16168341280516477692)
XLA Ops:
  0.0 1.5 %fetch.1 = (f32[3,16,32,256]{3,2,1,0:T(8,128)S(1)}, f32[48,256]{1,0:T(8,128)S(1)}, f32[48,256]{1,0:T(8,128)S(1)}) custom-call(f32[3,16,32,256]{3,2,1,0:T(8,128)} %own.1), custom_call_target="tpu_custom_call" | custom-call | tf_op jit(solution)/shard_map/fetch/pallas_call | solution.py:349
  1.6 2.0 %collective-permute-start = (f32[48,256]{1,0:T(8,128)S(1)}, f32[48,256]{1,0:T(8,128)S(1)}, u32[]{:S(2)}, u32[]{:S(2)}) collective-permute-start(f32[48,256]{1,0:T(8,128)S(1)} %get-tuple-element.12), channel_id=1, source_target_pairs={{2,0},{4,2},{6,4},{8,6},{10,8},{12,10},{14,12},{3,1},{5,3},{7,5},{... | collective-permute-start | bytes 147464 | tf_op jit(solution)/shard_map/ppermute | solution.py:361
  3.6 5.0 %collective-permute-start.1 = (f32[48,256]{1,0:T(8,128)S(1)}, f32[48,256]{1,0:T(8,128)S(1)}, u32[]{:S(2)}, u32[]{:S(2)}) collective-permute-start(f32[48,256]{1,0:T(8,128)S(1)} %get-tuple-element.13), channel_id=1, source_target_pairs={{0,2},{2,4},{4,6},{6,8},{8,10},{10,12},{12,14},{1,3},{3,5},{5,7},{... | collective-permute-start | bytes 147464 | tf_op jit(solution)/shard_map/ppermute | solution.py:362
  8.7 0.1 broadcast_in_dim.4.zonal
  8.8 0.1 broadcast_in_dim.5.coriolis
  8.8 2.2 %tendencies.1 = (f32[32,104,128]{2,1,0:T(8,128)}, f32[2,96,128]{2,1,0:T(8,128)S(1)}) custom-call(f32[3,16,32,256]{3,2,1,0:T(8,128)S(1)} %get-tuple-element.10.tile, f32[32,256]{1,0:T(8,128)S(1)} %broadcast_in_dim.4.zonal, f32[32,256]{1,0:T(8,128)S(1)} %broadcast_in_dim.5.coriolis), custom_call_target="tpu_custom_call" | custom-call | tf_op jit(solution)/shard_map/tendencies/pallas_call | solution.py:373
  11.1 0.0 collective-permute-done.north
  11.1 0.0 collective-permute-done.1.south
  11.1 0.7 seam_rows.1
  11.7 0.0 copy-start.2
  11.8 0.0 copy-start.3
  11.8 7.3 %all-to-all-start = ((f32[32,104,128]{2,1,0:T(8,128)}), f32[32,104,128]{2,1,0:T(8,128)S(1)}, u32[]{:S(2)}, u32[]{:S(2)}) async-start(f32[32,104,128]{2,1,0:T(8,128)} %seam_rows.1), calls=%async_computation | async-start | bytes 3407872 | tf_op jit(solution)/shard_map/all_to_all | solution.py:399
  19.1 24.8 %all-to-all-done = f32[32,104,128]{2,1,0:T(8,128)S(1)} async-done(((f32[32,104,128]{2,1,0:T(8,128)}), f32[32,104,128]{2,1,0:T(8,128)S(1)}, u32[]{:S(2)}, u32[]{:S(2)}) %all-to-all-start) | async-done | bytes 1703968 | tf_op jit(solution)/shard_map/all_to_all | solution.py:399
  43.9 0.0 copy-done.2
  43.9 0.0 copy-done.3
  43.9 3.3 %row_filter.1 = f32[2,16,3,2,16,128]{5,4,3,2,1,0:T(8,128)} custom-call(s32[1]{0:T(128)} %bitcast.own_row, s32[32]{0:T(128)S(1)} %copy-done.2, s32[32]{0:T(128)S(1)} %copy-done.3, f32[32]{0:T(128)S(1)} %get-tuple-element.16.zonal, f32[2,16,104,128]{3,2,1,0:T(8,128)S(1)} %bitcast.4, f32[32,32,32]{2,1,0:T(8,128)} %matrix.1), custom_call_target="tpu_custom_call" | custom-call | tf_op jit(solution)/shard_map/row_filter/pallas_call | solution.py:406
  47.2 0.0 copy-start
  47.3 4.1 %all-to-all-start.1 = ((f32[32,3,2,16,128]{4,3,2,1,0:T(8,128)}), f32[32,3,2,16,128]{4,3,2,1,0:T(8,128)S(1)}, u32[]{:S(2)}, u32[]{:S(2)}) async-start(f32[32,3,2,16,128]{4,3,2,1,0:T(8,128)} %bitcast.5), calls=%async_computation.1 | async-start | bytes 3145728 | tf_op jit(solution)/shard_map/all_to_all | solution.py:434
  51.4 0.0 copy-done
  51.4 0.0 copy-start.1
  51.4 0.1 slice.3
  51.5 0.4 collective-permute-start.2
  51.8 2.4 %collective-permute-done.2.other = f32[2,16,32,256]{3,2,1,0:T(8,128)S(1)} collective-permute-done((f32[2,16,32,256]{3,2,1,0:T(8,128)S(1)}, f32[2,16,32,256]{3,2,1,0:T(8,128)S(1)}, u32[]{:S(2)}, u32[]{:S(2)}) %collective-permute-start.2) | collective-permute-done | bytes 1048608 | tf_op jit(solution)/shard_map/ppermute | solution.py:363
  54.2 0.0 copy-done.1
  54.2 2.5 %base.1 = f32[32,3,2,16,128]{4,3,2,1,0:T(8,128)} custom-call(s32[1]{0:T(128)} %bitcast.3.own_part, f32[3,16,32,256]{3,2,1,0:T(8,128)S(1)} %copy-done, f32[2,16,32,256]{3,2,1,0:T(8,128)S(1)} %collective-permute-done.2.other, f32[32,32,32]{2,1,0:T(8,128)S(1)} %copy-done.1), custom_call_target="tpu_custom_call" | custom-call | tf_op jit(solution)/shard_map/base/pallas_call | solution.py:439
  56.7 18.0 %all-to-all-done.1.step = f32[32,3,2,16,128]{4,3,2,1,0:T(8,128)S(1)} async-done(((f32[32,3,2,16,128]{4,3,2,1,0:T(8,128)}), f32[32,3,2,16,128]{4,3,2,1,0:T(8,128)S(1)}, u32[]{:S(2)}, u32[]{:S(2)}) %all-to-all-start.1) | async-done | bytes 1572896 | tf_op jit(solution)/shard_map/all_to_all | solution.py:434
  74.8 2.4 %finish.1 = f32[3,16,32,256]{3,2,1,0:T(8,128)} custom-call(f32[32,3,2,16,128]{4,3,2,1,0:T(8,128)S(1)} %all-to-all-done.1.step, f32[32,3,2,16,128]{4,3,2,1,0:T(8,128)} %base.1), custom_call_target="tpu_custom_call" | custom-call | tf_op jit(solution)/shard_map/finish/pallas_call | solution.py:456
  (1 shorter events, 0.0 us)
Async XLA Ops:
  1.6 9.5 %collective-permute-start = (f32[48,256]{1,0:T(8,128)S(1)}, f32[48,256]{1,0:T(8,128)S(1)}, u32[]{:S(2)}, u32[]{:S(2)}) collective-permute-start(f32[48,256]{1,0:T(8,128)S(1)} %get-tuple-element.12), channel_id=1, source_target_pairs={{2,0},{4,2},{6,4},{8,6},{10,8},{12,10},{14,12},{3,1},{5,3},{7,5},{... | collective-permute-start | bytes 147464 | tf_op jit(solution)/shard_map/ppermute | solution.py:361
  3.6 7.5 %collective-permute-start.1 = (f32[48,256]{1,0:T(8,128)S(1)}, f32[48,256]{1,0:T(8,128)S(1)}, u32[]{:S(2)}, u32[]{:S(2)}) collective-permute-start(f32[48,256]{1,0:T(8,128)S(1)} %get-tuple-element.13), channel_id=1, source_target_pairs={{0,2},{2,4},{4,6},{6,8},{8,10},{10,12},{12,14},{1,3},{3,5},{5,7},{... | collective-permute-start | bytes 147464 | tf_op jit(solution)/shard_map/ppermute | solution.py:362
  11.7 32.2 %copy-start.2 = (s32[32]{0:T(128)S(1)}, s32[32]{0:T(128)}, u32[]{:S(2)}) copy-start(s32[32]{0:T(128)} %half_width.1) | copy-start | bytes 388
  11.8 32.1 %copy-start.3 = (s32[32]{0:T(128)S(1)}, s32[32]{0:T(128)}, u32[]{:S(2)}) copy-start(s32[32]{0:T(128)} %filter_mask.1) | copy-start | bytes 388
  11.8 32.1 %all-to-all-start = ((f32[32,104,128]{2,1,0:T(8,128)}), f32[32,104,128]{2,1,0:T(8,128)S(1)}, u32[]{:S(2)}, u32[]{:S(2)}) async-start(f32[32,104,128]{2,1,0:T(8,128)} %seam_rows.1), calls=%async_computation | async-start | bytes 3407872 | tf_op jit(solution)/shard_map/all_to_all | solution.py:399
  47.2 4.1 %copy-start = (f32[3,16,32,256]{3,2,1,0:T(8,128)S(1)}, f32[3,16,32,256]{3,2,1,0:T(8,128)}, u32[]{:S(2)}) copy-start(f32[3,16,32,256]{3,2,1,0:T(8,128)} %own.1) | copy-start | bytes 4718596
  47.3 27.5 %all-to-all-start.1 = ((f32[32,3,2,16,128]{4,3,2,1,0:T(8,128)}), f32[32,3,2,16,128]{4,3,2,1,0:T(8,128)S(1)}, u32[]{:S(2)}, u32[]{:S(2)}) async-start(f32[32,3,2,16,128]{4,3,2,1,0:T(8,128)} %bitcast.5), calls=%async_computation.1 | async-start | bytes 3145728 | tf_op jit(solution)/shard_map/all_to_all | solution.py:434
  51.4 2.8 %copy-start.1 = (f32[32,32,32]{2,1,0:T(8,128)S(1)}, f32[32,32,32]{2,1,0:T(8,128)}, u32[]{:S(2)}) copy-start(f32[32,32,32]{2,1,0:T(8,128)} %matrix.1) | copy-start | bytes 393220
  51.5 2.7 %collective-permute-start.2 = (f32[2,16,32,256]{3,2,1,0:T(8,128)S(1)}, f32[2,16,32,256]{3,2,1,0:T(8,128)S(1)}, u32[]{:S(2)}, u32[]{:S(2)}) collective-permute-start(f32[2,16,32,256]{3,2,1,0:T(8,128)S(1)} %slice.3), channel_id=1, source_target_pairs={{0,1},{1,0},{2,3},{3,2},{4,5},{5,4},{6,7},{7,6},{8,9},{9,8},{10,11... | collective-permute-start | bytes 3145736 | tf_op jit(solution)/shard_map/ppermute | solution.py:363

commit v14 on v12

--- a/solution.py
+++ b/solution.py
@@ -11,7 +11,7 @@
 HALF = 128
 SUBLANES = 8
 VMEM_LIMIT = 32 * 1024 * 1024
-GROUP = 4
+GROUP = 16
 LOADS = 4
 
 

time: 78.4 us -> 77.8 us (level); the launches traced: 77 us -> 77.4 us
  no operation moved by 1% of the time
where the time goes in v14:
time: 77.8 us; the launch traced here: 77.4 us
  waiting for transfers between devices  45.2 us (58%)
  starting transfers between devices  19.2 us (25%)
  Pallas kernels  12.5 us (16%)
    all_to_all x1, waiting for transfers between devices, per_device(): whole_rows = lax.all_to_all(tend, ('lev', 'lon'), 0, 0, tiled=True)  24.8 us
    all_to_all x1, waiting for transfers between devices, per_device(): lax.all_to_all(stepped.reshape((rows,) + stepped_shape[2:]), ('lev', 'lon...  18 us
    all_to_all x1, starting transfers between devices, per_device(): whole_rows = lax.all_to_all(tend, ('lev', 'lon'), 0, 0, tiled=True)  7.33 us
    ppermute x1, starting transfers between devices, per_device(): lax.ppermute(last, 'lat', [(i, i + 1) for i in range(lat_devices - 1)])  5.04 us
    all_to_all x1, starting transfers between devices, per_device(): lax.all_to_all(stepped.reshape((rows,) + stepped_shape[2:]), ('lev', 'lon...  4.46 us
    pallas_call x1, Pallas kernels, per_device(): pl.pallas_call(filter_kernel, out_shape=pltpu.HBM(stepped_shape, jnp.floa...  3.34 us
    pallas_call x1, Pallas kernels, per_device(): pl.pallas_call(base_kernel, out_shape=pltpu.HBM(returned.shape, jnp.float...  2.5 us
    ppermute x1, waiting for transfers between devices, per_device(): other = lax.ppermute(prognostic[:2], 'lev', [(0, 1), (1, 0)])  2.38 us
  transfers between devices with their start and end apart: 5, of which 3 were waited for; matrix products, arithmetic and copies ran while one was open for 0% of the time, Pallas kernels for 6%

profile of v14, /device:TPU:96, one launch (start us, length us, event | category | flops | bytes accessed | tf_op | source)
XLA Modules:
  0.0 77.4 jit_solution(5882152722077018307)
XLA Ops:
  0.0 1.5 %fetch.1 = (f32[3,16,32,256]{3,2,1,0:T(8,128)S(1)}, f32[48,256]{1,0:T(8,128)S(1)}, f32[48,256]{1,0:T(8,128)S(1)}) custom-call(f32[3,16,32,256]{3,2,1,0:T(8,128)} %own.1), custom_call_target="tpu_custom_call" | custom-call | tf_op jit(solution)/shard_map/fetch/pallas_call | solution.py:353
  1.6 2.0 %collective-permute-start = (f32[48,256]{1,0:T(8,128)S(1)}, f32[48,256]{1,0:T(8,128)S(1)}, u32[]{:S(2)}, u32[]{:S(2)}) collective-permute-start(f32[48,256]{1,0:T(8,128)S(1)} %get-tuple-element.12), channel_id=1, source_target_pairs={{2,0},{4,2},{6,4},{8,6},{10,8},{12,10},{14,12},{3,1},{5,3},{7,5},{... | collective-permute-start | bytes 147464 | tf_op jit(solution)/shard_map/ppermute | solution.py:365
  3.6 5.0 %collective-permute-start.1 = (f32[48,256]{1,0:T(8,128)S(1)}, f32[48,256]{1,0:T(8,128)S(1)}, u32[]{:S(2)}, u32[]{:S(2)}) collective-permute-start(f32[48,256]{1,0:T(8,128)S(1)} %get-tuple-element.13), channel_id=1, source_target_pairs={{0,2},{2,4},{4,6},{6,8},{8,10},{10,12},{12,14},{1,3},{3,5},{5,7},{... | collective-permute-start | bytes 147464 | tf_op jit(solution)/shard_map/ppermute | solution.py:366
  8.7 0.1 broadcast_in_dim.4.zonal
  8.8 0.1 broadcast_in_dim.5.coriolis
  8.8 2.2 %tendencies.1 = (f32[32,104,128]{2,1,0:T(8,128)}, f32[2,96,128]{2,1,0:T(8,128)S(1)}) custom-call(f32[3,16,32,256]{3,2,1,0:T(8,128)S(1)} %get-tuple-element.10.tile, f32[32,256]{1,0:T(8,128)S(1)} %broadcast_in_dim.4.zonal, f32[32,256]{1,0:T(8,128)S(1)} %broadcast_in_dim.5.coriolis), custom_call_target="tpu_custom_call" | custom-call | tf_op jit(solution)/shard_map/tendencies/pallas_call | solution.py:377
  11.1 0.0 collective-permute-done.north
  11.1 0.0 collective-permute-done.1.south
  11.1 0.7 seam_rows.1
  11.7 0.0 copy-start.2
  11.8 0.0 copy-start.3
  11.8 7.3 %all-to-all-start = ((f32[32,104,128]{2,1,0:T(8,128)}), f32[32,104,128]{2,1,0:T(8,128)S(1)}, u32[]{:S(2)}, u32[]{:S(2)}) async-start(f32[32,104,128]{2,1,0:T(8,128)} %seam_rows.1), calls=%async_computation | async-start | bytes 3407872 | tf_op jit(solution)/shard_map/all_to_all | solution.py:403
  19.1 24.8 %all-to-all-done = f32[32,104,128]{2,1,0:T(8,128)S(1)} async-done(((f32[32,104,128]{2,1,0:T(8,128)}), f32[32,104,128]{2,1,0:T(8,128)S(1)}, u32[]{:S(2)}, u32[]{:S(2)}) %all-to-all-start) | async-done | bytes 1703968 | tf_op jit(solution)/shard_map/all_to_all | solution.py:403
  43.9 0.0 copy-done.2
  43.9 0.0 copy-done.3
  43.9 3.3 %row_filter.1 = f32[2,16,3,2,16,128]{5,4,3,2,1,0:T(8,128)} custom-call(s32[1]{0:T(128)} %bitcast.own_row, s32[32]{0:T(128)S(1)} %copy-done.2, s32[32]{0:T(128)S(1)} %copy-done.3, f32[32]{0:T(128)S(1)} %get-tuple-element.16.zonal, f32[2,16,104,128]{3,2,1,0:T(8,128)S(1)} %bitcast.4, f32[32,32,32]{2,1,0:T(8,128)} %matrix.1), custom_call_target="tpu_custom_call" | custom-call | tf_op jit(solution)/shard_map/row_filter/pallas_call | solution.py:410
  47.2 0.0 copy-start
  47.3 4.5 %all-to-all-start.1 = ((f32[32,3,2,16,128]{4,3,2,1,0:T(8,128)}), f32[32,3,2,16,128]{4,3,2,1,0:T(8,128)S(1)}, u32[]{:S(2)}, u32[]{:S(2)}) async-start(f32[32,3,2,16,128]{4,3,2,1,0:T(8,128)} %bitcast.5), calls=%async_computation.1 | async-start | bytes 3145728 | tf_op jit(solution)/shard_map/all_to_all | solution.py:438
  51.7 0.0 copy-done
  51.7 0.0 copy-start.1
  51.7 0.1 slice.3
  51.8 0.4 collective-permute-start.2
  52.2 2.4 %collective-permute-done.2.other = f32[2,16,32,256]{3,2,1,0:T(8,128)S(1)} collective-permute-done((f32[2,16,32,256]{3,2,1,0:T(8,128)S(1)}, f32[2,16,32,256]{3,2,1,0:T(8,128)S(1)}, u32[]{:S(2)}, u32[]{:S(2)}) %collective-permute-start.2) | collective-permute-done | bytes 1048608 | tf_op jit(solution)/shard_map/ppermute | solution.py:367
  54.6 0.0 copy-done.1
  54.6 2.5 %base.1 = f32[32,3,2,16,128]{4,3,2,1,0:T(8,128)} custom-call(s32[1]{0:T(128)} %bitcast.3.own_part, f32[3,16,32,256]{3,2,1,0:T(8,128)S(1)} %copy-done, f32[2,16,32,256]{3,2,1,0:T(8,128)S(1)} %collective-permute-done.2.other, f32[32,32,32]{2,1,0:T(8,128)S(1)} %copy-done.1), custom_call_target="tpu_custom_call" | custom-call | tf_op jit(solution)/shard_map/base/pallas_call | solution.py:443
  57.1 18.0 %all-to-all-done.1.step = f32[32,3,2,16,128]{4,3,2,1,0:T(8,128)S(1)} async-done(((f32[32,3,2,16,128]{4,3,2,1,0:T(8,128)}), f32[32,3,2,16,128]{4,3,2,1,0:T(8,128)S(1)}, u32[]{:S(2)}, u32[]{:S(2)}) %all-to-all-start.1) | async-done | bytes 1572896 | tf_op jit(solution)/shard_map/all_to_all | solution.py:438
  75.1 2.3 %finish.1 = f32[3,16,32,256]{3,2,1,0:T(8,128)} custom-call(f32[32,3,2,16,128]{4,3,2,1,0:T(8,128)S(1)} %all-to-all-done.1.step, f32[32,3,2,16,128]{4,3,2,1,0:T(8,128)} %base.1), custom_call_target="tpu_custom_call" | custom-call | tf_op jit(solution)/shard_map/finish/pallas_call | solution.py:460
  (1 shorter events, 0.0 us)
Async XLA Ops:
  1.6 9.5 %collective-permute-start = (f32[48,256]{1,0:T(8,128)S(1)}, f32[48,256]{1,0:T(8,128)S(1)}, u32[]{:S(2)}, u32[]{:S(2)}) collective-permute-start(f32[48,256]{1,0:T(8,128)S(1)} %get-tuple-element.12), channel_id=1, source_target_pairs={{2,0},{4,2},{6,4},{8,6},{10,8},{12,10},{14,12},{3,1},{5,3},{7,5},{... | collective-permute-start | bytes 147464 | tf_op jit(solution)/shard_map/ppermute | solution.py:365
  3.6 7.5 %collective-permute-start.1 = (f32[48,256]{1,0:T(8,128)S(1)}, f32[48,256]{1,0:T(8,128)S(1)}, u32[]{:S(2)}, u32[]{:S(2)}) collective-permute-start(f32[48,256]{1,0:T(8,128)S(1)} %get-tuple-element.13), channel_id=1, source_target_pairs={{0,2},{2,4},{4,6},{6,8},{8,10},{10,12},{12,14},{1,3},{3,5},{5,7},{... | collective-permute-start | bytes 147464 | tf_op jit(solution)/shard_map/ppermute | solution.py:366
  11.7 32.2 %copy-start.2 = (s32[32]{0:T(128)S(1)}, s32[32]{0:T(128)}, u32[]{:S(2)}) copy-start(s32[32]{0:T(128)} %half_width.1) | copy-start | bytes 388
  11.8 32.1 %copy-start.3 = (s32[32]{0:T(128)S(1)}, s32[32]{0:T(128)}, u32[]{:S(2)}) copy-start(s32[32]{0:T(128)} %filter_mask.1) | copy-start | bytes 388
  11.8 32.1 %all-to-all-start = ((f32[32,104,128]{2,1,0:T(8,128)}), f32[32,104,128]{2,1,0:T(8,128)S(1)}, u32[]{:S(2)}, u32[]{:S(2)}) async-start(f32[32,104,128]{2,1,0:T(8,128)} %seam_rows.1), calls=%async_computation | async-start | bytes 3407872 | tf_op jit(solution)/shard_map/all_to_all | solution.py:403
  47.2 4.5 %copy-start = (f32[3,16,32,256]{3,2,1,0:T(8,128)S(1)}, f32[3,16,32,256]{3,2,1,0:T(8,128)}, u32[]{:S(2)}) copy-start(f32[3,16,32,256]{3,2,1,0:T(8,128)} %own.1) | copy-start | bytes 4718596
  47.3 27.8 %all-to-all-start.1 = ((f32[32,3,2,16,128]{4,3,2,1,0:T(8,128)}), f32[32,3,2,16,128]{4,3,2,1,0:T(8,128)S(1)}, u32[]{:S(2)}, u32[]{:S(2)}) async-start(f32[32,3,2,16,128]{4,3,2,1,0:T(8,128)} %bitcast.5), calls=%async_computation.1 | async-start | bytes 3145728 | tf_op jit(solution)/shard_map/all_to_all | solution.py:438
  51.7 2.8 %copy-start.1 = (f32[32,32,32]{2,1,0:T(8,128)S(1)}, f32[32,32,32]{2,1,0:T(8,128)}, u32[]{:S(2)}) copy-start(f32[32,32,32]{2,1,0:T(8,128)} %matrix.1) | copy-start | bytes 393220
  51.8 2.7 %collective-permute-start.2 = (f32[2,16,32,256]{3,2,1,0:T(8,128)S(1)}, f32[2,16,32,256]{3,2,1,0:T(8,128)S(1)}, u32[]{:S(2)}, u32[]{:S(2)}) collective-permute-start(f32[2,16,32,256]{3,2,1,0:T(8,128)S(1)} %slice.3), channel_id=1, source_target_pairs={{0,1},{1,0},{2,3},{3,2},{4,5},{5,4},{6,7},{7,6},{8,9},{9,8},{10,11... | collective-permute-start | bytes 3145736 | tf_op jit(solution)/shard_map/ppermute | solution.py:367

commit v15 on v14

--- a/solution.py
+++ b/solution.py
@@ -1,5 +1,6 @@
 import jax
 import jax.numpy as jnp
+import numpy as np
 from jax import lax
 from jax.experimental import pallas as pl
 from jax.experimental.pallas import tpu as pltpu
@@ -11,13 +12,19 @@
 HALF = 128
 SUBLANES = 8
 VMEM_LIMIT = 32 * 1024 * 1024
-GROUP = 16
+GROUP = 8
 LOADS = 4
 
 
 def latitudes(global_rows, row_total):
     latitude_angle = -0.5 * jnp.pi + (global_rows + 0.5) * jnp.pi / row_total
     return (jnp.cos(latitude_angle), jnp.sin(latitude_angle))
+
+
+def row_factors(row_total):
+    angle = -0.5 * np.pi + (np.arange(row_total) + 0.5) * np.pi / row_total
+    both = np.stack([0.25 / (np.cos(angle) + 0.05), 0.5 * np.sin(angle)], axis=1).astype(np.float32)
+    return np.repeat(both, HALF, axis=1)
 
 
 def flip(tiles):
@@ -34,9 +41,12 @@
     return tiles
 
 
-def fetch_kernel(prog, tile, first, last, sems):
+def fetch_kernel(prog, table, tile, first, last, factors, sems, table_sem):
     fields, levels, rows, _ = prog.shape
     per_load = levels // LOADS
+    own = pl.ds(pl.multiple_of(lax.axis_index("lat") * rows, rows), rows)
+    extra = pltpu.make_async_copy(table.at[own], factors, table_sem)
+    extra.start()
     loads = []
     for f in range(fields):
         for load in range(LOADS):
@@ -50,9 +60,10 @@
             c = f * levels + l
             last[c : c + 1, :] = tile[f, l, rows - 1 : rows, :]
             first[c : c + 1, :] = tile[f, l, 0:1, :]
-
-
-def tendency_kernel(tile, zonal, coriolis, out, ends, stage, sems):
+    extra.wait()
+
+
+def tendency_kernel(tile, factors, out, ends, stage, sems):
     _, levels, rows, width = tile.shape
     chans = 3 * levels
     payload = 2 * chans
@@ -64,7 +75,9 @@
     copies = []
     for j0 in range(0, rows, SUBLANES):
         j1 = j0 + SUBLANES
-        zon, cor = zonal[j0:j1, :], coriolis[j0:j1, :]
+        zon, cor = (
+            jnp.concatenate([factors[j0:j1, at : at + HALF]] * 2, axis=1) for at in (0, HALF)
+        )
         edge_rows = jnp.zeros((SUBLANES, HALF), jnp.float32)
         for l0 in range(0, levels, SUBLANES):
             tends = [[], [], []]
@@ -350,27 +363,26 @@
 
 
     with jax.named_scope("fetch"):
-        tile, first, last = pl.pallas_call(
+        tile, first, last, factors = pl.pallas_call(
             fetch_kernel,
             out_shape=(
                 pltpu.VMEM(prognostic.shape, jnp.float32),
                 pltpu.VMEM((chans, width), jnp.float32),
                 pltpu.VMEM((chans, width), jnp.float32),
+                pltpu.VMEM((rows, 2 * HALF), jnp.float32),
             ),
-            in_specs=[hbm],
-            out_specs=(vmem, vmem, vmem),
-            scratch_shapes=[pltpu.SemaphoreType.DMA((fields, LOADS))],
-            compiler_params=params,
-        )(in_hbm(prognostic))
+            in_specs=[hbm, hbm],
+            out_specs=(vmem,) * 4,
+            scratch_shapes=[pltpu.SemaphoreType.DMA((fields, LOADS)), pltpu.SemaphoreType.DMA],
+            compiler_params=params,
+        )(in_hbm(prognostic), in_hbm(jnp.asarray(row_factors(rows * lat_devices))))
     north = lax.ppermute(first, "lat", [(i + 1, i) for i in range(lat_devices - 1)])
     south = lax.ppermute(last, "lat", [(i, i + 1) for i in range(lat_devices - 1)])
     other = lax.ppermute(prognostic[:2], "lev", [(0, 1), (1, 0)])
 
     global_rows = (lat_index * rows + jnp.arange(rows)).astype(jnp.float32)
-    cosine, sine = latitudes(global_rows, rows * lat_devices)
+    cosine, _ = latitudes(global_rows, rows * lat_devices)
     zonal = 0.25 / (cosine + 0.05)
-    zonal_field = jnp.broadcast_to(zonal[:, None], (rows, width))
-    coriolis_field = jnp.broadcast_to((0.5 * sine)[:, None], (rows, width))
 
     sent_rows = halves * chans + SUBLANES
     with jax.named_scope("tendencies"):
@@ -380,14 +392,14 @@
                 pltpu.HBM((rows, sent_rows, HALF), jnp.float32),
                 pltpu.VMEM((2, halves * chans, HALF), jnp.float32),
             ),
-            in_specs=[vmem, vmem, vmem],
+            in_specs=[vmem, vmem],
             out_specs=(hbm, vmem),
             scratch_shapes=[
                 pltpu.VMEM((rows, sent_rows, HALF), jnp.float32),
                 pltpu.SemaphoreType.DMA((rows // SUBLANES,)),
             ],
             compiler_params=params,
-        )(in_vmem(tile), in_vmem(zonal_field), in_vmem(coriolis_field))
+        )(in_vmem(tile), in_vmem(factors))
 
     with jax.named_scope("seam_rows"):
         tend = pl.pallas_call(

time: 77.8 us -> 77.8 us (level)
  no operation moved by 1% of the time
where the time goes in v15:
time: 77.8 us; the launch traced here: 76.8 us
  waiting for transfers between devices  45.2 us (58%)
  starting transfers between devices  18.8 us (24%)
  Pallas kernels  12.5 us (16%)
    all_to_all x1, waiting for transfers between devices, per_device(): whole_rows = lax.all_to_all(tend, ('lev', 'lon'), 0, 0, tiled=True)  24.7 us
    all_to_all x1, waiting for transfers between devices, per_device(): lax.all_to_all(stepped.reshape((rows,) + stepped_shape[2:]), ('lev', 'lon...  18 us
    all_to_all x1, starting transfers between devices, per_device(): whole_rows = lax.all_to_all(tend, ('lev', 'lon'), 0, 0, tiled=True)  7.33 us
    ppermute x1, starting transfers between devices, per_device(): lax.ppermute(last, 'lat', [(i, i + 1) for i in range(lat_devices - 1)])  5.04 us
    all_to_all x1, starting transfers between devices, per_device(): lax.all_to_all(stepped.reshape((rows,) + stepped_shape[2:]), ('lev', 'lon...  4.11 us
    pallas_call x1, Pallas kernels, per_device(): pl.pallas_call(filter_kernel, out_shape=pltpu.HBM(stepped_shape, jnp.floa...  3.34 us
    pallas_call x1, Pallas kernels, per_device(): pl.pallas_call(base_kernel, out_shape=pltpu.HBM(returned.shape, jnp.float...  2.48 us
    ppermute x1, waiting for transfers between devices, per_device(): other = lax.ppermute(prognostic[:2], 'lev', [(0, 1), (1, 0)])  2.4 us
  transfers between devices with their start and end apart: 5, of which 3 were waited for; matrix products, arithmetic and copies ran while one was open for 0% of the time, Pallas kernels for 6%

profile of v15, /device:TPU:96, one launch (start us, length us, event | category | flops | bytes accessed | tf_op | source)
XLA Modules:
  0.0 76.8 jit_solution(14331951955139340238)
XLA Ops:
  0.0 1.6 %fetch.1 = (f32[3,16,32,256]{3,2,1,0:T(8,128)S(1)}, f32[48,256]{1,0:T(8,128)S(1)}, f32[48,256]{1,0:T(8,128)S(1)}, f32[32,256]{1,0:T(8,128)S(1)}) custom-call(f32[3,16,32,256]{3,2,1,0:T(8,128)} %own.1, f32[256,256]{1,0:T(8,128)} %constant.32.clone.table), custom_call_target="tpu_custom_call" | custom-call | tf_op jit(solution)/shard_map/fetch/pallas_call | solution.py:366
  1.6 2.0 %collective-permute-start = (f32[48,256]{1,0:T(8,128)S(1)}, f32[48,256]{1,0:T(8,128)S(1)}, u32[]{:S(2)}, u32[]{:S(2)}) collective-permute-start(f32[48,256]{1,0:T(8,128)S(1)} %get-tuple-element.14), channel_id=1, source_target_pairs={{2,0},{4,2},{6,4},{8,6},{10,8},{12,10},{14,12},{3,1},{5,3},{7,5},{... | collective-permute-start | bytes 147464 | tf_op jit(solution)/shard_map/ppermute | solution.py:379
  3.6 5.0 %collective-permute-start.1 = (f32[48,256]{1,0:T(8,128)S(1)}, f32[48,256]{1,0:T(8,128)S(1)}, u32[]{:S(2)}, u32[]{:S(2)}) collective-permute-start(f32[48,256]{1,0:T(8,128)S(1)} %get-tuple-element.15), channel_id=1, source_target_pairs={{0,2},{2,4},{4,6},{6,8},{8,10},{10,12},{12,14},{1,3},{3,5},{5,7},{... | collective-permute-start | bytes 147464 | tf_op jit(solution)/shard_map/ppermute | solution.py:380
  8.6 2.2 %tendencies.1 = (f32[32,104,128]{2,1,0:T(8,128)}, f32[2,96,128]{2,1,0:T(8,128)S(1)}) custom-call(f32[3,16,32,256]{3,2,1,0:T(8,128)S(1)} %get-tuple-element.11.tile, f32[32,256]{1,0:T(8,128)S(1)} %get-tuple-element.12.factors), custom_call_target="tpu_custom_call" | custom-call | tf_op jit(solution)/shard_map/tendencies/pallas_call | solution.py:389
  10.8 0.0 collective-permute-done.north
  10.8 0.0 collective-permute-done.1.south
  10.8 0.7 seam_rows.1
  11.5 0.0 copy-start.2
  11.5 0.0 copy-start.3
  11.5 7.3 %all-to-all-start = ((f32[32,104,128]{2,1,0:T(8,128)}), f32[32,104,128]{2,1,0:T(8,128)S(1)}, u32[]{:S(2)}, u32[]{:S(2)}) async-start(f32[32,104,128]{2,1,0:T(8,128)} %seam_rows.1), calls=%async_computation | async-start | bytes 3407872 | tf_op jit(solution)/shard_map/all_to_all | solution.py:415
  18.9 24.7 %all-to-all-done = f32[32,104,128]{2,1,0:T(8,128)S(1)} async-done(((f32[32,104,128]{2,1,0:T(8,128)}), f32[32,104,128]{2,1,0:T(8,128)S(1)}, u32[]{:S(2)}, u32[]{:S(2)}) %all-to-all-start) | async-done | bytes 1703968 | tf_op jit(solution)/shard_map/all_to_all | solution.py:415
  43.6 0.0 copy-done.2
  43.6 0.0 copy-done.3
  43.6 3.3 %row_filter.1 = f32[2,16,3,2,16,128]{5,4,3,2,1,0:T(8,128)} custom-call(s32[1]{0:T(128)} %bitcast.own_row, s32[32]{0:T(128)S(1)} %copy-done.2, s32[32]{0:T(128)S(1)} %copy-done.3, f32[32]{0:T(128)S(1)} %add_divide_fusion.zonal, f32[2,16,104,128]{3,2,1,0:T(8,128)S(1)} %bitcast.4, f32[32,32,32]{2,1,0:T(8,128)} %matrix.1), custom_call_target="tpu_custom_call" | custom-call | tf_op jit(solution)/shard_map/row_filter/pallas_call | solution.py:422
  47.0 0.0 copy-start
  47.0 4.1 %all-to-all-start.1 = ((f32[32,3,2,16,128]{4,3,2,1,0:T(8,128)}), f32[32,3,2,16,128]{4,3,2,1,0:T(8,128)S(1)}, u32[]{:S(2)}, u32[]{:S(2)}) async-start(f32[32,3,2,16,128]{4,3,2,1,0:T(8,128)} %bitcast.5), calls=%async_computation.1 | async-start | bytes 3145728 | tf_op jit(solution)/shard_map/all_to_all | solution.py:450
  51.1 0.0 copy-done
  51.1 0.0 copy-start.1
  51.2 0.1 slice.3
  51.2 0.4 collective-permute-start.2
  51.6 2.4 %collective-permute-done.2.other = f32[2,16,32,256]{3,2,1,0:T(8,128)S(1)} collective-permute-done((f32[2,16,32,256]{3,2,1,0:T(8,128)S(1)}, f32[2,16,32,256]{3,2,1,0:T(8,128)S(1)}, u32[]{:S(2)}, u32[]{:S(2)}) %collective-permute-start.2) | collective-permute-done | bytes 1048608 | tf_op jit(solution)/shard_map/ppermute | solution.py:381
  54.0 0.0 copy-done.1
  54.0 2.5 %base.1 = f32[32,3,2,16,128]{4,3,2,1,0:T(8,128)} custom-call(s32[1]{0:T(128)} %bitcast.3.own_part, f32[3,16,32,256]{3,2,1,0:T(8,128)S(1)} %copy-done, f32[2,16,32,256]{3,2,1,0:T(8,128)S(1)} %collective-permute-done.2.other, f32[32,32,32]{2,1,0:T(8,128)S(1)} %copy-done.1), custom_call_target="tpu_custom_call" | custom-call | tf_op jit(solution)/shard_map/base/pallas_call | solution.py:455
  56.5 18.0 %all-to-all-done.1.step = f32[32,3,2,16,128]{4,3,2,1,0:T(8,128)S(1)} async-done(((f32[32,3,2,16,128]{4,3,2,1,0:T(8,128)}), f32[32,3,2,16,128]{4,3,2,1,0:T(8,128)S(1)}, u32[]{:S(2)}, u32[]{:S(2)}) %all-to-all-start.1) | async-done | bytes 1572896 | tf_op jit(solution)/shard_map/all_to_all | solution.py:450
  74.5 2.3 %finish.1 = f32[3,16,32,256]{3,2,1,0:T(8,128)} custom-call(f32[32,3,2,16,128]{4,3,2,1,0:T(8,128)S(1)} %all-to-all-done.1.step, f32[32,3,2,16,128]{4,3,2,1,0:T(8,128)} %base.1), custom_call_target="tpu_custom_call" | custom-call | tf_op jit(solution)/shard_map/finish/pallas_call | solution.py:472
  (1 shorter events, 0.0 us)
Async XLA Ops:
  1.6 9.2 %collective-permute-start = (f32[48,256]{1,0:T(8,128)S(1)}, f32[48,256]{1,0:T(8,128)S(1)}, u32[]{:S(2)}, u32[]{:S(2)}) collective-permute-start(f32[48,256]{1,0:T(8,128)S(1)} %get-tuple-element.14), channel_id=1, source_target_pairs={{2,0},{4,2},{6,4},{8,6},{10,8},{12,10},{14,12},{3,1},{5,3},{7,5},{... | collective-permute-start | bytes 147464 | tf_op jit(solution)/shard_map/ppermute | solution.py:379
  3.6 7.2 %collective-permute-start.1 = (f32[48,256]{1,0:T(8,128)S(1)}, f32[48,256]{1,0:T(8,128)S(1)}, u32[]{:S(2)}, u32[]{:S(2)}) collective-permute-start(f32[48,256]{1,0:T(8,128)S(1)} %get-tuple-element.15), channel_id=1, source_target_pairs={{0,2},{2,4},{4,6},{6,8},{8,10},{10,12},{12,14},{1,3},{3,5},{5,7},{... | collective-permute-start | bytes 147464 | tf_op jit(solution)/shard_map/ppermute | solution.py:380
  11.5 32.1 %copy-start.2 = (s32[32]{0:T(128)S(1)}, s32[32]{0:T(128)}, u32[]{:S(2)}) copy-start(s32[32]{0:T(128)} %half_width.1) | copy-start | bytes 388
  11.5 32.1 %copy-start.3 = (s32[32]{0:T(128)S(1)}, s32[32]{0:T(128)}, u32[]{:S(2)}) copy-start(s32[32]{0:T(128)} %filter_mask.1) | copy-start | bytes 388
  11.5 32.1 %all-to-all-start = ((f32[32,104,128]{2,1,0:T(8,128)}), f32[32,104,128]{2,1,0:T(8,128)S(1)}, u32[]{:S(2)}, u32[]{:S(2)}) async-start(f32[32,104,128]{2,1,0:T(8,128)} %seam_rows.1), calls=%async_computation | async-start | bytes 3407872 | tf_op jit(solution)/shard_map/all_to_all | solution.py:415
  47.0 4.1 %copy-start = (f32[3,16,32,256]{3,2,1,0:T(8,128)S(1)}, f32[3,16,32,256]{3,2,1,0:T(8,128)}, u32[]{:S(2)}) copy-start(f32[3,16,32,256]{3,2,1,0:T(8,128)} %own.1) | copy-start | bytes 4718596
  47.0 27.5 %all-to-all-start.1 = ((f32[32,3,2,16,128]{4,3,2,1,0:T(8,128)}), f32[32,3,2,16,128]{4,3,2,1,0:T(8,128)S(1)}, u32[]{:S(2)}, u32[]{:S(2)}) async-start(f32[32,3,2,16,128]{4,3,2,1,0:T(8,128)} %bitcast.5), calls=%async_computation.1 | async-start | bytes 3145728 | tf_op jit(solution)/shard_map/all_to_all | solution.py:450
  51.1 2.8 %copy-start.1 = (f32[32,32,32]{2,1,0:T(8,128)S(1)}, f32[32,32,32]{2,1,0:T(8,128)}, u32[]{:S(2)}) copy-start(f32[32,32,32]{2,1,0:T(8,128)} %matrix.1) | copy-start | bytes 393220
  51.2 2.7 %collective-permute-start.2 = (f32[2,16,32,256]{3,2,1,0:T(8,128)S(1)}, f32[2,16,32,256]{3,2,1,0:T(8,128)S(1)}, u32[]{:S(2)}, u32[]{:S(2)}) collective-permute-start(f32[2,16,32,256]{3,2,1,0:T(8,128)S(1)} %slice.3), channel_id=1, source_target_pairs={{0,1},{1,0},{2,3},{3,2},{4,5},{5,4},{6,7},{7,6},{8,9},{9,8},{10,11... | collective-permute-start | bytes 3145736 | tf_op jit(solution)/shard_map/ppermute | solution.py:381

commit v16 on v13

--- a/solution.py
+++ b/solution.py
@@ -12,7 +12,7 @@
 SUBLANES = 8
 VMEM_LIMIT = 32 * 1024 * 1024
 GROUP = 8
-LOADS = 4
+LOADS = 1
 
 
 def latitudes(global_rows, row_total):

time: 78 us -> 77.7 us (level)
  no operation moved by 1% of the time
where the time goes in v16:
time: 77.7 us; the launch traced here: 77 us
  waiting for transfers between devices  45.2 us (58%)
  starting transfers between devices  18.9 us (24%)
  Pallas kernels  12.5 us (16%)
    all_to_all x1, waiting for transfers between devices, per_device(): whole_rows = lax.all_to_all(tend, ('lev', 'lon'), 0, 0, tiled=True)  24.8 us
    all_to_all x1, waiting for transfers between devices, per_device(): lax.all_to_all(stepped.reshape((rows,) + stepped_shape[2:]), ('lev', 'lon...  18 us
    all_to_all x1, starting transfers between devices, per_device(): whole_rows = lax.all_to_all(tend, ('lev', 'lon'), 0, 0, tiled=True)  7.33 us
    ppermute x1, starting transfers between devices, per_device(): lax.ppermute(last, 'lat', [(i, i + 1) for i in range(lat_devices - 1)])  5.04 us
    all_to_all x1, starting transfers between devices, per_device(): lax.all_to_all(stepped.reshape((rows,) + stepped_shape[2:]), ('lev', 'lon...  4.12 us
    pallas_call x1, Pallas kernels, per_device(): pl.pallas_call(filter_kernel, out_shape=pltpu.HBM(stepped_shape, jnp.floa...  3.34 us
    pallas_call x1, Pallas kernels, per_device(): pl.pallas_call(base_kernel, out_shape=pltpu.HBM(returned.shape, jnp.float...  2.5 us
    ppermute x1, waiting for transfers between devices, per_device(): other = lax.ppermute(prognostic[:2], 'lev', [(0, 1), (1, 0)])  2.4 us
  transfers between devices with their start and end apart: 5, of which 3 were waited for; matrix products, arithmetic and copies ran while one was open for 0% of the time, Pallas kernels for 6%

profile of v16, /device:TPU:96, one launch (start us, length us, event | category | flops | bytes accessed | tf_op | source)
XLA Modules:
  0.0 77.0 jit_solution(2544038319630172870)
XLA Ops:
  0.0 1.4 %fetch.1 = (f32[3,16,32,256]{3,2,1,0:T(8,128)S(1)}, f32[48,256]{1,0:T(8,128)S(1)}, f32[48,256]{1,0:T(8,128)S(1)}) custom-call(f32[3,16,32,256]{3,2,1,0:T(8,128)} %own.1), custom_call_target="tpu_custom_call" | custom-call | tf_op jit(solution)/shard_map/fetch/pallas_call | solution.py:349
  1.4 2.0 %collective-permute-start = (f32[48,256]{1,0:T(8,128)S(1)}, f32[48,256]{1,0:T(8,128)S(1)}, u32[]{:S(2)}, u32[]{:S(2)}) collective-permute-start(f32[48,256]{1,0:T(8,128)S(1)} %get-tuple-element.12), channel_id=1, source_target_pairs={{2,0},{4,2},{6,4},{8,6},{10,8},{12,10},{14,12},{3,1},{5,3},{7,5},{... | collective-permute-start | bytes 147464 | tf_op jit(solution)/shard_map/ppermute | solution.py:361
  3.4 5.0 %collective-permute-start.1 = (f32[48,256]{1,0:T(8,128)S(1)}, f32[48,256]{1,0:T(8,128)S(1)}, u32[]{:S(2)}, u32[]{:S(2)}) collective-permute-start(f32[48,256]{1,0:T(8,128)S(1)} %get-tuple-element.13), channel_id=1, source_target_pairs={{0,2},{2,4},{4,6},{6,8},{8,10},{10,12},{12,14},{1,3},{3,5},{5,7},{... | collective-permute-start | bytes 147464 | tf_op jit(solution)/shard_map/ppermute | solution.py:362
  8.5 0.1 broadcast_in_dim.4.zonal
  8.6 0.1 broadcast_in_dim.5.coriolis
  8.7 2.2 %tendencies.1 = (f32[32,104,128]{2,1,0:T(8,128)}, f32[2,96,128]{2,1,0:T(8,128)S(1)}) custom-call(f32[3,16,32,256]{3,2,1,0:T(8,128)S(1)} %get-tuple-element.10.tile, f32[32,256]{1,0:T(8,128)S(1)} %broadcast_in_dim.4.zonal, f32[32,256]{1,0:T(8,128)S(1)} %broadcast_in_dim.5.coriolis), custom_call_target="tpu_custom_call" | custom-call | tf_op jit(solution)/shard_map/tendencies/pallas_call | solution.py:373
  10.9 0.0 collective-permute-done.north
  10.9 0.0 collective-permute-done.1.south
  10.9 0.7 seam_rows.1
  11.6 0.0 copy-start.2
  11.6 0.0 copy-start.3
  11.6 7.3 %all-to-all-start = ((f32[32,104,128]{2,1,0:T(8,128)}), f32[32,104,128]{2,1,0:T(8,128)S(1)}, u32[]{:S(2)}, u32[]{:S(2)}) async-start(f32[32,104,128]{2,1,0:T(8,128)} %seam_rows.1), calls=%async_computation | async-start | bytes 3407872 | tf_op jit(solution)/shard_map/all_to_all | solution.py:399
  19.0 24.8 %all-to-all-done = f32[32,104,128]{2,1,0:T(8,128)S(1)} async-done(((f32[32,104,128]{2,1,0:T(8,128)}), f32[32,104,128]{2,1,0:T(8,128)S(1)}, u32[]{:S(2)}, u32[]{:S(2)}) %all-to-all-start) | async-done | bytes 1703968 | tf_op jit(solution)/shard_map/all_to_all | solution.py:399
  43.7 0.0 copy-done.2
  43.8 0.0 copy-done.3
  43.8 3.3 %row_filter.1 = f32[2,16,3,2,16,128]{5,4,3,2,1,0:T(8,128)} custom-call(s32[1]{0:T(128)} %bitcast.own_row, s32[32]{0:T(128)S(1)} %copy-done.2, s32[32]{0:T(128)S(1)} %copy-done.3, f32[32]{0:T(128)S(1)} %get-tuple-element.16.zonal, f32[2,16,104,128]{3,2,1,0:T(8,128)S(1)} %bitcast.4, f32[32,32,32]{2,1,0:T(8,128)} %matrix.1), custom_call_target="tpu_custom_call" | custom-call | tf_op jit(solution)/shard_map/row_filter/pallas_call | solution.py:406
  47.1 0.0 copy-start
  47.1 4.1 %all-to-all-start.1 = ((f32[32,3,2,16,128]{4,3,2,1,0:T(8,128)}), f32[32,3,2,16,128]{4,3,2,1,0:T(8,128)S(1)}, u32[]{:S(2)}, u32[]{:S(2)}) async-start(f32[32,3,2,16,128]{4,3,2,1,0:T(8,128)} %bitcast.5), calls=%async_computation.1 | async-start | bytes 3145728 | tf_op jit(solution)/shard_map/all_to_all | solution.py:434
  51.2 0.0 copy-done
  51.2 0.0 copy-start.1
  51.3 0.1 slice.3
  51.3 0.4 collective-permute-start.2
  51.7 2.4 %collective-permute-done.2.other = f32[2,16,32,256]{3,2,1,0:T(8,128)S(1)} collective-permute-done((f32[2,16,32,256]{3,2,1,0:T(8,128)S(1)}, f32[2,16,32,256]{3,2,1,0:T(8,128)S(1)}, u32[]{:S(2)}, u32[]{:S(2)}) %collective-permute-start.2) | collective-permute-done | bytes 1048608 | tf_op jit(solution)/shard_map/ppermute | solution.py:363
  54.1 0.0 copy-done.1
  54.1 2.5 %base.1 = f32[32,3,2,16,128]{4,3,2,1,0:T(8,128)} custom-call(s32[1]{0:T(128)} %bitcast.3.own_part, f32[3,16,32,256]{3,2,1,0:T(8,128)S(1)} %copy-done, f32[2,16,32,256]{3,2,1,0:T(8,128)S(1)} %collective-permute-done.2.other, f32[32,32,32]{2,1,0:T(8,128)S(1)} %copy-done.1), custom_call_target="tpu_custom_call" | custom-call | tf_op jit(solution)/shard_map/base/pallas_call | solution.py:439
  56.6 18.0 %all-to-all-done.1.step = f32[32,3,2,16,128]{4,3,2,1,0:T(8,128)S(1)} async-done(((f32[32,3,2,16,128]{4,3,2,1,0:T(8,128)}), f32[32,3,2,16,128]{4,3,2,1,0:T(8,128)S(1)}, u32[]{:S(2)}, u32[]{:S(2)}) %all-to-all-start.1) | async-done | bytes 1572896 | tf_op jit(solution)/shard_map/all_to_all | solution.py:434
  74.6 2.4 %finish.1 = f32[3,16,32,256]{3,2,1,0:T(8,128)} custom-call(f32[32,3,2,16,128]{4,3,2,1,0:T(8,128)S(1)} %all-to-all-done.1.step, f32[32,3,2,16,128]{4,3,2,1,0:T(8,128)} %base.1), custom_call_target="tpu_custom_call" | custom-call | tf_op jit(solution)/shard_map/finish/pallas_call | solution.py:456
  (1 shorter events, 0.0 us)
Async XLA Ops:
  1.4 9.5 %collective-permute-start = (f32[48,256]{1,0:T(8,128)S(1)}, f32[48,256]{1,0:T(8,128)S(1)}, u32[]{:S(2)}, u32[]{:S(2)}) collective-permute-start(f32[48,256]{1,0:T(8,128)S(1)} %get-tuple-element.12), channel_id=1, source_target_pairs={{2,0},{4,2},{6,4},{8,6},{10,8},{12,10},{14,12},{3,1},{5,3},{7,5},{... | collective-permute-start | bytes 147464 | tf_op jit(solution)/shard_map/ppermute | solution.py:361
  3.4 7.5 %collective-permute-start.1 = (f32[48,256]{1,0:T(8,128)S(1)}, f32[48,256]{1,0:T(8,128)S(1)}, u32[]{:S(2)}, u32[]{:S(2)}) collective-permute-start(f32[48,256]{1,0:T(8,128)S(1)} %get-tuple-element.13), channel_id=1, source_target_pairs={{0,2},{2,4},{4,6},{6,8},{8,10},{10,12},{12,14},{1,3},{3,5},{5,7},{... | collective-permute-start | bytes 147464 | tf_op jit(solution)/shard_map/ppermute | solution.py:362
  11.6 32.2 %copy-start.2 = (s32[32]{0:T(128)S(1)}, s32[32]{0:T(128)}, u32[]{:S(2)}) copy-start(s32[32]{0:T(128)} %half_width.1) | copy-start | bytes 388
  11.6 32.1 %copy-start.3 = (s32[32]{0:T(128)S(1)}, s32[32]{0:T(128)}, u32[]{:S(2)}) copy-start(s32[32]{0:T(128)} %filter_mask.1) | copy-start | bytes 388
  11.6 32.1 %all-to-all-start = ((f32[32,104,128]{2,1,0:T(8,128)}), f32[32,104,128]{2,1,0:T(8,128)S(1)}, u32[]{:S(2)}, u32[]{:S(2)}) async-start(f32[32,104,128]{2,1,0:T(8,128)} %seam_rows.1), calls=%async_computation | async-start | bytes 3407872 | tf_op jit(solution)/shard_map/all_to_all | solution.py:399
  47.1 4.1 %copy-start = (f32[3,16,32,256]{3,2,1,0:T(8,128)S(1)}, f32[3,16,32,256]{3,2,1,0:T(8,128)}, u32[]{:S(2)}) copy-start(f32[3,16,32,256]{3,2,1,0:T(8,128)} %own.1) | copy-start | bytes 4718596
  47.1 27.5 %all-to-all-start.1 = ((f32[32,3,2,16,128]{4,3,2,1,0:T(8,128)}), f32[32,3,2,16,128]{4,3,2,1,0:T(8,128)S(1)}, u32[]{:S(2)}, u32[]{:S(2)}) async-start(f32[32,3,2,16,128]{4,3,2,1,0:T(8,128)} %bitcast.5), calls=%async_computation.1 | async-start | bytes 3145728 | tf_op jit(solution)/shard_map/all_to_all | solution.py:434
  51.2 2.8 %copy-start.1 = (f32[32,32,32]{2,1,0:T(8,128)S(1)}, f32[32,32,32]{2,1,0:T(8,128)}, u32[]{:S(2)}) copy-start(f32[32,32,32]{2,1,0:T(8,128)} %matrix.1) | copy-start | bytes 393220
  51.3 2.7 %collective-permute-start.2 = (f32[2,16,32,256]{3,2,1,0:T(8,128)S(1)}, f32[2,16,32,256]{3,2,1,0:T(8,128)S(1)}, u32[]{:S(2)}, u32[]{:S(2)}) collective-permute-start(f32[2,16,32,256]{3,2,1,0:T(8,128)S(1)} %slice.3), channel_id=1, source_target_pairs={{0,1},{1,0},{2,3},{3,2},{4,5},{5,4},{6,7},{7,6},{8,9},{9,8},{10,11... | collective-permute-start | bytes 3145736 | tf_op jit(solution)/shard_map/ppermute | solution.py:363
